TPU v7x, 32 devices: a whole 2x2x4 slice. The times are simulated.
32 devices in a mesh: tm: 8 (over z, x), heads: 4 (over y, core).
Axes of the slice: x: 2, y: 2, z: 4, core: 2. Of those that a mesh axis runs over, the one named last changes fastest.
Arguments:
- slab_tokens: bfloat16 [4096, 3584], P('tm', 'heads'), may hold values from -14 to 14
- memory: bfloat16 [4096, 3584], P('tm', 'heads'), may hold values from -14 to 14
- query_weight: bfloat16 [3584, 3584], P(None, 'heads'), may hold values from -0.09375 to 0.09375
- key_weight: bfloat16 [3584, 512], P(None, 'heads'), may hold values from -0.09375 to 0.09375
- value_weight: bfloat16 [3584, 512], P(None, 'heads'), may hold values from -0.09375 to 0.09375
- query_down: bfloat16 [16, 3584], replicated, may hold values from -0.09375 to 0.09375
- query_up: bfloat16 [16, 3584], P(None, 'heads'), may hold values from -1.5 to 1.5
- value_down: bfloat16 [16, 3584], replicated, may hold values from -0.09375 to 0.09375
- value_up: bfloat16 [16, 512], P(None, 'heads'), may hold values from -1.5 to 1.5
- tag_weight: bfloat16 [3584, 8], P('heads'), may hold values from -0.75 to 0.75
- retrieval: int32 [32, 8], P('tm'), may hold values from 0 to 31, as said below
- boundary: int32 [32], P('tm'), may hold values from 0 to 127
- grad_tags: float32 [4096, 8], P('tm'), may hold values from -0.375 to 0.375
Outputs:
- tag_logits: float32 [4096, 8], P('tm')
- query_down_grad: float32 [16, 3584], P(None, 'heads')
- query_up_grad: float32 [16, 3584], P(None, 'heads')
- value_down_grad: float32 [16, 3584], P(None, 'heads')
- value_up_grad: float32 [16, 512], P(None, 'heads')
Inputs may be any that keep to these rules, and one draw needn't show every extreme that they name: `retrieval`: each row names 8 different memory blocks; the rows of one index of tm name at most 1 different blocks held by any one index of tm.
All inputs are finite; a program needn't handle non-finite values.
Results may differ from a plain program's by a relative error of at most 0.035.
The roundings to bfloat16 on the way count: a program that leaves them out, or rounds other values in their place, can miss the bound.
Values may be sent and summed in bfloat16 or wider, within the bound.
No kernel may reach another device: no remote copies, remote signals or barrier semaphores. Data moves between devices by JAX's collectives and lax.ppermute only.
A program may use at most 128 MiB of HBM per device.

v0:
```python
import jax
import jax.numpy as jnp
from jax import lax
from jax.experimental import pallas as pl
from jax.experimental.pallas import tpu as pltpu
from jax.sharding import PartitionSpec as P

HD = 128
RANK = 16
TOP = 8
BLK = 128
CAP = 1


HIGHEST = lax.Precision.HIGHEST


def attend(query, all_keys, all_values, split_row, out_grad):
    span_count, row_count, query_width = query.shape
    key_count, kv_width = (all_keys.shape[1], all_keys.shape[2])
    kv_heads = kv_width // HD
    group_size = query_width // kv_width
    score_scale = HD ** (-0.5)
    query_heads = query.reshape(span_count, row_count, kv_heads, group_size, HD)
    key_heads = all_keys.reshape(span_count, key_count, kv_heads, HD)
    value_heads = all_values.reshape(span_count, key_count, kv_heads, HD)
    grad_heads = out_grad.reshape(span_count, row_count, kv_heads, group_size, HD)
    scores = (
        jnp.einsum("crngd,cknd->cngrk", query_heads, key_heads, preferred_element_type=jnp.float32)
        * score_scale
    )
    row_ids = jnp.arange(row_count, dtype=jnp.int32)[:, None]
    col_ids = jnp.arange(BLK, dtype=jnp.int32)[None, :]
    edge_at = split_row[:, None, None]
    local_seen = (col_ids <= row_ids) & ((col_ids >= edge_at) | (row_ids < edge_at))
    visible = jnp.concatenate(
        [jnp.ones((span_count, row_count, key_count - BLK), jnp.bool_), local_seen], axis=2
    )
    scores = jnp.where(visible[:, None, None], scores, -jnp.inf)
    row_max = jnp.max(scores, axis=-1, keepdims=True)
    weights = jnp.exp(scores - row_max)
    probs = weights / jnp.sum(weights, axis=-1, keepdims=True)
    probs_low = probs.astype(jnp.bfloat16)
    attended = jnp.einsum(
        "cngrk,cknd->crngd", probs_low, value_heads, preferred_element_type=jnp.float32
    ).astype(jnp.bfloat16)
    prob_grad = jnp.einsum(
        "crngd,cknd->cngrk", grad_heads, value_heads, preferred_element_type=jnp.float32
    )
    row_dot = jnp.sum(grad_heads.astype(jnp.float32) * attended.astype(jnp.float32), axis=-1)
    row_dot = jnp.transpose(row_dot, (0, 2, 3, 1))[..., None]
    score_grad = (probs * (prob_grad - row_dot) * score_scale).astype(jnp.bfloat16)
    query_grad = jnp.einsum(
        "cngrk,cknd->crngd", score_grad, key_heads, preferred_element_type=jnp.float32
    ).astype(jnp.bfloat16)
    value_grad = jnp.einsum(
        "cngrk,crngd->cknd", probs_low, grad_heads, preferred_element_type=jnp.float32
    )
    return (
        attended.reshape(span_count, row_count, query_width),
        query_grad.reshape(span_count, row_count, query_width),
        value_grad.reshape(span_count, key_count, kv_width),
    )


def choose_slots(needed, places):
    slot_ids = jnp.arange(CAP, dtype=jnp.int32)
    return needed[:, None, :] * (places[:, None, :] == slot_ids[None, :, None]).astype(jnp.int32)


def general(
    slab_tokens,
    memory,
    query_weight,
    key_weight,
    value_weight,
    query_down,
    query_up,
    value_down,
    value_up,
    tag_weight,
    retrieval,
    boundary,
    grad_tags,
):
    tok_rows = slab_tokens.shape[0]
    mem_rows = memory.shape[0]
    query_width = query_weight.shape[1]
    kv_width = key_weight.shape[1]
    span_count = tok_rows // BLK
    block_count = mem_rows // BLK
    pair_weight = jnp.concatenate([key_weight, value_weight], 1)
    adapter_pair = jnp.concatenate([query_down, value_down], 0)
    contract_last = (((1,), (1,)), ((), ()))
    contract_first = (((0,), (0,)), ((), ()))
    token_piece = lax.all_gather(slab_tokens, "heads", axis=1, tiled=True)
    memory_piece = lax.all_gather(memory, "heads", axis=1, tiled=True)
    query_acc = jnp.dot(token_piece, query_weight, preferred_element_type=jnp.float32)
    pair_acc = jnp.dot(token_piece, pair_weight, preferred_element_type=jnp.float32)
    low_acc = lax.dot_general(
        token_piece, adapter_pair, contract_last, preferred_element_type=jnp.float32
    )
    memory_acc = jnp.dot(memory_piece, pair_weight, preferred_element_type=jnp.float32)
    memory_low_acc = lax.dot_general(
        memory_piece, adapter_pair[RANK:], contract_last, preferred_element_type=jnp.float32
    )
    query_acc, pair_acc, low_acc, memory_acc, memory_low_acc = (
        query_acc,
        pair_acc,
        low_acc,
        memory_acc,
        memory_low_acc,
    )
    low_tokens = low_acc.astype(jnp.bfloat16)
    low_query = low_tokens[:, :RANK]
    low_value = low_tokens[:, RANK:]
    queries = (query_acc + jnp.dot(low_query, query_up, preferred_element_type=jnp.float32)).astype(
        jnp.bfloat16
    )
    keys_local = pair_acc[:, :kv_width].astype(jnp.bfloat16)
    values_local = (
        pair_acc[:, kv_width:] + jnp.dot(low_value, value_up, preferred_element_type=jnp.float32)
    ).astype(jnp.bfloat16)
    memory_low = memory_low_acc.astype(jnp.bfloat16)
    memory_pair = (
        jnp.concatenate(
            [
                memory_acc[:, :kv_width],
                memory_acc[:, kv_width:]
                + jnp.dot(memory_low, value_up, preferred_element_type=jnp.float32),
            ],
            1,
        )
        .astype(jnp.bfloat16)
        .reshape(block_count, BLK, 2 * kv_width)
    )
    peer_count = lax.axis_size("tm")
    every_block = jnp.arange(peer_count * block_count, dtype=jnp.int32)
    wanted = (
        jnp.any(retrieval.reshape(-1, 1) == every_block[None, :], axis=0)
        .astype(jnp.int32)
        .reshape(peer_count, block_count)
    )
    places = jnp.cumsum(wanted, axis=1) - wanted
    requested = choose_slots(wanted, places)
    asked_for = lax.all_to_all(requested, "tm", split_axis=0, concat_axis=0, tiled=True)
    rows_needed = retrieval // block_count * CAP + jnp.take(places.reshape(-1), retrieval)
    asked_low = asked_for.astype(jnp.bfloat16)
    outgoing = jnp.einsum(
        "rcm,mbw->rcbw", asked_low, memory_pair, preferred_element_type=jnp.float32
    ).astype(jnp.bfloat16)
    fetched = lax.all_to_all(outgoing, "tm", split_axis=0, concat_axis=0, tiled=True)
    slot_rows = fetched.reshape(peer_count * CAP, BLK, 2 * kv_width)
    picked = jnp.take(slot_rows, rows_needed.reshape(-1), axis=0).reshape(
        span_count, TOP * BLK, 2 * kv_width
    )
    all_keys = jnp.concatenate(
        [picked[..., :kv_width], keys_local.reshape(span_count, BLK, kv_width)], 1
    )
    all_values = jnp.concatenate(
        [picked[..., kv_width:], values_local.reshape(span_count, BLK, kv_width)], 1
    )
    attended_grad = lax.dot_general(
        grad_tags, tag_weight.astype(jnp.float32), contract_last, precision=HIGHEST
    ).astype(jnp.bfloat16)
    attended, query_grad, value_grad = attend(
        queries.reshape(span_count, BLK, query_width),
        all_keys,
        all_values,
        boundary,
        attended_grad.reshape(span_count, BLK, query_width),
    )
    attended = attended.reshape(tok_rows, query_width)
    query_grad = query_grad.reshape(tok_rows, query_width)
    logits_out = lax.psum(
        jnp.dot(attended, tag_weight, preferred_element_type=jnp.float32), "heads"
    )
    local_grad = value_grad[:, TOP * BLK :].reshape(tok_rows, kv_width)
    slot_grads = value_grad[:, : TOP * BLK].reshape(span_count * TOP, BLK * kv_width)
    slot_hits = (
        rows_needed.reshape(-1, 1) == jnp.arange(peer_count * CAP, dtype=jnp.int32)[None, :]
    ).astype(jnp.float32)
    grad_buffer = lax.dot_general(slot_hits, slot_grads, contract_first, precision=HIGHEST).reshape(
        peer_count * CAP, BLK, kv_width
    )
    up_wide = value_up.astype(jnp.float32)
    returned = lax.all_to_all(
        grad_buffer.reshape(peer_count, CAP, BLK, kv_width),
        "tm",
        split_axis=0,
        concat_axis=0,
        tiled=True,
    )
    owned_grad = jnp.einsum(
        "rcm,rcbw->mbw", asked_for.astype(jnp.float32), returned, precision=HIGHEST
    ).reshape(mem_rows, kv_width)
    memory_cot = lax.dot_general(up_wide, owned_grad, contract_last, precision=HIGHEST)
    up_memory = lax.dot_general(
        memory_low.astype(jnp.float32), owned_grad, contract_first, precision=HIGHEST
    )
    query_cot = lax.dot_general(
        query_up, query_grad, contract_last, preferred_element_type=jnp.float32
    )
    value_cot = lax.dot_general(up_wide, local_grad, contract_last, precision=HIGHEST)
    query_cot, value_cot, memory_cot = lax.psum((query_cot, value_cot, memory_cot), "heads")
    query_down_grad = jnp.dot(
        query_cot.astype(jnp.bfloat16), slab_tokens, preferred_element_type=jnp.float32
    )
    value_down_grad = jnp.dot(
        value_cot.astype(jnp.bfloat16), slab_tokens, preferred_element_type=jnp.float32
    ) + jnp.dot(memory_cot.astype(jnp.bfloat16), memory, preferred_element_type=jnp.float32)
    query_up_grad = lax.dot_general(
        low_query, query_grad, contract_first, preferred_element_type=jnp.float32
    )
    value_up_grad = (
        lax.dot_general(
            low_value.astype(jnp.float32), local_grad, contract_first, precision=HIGHEST
        )
        + up_memory
    )
    query_down_grad, query_up_grad, value_down_grad, value_up_grad = lax.psum(
        (query_down_grad, query_up_grad, value_down_grad, value_up_grad), "tm"
    )
    return (logits_out, query_down_grad, query_up_grad, value_down_grad, value_up_grad)


LOG2E = 1.4426950408889634
NT = (((1,), (1,)), ((), ()))
PACK = 2 * BLK + RANK
STRIP = 16
PAIR = 2
MIB = 1024 * 1024
FLAG = jax.ShapeDtypeStruct((8, 128), jnp.float32)


def dot_nt(a, b, precision=None):
    return lax.dot_general(a, b, NT, precision=precision, preferred_element_type=jnp.float32)


def dot_nn(a, b, precision=None):
    return jnp.dot(a, b, precision=precision, preferred_element_type=jnp.float32)


def piece_rows(place_ref, j, width):
    return pl.ds(pl.multiple_of(lax.bitwise_xor(place_ref[0], j) * width, width), width)


def start_copies(pairs, sems, first=0):
    copies = [pltpu.make_async_copy(src, dst, sems.at[first + n]) for n, (src, dst) in enumerate(pairs)]
    for copy in copies:
        copy.start()
    return copies


def wait_all(copies):
    for copy in copies:
        copy.wait()


def memory_pieces(place_ref, js, xs, hbm, scratch, sems):
    x_s, wk_s, wv_s, down_s = scratch
    width = x_s.shape[2]
    groups = []
    for n, j in enumerate(js):
        here = piece_rows(place_ref, j, width)
        pairs = [
            (xs[n], x_s.at[n]),
            (hbm[0].at[here, :], wk_s.at[n]),
            (hbm[1].at[here, :], wv_s.at[n]),
            (hbm[2].at[:, here], down_s.at[n]),
        ]
        groups.append(start_copies(pairs, sems, 4 * n))
    return groups


def memory_terms(n, scratch):
    x_s, wk_s, wv_s, down_s = scratch
    x = x_s[n]
    return dot_nn(x, jnp.concatenate([wk_s[n], wv_s[n]], 1)), dot_nt(x, down_s[n])


def memory_early_kernel(place_ref, x0, x1, *refs):
    hbm, acc_ref, low_ref, flag_ref, scratch, sems = refs[:3], refs[4], refs[5], refs[6], refs[7:11], refs[11]
    flag_ref[...] = jnp.zeros_like(flag_ref)
    groups = memory_pieces(place_ref, (0, 1), (x0, x1), hbm, scratch, sems)
    for n in range(2):
        wait_all(groups[n])
        term, low_term = memory_terms(n, scratch)
        if n == 0:
            acc_ref[...] = term
            low_ref[...] = low_term
        else:
            acc_ref[...] += term
            low_ref[...] += low_term


def memory_kernel(first, peers, last, place_ref, asked_ref, x2, x3, acc_hbm, low_hbm, *refs):
    hbm, up_ref, other, out_ref, flag_ref = refs[:3], refs[3], refs[4], refs[5], refs[6]
    scratch, sems, acc_s, low_s, acc_sems = refs[7:11], refs[11], refs[12], refs[13], refs[14]
    at = pl.ds(first, x2.shape[0])
    sums = start_copies([(acc_hbm.at[at, :], acc_s), (low_hbm.at[at, :], low_s)], acc_sems)
    groups = memory_pieces(place_ref, (2, 3), (x2, x3), hbm, scratch, sems)
    flag_ref[...] = jnp.zeros_like(flag_ref)
    wait_all(sums)
    acc = acc_s[...]
    low = low_s[...]
    for n in range(2):
        wait_all(groups[n])
        term, low_term = memory_terms(n, scratch)
        acc = acc + term
        low = low + low_term
    values = (acc[:, HD:] + dot_nn(low.astype(jnp.bfloat16), up_ref[...])).astype(jnp.bfloat16)
    keys = acc[:, :HD].astype(jnp.bfloat16)
    low_t = jnp.transpose(low).astype(jnp.bfloat16)
    if last:
        pair_ref = refs[15]
        offset = other.shape[0]
        pair_ref[:offset] = other[...]
    else:
        pair_ref = out_ref
        offset = 0
    for b in range(acc.shape[0] // BLK):
        at = slice(b * BLK, (b + 1) * BLK)
        pair_ref[offset + b, 0:BLK, :] = keys[at]
        pair_ref[offset + b, BLK : 2 * BLK, :] = values[at]
        pair_ref[offset + b, 2 * BLK : PACK, :] = low_t[:, at]
    if last:
        for r in range(peers):
            out_ref[r] = pair_ref[asked_ref[r]]


WQ_CUTS = 4


def project_pieces(place_ref, js, xs, hbm, scratch, sems):
    wq_hbm, wk_hbm, wv_hbm, qd_hbm, vd_hbm = hbm
    x_s, wq_s, wk_s, wv_s, qd_s, vd_s = scratch
    width = x_s.shape[2]
    part = width // WQ_CUTS
    groups = []
    for n, j in enumerate(js):
        here = piece_rows(place_ref, j, width)
        start = lax.bitwise_xor(place_ref[0], j) * width
        pairs = [(xs[n], x_s.at[n])]
        for m in range(WQ_CUTS):
            rows = pl.ds(pl.multiple_of(start + m * part, part), part)
            pairs.append((wq_hbm.at[rows, :], wq_s.at[n, pl.ds(m * part, part), :]))
        pairs += [
            (wk_hbm.at[here, :], wk_s.at[n]),
            (wv_hbm.at[here, :], wv_s.at[n]),
            (qd_hbm.at[:, here], qd_s.at[n]),
            (vd_hbm.at[:, here], vd_s.at[n]),
        ]
        groups.append(start_copies(pairs, sems, len(pairs) * n))
    return groups


def project_terms(n, scratch):
    x_s, wq_s, wk_s, wv_s, qd_s, vd_s = scratch
    x = x_s[n]
    return (
        dot_nn(x, wq_s[n]),
        dot_nn(x, jnp.concatenate([wk_s[n], wv_s[n]], 1)),
        dot_nt(x, jnp.concatenate([qd_s[n], vd_s[n]], 0)),
    )


def project_early_kernel(place_ref, x0, x1, *refs):
    hbm, outs, flag_ref, scratch, sems = refs[:5], refs[7:10], refs[10], refs[11:17], refs[17]
    flag_ref[...] = jnp.zeros_like(flag_ref)
    groups = project_pieces(place_ref, (0, 1), (x0, x1), hbm, scratch, sems)
    for n in range(2):
        wait_all(groups[n])
        for ref, term in zip(outs, project_terms(n, scratch)):
            if n == 0:
                ref[...] = term
            else:
                ref[...] += term


def project_kernel(first, place_ref, x2, x3, *refs):
    hbm, early, (qup_ref, vup_ref) = refs[:5], refs[5:8], refs[8:10]
    q_ref, k_ref, v_ref, low_ref = refs[10:14]
    scratch, sems, sum_refs, sum_sems = refs[14:20], refs[20], refs[21:24], refs[24]
    groups = project_pieces(place_ref, (2, 3), (x2, x3), hbm, scratch, sems)
    at = pl.ds(first, x2.shape[0])
    loads = start_copies([(src.at[at, :], dst) for src, dst in zip(early, sum_refs)], sum_sems)
    for n in range(2):
        wait_all(groups[n])
        if n == 0:
            wait_all(loads)
            sums = [ref[...] for ref in sum_refs]
        sums = [a + b for a, b in zip(sums, project_terms(n, scratch))]
    q_acc, kv_acc, low_acc = sums
    low = low_acc.astype(jnp.bfloat16)
    q_ref[...] = (q_acc + dot_nn(low[:, :RANK], qup_ref[...])).astype(jnp.bfloat16)
    k_ref[...] = kv_acc[:, :HD].astype(jnp.bfloat16)
    v_ref[...] = (kv_acc[:, HD:] + dot_nn(low[:, RANK:], vup_ref[...])).astype(jnp.bfloat16)
    low_ref[...] = jnp.transpose(low_acc).astype(jnp.bfloat16)


def attention_kernel(cuts, peers, heads, bound_ref, *refs):
    parts = refs[: 4 * cuts]
    got, grad_hbm, grad_t_hbm, qup_ref, vup_ref, tag_ref, cot_ref, up_ref, mcot_ref = refs[4 * cuts : 4 * cuts + 9]
    (q_s, k_own, v_own, low_s, low_m_s, grad_ref, grad_t_ref, k_all, v_all, kt_all, vt_all, kt_own, vt_own, bias_s, s_s, e_s, dp_s,
     p_s, ds_s, att_s, dq_s, dv_s, sems) = refs[4 * cuts + 9 :]
    seen = peers * BLK
    pairs = []
    for b in range(peers):
        at = slice(b * BLK, (b + 1) * BLK)
        pairs.append((got.at[b, pl.ds(0, BLK), :], k_all.at[at, :]))
        pairs.append((got.at[b, pl.ds(BLK, BLK), :], v_all.at[at, :]))
        pairs.append((got.at[b, pl.ds(2 * BLK, RANK), :], low_m_s.at[b]))
    for t in range(cuts):
        q_c, k_c, v_c, low_c = parts[4 * t : 4 * t + 4]
        rows = q_c.shape[0]
        at = slice(t * rows, (t + 1) * rows)
        pairs += [(q_c, q_s.at[at, :]), (k_c, k_own.at[at, :]), (v_c, v_own.at[at, :]), (low_c, low_s.at[:, at])]
    pairs += [(grad_hbm, grad_ref), (grad_t_hbm, grad_t_ref)]
    copies = start_copies(pairs, sems)
    wait_all(copies[: 3 * peers])
    for b in range(peers):
        at = slice(b * BLK, (b + 1) * BLK)
        kt_all[:, at] = jnp.transpose(k_all[at, :])
        vt_all[:, at] = jnp.transpose(v_all[at, :])
    wait_all(copies[3 * peers :])
    dv_s[...] = jnp.zeros_like(dv_s)
    up_ref[...] = jnp.zeros_like(up_ref)
    scale = HD ** (-0.5)
    up_wide = vup_ref[...].astype(jnp.float32)
    query_width = heads * HD

    def pair_step(c, carry):
        base = c * (PAIR * BLK)
        rows = pl.ds(pl.multiple_of(base, PAIR * BLK), PAIR * BLK)
        own_rows = [pl.ds(pl.multiple_of(base + b * BLK, BLK), BLK) for b in range(PAIR)]
        row_ids = lax.broadcasted_iota(jnp.int32, (BLK, BLK), 0)
        col_ids = lax.broadcasted_iota(jnp.int32, (BLK, BLK), 1)
        for b in range(PAIR):
            kt_own[:, b * BLK : (b + 1) * BLK] = jnp.transpose(k_own[own_rows[b], :])
            vt_own[:, b * BLK : (b + 1) * BLK] = jnp.transpose(v_own[own_rows[b], :])
            edge = bound_ref[c * PAIR + b]
            visible = (col_ids <= row_ids) & ((col_ids >= edge) | (row_ids < edge))
            bias_s[b * BLK : (b + 1) * BLK, :] = jnp.where(visible, 0.0, -jnp.inf)

        def head_cols(h):
            return slice(h * HD, (h + 1) * HD)

        def times_keys(out_ref, left_ref, h, all_t, own_t):
            out_ref[:, :seen] = dot_nn(left_ref[rows, head_cols(h)], all_t[...])
            for b in range(PAIR):
                at = slice(b * BLK, (b + 1) * BLK)
                out_ref[at, seen:] = dot_nn(left_ref[own_rows[b], head_cols(h)], own_t[:, at])

        def over_keys(left_ref, first, all_ref, own_ref):
            whole = dot_nn(left_ref[first : first + PAIR * BLK, :seen], all_ref[...])
            mine = [
                dot_nn(left_ref[first + b * BLK : first + (b + 1) * BLK, seen:], own_ref[own_rows[b], :])
                for b in range(PAIR)
            ]
            return (whole + jnp.concatenate(mine, 0)).astype(jnp.bfloat16)

        def scores(h):
            times_keys(s_s.at[h % 2], q_s, h, kt_all, kt_own)

        def prob_grads(h):
            times_keys(dp_s.at[h % 3], grad_ref, h, vt_all, vt_own)

        def softmax(h):
            for r in range(0, PAIR * BLK, STRIP):
                at = slice(r, r + STRIP)
                s = s_s[h % 2, at, :]
                s = jnp.concatenate([s[:, :seen], s[:, seen:] + bias_s[at, :]], 1) * (scale * LOG2E)
                w = jnp.exp2(s - jnp.max(s, axis=1, keepdims=True))
                probs = w * (1.0 / jnp.sum(w, axis=1, keepdims=True))
                e_s[h % 2, at, :] = probs
                first = h * PAIR * BLK + r
                p_s[first : first + STRIP, :] = probs.astype(jnp.bfloat16)

        def attend_head(h):
            att_s[:, head_cols(h)] = over_keys(p_s, h * PAIR * BLK, v_all, v_own)

        def score_grads(h):
            for r in range(0, PAIR * BLK, STRIP):
                at = slice(r, r + STRIP)
                g = grad_ref[pl.ds(pl.multiple_of(base + r, STRIP), STRIP), head_cols(h)]
                dot = jnp.sum(
                    g.astype(jnp.float32) * att_s[at, head_cols(h)].astype(jnp.float32), axis=1, keepdims=True
                )
                ds_s[h % 2, at, :] = (e_s[h % 2, at, :] * ((dp_s[h % 3, at, :] - dot) * scale)).astype(jnp.bfloat16)
            dq_s[:, head_cols(h)] = over_keys(ds_s.at[h % 2], 0, k_all, k_own)

        scores(0)
        prob_grads(0)
        for h in range(heads + 1):
            if h < heads:
                softmax(h)
            if h + 1 < heads:
                scores(h + 1)
                prob_grads(h + 1)
            if h > 0:
                score_grads(h - 1)
            if h < heads:
                attend_head(h)
        g_t = jnp.concatenate([grad_t_ref[h * HD : (h + 1) * HD, rows] for h in range(heads)], 1)
        dv_s[...] += dot_nn(g_t, p_s[:, :seen])
        dv_own = []
        for b in range(PAIR):
            g_b = jnp.concatenate([grad_t_ref[h * HD : (h + 1) * HD, own_rows[b]] for h in range(heads)], 1)
            starts = [(h * PAIR + b) * BLK for h in range(heads)]
            p_b = jnp.concatenate([p_s[n : n + BLK, seen:] for n in starts], 0)
            dv_own.append(dot_nn(g_b, p_b))
        dv_own = jnp.concatenate(dv_own, 1)
        dq = dq_s[...]
        cot_ref[0:RANK, rows] = dot_nt(qup_ref[...], dq)
        cot_ref[RANK : 2 * RANK, rows] = dot_nn(up_wide, dv_own, HIGHEST)
        cot_ref[2 * RANK :, rows] = dot_nt(tag_ref[...], att_s[...])
        up_ref[:, :query_width] += dot_nn(low_s[0:RANK, rows], dq)
        up_ref[:, query_width:] += dot_nt(low_s[RANK:, rows].astype(jnp.float32), dv_own, HIGHEST)
        return carry

    lax.fori_loop(0, q_s.shape[0] // (PAIR * BLK), pair_step, 0)
    dv = dv_s[...]
    mcot = dot_nn(up_wide, dv, HIGHEST)
    low_m = jnp.concatenate([low_m_s[b] for b in range(peers)], 1).astype(jnp.float32)
    up_ref[:, query_width:] += dot_nt(low_m, dv, HIGHEST)
    for b in range(peers):
        mcot_ref[b] = mcot[:, b * BLK : (b + 1) * BLK]


def own_kernel(peers, asked_ref, back_ref, out_ref, sum_s):
    sum_s[...] = jnp.zeros_like(sum_s)
    for r in range(peers):
        block = asked_ref[r]
        sum_s[block] = sum_s[block] + back_ref[r]
    out_ref[...] = jnp.concatenate([sum_s[m] for m in range(sum_s.shape[0])], 1)


def first_down_kernel(c0, c1, c2, c3, slab_ref, up_ref, dep_ref, logit_ref, query_ref, value_ref):
    cot = (c0[...] + c1[...]) + (c2[...] + c3[...])
    logit_ref[...] = cot[2 * RANK :]
    both = dot_nn(cot[: 2 * RANK].astype(jnp.bfloat16), slab_ref[...])
    width = both.shape[1]
    query_ref[:, :width] = both[:RANK]
    query_ref[:, width:] = up_ref[...]
    value_ref[...] = both[RANK:]


def second_down_kernel(c0, c1, c2, c3, memory_ref, value_ref, out_ref):
    cot = (c0[...] + c1[...]) + (c2[...] + c3[...])
    out_ref[...] = value_ref[...] + dot_nn(cot.astype(jnp.bfloat16), memory_ref[...])


def finish_kernel(q0, q1, v0, v1, query_down_ref, query_up_ref, value_down_ref, value_up_ref):
    query = q0[...] + q1[...]
    value_down_ref[...] = v0[...] + v1[...]
    at = 0
    for out_ref in (query_down_ref, query_up_ref, value_up_ref):
        out_ref[...] = query[:, at : at + out_ref.shape[1]]
        at += out_ref.shape[1]


def swap(x, bit, axis="heads"):
    return lax.ppermute(x, axis, [(i, i ^ bit) for i in range(lax.axis_size(axis))])


def split_after(x, cuts, *deps):
    rows = x.shape[0] // cuts
    half = rows // 2

    def body(x_ref, *refs):
        outs, flag_ref, sems = refs[len(deps) : len(deps) + cuts], refs[len(deps) + cuts], refs[-1]
        pairs = [
            (x_ref.at[pl.ds(n * rows + m * half, half), :], outs[n].at[pl.ds(m * half, half), :])
            for n in range(cuts)
            for m in range(2)
        ]
        copies = start_copies(pairs, sems)
        flag_ref[...] = jnp.zeros_like(flag_ref)
        wait_all(copies)

    part = jax.ShapeDtypeStruct((rows, x.shape[1]), x.dtype)
    *parts, flag = pl.pallas_call(
        body,
        out_shape=[part] * cuts + [FLAG],
        in_specs=[hbm()] + [anywhere()] * len(deps),
        out_specs=[anywhere()] * cuts + [vmem()],
        scratch_shapes=[pltpu.SemaphoreType.DMA((2 * cuts,))],
        name="split_rows",
    )(x, *deps)
    return parts, flag


def grad_kernel(tag_ref, grad_tags_ref, grad_ref, grad_t_ref, flag_ref):
    first = (((0,), (0,)), ((), ()))
    tag = tag_ref[...].astype(jnp.float32)
    grad_tags = grad_tags_ref[...]
    f32 = jnp.float32
    grad_ref[...] = lax.dot_general(
        grad_tags, tag, first, precision=HIGHEST, preferred_element_type=f32
    ).astype(jnp.bfloat16)
    grad_t_ref[...] = lax.dot_general(
        tag, grad_tags, first, precision=HIGHEST, preferred_element_type=f32
    ).astype(jnp.bfloat16)
    flag_ref[...] = jnp.zeros_like(flag_ref)


def after(x, dep):
    return pl.pallas_call(
        lambda x_ref, dep_ref, out_ref: None,
        out_shape=jax.ShapeDtypeStruct(x.shape, x.dtype),
        in_specs=[anywhere(), anywhere()],
        out_specs=anywhere(),
        input_output_aliases={0: 0},
        name="in_order",
    )(x, dep)


def anywhere():
    return pl.BlockSpec(memory_space=pl.ANY)


def hbm():
    return pl.BlockSpec(memory_space=pltpu.HBM)


def smem():
    return pl.BlockSpec(memory_space=pltpu.SMEM)


def vmem():
    return pl.BlockSpec(memory_space=pltpu.VMEM)


def shaped(*shape, dtype=jnp.float32):
    return jax.ShapeDtypeStruct(shape, dtype)


def run(body, name, out_shape, in_specs, scratch=(), flops=0, moved=0, room=8):
    many = isinstance(out_shape, (tuple, list))
    return pl.pallas_call(
        body,
        out_shape=out_shape,
        in_specs=in_specs,
        out_specs=tuple(vmem() for _ in out_shape) if many else vmem(),
        scratch_shapes=list(scratch),
        compiler_params=pltpu.CompilerParams(vmem_limit_bytes=room * MIB),
        cost_estimate=pl.CostEstimate(flops=flops, bytes_accessed=moved, transcendentals=0),
        name=name,
    )


def fast(
    slab_tokens,
    memory,
    query_weight,
    key_weight,
    value_weight,
    query_down,
    query_up,
    value_down,
    value_up,
    tag_weight,
    retrieval,
    boundary,
    grad_tags,
):
    tok_rows, width = slab_tokens.shape
    mem_rows = memory.shape[0]
    query_width = query_weight.shape[1]
    heads = query_width // HD
    spans = tok_rows // BLK
    blocks = mem_rows // BLK
    peers = lax.axis_size("tm")
    f32 = jnp.float32
    bf16 = jnp.bfloat16
    mem_cuts, tok_cuts = 2, 2

    def memory_scratch(rows):
        return [
            pltpu.VMEM((2, rows, width), bf16),
            pltpu.VMEM((2, width, HD), bf16),
            pltpu.VMEM((2, width, HD), bf16),
            pltpu.VMEM((2, RANK, width), bf16),
            pltpu.SemaphoreType.DMA((8,)),
        ]

    def project_scratch(rows):
        return [
            pltpu.VMEM((2, rows, width), bf16),
            pltpu.VMEM((2, width, query_width), bf16),
            pltpu.VMEM((2, width, HD), bf16),
            pltpu.VMEM((2, width, HD), bf16),
            pltpu.VMEM((2, RANK, width), bf16),
            pltpu.VMEM((2, RANK, width), bf16),
            pltpu.SemaphoreType.DMA((2 * (WQ_CUTS + 5),)),
        ]

    named = retrieval[0]
    owner_ids = jnp.arange(peers, dtype=jnp.int32)
    wanted = jnp.sum(
        jnp.where(named[None, :] // blocks == owner_ids[:, None], named[None, :] % blocks, 0), axis=1
    ).astype(jnp.int32)
    place = lax.axis_index("heads").astype(jnp.int32).reshape(1)
    tag_t = tag_weight.T
    tags = tag_t.shape[0]

    mem_split, split_flag = split_after(memory, mem_cuts)
    mem_far = [swap(m, 2) for m in mem_split]
    mem_near = swap(memory, 1)
    tok_near = swap(slab_tokens, 1)
    grad, grad_t, grad_flag = run(
        grad_kernel,
        "attended_cotangent",
        (shaped(tok_rows, query_width, dtype=bf16), shaped(query_width, tok_rows, dtype=bf16), FLAG),
        [vmem()] * 2,
        room=10,
    )(tag_t, grad_tags.T)
    mem_acc, mem_low, mem_flag = run(
        memory_early_kernel,
        "memory_near_half",
        (shaped(mem_rows, 2 * HD), shaped(mem_rows, RANK), FLAG),
        [smem(), hbm(), anywhere()] + [hbm()] * 3 + [anywhere()],
        memory_scratch(mem_rows),
        room=14,
    )(place, memory, mem_near, key_weight, value_weight, value_down, grad_flag)
    asked = lax.all_to_all(after(wanted, mem_flag), "tm", split_axis=0, concat_axis=0, tiled=True)
    tok_split, _ = split_after(slab_tokens, tok_cuts, split_flag)
    tok_far = [swap(x, 2) for x in tok_split]

    rows = tok_rows // tok_cuts
    weights = (query_weight, key_weight, value_weight, query_down, value_down)
    *early, early_flag = run(
        project_early_kernel,
        "project_near_half",
        (shaped(tok_rows, query_width), shaped(tok_rows, 2 * HD), shaped(tok_rows, 2 * RANK), FLAG),
        [smem(), hbm(), anywhere()] + [hbm()] * 5 + [anywhere()] * 2,
        project_scratch(tok_rows),
        room=24,
    )(place, slab_tokens, tok_near, *weights, mem_flag, asked)
    mem_far = [mem_far[0]] + [after(m, early_flag) for m in mem_far[1:]]
    mem_cross = [swap(m, 1) for m in mem_far]
    cut_rows = mem_rows // mem_cuts
    before = []
    for t in range(mem_cuts):
        last = t == mem_cuts - 1
        scratch = memory_scratch(cut_rows) + [
            pltpu.VMEM((cut_rows, 2 * HD), f32),
            pltpu.VMEM((cut_rows, RANK), f32),
            pltpu.SemaphoreType.DMA((2,)),
        ]
        if last:
            other = jnp.concatenate(before, 0) if len(before) > 1 else before[0]
            out_shape = shaped(peers, PACK, HD, dtype=bf16)
            scratch.append(pltpu.VMEM((blocks, PACK, HD), bf16))
        else:
            other = early_flag
            out_shape = shaped(cut_rows // BLK, PACK, HD, dtype=bf16)
        result, pair_flag = run(
            lambda *refs, t=t, last=last: memory_kernel(t * cut_rows, peers, last, *refs),
            "memory_pairs",
            (out_shape, FLAG),
            [smem()] * 2 + [anywhere()] * 4 + [hbm()] * 3 + [vmem()] * 2,
            scratch,
            room=14,
        )(
            place, asked if last else place, mem_far[t], mem_cross[t], mem_acc, mem_low,
            key_weight, value_weight, value_down, value_up, other,
        )
        before.append(result)
    got = lax.all_to_all(before[-1], "tm", split_axis=0, concat_axis=0, tiled=True)

    tok_far = [after(x, pair_flag) for x in tok_far]
    tok_cross = [swap(x, 1) for x in tok_far]
    parts = []
    for t in range(tok_cuts):
        parts += run(
            lambda *refs, t=t: project_kernel(t * rows, *refs),
            "project_far_half",
            (
                shaped(rows, query_width, dtype=bf16),
                shaped(rows, HD, dtype=bf16),
                shaped(rows, HD, dtype=bf16),
                shaped(2 * RANK, rows, dtype=bf16),
            ),
            [smem()] + [anywhere()] * 2 + [hbm()] * 5 + [anywhere()] * 3 + [vmem()] * 2,
            project_scratch(rows)
            + [
                pltpu.VMEM((rows, query_width), f32),
                pltpu.VMEM((rows, 2 * HD), f32),
                pltpu.VMEM((rows, 2 * RANK), f32),
                pltpu.SemaphoreType.DMA((3,)),
            ],
            flops=2 * rows * 2 * width * (query_width + 3 * HD),
            moved=4 * width * (rows + query_width + 3 * HD),
            room=24,
        )(place, tok_far[t], tok_cross[t], *weights, *early, query_up, value_up)

    seen = peers * BLK
    total = seen + BLK
    cot, ups, mcot = run(
        lambda *refs: attention_kernel(tok_cuts, peers, heads, *refs),
        "span_attention",
        (shaped(2 * RANK + tags, tok_rows), shaped(RANK, query_width + HD), shaped(peers, RANK, BLK)),
        [smem()] + [anywhere()] * (4 * tok_cuts + 3) + [vmem()] * 3,
        [
            pltpu.VMEM((tok_rows, query_width), bf16),
            pltpu.VMEM((tok_rows, HD), bf16),
            pltpu.VMEM((tok_rows, HD), bf16),
            pltpu.VMEM((2 * RANK, tok_rows), bf16),
            pltpu.VMEM((peers, RANK, BLK), bf16),
            pltpu.VMEM((tok_rows, query_width), bf16),
            pltpu.VMEM((query_width, tok_rows), bf16),
            pltpu.VMEM((seen, HD), bf16),
            pltpu.VMEM((seen, HD), bf16),
            pltpu.VMEM((HD, seen), bf16),
            pltpu.VMEM((HD, seen), bf16),
            pltpu.VMEM((HD, PAIR * BLK), bf16),
            pltpu.VMEM((HD, PAIR * BLK), bf16),
            pltpu.VMEM((PAIR * BLK, BLK), f32),
            pltpu.VMEM((2, PAIR * BLK, total), f32),
            pltpu.VMEM((2, PAIR * BLK, total), f32),
            pltpu.VMEM((3, PAIR * BLK, total), f32),
            pltpu.VMEM((heads * PAIR * BLK, total), bf16),
            pltpu.VMEM((2, PAIR * BLK, total), bf16),
            pltpu.VMEM((PAIR * BLK, query_width), bf16),
            pltpu.VMEM((PAIR * BLK, query_width), bf16),
            pltpu.VMEM((HD, seen), f32),
            pltpu.SemaphoreType.DMA((3 * peers + 4 * tok_cuts + 2,)),
        ],
        flops=20 * tok_rows * query_width * total,
        moved=4 * tok_rows * query_width,
        room=34,
    )(boundary, *parts, got, grad, grad_t, query_up, value_up, tag_t)

    back = lax.all_to_all(mcot, "tm", split_axis=0, concat_axis=0, tiled=True)
    cots = [cot] + [swap(cot, d) for d in range(1, 4)]
    own = run(
        lambda *refs: own_kernel(peers, *refs),
        "owned_cotangent",
        shaped(RANK, mem_rows),
        [smem()] + [vmem()],
        [pltpu.VMEM((blocks, RANK, BLK), f32)],
    )(asked, back)
    logits, query_sum, value_part = run(
        first_down_kernel,
        "first_down",
        (shaped(tags, tok_rows), shaped(RANK, width + ups.shape[1]), shaped(RANK, width)),
        [vmem()] * 6 + [anywhere()],
        flops=4 * RANK * tok_rows * width,
        moved=2 * tok_rows * width,
    )(*cots, slab_tokens, ups, own)
    owns = [own] + [swap(own, d) for d in range(1, 4)]
    value_sum = run(
        second_down_kernel,
        "second_down",
        shaped(RANK, width),
        [vmem()] * 6,
        flops=2 * RANK * mem_rows * width,
        moved=2 * mem_rows * width,
    )(*owns, memory, value_part)
    for bit in (1, 2):
        query_sum = query_sum + swap(query_sum, bit, "tm")
        value_sum = value_sum + swap(value_sum, bit, "tm")
    query_down_grad, query_up_grad, value_down_grad, value_up_grad = run(
        finish_kernel,
        "finish_outputs",
        (shaped(RANK, width), shaped(RANK, query_width), shaped(RANK, width), shaped(RANK, HD)),
        [vmem()] * 4,
    )(query_sum, swap(query_sum, 4, "tm"), value_sum, swap(value_sum, 4, "tm"))
    return (logits.T, query_down_grad, query_up_grad, value_down_grad, value_up_grad)


def solution(mesh):
    in_specs = (
        P("tm", "heads"),
        P("tm", "heads"),
        P(None, "heads"),
        P(None, "heads"),
        P(None, "heads"),
        P(),
        P(None, "heads"),
        P(),
        P(None, "heads"),
        P("heads", None),
        P("tm", None),
        P("tm"),
        P("tm", None),
    )
    out_specs = (
        P("tm", None),
        P(None, "heads"),
        P(None, "heads"),
        P(None, "heads"),
        P(None, "heads"),
    )
    fits = mesh.shape["heads"] == 4 and mesh.shape["tm"] == 8 == TOP * CAP
    local = fast if fits else general
    return jax.shard_map(local, mesh=mesh, in_specs=in_specs, out_specs=out_specs, check_vma=False)
```

profile of v0, /device:TPU:0, one launch (start us, length us, event | category | flops | bytes accessed | tf_op | source)
XLA Modules:
  0.0 225.7 jit_solution(150573471507519562)
XLA Ops:
  1.2 29.5 %split_rows.2 = (bf16[256,896]{1,0:T(8,128)(2,1)}, bf16[256,896]{1,0:T(8,128)(2,1)}, f32[8,128]{1,0:T(8,128)}) custom-call(bf16[512,896]{1,0:T(8,128)(2,1)} %memory_ref.1), custom_call_target="tpu_custom_call" | custom-call | tf_op jit(solution)/shard_map/split_rows/pallas_call | solution.py:583
  30.8 3.0 %collective-permute-start.5 = (bf16[256,896]{1,0:T(8,128)(2,1)}, bf16[256,896]{1,0:T(8,128)(2,1)}, u32[]{:S(2)}, u32[]{:S(2)}) collective-permute-start(bf16[256,896]{1,0:T(8,128)(2,1)} %get-tuple-element.49), channel_id=1, source_target_pairs={{0,2},{1,3},{2,0},{3,1},{4,6},{5,7},{6,4},{7,5},{8,10},{9,11},{10,... | collective-permute-start | bytes 1376264 | tf_op jit(solution)/shard_map/ppermute | solution.py:564
  33.8 0.7 copy-done.34
  35.3 3.0 %attended_cotangent.1 = (bf16[512,896]{1,0:T(8,128)(2,1)S(1)}, bf16[896,512]{1,0:T(8,128)(2,1)S(1)}, f32[8,128]{1,0:T(8,128)S(1)}) custom-call(bf16[8,896]{1,0:T(8,128)(2,1)S(1)} %bitcast.10, f32[8,512]{1,0:T(8,128)S(1)} %bitcast.9), custom_call_target="tpu_custom_call" | custom-call | tf_op jit(solution)/shard_map/attended_cotangent/pallas_call | solution.py:712
  38.3 0.9 copy-done.39
  39.3 0.9 copy-done.41
  41.5 0.9 copy-done.26
  42.5 1.2 copy-done.2
  43.7 1.2 copy-done.5
  44.8 1.2 copy-done.10
  46.0 0.9 copy-done.14
  46.9 1.2 copy-done.27
  48.1 3.2 %memory_near_half.1 = (f32[512,256]{1,0:T(8,128)S(1)}, f32[512,16]{1,0:T(8,128)S(1)}, f32[8,128]{1,0:T(8,128)S(1)}) custom-call(s32[1]{0:T(128)} %bitcast.place_ref.refs_0_.refs_1_, bf16[512,896]{1,0:T(8,128)(2,1)S(1)} %copy-done.10, bf16[512,896]{1,0:T(8,128)(2,1)S(1)} %copy-done.27, bf16[3584,128]{1,0:T(8,128)(2,1)S(1)} %copy-done.2, ...), custom_call_target="tpu_custom_call" | custom-call | tf_op jit(solution)/shard_map/memory_near_half/pallas_call | solution.py:719
  51.3 0.7 copy-done.21
  52.6 1.3 copy.24
  53.9 6.2 %all-to-all-start = ((s32[8,1,1]{2,1,0:T(1,128)}), s32[8,1,1]{2,1,0:T(1,128)S(1)}, u32[]{:S(2)}, u32[]{:S(2)}) async-start(s32[8,1,1]{2,1,0:T(1,128)} %copy.24), calls=%async_computation | async-start | bytes 8192 | tf_op jit(solution)/shard_map/all_to_all | solution.py:727
  60.2 6.3 %all-to-all-done = s32[8,1,1]{2,1,0:T(1,128)S(1)} async-done(((s32[8,1,1]{2,1,0:T(1,128)}), s32[8,1,1]{2,1,0:T(1,128)S(1)}, u32[]{:S(2)}, u32[]{:S(2)}) %all-to-all-start) | async-done | bytes 64 | tf_op jit(solution)/shard_map/all_to_all | solution.py:727
  66.8 2.8 %copy-done = bf16[3584,896]{1,0:T(8,128)(2,1)S(1)} copy-done((bf16[3584,896]{1,0:T(8,128)(2,1)S(1)}, bf16[3584,896]{1,0:T(8,128)(2,1)}, u32[]{:S(2)}) %copy-start) | copy-done | bytes 6422552
  69.6 1.2 copy-done.3
  70.8 1.2 copy-done.6
  72.0 1.2 copy-done.8
  73.2 0.9 copy-done.15
  74.1 0.9 copy-done.24
  75.6 6.7 %project_near_half.1 = (f32[512,896]{1,0:T(8,128)S(1)}, f32[512,256]{1,0:T(8,128)S(1)}, f32[512,32]{1,0:T(8,128)S(1)}, f32[8,128]{1,0:T(8,128)S(1)}) custom-call(s32[1]{0:T(128)} %bitcast.place_ref.refs_0_.refs_1_, bf16[512,896]{1,0:T(8,128)(2,1)S(1)} %copy-done.8, bf16[512,896]{1,0:T(8,128)(2,1)} %collective-permute-done.3.x1, ...), custom_call_target="tpu_custom_call" | custom-call | tf_op jit(solution)/shard_map/project_near_half/pallas_call | solution.py:733
  82.4 1.2 copy-done.12
  84.9 0.8 copy-done.17
  85.7 29.5 %split_rows.3 = (bf16[256,896]{1,0:T(8,128)(2,1)}, bf16[256,896]{1,0:T(8,128)(2,1)}, f32[8,128]{1,0:T(8,128)}) custom-call(bf16[512,896]{1,0:T(8,128)(2,1)} %slab_ref.1, f32[8,128]{1,0:T(8,128)} %get-tuple-element.41.refs_0_), custom_call_target="tpu_custom_call" | custom-call | tf_op jit(solution)/shard_map/split_rows/pallas_call | solution.py:583
  115.2 1.6 collective-permute-start.8
  117.4 0.9 copy-done.22
  119.0 2.6 %memory_pairs.2 = (bf16[2,272,128]{2,1,0:T(8,128)(2,1)S(1)}, f32[8,128]{1,0:T(8,128)}) custom-call(s32[1]{0:T(128)} %bitcast.place_ref.refs_0_.refs_1_, s32[1]{0:T(128)} %bitcast.place_ref.refs_0_.refs_1_, bf16[256,896]{1,0:T(8,128)(2,1)} %collective-permute-done.5.refs_2_, bf16[256,896]{1,0:T(8,128)(2,1)} %collective-permute-done.6.refs_3_, ...), custom_call_target="tpu_custom_call" | custom-call | tf_op jit(solution)/shard_map/memory_pairs/pallas_call | solution.py:759
  121.6 1.0 copy-done.18
  122.6 0.9 copy-done.23
  123.5 3.4 %memory_pairs.3 = (bf16[8,272,128]{2,1,0:T(8,128)(2,1)S(1)}, f32[8,128]{1,0:T(8,128)S(1)}) custom-call(s32[1]{0:T(128)} %bitcast.place_ref.refs_0_.refs_1_, s32[8]{0:T(128)S(1)} %reduce.refs_6_.refs_1_.refs_0_, bf16[256,896]{1,0:T(8,128)(2,1)S(1)} %copy-done.18, bf16[256,896]{1,0:T(8,128)(2,1)} %collective-permute-done.4.refs_3_, ...), custom_call_target="tpu_custom_call" | custom-call | tf_op jit(solution)/shard_map/memory_pairs/pallas_call | solution.py:759
  127.0 0.8 copy-done.28
  128.3 3.7 %all-to-all-start.1 = ((bf16[8,272,128]{2,1,0:T(8,128)(2,1)}), bf16[8,272,128]{2,1,0:T(8,128)(2,1)S(1)}, u32[]{:S(2)}, u32[]{:S(2)}) async-start(bf16[8,272,128]{2,1,0:T(8,128)(2,1)} %copy-done.28), calls=%async_computation.1 | async-start | bytes 1114112 | tf_op jit(solution)/shard_map/all_to_all | solution.py:771
  132.2 6.2 %collective-permute-done.x_ref = bf16[256,896]{1,0:T(8,128)(2,1)} collective-permute-done((bf16[256,896]{1,0:T(8,128)(2,1)}, bf16[256,896]{1,0:T(8,128)(2,1)}, u32[]{:S(2)}, u32[]{:S(2)}) %collective-permute-start) | collective-permute-done | bytes 458784 | tf_op jit(solution)/shard_map/ppermute | solution.py:564
  138.4 2.8 %copy-done.1 = bf16[3584,896]{1,0:T(8,128)(2,1)S(1)} copy-done((bf16[3584,896]{1,0:T(8,128)(2,1)S(1)}, bf16[3584,896]{1,0:T(8,128)(2,1)}, u32[]{:S(2)}) %copy-start.1) | copy-done | bytes 6422552
  141.2 1.5 copy-done.13
  142.7 0.9 copy-done.20
  143.7 0.9 copy-done.25
  144.6 5.9 %project_far_half.3 = (bf16[256,896]{1,0:T(8,128)(2,1)S(1)}, bf16[256,128]{1,0:T(8,128)(2,1)S(1)}, bf16[256,128]{1,0:T(8,128)(2,1)S(1)}, bf16[32,256]{1,0:T(8,128)(2,1)S(1)}) custom-call(s32[1]{0:T(128)} %bitcast.place_ref.refs_0_.refs_1_, bf16[256,896]{1,0:T(8,128)(2,1)} %in_order.7.refs_1_, bf16[256,896]{1,0:T(8,128)(2,1)S(1)} %collective-permute-done.9.refs_2_, ...), custom_call_target="tpu_custom_call" | custom-call | flops 1174405120 | bytes 5505024 | tf_op jit(solution)/shard_map/project_far_half/pallas_call | solution.py:777
  150.5 0.8 copy-done.43
  152.6 6.0 %project_far_half.2 = (bf16[256,896]{1,0:T(8,128)(2,1)S(1)}, bf16[256,128]{1,0:T(8,128)(2,1)S(1)}, bf16[256,128]{1,0:T(8,128)(2,1)S(1)}, bf16[32,256]{1,0:T(8,128)(2,1)S(1)}) custom-call(s32[1]{0:T(128)} %bitcast.place_ref.refs_0_.refs_1_, bf16[256,896]{1,0:T(8,128)(2,1)} %in_order.6.refs_1_, bf16[256,896]{1,0:T(8,128)(2,1)S(1)} %collective-permute-done.7.refs_2_, ...), custom_call_target="tpu_custom_call" | custom-call | flops 1174405120 | bytes 5505024 | tf_op jit(solution)/shard_map/project_far_half/pallas_call | solution.py:777
  158.5 0.8 copy-done.45
  159.4 1.2 copy-done.40
  160.5 1.2 copy-done.42
  161.7 1.0 copy-done.44
  162.7 1.0 copy-done.46
  163.7 21.7 %span_attention.1 = (f32[40,512]{1,0:T(8,128)S(1)}, f32[16,1024]{1,0:T(8,128)S(1)}, f32[8,16,128]{2,1,0:T(8,128)}) custom-call(s32[4]{0:T(128)S(1)} %copy-done.51, bf16[256,896]{1,0:T(8,128)(2,1)S(1)} %copy-done.46, bf16[256,128]{1,0:T(8,128)(2,1)S(1)} %get-tuple-element.56.refs_2_, bf16[256,128]{1,0:T(8,128)(2,1)S(1)} %get-tuple-element.57.refs_3_, ...), custom_call_target="tpu_custom_call" | custom-call | flops 10569646080 | bytes 1835008 | tf_op jit(solution)/shard_map/span_attention/pallas_call | solution.py:801
  185.4 3.4 %all-to-all-start.2 = ((f32[8,16,128]{2,1,0:T(8,128)}), f32[8,16,128]{2,1,0:T(8,128)S(1)}, u32[]{:S(2)}, u32[]{:S(2)}) async-start(f32[8,16,128]{2,1,0:T(8,128)} %get-tuple-element.69), calls=%async_computation.2 | async-start | bytes 131072 | tf_op jit(solution)/shard_map/all_to_all | solution.py:836
  189.4 1.5 collective-permute-start.11
  190.9 4.8 %all-to-all-done.2.refs_1_ = f32[8,16,128]{2,1,0:T(8,128)S(1)} async-done(((f32[8,16,128]{2,1,0:T(8,128)}), f32[8,16,128]{2,1,0:T(8,128)S(1)}, u32[]{:S(2)}, u32[]{:S(2)}) %all-to-all-start.2) | async-done | bytes 65568 | tf_op jit(solution)/shard_map/all_to_all | solution.py:836
  196.3 0.8 first_down.1
  197.1 0.9 collective-permute-start.13
  197.9 4.0 %collective-permute-done.13 = f32[16,1920]{1,0:T(8,128)S(1)} collective-permute-done((f32[16,1920]{1,0:T(8,128)S(1)}, f32[16,1920]{1,0:T(8,128)S(1)}, u32[]{:S(2)}, u32[]{:S(2)}) %collective-permute-start.13) | collective-permute-done | bytes 122912 | tf_op jit(solution)/shard_map/ppermute | solution.py:564
  202.0 1.4 collective-permute-start.14
  203.4 1.4 collective-permute-start.17
  205.2 2.1 collective-permute-done.17.c2
  207.3 0.8 collective-permute-done.18.c3
  208.3 1.5 collective-permute-start.19
  209.9 2.5 %collective-permute-start.15 = (f32[16,1920]{1,0:T(8,128)S(1)}, f32[16,1920]{1,0:T(8,128)S(1)}, u32[]{:S(2)}, u32[]{:S(2)}) collective-permute-start(f32[16,1920]{1,0:T(8,128)S(1)} %add.21.q0), channel_id=1, source_target_pairs={{0,16},{4,20},{8,24},{12,28},{16,0},{20,4},{24,8},{28,12},{1,17},{... | collective-permute-start | bytes 368648 | tf_op jit(solution)/shard_map/ppermute | solution.py:564
  212.6 0.9 collective-permute-start.20
  213.5 6.4 %collective-permute-done.20 = f32[16,896]{1,0:T(8,128)S(1)} collective-permute-done((f32[16,896]{1,0:T(8,128)S(1)}, f32[16,896]{1,0:T(8,128)S(1)}, u32[]{:S(2)}, u32[]{:S(2)}) %collective-permute-start.20) | collective-permute-done | bytes 57376 | tf_op jit(solution)/shard_map/ppermute | solution.py:564
  219.9 5.1 %collective-permute-done.21.v1 = f32[16,896]{1,0:T(8,128)S(1)} collective-permute-done((f32[16,896]{1,0:T(8,128)S(1)}, f32[16,896]{1,0:T(8,128)S(1)}, u32[]{:S(2)}, u32[]{:S(2)}) %collective-permute-start.21) | collective-permute-done | bytes 57376 | tf_op jit(solution)/shard_map/ppermute | solution.py:564
  (117 shorter events, 11.8 us)
Async XLA Ops:
  0.6 40.9 %collective-permute-start.1 = (bf16[512,896]{1,0:T(8,128)(2,1)}, bf16[512,896]{1,0:T(8,128)(2,1)S(1)}, u32[]{:S(2)}, u32[]{:S(2)}) collective-permute-start(bf16[512,896]{1,0:T(8,128)(2,1)} %memory_ref.1), channel_id=1, source_target_pairs={{0,1},{1,0},{2,3},{3,2},{4,5},{5,4},{6,7},{7,6},{8,9},{9,8},{10,11... | collective-permute-start | bytes 2752520 | tf_op jit(solution)/shard_map/ppermute | solution.py:564
  1.1 65.6 %collective-permute-start.3 = (bf16[512,896]{1,0:T(8,128)(2,1)}, bf16[512,896]{1,0:T(8,128)(2,1)}, u32[]{:S(2)}, u32[]{:S(2)}) collective-permute-start(bf16[512,896]{1,0:T(8,128)(2,1)} %slab_ref.1), channel_id=1, source_target_pairs={{0,1},{1,0},{2,3},{3,2},{4,5},{5,4},{6,7},{7,6},{8,9},{9,8},{10,11... | collective-permute-start | bytes 2752520 | tf_op jit(solution)/shard_map/ppermute | solution.py:564
  30.8 29.4 %collective-permute-start.5 = (bf16[256,896]{1,0:T(8,128)(2,1)}, bf16[256,896]{1,0:T(8,128)(2,1)}, u32[]{:S(2)}, u32[]{:S(2)}) collective-permute-start(bf16[256,896]{1,0:T(8,128)(2,1)} %get-tuple-element.49), channel_id=1, source_target_pairs={{0,2},{1,3},{2,0},{3,1},{4,6},{5,7},{6,4},{7,5},{8,10},{9,11},{10,... | collective-permute-start | bytes 1376264 | tf_op jit(solution)/shard_map/ppermute | solution.py:564
  33.8 51.1 %collective-permute-start.2 = (bf16[256,896]{1,0:T(8,128)(2,1)}, bf16[256,896]{1,0:T(8,128)(2,1)S(1)}, u32[]{:S(2)}, u32[]{:S(2)}) collective-permute-start(bf16[256,896]{1,0:T(8,128)(2,1)} %get-tuple-element.45), channel_id=1, source_target_pairs={{0,2},{1,3},{2,0},{3,1},{4,6},{5,7},{6,4},{7,5},{8,10},{9,11},{10,... | collective-permute-start | bytes 1376264 | tf_op jit(solution)/shard_map/ppermute | solution.py:564
  38.3 0.9 copy-start.39
  39.3 0.9 copy-start.41
  41.5 0.9 copy-start.26
  42.5 1.2 copy-start.2
  43.6 1.2 copy-start.5
  44.8 1.2 copy-start.10
  46.0 0.9 copy-start.14
  46.9 1.2 copy-start.27
  48.1 69.3 %copy-start.4 = (bf16[3584,128]{1,0:T(8,128)(2,1)S(1)}, bf16[3584,128]{1,0:T(8,128)(2,1)}, u32[]{:S(2)}) copy-start(bf16[3584,128]{1,0:T(8,128)(2,1)} %refs_4_.5) | copy-start | bytes 2752516
  48.1 69.3 %copy-start.7 = (bf16[3584,128]{1,0:T(8,128)(2,1)S(1)}, bf16[3584,128]{1,0:T(8,128)(2,1)}, u32[]{:S(2)}) copy-start(bf16[3584,128]{1,0:T(8,128)(2,1)} %refs_5_.3) | copy-start | bytes 2752516
  48.1 69.3 %copy-start.16 = (bf16[16,3584]{1,0:T(8,128)(2,1)S(1)}, bf16[16,3584]{1,0:T(8,128)(2,1)}, u32[]{:S(2)}) copy-start(bf16[16,3584]{1,0:T(8,128)(2,1)} %refs_7_.7) | copy-start | bytes 344068
  52.6 64.8 %copy-start.30 = (bf16[16,128]{1,0:T(8,128)(2,1)S(1)}, bf16[16,128]{1,0:T(8,128)(2,1)}, u32[]{:S(2)}) copy-start(bf16[16,128]{1,0:T(8,128)(2,1)} %refs_13_.1) | copy-start | bytes 12292
  53.9 12.6 %all-to-all-start = ((s32[8,1,1]{2,1,0:T(1,128)}), s32[8,1,1]{2,1,0:T(1,128)S(1)}, u32[]{:S(2)}, u32[]{:S(2)}) async-start(s32[8,1,1]{2,1,0:T(1,128)} %copy.24), calls=%async_computation | async-start | bytes 8192 | tf_op jit(solution)/shard_map/all_to_all | solution.py:727
  60.2 57.2 %collective-permute-start.6 = (bf16[256,896]{1,0:T(8,128)(2,1)}, bf16[256,896]{1,0:T(8,128)(2,1)}, u32[]{:S(2)}, u32[]{:S(2)}) collective-permute-start(bf16[256,896]{1,0:T(8,128)(2,1)} %collective-permute-done.5.refs_2_), channel_id=1, source_target_pairs={{0,1},{1,0},{2,3},{3,2},{4,5},{5,4},{6,7},{7,6},{8,9},{9,8},{10,11... | collective-permute-start | bytes 1376264 | tf_op jit(solution)/shard_map/ppermute | solution.py:564
  66.8 2.8 %copy-start = (bf16[3584,896]{1,0:T(8,128)(2,1)S(1)}, bf16[3584,896]{1,0:T(8,128)(2,1)}, u32[]{:S(2)}) copy-start(bf16[3584,896]{1,0:T(8,128)(2,1)} %refs_3_.5) | copy-start | bytes 19267588
  69.6 1.2 copy-start.3
  70.8 1.2 copy-start.6
  72.0 1.2 copy-start.8
  73.2 0.9 copy-start.15
  74.1 0.9 copy-start.24
  82.4 1.2 copy-start.12
  84.9 53.5 %copy-start.29 = (bf16[16,896]{1,0:T(8,128)(2,1)S(1)}, bf16[16,896]{1,0:T(8,128)(2,1)}, u32[]{:S(2)}) copy-start(bf16[16,896]{1,0:T(8,128)(2,1)} %refs_12_.5) | copy-start | bytes 86020
  84.9 0.8 copy-start.17
  85.7 35.9 %collective-permute-start.4 = (bf16[256,896]{1,0:T(8,128)(2,1)}, bf16[256,896]{1,0:T(8,128)(2,1)}, u32[]{:S(2)}, u32[]{:S(2)}) collective-permute-start(bf16[256,896]{1,0:T(8,128)(2,1)} %in_order.5.refs_2_), channel_id=1, source_target_pairs={{0,1},{1,0},{2,3},{3,2},{4,5},{5,4},{6,7},{7,6},{8,9},{9,8},{10,11... | collective-permute-start | bytes 1376264 | tf_op jit(solution)/shard_map/ppermute | solution.py:564
  115.2 16.8 %collective-permute-start.8 = (bf16[256,896]{1,0:T(8,128)(2,1)}, bf16[256,896]{1,0:T(8,128)(2,1)}, u32[]{:S(2)}, u32[]{:S(2)}) collective-permute-start(bf16[256,896]{1,0:T(8,128)(2,1)} %get-tuple-element.59), channel_id=1, source_target_pairs={{0,2},{1,3},{2,0},{3,1},{4,6},{5,7},{6,4},{7,5},{8,10},{9,11},{10,... | collective-permute-start | bytes 1376264 | tf_op jit(solution)/shard_map/ppermute | solution.py:564
  116.8 21.6 %collective-permute-start = (bf16[256,896]{1,0:T(8,128)(2,1)}, bf16[256,896]{1,0:T(8,128)(2,1)}, u32[]{:S(2)}, u32[]{:S(2)}) collective-permute-start(bf16[256,896]{1,0:T(8,128)(2,1)} %get-tuple-element.42), channel_id=1, source_target_pairs={{0,2},{1,3},{2,0},{3,1},{4,6},{5,7},{6,4},{7,5},{8,10},{9,11},{10,... | collective-permute-start | bytes 1376264 | tf_op jit(solution)/shard_map/ppermute | solution.py:564
  117.4 1.0 copy-start.22
  121.6 1.0 copy-start.18
  122.6 0.9 copy-start.23
  126.9 0.8 copy-start.28
  128.3 31.0 %all-to-all-start.1 = ((bf16[8,272,128]{2,1,0:T(8,128)(2,1)}), bf16[8,272,128]{2,1,0:T(8,128)(2,1)S(1)}, u32[]{:S(2)}, u32[]{:S(2)}) async-start(bf16[8,272,128]{2,1,0:T(8,128)(2,1)} %copy-done.28), calls=%async_computation.1 | async-start | bytes 1114112 | tf_op jit(solution)/shard_map/all_to_all | solution.py:771
  132.1 6.3 %collective-permute-start.9 = (bf16[256,896]{1,0:T(8,128)(2,1)}, bf16[256,896]{1,0:T(8,128)(2,1)S(1)}, u32[]{:S(2)}, u32[]{:S(2)}) collective-permute-start(bf16[256,896]{1,0:T(8,128)(2,1)} %in_order.7.refs_1_), channel_id=1, source_target_pairs={{0,1},{1,0},{2,3},{3,2},{4,5},{5,4},{6,7},{7,6},{8,9},{9,8},{10,11... | collective-permute-start | bytes 1376264 | tf_op jit(solution)/shard_map/ppermute | solution.py:564
  138.4 14.2 %collective-permute-start.7 = (bf16[256,896]{1,0:T(8,128)(2,1)}, bf16[256,896]{1,0:T(8,128)(2,1)S(1)}, u32[]{:S(2)}, u32[]{:S(2)}) collective-permute-start(bf16[256,896]{1,0:T(8,128)(2,1)} %in_order.6.refs_1_), channel_id=1, source_target_pairs={{0,1},{1,0},{2,3},{3,2},{4,5},{5,4},{6,7},{7,6},{8,9},{9,8},{10,11... | collective-permute-start | bytes 1376264 | tf_op jit(solution)/shard_map/ppermute | solution.py:564
  138.4 2.8 %copy-start.1 = (bf16[3584,896]{1,0:T(8,128)(2,1)S(1)}, bf16[3584,896]{1,0:T(8,128)(2,1)}, u32[]{:S(2)}) copy-start(bf16[3584,896]{1,0:T(8,128)(2,1)} %refs_3_.5) | copy-start | bytes 19267588
  141.2 1.5 copy-start.13
  142.7 0.9 copy-start.20
  143.7 0.9 copy-start.25
  152.5 6.8 %copy-start.38 = (bf16[896,8]{0,1:T(8,128)(2,1)S(1)}, bf16[896,8]{0,1:T(8,128)(2,1)}, u32[]{:S(2)}) copy-start(bf16[896,8]{0,1:T(8,128)(2,1)} %param.22) | copy-start | bytes 43012
  152.5 6.8 %copy-start.51 = (s32[4]{0:T(128)S(1)}, s32[4]{0:T(128)}, u32[]{:S(2)}) copy-start(s32[4]{0:T(128)} %refs_0_.5) | copy-start | bytes 52
  152.5 6.8 %copy-start.48 = (bf16[256,128]{1,0:T(8,128)(2,1)S(1)}, bf16[256,128]{1,0:T(8,128)(2,1)}, u32[]{:S(2)}) copy-start(bf16[256,128]{1,0:T(8,128)(2,1)} %copy-done.47) | copy-start | bytes 196612
  152.6 6.8 %copy-start.50 = (bf16[256,128]{1,0:T(8,128)(2,1)S(1)}, bf16[256,128]{1,0:T(8,128)(2,1)}, u32[]{:S(2)}) copy-start(bf16[256,128]{1,0:T(8,128)(2,1)} %copy-done.49) | copy-start | bytes 196612
  159.3 1.2 copy-start.40
  160.5 1.2 copy-start.42
  161.7 1.0 copy-start.44
  162.7 1.0 copy-start.46
  163.7 32.6 %copy-start.9 = (bf16[512,896]{1,0:T(8,128)(2,1)S(1)}, bf16[512,896]{1,0:T(8,128)(2,1)}, u32[]{:S(2)}) copy-start(bf16[512,896]{1,0:T(8,128)(2,1)} %slab_ref.1) | copy-start | bytes 2752516
  163.7 44.3 %copy-start.11 = (bf16[512,896]{1,0:T(8,128)(2,1)S(1)}, bf16[512,896]{1,0:T(8,128)(2,1)}, u32[]{:S(2)}) copy-start(bf16[512,896]{1,0:T(8,128)(2,1)} %memory_ref.1) | copy-start | bytes 2752516
  185.4 10.3 %all-to-all-start.2 = ((f32[8,16,128]{2,1,0:T(8,128)}), f32[8,16,128]{2,1,0:T(8,128)S(1)}, u32[]{:S(2)}, u32[]{:S(2)}) async-start(f32[8,16,128]{2,1,0:T(8,128)} %get-tuple-element.69), calls=%async_computation.2 | async-start | bytes 131072 | tf_op jit(solution)/shard_map/all_to_all | solution.py:836
  188.8 7.5 %collective-permute-start.10 = (f32[40,512]{1,0:T(8,128)S(1)}, f32[40,512]{1,0:T(8,128)S(1)}, u32[]{:S(2)}, u32[]{:S(2)}) collective-permute-start(f32[40,512]{1,0:T(8,128)S(1)} %get-tuple-element.67.c0), channel_id=1, source_target_pairs={{0,1},{1,0},{2,3},{3,2},{4,5},{5,4},{6,7},{7,6},{8,9},{9,8},{10,11... | collective-permute-start | bytes 245768 | tf_op jit(solution)/shard_map/ppermute | solution.py:564
  189.4 6.9 %collective-permute-start.11 = (f32[40,512]{1,0:T(8,128)S(1)}, f32[40,512]{1,0:T(8,128)S(1)}, u32[]{:S(2)}, u32[]{:S(2)}) collective-permute-start(f32[40,512]{1,0:T(8,128)S(1)} %get-tuple-element.67.c0), channel_id=1, source_target_pairs={{0,2},{1,3},{2,0},{3,1},{4,6},{5,7},{6,4},{7,5},{8,10},{9,11},{10,... | collective-permute-start | bytes 245768 | tf_op jit(solution)/shard_map/ppermute | solution.py:564
  190.9 5.4 %collective-permute-start.12 = (f32[40,512]{1,0:T(8,128)S(1)}, f32[40,512]{1,0:T(8,128)S(1)}, u32[]{:S(2)}, u32[]{:S(2)}) collective-permute-start(f32[40,512]{1,0:T(8,128)S(1)} %get-tuple-element.67.c0), channel_id=1, source_target_pairs={{0,3},{1,2},{2,1},{3,0},{4,7},{5,6},{6,5},{7,4},{8,11},{9,10},{10,... | collective-permute-start | bytes 245768 | tf_op jit(solution)/shard_map/ppermute | solution.py:564
  197.1 4.9 %collective-permute-start.13 = (f32[16,1920]{1,0:T(8,128)S(1)}, f32[16,1920]{1,0:T(8,128)S(1)}, u32[]{:S(2)}, u32[]{:S(2)}) collective-permute-start(f32[16,1920]{1,0:T(8,128)S(1)} %get-tuple-element.71), channel_id=1, source_target_pairs={{0,4},{4,0},{8,12},{12,8},{16,20},{20,16},{24,28},{28,24},{1,5},{5... | collective-permute-start | bytes 368648 | tf_op jit(solution)/shard_map/ppermute | solution.py:564
  202.0 7.9 %collective-permute-start.14 = (f32[16,1920]{1,0:T(8,128)S(1)}, f32[16,1920]{1,0:T(8,128)S(1)}, u32[]{:S(2)}, u32[]{:S(2)}) collective-permute-start(f32[16,1920]{1,0:T(8,128)S(1)} %add.20), channel_id=1, source_target_pairs={{0,8},{4,12},{8,0},{12,4},{16,24},{20,28},{24,16},{28,20},{1,9},{5... | collective-permute-start | bytes 368648 | tf_op jit(solution)/shard_map/ppermute | solution.py:564
  203.4 1.9 collective-permute-start.16
  203.4 3.9 %collective-permute-start.17 = (f32[16,512]{1,0:T(8,128)S(1)}, f32[16,512]{1,0:T(8,128)S(1)}, u32[]{:S(2)}, u32[]{:S(2)}) collective-permute-start(f32[16,512]{1,0:T(8,128)S(1)} %owned_cotangent.1.dep_ref.c0), channel_id=1, source_target_pairs={{0,2},{1,3},{2,0},{3,1},{4,6},{5,7},{6,4},{7,5},{8,10},{9,11},{10,... | collective-permute-start | bytes 98312 | tf_op jit(solution)/shard_map/ppermute | solution.py:564
  204.7 3.3 %collective-permute-start.18 = (f32[16,512]{1,0:T(8,128)S(1)}, f32[16,512]{1,0:T(8,128)S(1)}, u32[]{:S(2)}, u32[]{:S(2)}) collective-permute-start(f32[16,512]{1,0:T(8,128)S(1)} %owned_cotangent.1.dep_ref.c0), channel_id=1, source_target_pairs={{0,3},{1,2},{2,1},{3,0},{4,7},{5,6},{6,5},{7,4},{8,11},{9,10},{10,... | collective-permute-start | bytes 98312 | tf_op jit(solution)/shard_map/ppermute | solution.py:564
  208.3 4.2 %collective-permute-start.19 = (f32[16,896]{1,0:T(8,128)S(1)}, f32[16,896]{1,0:T(8,128)S(1)}, u32[]{:S(2)}, u32[]{:S(2)}) collective-permute-start(f32[16,896]{1,0:T(8,128)S(1)} %second_down.1), channel_id=1, source_target_pairs={{0,4},{4,0},{8,12},{12,8},{16,20},{20,16},{24,28},{28,24},{1,5},{5... | collective-permute-start | bytes 172040 | tf_op jit(solution)/shard_map/ppermute | solution.py:564
  209.9 15.1 %collective-permute-start.15 = (f32[16,1920]{1,0:T(8,128)S(1)}, f32[16,1920]{1,0:T(8,128)S(1)}, u32[]{:S(2)}, u32[]{:S(2)}) collective-permute-start(f32[16,1920]{1,0:T(8,128)S(1)} %add.21.q0), channel_id=1, source_target_pairs={{0,16},{4,20},{8,24},{12,28},{16,0},{20,4},{24,8},{28,12},{1,17},{... | collective-permute-start | bytes 368648 | tf_op jit(solution)/shard_map/ppermute | solution.py:564
  212.6 7.3 %collective-permute-start.20 = (f32[16,896]{1,0:T(8,128)S(1)}, f32[16,896]{1,0:T(8,128)S(1)}, u32[]{:S(2)}, u32[]{:S(2)}) collective-permute-start(f32[16,896]{1,0:T(8,128)S(1)} %add.22), channel_id=1, source_target_pairs={{0,8},{4,12},{8,0},{12,4},{16,24},{20,28},{24,16},{28,20},{1,9},{5... | collective-permute-start | bytes 172040 | tf_op jit(solution)/shard_map/ppermute | solution.py:564
  219.9 5.1 %collective-permute-start.21 = (f32[16,896]{1,0:T(8,128)S(1)}, f32[16,896]{1,0:T(8,128)S(1)}, u32[]{:S(2)}, u32[]{:S(2)}) collective-permute-start(f32[16,896]{1,0:T(8,128)S(1)} %add.23.v0), channel_id=1, source_target_pairs={{0,16},{4,20},{8,24},{12,28},{16,0},{20,4},{24,8},{28,12},{1,17},{... | collective-permute-start | bytes 172040 | tf_op jit(solution)/shard_map/ppermute | solution.py:564
  (13 other events, 8.8 us)
where the time goes:
time: 227 us; the launch traced here: 226 us
  Pallas kernels  114 us (50%)
  local copies, waits for them, and re-layouts  43 us (19%)
  waiting for transfers between devices  35.9 us (16%)
  starting transfers between devices  30.4 us (13%)
    pallas_call x2, Pallas kernels, split_after(): pl.pallas_call(body, out_shape=[part] * cuts + [FLAG], in_specs=[hbm()] +...  59 us
    unnamed x104, local copies, waits for them, and re-layouts  41.7 us
    ppermute x22, waiting for transfers between devices, swap(): lax.ppermute(x, axis, [(i, i ^ bit) for i in range(lax.axis_size(axis))])  24.8 us
    pallas_call x1, Pallas kernels, fast(): run(lambda *refs: attention_kernel(tok_cuts, peers, heads, *refs), 'span_...  21.7 us
    ppermute x22, starting transfers between devices, swap(): lax.ppermute(x, axis, [(i, i ^ bit) for i in range(lax.axis_size(axis))])  17.1 us
    pallas_call x2, Pallas kernels, fast(): run(lambda *refs, t=t: project_kernel(t * rows, *refs), 'project_far_half...  11.9 us
    pallas_call x1, Pallas kernels, fast(): run(project_early_kernel, 'project_near_half', (shaped(tok_rows, query_wi...  6.7 us
    all_to_all x1, waiting for transfers between devices, fast(): lax.all_to_all(after(wanted, mem_flag), 'tm', split_axis=0, concat_axis=0...  6.3 us
  transfers between devices with their start and end apart: 25, of which 9 were waited for; matrix products, arithmetic and copies ran while one was open for 1% of the time, Pallas kernels for 40%

commit v1 on v0

--- a/solution.py
+++ b/solution.py
@@ -230,7 +230,7 @@
 STRIP = 16
 PAIR = 2
 MIB = 1024 * 1024
-FLAG = jax.ShapeDtypeStruct((8, 128), jnp.float32)
+ROOM = 60
 
 
 def dot_nt(a, b, precision=None):
@@ -279,10 +279,12 @@
     return dot_nn(x, jnp.concatenate([wk_s[n], wv_s[n]], 1)), dot_nt(x, down_s[n])
 
 
-def memory_early_kernel(place_ref, x0, x1, *refs):
-    hbm, acc_ref, low_ref, flag_ref, scratch, sems = refs[:3], refs[4], refs[5], refs[6], refs[7:11], refs[11]
-    flag_ref[...] = jnp.zeros_like(flag_ref)
+def memory_early_kernel(blocks, place_ref, named_ref, x0, x1, *refs):
+    hbm, acc_ref, low_ref, wanted_ref, scratch, sems = refs[:3], refs[3], refs[4], refs[5], refs[6:10], refs[10]
     groups = memory_pieces(place_ref, (0, 1), (x0, x1), hbm, scratch, sems)
+    for slot in range(TOP):
+        block = named_ref[0, slot]
+        wanted_ref[lax.div(block, blocks)] = lax.rem(block, blocks)
     for n in range(2):
         wait_all(groups[n])
         term, low_term = memory_terms(n, scratch)
@@ -294,13 +296,11 @@
             low_ref[...] += low_term
 
 
-def memory_kernel(first, peers, last, place_ref, asked_ref, x2, x3, acc_hbm, low_hbm, *refs):
-    hbm, up_ref, other, out_ref, flag_ref = refs[:3], refs[3], refs[4], refs[5], refs[6]
-    scratch, sems, acc_s, low_s, acc_sems = refs[7:11], refs[11], refs[12], refs[13], refs[14]
-    at = pl.ds(first, x2.shape[0])
-    sums = start_copies([(acc_hbm.at[at, :], acc_s), (low_hbm.at[at, :], low_s)], acc_sems)
+def memory_kernel(peers, place_ref, asked_ref, x2, x3, acc_hbm, low_hbm, *refs):
+    hbm, up_ref, out_ref = refs[:3], refs[3], refs[4]
+    scratch, sems, acc_s, low_s, acc_sems, pair_ref = refs[5:9], refs[9], refs[10], refs[11], refs[12], refs[13]
+    sums = start_copies([(acc_hbm, acc_s), (low_hbm, low_s)], acc_sems)
     groups = memory_pieces(place_ref, (2, 3), (x2, x3), hbm, scratch, sems)
-    flag_ref[...] = jnp.zeros_like(flag_ref)
     wait_all(sums)
     acc = acc_s[...]
     low = low_s[...]
@@ -312,21 +312,13 @@
     values = (acc[:, HD:] + dot_nn(low.astype(jnp.bfloat16), up_ref[...])).astype(jnp.bfloat16)
     keys = acc[:, :HD].astype(jnp.bfloat16)
     low_t = jnp.transpose(low).astype(jnp.bfloat16)
-    if last:
-        pair_ref = refs[15]
-        offset = other.shape[0]
-        pair_ref[:offset] = other[...]
-    else:
-        pair_ref = out_ref
-        offset = 0
     for b in range(acc.shape[0] // BLK):
         at = slice(b * BLK, (b + 1) * BLK)
-        pair_ref[offset + b, 0:BLK, :] = keys[at]
-        pair_ref[offset + b, BLK : 2 * BLK, :] = values[at]
-        pair_ref[offset + b, 2 * BLK : PACK, :] = low_t[:, at]
-    if last:
-        for r in range(peers):
-            out_ref[r] = pair_ref[asked_ref[r]]
+        pair_ref[b, 0:BLK, :] = keys[at]
+        pair_ref[b, BLK : 2 * BLK, :] = values[at]
+        pair_ref[b, 2 * BLK : PACK, :] = low_t[:, at]
+    for r in range(peers):
+        out_ref[r] = pair_ref[asked_ref[r]]
 
 
 WQ_CUTS = 4
@@ -366,9 +358,19 @@
 
 
 def project_early_kernel(place_ref, x0, x1, *refs):
-    hbm, outs, flag_ref, scratch, sems = refs[:5], refs[7:10], refs[10], refs[11:17], refs[17]
-    flag_ref[...] = jnp.zeros_like(flag_ref)
+    hbm, (tag_ref, tags_t_ref), outs, (grad_ref, grad_t_ref) = refs[:5], refs[5:7], refs[8:11], refs[11:13]
+    scratch, sems = refs[13:19], refs[19]
     groups = project_pieces(place_ref, (0, 1), (x0, x1), hbm, scratch, sems)
+    first = (((0,), (0,)), ((), ()))
+    tag = tag_ref[...].astype(jnp.float32)
+    tags_t = tags_t_ref[...]
+    f32 = jnp.float32
+    grad_ref[...] = lax.dot_general(
+        tags_t, tag, first, precision=HIGHEST, preferred_element_type=f32
+    ).astype(jnp.bfloat16)
+    grad_t_ref[...] = lax.dot_general(
+        tag, tags_t, first, precision=HIGHEST, preferred_element_type=f32
+    ).astype(jnp.bfloat16)
     for n in range(2):
         wait_all(groups[n])
         for ref, term in zip(outs, project_terms(n, scratch)):
@@ -378,52 +380,39 @@
                 ref[...] += term
 
 
-def project_kernel(first, place_ref, x2, x3, *refs):
-    hbm, early, (qup_ref, vup_ref) = refs[:5], refs[5:8], refs[8:10]
-    q_ref, k_ref, v_ref, low_ref = refs[10:14]
-    scratch, sems, sum_refs, sum_sems = refs[14:20], refs[20], refs[21:24], refs[24]
-    groups = project_pieces(place_ref, (2, 3), (x2, x3), hbm, scratch, sems)
-    at = pl.ds(first, x2.shape[0])
-    loads = start_copies([(src.at[at, :], dst) for src, dst in zip(early, sum_refs)], sum_sems)
-    for n in range(2):
-        wait_all(groups[n])
-        if n == 0:
-            wait_all(loads)
-            sums = [ref[...] for ref in sum_refs]
-        sums = [a + b for a, b in zip(sums, project_terms(n, scratch))]
-    q_acc, kv_acc, low_acc = sums
-    low = low_acc.astype(jnp.bfloat16)
-    q_ref[...] = (q_acc + dot_nn(low[:, :RANK], qup_ref[...])).astype(jnp.bfloat16)
-    k_ref[...] = kv_acc[:, :HD].astype(jnp.bfloat16)
-    v_ref[...] = (kv_acc[:, HD:] + dot_nn(low[:, RANK:], vup_ref[...])).astype(jnp.bfloat16)
-    low_ref[...] = jnp.transpose(low_acc).astype(jnp.bfloat16)
-
-
-def attention_kernel(cuts, peers, heads, bound_ref, *refs):
-    parts = refs[: 4 * cuts]
-    got, grad_hbm, grad_t_hbm, qup_ref, vup_ref, tag_ref, cot_ref, up_ref, mcot_ref = refs[4 * cuts : 4 * cuts + 9]
+def attention_kernel(peers, heads, place_ref, bound_ref, x3, x2, *refs):
+    hbm, early, got, grad_hbm, grad_t_hbm = refs[:5], refs[5:8], refs[8], refs[9], refs[10]
+    qup_ref, vup_ref, tag_ref, cot_ref, up_ref, mcot_ref = refs[11:17]
+    scratch, sems, sum_refs = refs[17:23], refs[23], refs[24:27]
     (q_s, k_own, v_own, low_s, low_m_s, grad_ref, grad_t_ref, k_all, v_all, kt_all, vt_all, kt_own, vt_own, bias_s, s_s, e_s, dp_s,
-     p_s, ds_s, att_s, dq_s, dv_s, sems) = refs[4 * cuts + 9 :]
+     p_s, ds_s, att_s, dq_s, dv_s, more_sems) = refs[27:]
     seen = peers * BLK
-    pairs = []
+    groups = project_pieces(place_ref, (3, 2), (x3, x2), hbm, scratch, sems)
+    pairs = list(zip(early, sum_refs))
     for b in range(peers):
         at = slice(b * BLK, (b + 1) * BLK)
         pairs.append((got.at[b, pl.ds(0, BLK), :], k_all.at[at, :]))
         pairs.append((got.at[b, pl.ds(BLK, BLK), :], v_all.at[at, :]))
         pairs.append((got.at[b, pl.ds(2 * BLK, RANK), :], low_m_s.at[b]))
-    for t in range(cuts):
-        q_c, k_c, v_c, low_c = parts[4 * t : 4 * t + 4]
-        rows = q_c.shape[0]
-        at = slice(t * rows, (t + 1) * rows)
-        pairs += [(q_c, q_s.at[at, :]), (k_c, k_own.at[at, :]), (v_c, v_own.at[at, :]), (low_c, low_s.at[:, at])]
     pairs += [(grad_hbm, grad_ref), (grad_t_hbm, grad_t_ref)]
-    copies = start_copies(pairs, sems)
-    wait_all(copies[: 3 * peers])
+    copies = start_copies(pairs, more_sems)
+    wait_all(groups[0])
+    for ref, term in zip(sum_refs, project_terms(0, scratch)):
+        if ref is sum_refs[0]:
+            wait_all(copies[:3])
+        ref[...] += term
+    wait_all(groups[1])
+    q_acc, kv_acc, low_acc = [ref[...] + term for ref, term in zip(sum_refs, project_terms(1, scratch))]
+    low = low_acc.astype(jnp.bfloat16)
+    q_s[...] = (q_acc + dot_nn(low[:, :RANK], qup_ref[...])).astype(jnp.bfloat16)
+    k_own[...] = kv_acc[:, :HD].astype(jnp.bfloat16)
+    v_own[...] = (kv_acc[:, HD:] + dot_nn(low[:, RANK:], vup_ref[...])).astype(jnp.bfloat16)
+    low_s[...] = jnp.transpose(low_acc).astype(jnp.bfloat16)
+    wait_all(copies[3:])
     for b in range(peers):
         at = slice(b * BLK, (b + 1) * BLK)
         kt_all[:, at] = jnp.transpose(k_all[at, :])
         vt_all[:, at] = jnp.transpose(v_all[at, :])
-    wait_all(copies[3 * peers :])
     dv_s[...] = jnp.zeros_like(dv_s)
     up_ref[...] = jnp.zeros_like(up_ref)
     scale = HD ** (-0.5)
@@ -551,9 +540,14 @@
     out_ref[...] = value_ref[...] + dot_nn(cot.astype(jnp.bfloat16), memory_ref[...])
 
 
-def finish_kernel(q0, q1, v0, v1, query_down_ref, query_up_ref, value_down_ref, value_up_ref):
-    query = q0[...] + q1[...]
-    value_down_ref[...] = v0[...] + v1[...]
+def finish_kernel(*refs):
+    query, value = [
+        (ref[0][...].astype(jnp.float32) + ref[1][...].astype(jnp.float32))
+        + (ref[2][...].astype(jnp.float32) + ref[3][...].astype(jnp.float32))
+        for ref in (refs[:4], refs[4:8])
+    ]
+    query_down_ref, query_up_ref, value_down_ref, value_up_ref = refs[8:]
+    value_down_ref[...] = value
     at = 0
     for out_ref in (query_down_ref, query_up_ref, value_up_ref):
         out_ref[...] = query[:, at : at + out_ref.shape[1]]
@@ -562,47 +556,6 @@
 
 def swap(x, bit, axis="heads"):
     return lax.ppermute(x, axis, [(i, i ^ bit) for i in range(lax.axis_size(axis))])
-
-
-def split_after(x, cuts, *deps):
-    rows = x.shape[0] // cuts
-    half = rows // 2
-
-    def body(x_ref, *refs):
-        outs, flag_ref, sems = refs[len(deps) : len(deps) + cuts], refs[len(deps) + cuts], refs[-1]
-        pairs = [
-            (x_ref.at[pl.ds(n * rows + m * half, half), :], outs[n].at[pl.ds(m * half, half), :])
-            for n in range(cuts)
-            for m in range(2)
-        ]
-        copies = start_copies(pairs, sems)
-        flag_ref[...] = jnp.zeros_like(flag_ref)
-        wait_all(copies)
-
-    part = jax.ShapeDtypeStruct((rows, x.shape[1]), x.dtype)
-    *parts, flag = pl.pallas_call(
-        body,
-        out_shape=[part] * cuts + [FLAG],
-        in_specs=[hbm()] + [anywhere()] * len(deps),
-        out_specs=[anywhere()] * cuts + [vmem()],
-        scratch_shapes=[pltpu.SemaphoreType.DMA((2 * cuts,))],
-        name="split_rows",
-    )(x, *deps)
-    return parts, flag
-
-
-def grad_kernel(tag_ref, grad_tags_ref, grad_ref, grad_t_ref, flag_ref):
-    first = (((0,), (0,)), ((), ()))
-    tag = tag_ref[...].astype(jnp.float32)
-    grad_tags = grad_tags_ref[...]
-    f32 = jnp.float32
-    grad_ref[...] = lax.dot_general(
-        grad_tags, tag, first, precision=HIGHEST, preferred_element_type=f32
-    ).astype(jnp.bfloat16)
-    grad_t_ref[...] = lax.dot_general(
-        tag, grad_tags, first, precision=HIGHEST, preferred_element_type=f32
-    ).astype(jnp.bfloat16)
-    flag_ref[...] = jnp.zeros_like(flag_ref)
 
 
 def after(x, dep):
@@ -620,10 +573,6 @@
     return pl.BlockSpec(memory_space=pl.ANY)
 
 
-def hbm():
-    return pl.BlockSpec(memory_space=pltpu.HBM)
-
-
 def smem():
     return pl.BlockSpec(memory_space=pltpu.SMEM)
 
@@ -636,13 +585,13 @@
     return jax.ShapeDtypeStruct(shape, dtype)
 
 
-def run(body, name, out_shape, in_specs, scratch=(), flops=0, moved=0, room=8):
+def run(body, name, out_shape, in_specs, scratch=(), flops=0, moved=0, room=ROOM, out_specs=None):
     many = isinstance(out_shape, (tuple, list))
     return pl.pallas_call(
         body,
         out_shape=out_shape,
         in_specs=in_specs,
-        out_specs=tuple(vmem() for _ in out_shape) if many else vmem(),
+        out_specs=out_specs or (tuple(vmem() for _ in out_shape) if many else vmem()),
         scratch_shapes=list(scratch),
         compiler_params=pltpu.CompilerParams(vmem_limit_bytes=room * MIB),
         cost_estimate=pl.CostEstimate(flops=flops, bytes_accessed=moved, transcendentals=0),
@@ -674,7 +623,6 @@
     peers = lax.axis_size("tm")
     f32 = jnp.float32
     bf16 = jnp.bfloat16
-    mem_cuts, tok_cuts = 2, 2
 
     def memory_scratch(rows):
         return [
@@ -696,114 +644,67 @@
             pltpu.SemaphoreType.DMA((2 * (WQ_CUTS + 5),)),
         ]
 
-    named = retrieval[0]
-    owner_ids = jnp.arange(peers, dtype=jnp.int32)
-    wanted = jnp.sum(
-        jnp.where(named[None, :] // blocks == owner_ids[:, None], named[None, :] % blocks, 0), axis=1
-    ).astype(jnp.int32)
     place = lax.axis_index("heads").astype(jnp.int32).reshape(1)
     tag_t = tag_weight.T
     tags = tag_t.shape[0]
-
-    mem_split, split_flag = split_after(memory, mem_cuts)
-    mem_far = [swap(m, 2) for m in mem_split]
+    mem_far = swap(memory, 2)
     mem_near = swap(memory, 1)
     tok_near = swap(slab_tokens, 1)
-    grad, grad_t, grad_flag = run(
-        grad_kernel,
-        "attended_cotangent",
-        (shaped(tok_rows, query_width, dtype=bf16), shaped(query_width, tok_rows, dtype=bf16), FLAG),
-        [vmem()] * 2,
-        room=10,
-    )(tag_t, grad_tags.T)
-    mem_acc, mem_low, mem_flag = run(
-        memory_early_kernel,
+    tok_far = swap(tok_near, 2)
+    mem_acc, mem_low, wanted = run(
+        lambda *refs: memory_early_kernel(blocks, *refs),
         "memory_near_half",
-        (shaped(mem_rows, 2 * HD), shaped(mem_rows, RANK), FLAG),
-        [smem(), hbm(), anywhere()] + [hbm()] * 3 + [anywhere()],
+        (shaped(mem_rows, 2 * HD), shaped(mem_rows, RANK), shaped(peers, dtype=jnp.int32)),
+        [smem()] * 2 + [anywhere()] * 5,
         memory_scratch(mem_rows),
-        room=14,
-    )(place, memory, mem_near, key_weight, value_weight, value_down, grad_flag)
-    asked = lax.all_to_all(after(wanted, mem_flag), "tm", split_axis=0, concat_axis=0, tiled=True)
-    tok_split, _ = split_after(slab_tokens, tok_cuts, split_flag)
-    tok_far = [swap(x, 2) for x in tok_split]
-
-    rows = tok_rows // tok_cuts
+        out_specs=(vmem(), vmem(), smem()),
+    )(place, retrieval, memory, mem_near, key_weight, value_weight, value_down)
+    asked = lax.all_to_all(wanted, "tm", split_axis=0, concat_axis=0, tiled=True)
     weights = (query_weight, key_weight, value_weight, query_down, value_down)
-    *early, early_flag = run(
+    *early, grad, grad_t = run(
         project_early_kernel,
         "project_near_half",
-        (shaped(tok_rows, query_width), shaped(tok_rows, 2 * HD), shaped(tok_rows, 2 * RANK), FLAG),
-        [smem(), hbm(), anywhere()] + [hbm()] * 5 + [anywhere()] * 2,
+        (
+            shaped(tok_rows, query_width),
+            shaped(tok_rows, 2 * HD),
+            shaped(tok_rows, 2 * RANK),
+            shaped(tok_rows, query_width, dtype=bf16),
+            shaped(query_width, tok_rows, dtype=bf16),
+        ),
+        [smem()] + [anywhere()] * 7 + [vmem()] * 2 + [smem()],
         project_scratch(tok_rows),
-        room=24,
-    )(place, slab_tokens, tok_near, *weights, mem_flag, asked)
-    mem_far = [mem_far[0]] + [after(m, early_flag) for m in mem_far[1:]]
-    mem_cross = [swap(m, 1) for m in mem_far]
-    cut_rows = mem_rows // mem_cuts
-    before = []
-    for t in range(mem_cuts):
-        last = t == mem_cuts - 1
-        scratch = memory_scratch(cut_rows) + [
-            pltpu.VMEM((cut_rows, 2 * HD), f32),
-            pltpu.VMEM((cut_rows, RANK), f32),
+    )(place, slab_tokens, tok_near, *weights, tag_t, grad_tags.T, wanted)
+    mem_far = after(mem_far, early[2])
+    mem_cross = swap(mem_far, 1)
+    pairs = run(
+        lambda *refs: memory_kernel(peers, *refs),
+        "memory_pairs",
+        shaped(peers, PACK, HD, dtype=bf16),
+        [smem()] * 2 + [anywhere()] * 7 + [vmem()],
+        memory_scratch(mem_rows)
+        + [
+            pltpu.VMEM((mem_rows, 2 * HD), f32),
+            pltpu.VMEM((mem_rows, RANK), f32),
             pltpu.SemaphoreType.DMA((2,)),
-        ]
-        if last:
-            other = jnp.concatenate(before, 0) if len(before) > 1 else before[0]
-            out_shape = shaped(peers, PACK, HD, dtype=bf16)
-            scratch.append(pltpu.VMEM((blocks, PACK, HD), bf16))
-        else:
-            other = early_flag
-            out_shape = shaped(cut_rows // BLK, PACK, HD, dtype=bf16)
-        result, pair_flag = run(
-            lambda *refs, t=t, last=last: memory_kernel(t * cut_rows, peers, last, *refs),
-            "memory_pairs",
-            (out_shape, FLAG),
-            [smem()] * 2 + [anywhere()] * 4 + [hbm()] * 3 + [vmem()] * 2,
-            scratch,
-            room=14,
-        )(
-            place, asked if last else place, mem_far[t], mem_cross[t], mem_acc, mem_low,
-            key_weight, value_weight, value_down, value_up, other,
-        )
-        before.append(result)
-    got = lax.all_to_all(before[-1], "tm", split_axis=0, concat_axis=0, tiled=True)
-
-    tok_far = [after(x, pair_flag) for x in tok_far]
-    tok_cross = [swap(x, 1) for x in tok_far]
-    parts = []
-    for t in range(tok_cuts):
-        parts += run(
-            lambda *refs, t=t: project_kernel(t * rows, *refs),
-            "project_far_half",
-            (
-                shaped(rows, query_width, dtype=bf16),
-                shaped(rows, HD, dtype=bf16),
-                shaped(rows, HD, dtype=bf16),
-                shaped(2 * RANK, rows, dtype=bf16),
-            ),
-            [smem()] + [anywhere()] * 2 + [hbm()] * 5 + [anywhere()] * 3 + [vmem()] * 2,
-            project_scratch(rows)
-            + [
-                pltpu.VMEM((rows, query_width), f32),
-                pltpu.VMEM((rows, 2 * HD), f32),
-                pltpu.VMEM((rows, 2 * RANK), f32),
-                pltpu.SemaphoreType.DMA((3,)),
-            ],
-            flops=2 * rows * 2 * width * (query_width + 3 * HD),
-            moved=4 * width * (rows + query_width + 3 * HD),
-            room=24,
-        )(place, tok_far[t], tok_cross[t], *weights, *early, query_up, value_up)
+            pltpu.VMEM((blocks, PACK, HD), bf16),
+        ],
+    )(place, asked, mem_far, mem_cross, mem_acc, mem_low, key_weight, value_weight, value_down, value_up)
+    got = lax.all_to_all(pairs, "tm", split_axis=0, concat_axis=0, tiled=True)
+    tok_far = after(tok_far, pairs)
+    tok_cross = swap(tok_far, 1)
 
     seen = peers * BLK
     total = seen + BLK
     cot, ups, mcot = run(
-        lambda *refs: attention_kernel(tok_cuts, peers, heads, *refs),
+        lambda *refs: attention_kernel(peers, heads, *refs),
         "span_attention",
         (shaped(2 * RANK + tags, tok_rows), shaped(RANK, query_width + HD), shaped(peers, RANK, BLK)),
-        [smem()] + [anywhere()] * (4 * tok_cuts + 3) + [vmem()] * 3,
-        [
+        [smem()] * 2 + [anywhere()] * 13 + [vmem()] * 3,
+        project_scratch(tok_rows)
+        + [
+            pltpu.VMEM((tok_rows, query_width), f32),
+            pltpu.VMEM((tok_rows, 2 * HD), f32),
+            pltpu.VMEM((tok_rows, 2 * RANK), f32),
             pltpu.VMEM((tok_rows, query_width), bf16),
             pltpu.VMEM((tok_rows, HD), bf16),
             pltpu.VMEM((tok_rows, HD), bf16),
@@ -826,12 +727,11 @@
             pltpu.VMEM((PAIR * BLK, query_width), bf16),
             pltpu.VMEM((PAIR * BLK, query_width), bf16),
             pltpu.VMEM((HD, seen), f32),
-            pltpu.SemaphoreType.DMA((3 * peers + 4 * tok_cuts + 2,)),
+            pltpu.SemaphoreType.DMA((3 * peers + 5,)),
         ],
         flops=20 * tok_rows * query_width * total,
         moved=4 * tok_rows * query_width,
-        room=34,
-    )(boundary, *parts, got, grad, grad_t, query_up, value_up, tag_t)
+    )(place, boundary, tok_far, tok_cross, *weights, *early, got, grad, grad_t, query_up, value_up, tag_t)
 
     back = lax.all_to_all(mcot, "tm", split_axis=0, concat_axis=0, tiled=True)
     cots = [cot] + [swap(cot, d) for d in range(1, 4)]
@@ -841,6 +741,7 @@
         shaped(RANK, mem_rows),
         [smem()] + [vmem()],
         [pltpu.VMEM((blocks, RANK, BLK), f32)],
+        room=8,
     )(asked, back)
     logits, query_sum, value_part = run(
         first_down_kernel,
@@ -849,6 +750,7 @@
         [vmem()] * 6 + [anywhere()],
         flops=4 * RANK * tok_rows * width,
         moved=2 * tok_rows * width,
+        room=8,
     )(*cots, slab_tokens, ups, own)
     owns = [own] + [swap(own, d) for d in range(1, 4)]
     value_sum = run(
@@ -858,16 +760,19 @@
         [vmem()] * 6,
         flops=2 * RANK * mem_rows * width,
         moved=2 * mem_rows * width,
+        room=8,
     )(*owns, memory, value_part)
-    for bit in (1, 2):
-        query_sum = query_sum + swap(query_sum, bit, "tm")
-        value_sum = value_sum + swap(value_sum, bit, "tm")
+    sums = []
+    for part in (query_sum, value_sum):
+        part = (part + swap(part, 1, "tm")).astype(bf16)
+        sums += [part] + [swap(part, bit, "tm") for bit in (2, 4, 6)]
     query_down_grad, query_up_grad, value_down_grad, value_up_grad = run(
         finish_kernel,
         "finish_outputs",
         (shaped(RANK, width), shaped(RANK, query_width), shaped(RANK, width), shaped(RANK, HD)),
-        [vmem()] * 4,
-    )(query_sum, swap(query_sum, 4, "tm"), value_sum, swap(value_sum, 4, "tm"))
+        [vmem()] * 8,
+        room=8,
+    )(*sums)
     return (logits.T, query_down_grad, query_up_grad, value_down_grad, value_up_grad)
 
 

time: 227 us -> 128 us (0.56)
  Pallas kernels: 114 us -> 47.9 us
  local copies, waits for them, and re-layouts: 43 us -> 7.32 us
  blocking collectives: 0 us -> 12.1 us
  starting transfers between devices: 30.4 us -> 26.2 us
  waiting for transfers between devices: 35.9 us -> 32.4 us
    pallas_call x9 -> x3, Pallas kernels: 105 us -> 36.6 us  [the longest x1 27.2 us: fast(): run(lambda *refs: attention_kernel(peers, heads, *refs), 'span_attention'...]
    unnamed x104 -> x26, local copies, waits for them, and re-layouts: 41.7 us -> 7.24 us
    all_to_all x0 -> x1, blocking collectives: none -> 12.1 us  [fast(): lax.all_to_all(wanted, 'tm', split_axis=0, concat_axis=0, tiled=True)]
    ppermute x22 -> x20, waiting for transfers between devices: 24.8 us -> 16.8 us  [swap(): lax.ppermute(x, axis, [(i, i ^ bit) for i in range(lax.axis_size(axis))])]
    all_to_all x2 -> x1, starting transfers between devices: 9.95 us -> 3.73 us  [fast(): got = lax.all_to_all(pairs, 'tm', split_axis=0, concat_axis=0, tiled=True)]
    all_to_all x2 -> x1, waiting for transfers between devices: 6.31 us -> 10.6 us  [fast(): got = lax.all_to_all(pairs, 'tm', split_axis=0, concat_axis=0, tiled=True)]
    pallas_call x1, Pallas kernels: 6.7 us -> 9.03 us  [fast(): run(project_early_kernel, 'project_near_half', (shaped(tok_rows, query_wi...]
    ppermute x22 -> x20, starting transfers between devices: 17.1 us -> 18.9 us  [swap(): lax.ppermute(x, axis, [(i, i ^ bit) for i in range(lax.axis_size(axis))])]
  transfers between devices with their start and end apart: 25 -> 22, of which waited for: 9 -> 9; matrix products, arithmetic and copies ran while one was open for 1% -> 1% of each run, Pallas kernels for 40% -> 15%
where the time goes in v1:
time: 128 us
  Pallas kernels  47.9 us (37%)
  waiting for transfers between devices  32.4 us (25%)
  starting transfers between devices  26.2 us (20%)
  blocking collectives  12.1 us (9%)
  local copies, waits for them, and re-layouts  7.32 us (6%)
    pallas_call x1, Pallas kernels, fast(): run(lambda *refs: attention_kernel(peers, heads, *refs), 'span_attention'...  27.2 us
    ppermute x20, starting transfers between devices, swap(): lax.ppermute(x, axis, [(i, i ^ bit) for i in range(lax.axis_size(axis))])  18.9 us
    ppermute x20, waiting for transfers between devices, swap(): lax.ppermute(x, axis, [(i, i ^ bit) for i in range(lax.axis_size(axis))])  16.8 us
    all_to_all x1, blocking collectives, fast(): lax.all_to_all(wanted, 'tm', split_axis=0, concat_axis=0, tiled=True)  12.1 us
    all_to_all x1, waiting for transfers between devices, fast(): got = lax.all_to_all(pairs, 'tm', split_axis=0, concat_axis=0, tiled=True)  10.6 us
    pallas_call x1, Pallas kernels, fast(): run(project_early_kernel, 'project_near_half', (shaped(tok_rows, query_wi...  9.03 us
    unnamed x26, local copies, waits for them, and re-layouts  7.24 us
    pallas_call x1, Pallas kernels, fast(): run(lambda *refs: memory_kernel(peers, *refs), 'memory_pairs', shaped(pee...  5.13 us
  transfers between devices with their start and end apart: 22, of which 9 were waited for; matrix products, arithmetic and copies ran while one was open for 1% of the time, Pallas kernels for 15%

profile of v1, /device:TPU:0, one launch (start us, length us, event | category | flops | bytes accessed | tf_op | source)
XLA Modules:
  0.0 127.5 jit_solution(4649150911674336598)
XLA Ops:
  0.6 0.5 collective-permute-start.2
  1.1 0.1 collective-permute-start
  1.2 2.9 %collective-permute-start.3 = (bf16[512,896]{1,0:T(8,128)(2,1)}, bf16[512,896]{1,0:T(8,128)(2,1)S(1)}, u32[]{:S(2)}, u32[]{:S(2)}) collective-permute-start(bf16[512,896]{1,0:T(8,128)(2,1)} %memory_ref.1), channel_id=1, source_target_pairs={{0,2},{1,3},{2,0},{3,1},{4,6},{5,7},{6,4},{7,5},{8,10},{9,11},{10,... | collective-permute-start | bytes 2752520 | tf_op jit(solution)/shard_map/ppermute | solution.py:558
  4.2 0.0 collective-permute-done.2.refs_3_
  4.2 0.9 copy-done.7
  5.1 4.3 %memory_near_half.1 = (f32[512,256]{1,0:T(8,128)}, f32[512,16]{1,0:T(8,128)}, s32[8]{0:T(128)}) custom-call(s32[1]{0:T(128)} %bitcast.refs_0_.place_ref, s32[4,8]{1,0:T(4,128)} %refs_1_.3, bf16[512,896]{1,0:T(8,128)(2,1)} %memory_ref.1, bf16[512,896]{1,0:T(8,128)(2,1)} %copy-done.7, bf16[3584,128]{1,0:T(8,128)(2,1)} %refs_5_.3, bf16[3584,128]{1,0:T(8,128)(2,1)} %refs_6_.5, ...), custom_call_target="tpu_custom_call" | custom-call | tf_op jit(solution)/shard_map/memory_near_half/pallas_call | solution.py:654
  9.4 0.0 copy-start.11
  9.5 0.0 collective-permute-done.x1
  9.5 0.9 copy-done.6
  10.4 9.0 %project_near_half.1 = (f32[512,896]{1,0:T(8,128)}, f32[512,256]{1,0:T(8,128)}, f32[512,32]{1,0:T(8,128)}, bf16[512,896]{1,0:T(8,128)(2,1)}, bf16[896,512]{1,0:T(8,128)(2,1)}) custom-call(s32[1]{0:T(128)} %bitcast.refs_0_.place_ref, bf16[512,896]{1,0:T(8,128)(2,1)} %slab_ref.1, bf16[512,896]{1,0:T(8,128)(2,1)} %copy-done.6, bf16[3584,896]{1,0:T(8,128)(2,1)} %refs_4_.5, ...), custom_call_target="tpu_custom_call" | custom-call | tf_op jit(solution)/shard_map/project_near_half/pallas_call | solution.py:664
  19.4 5.5 %collective-permute-done.3.x_ref = bf16[512,896]{1,0:T(8,128)(2,1)S(1)} collective-permute-done((bf16[512,896]{1,0:T(8,128)(2,1)}, bf16[512,896]{1,0:T(8,128)(2,1)S(1)}, u32[]{:S(2)}, u32[]{:S(2)}) %collective-permute-start.3) | collective-permute-done | bytes 917536 | tf_op jit(solution)/shard_map/ppermute | solution.py:558
  25.0 0.9 copy-done.5
  25.9 0.0 collective-permute-start.4
  25.9 1.7 %collective-permute-start.1 = (bf16[512,896]{1,0:T(8,128)(2,1)}, bf16[512,896]{1,0:T(8,128)(2,1)S(1)}, u32[]{:S(2)}, u32[]{:S(2)}) collective-permute-start(bf16[512,896]{1,0:T(8,128)(2,1)} %copy-done.6), channel_id=1, source_target_pairs={{0,2},{1,3},{2,0},{3,1},{4,6},{5,7},{6,4},{7,5},{8,10},{9,11},{10,... | collective-permute-start | bytes 2752520 | tf_op jit(solution)/shard_map/ppermute | solution.py:558
  27.7 0.1 copy.21
  27.7 12.1 %all_to_all.21 = s32[8,1,1]{2,1,0:T(1,128)S(1)} all-to-all(s32[8,1,1]{2,1,0:T(1,128)S(1)} %copy.21), channel_id=1, replica_groups=mesh['tm'=8,'heads'=4] {'tm'}, dimensions={0} | all-to-all | bytes 64 | tf_op jit(solution)/shard_map/all_to_all | solution.py:662
  39.8 0.8 reduce.refs_1_.refs_0_
  40.5 0.0 collective-permute-done.4.refs_3_
  40.6 0.9 copy-done.8
  41.5 5.1 %memory_pairs.1.dep_ref = bf16[8,272,128]{2,1,0:T(8,128)(2,1)} custom-call(s32[1]{0:T(128)} %bitcast.refs_0_.place_ref, s32[8]{0:T(128)} %reduce.refs_1_.refs_0_, bf16[512,896]{1,0:T(8,128)(2,1)} %in_order.2.refs_2_, bf16[512,896]{1,0:T(8,128)(2,1)} %copy-done.8, f32[512,256]{1,0:T(8,128)} %get-tuple-element.25.refs_4_, ...), custom_call_target="tpu_custom_call" | custom-call | tf_op jit(solution)/shard_map/memory_pairs/pallas_call | solution.py:679
  46.6 3.7 %all-to-all-start.1 = ((bf16[8,272,128]{2,1,0:T(8,128)(2,1)}), bf16[8,272,128]{2,1,0:T(8,128)(2,1)S(1)}, u32[]{:S(2)}, u32[]{:S(2)}) async-start(bf16[8,272,128]{2,1,0:T(8,128)(2,1)} %memory_pairs.1.dep_ref), calls=%async_computation.1 | async-start | bytes 1114112 | tf_op jit(solution)/shard_map/all_to_all | solution.py:692
  50.4 0.0 collective-permute-done.1.x_ref
  50.4 0.9 copy-done.9
  51.3 0.0 collective-permute-start.5
  51.3 2.7 %collective-permute-done.5.refs_3_ = bf16[512,896]{1,0:T(8,128)(2,1)S(1)} collective-permute-done((bf16[512,896]{1,0:T(8,128)(2,1)}, bf16[512,896]{1,0:T(8,128)(2,1)S(1)}, u32[]{:S(2)}, u32[]{:S(2)}) %collective-permute-start.5) | collective-permute-done | bytes 917536 | tf_op jit(solution)/shard_map/ppermute | solution.py:558
  54.0 10.6 %all-to-all-done.1.refs_12_ = bf16[8,272,128]{2,1,0:T(8,128)(2,1)S(1)} async-done(((bf16[8,272,128]{2,1,0:T(8,128)(2,1)}), bf16[8,272,128]{2,1,0:T(8,128)(2,1)S(1)}, u32[]{:S(2)}, u32[]{:S(2)}) %all-to-all-start.1) | async-done | bytes 557088 | tf_op jit(solution)/shard_map/all_to_all | solution.py:692
  64.6 0.8 copy-done.10
  65.4 27.2 %span_attention.1 = (f32[40,512]{1,0:T(8,128)}, f32[16,1024]{1,0:T(8,128)}, f32[8,16,128]{2,1,0:T(8,128)}) custom-call(s32[1]{0:T(128)} %bitcast.refs_0_.place_ref, s32[4]{0:T(128)} %refs_1_.5, bf16[512,896]{1,0:T(8,128)(2,1)} %in_order.3.refs_2_, bf16[512,896]{1,0:T(8,128)(2,1)} %copy-done.12, bf16[3584,896]{1,0:T(8,128)(2,1)} %refs_4_.5, ...), custom_call_target="tpu_custom_call" | custom-call | flops 10569646080 | bytes 1835008 | tf_op jit(solution)/shard_map/span_attention/pallas_call | solution.py:698
  92.6 3.6 %all-to-all-start.2 = ((f32[8,16,128]{2,1,0:T(8,128)}), f32[8,16,128]{2,1,0:T(8,128)S(1)}, u32[]{:S(2)}, u32[]{:S(2)}) async-start(f32[8,16,128]{2,1,0:T(8,128)} %get-tuple-element.33), calls=%async_computation.2 | async-start | bytes 131072 | tf_op jit(solution)/shard_map/all_to_all | solution.py:736
  96.2 0.0 collective-permute-start.8
  96.2 0.7 collective-permute-start.7
  97.0 1.1 collective-permute-start.6
  98.1 5.0 %all-to-all-done.2.refs_1_ = f32[8,16,128]{2,1,0:T(8,128)S(1)} async-done(((f32[8,16,128]{2,1,0:T(8,128)}), f32[8,16,128]{2,1,0:T(8,128)S(1)}, u32[]{:S(2)}, u32[]{:S(2)}) %all-to-all-start.2) | async-done | bytes 65568 | tf_op jit(solution)/shard_map/all_to_all | solution.py:736
  103.1 0.6 owned_cotangent.1.dep_ref.c0
  103.7 0.0 collective-permute-done.8.c3
  103.7 0.0 collective-permute-done.7.c2
  103.7 0.0 collective-permute-done.6.c1
  103.8 0.9 copy-done.2
  104.7 0.8 copy-done.3
  105.5 0.8 first_down.1
  106.2 0.4 collective-permute-start.9
  106.6 0.7 collective-permute-start.15
  107.3 0.7 collective-permute-start.14
  108.0 0.5 collective-permute-start.13
  108.5 1.7 %collective-permute-done.15.c3 = f32[16,512]{1,0:T(8,128)S(1)} collective-permute-done((f32[16,512]{1,0:T(8,128)S(1)}, f32[16,512]{1,0:T(8,128)S(1)}, u32[]{:S(2)}, u32[]{:S(2)}) %collective-permute-start.15) | collective-permute-done | bytes 32800 | tf_op jit(solution)/shard_map/ppermute | solution.py:558
  110.2 1.2 collective-permute-done.14.c2
  111.4 0.0 collective-permute-done.13.c1
  111.4 0.2 second_down.1
  111.6 1.0 collective-permute-start.16
  112.6 0.0 collective-permute-done.9
  112.6 3.0 %collective-permute-start.12 = (bf16[16,1920]{1,0:T(8,128)(2,1)S(1)}, bf16[16,1920]{1,0:T(8,128)(2,1)S(1)}, u32[]{:S(2)}, u32[]{:S(2)}) collective-permute-start(bf16[16,1920]{1,0:T(8,128)(2,1)S(1)} %add_convert_fusion.refs_0_), channel_id=1, source_target_pairs={{0,24},{4,28},{8,16},{12,20},{16,8},{20,12},{24,0},{28,4},{1,25},{... | collective-permute-start | bytes 184328 | tf_op jit(solution)/shard_map/ppermute | solution.py:558
  115.6 0.0 collective-permute-start.11
  115.6 1.5 %collective-permute-start.10 = (bf16[16,1920]{1,0:T(8,128)(2,1)S(1)}, bf16[16,1920]{1,0:T(8,128)(2,1)S(1)}, u32[]{:S(2)}, u32[]{:S(2)}) collective-permute-start(bf16[16,1920]{1,0:T(8,128)(2,1)S(1)} %add_convert_fusion.refs_0_), channel_id=1, source_target_pairs={{0,8},{4,12},{8,0},{12,4},{16,24},{20,28},{24,16},{28,20},{1,9},{5... | collective-permute-start | bytes 184328 | tf_op jit(solution)/shard_map/ppermute | solution.py:558
  117.1 0.0 collective-permute-done.16
  117.1 3.0 %collective-permute-start.19 = (bf16[16,896]{1,0:T(8,128)(2,1)S(1)}, bf16[16,896]{1,0:T(8,128)(2,1)S(1)}, u32[]{:S(2)}, u32[]{:S(2)}) collective-permute-start(bf16[16,896]{1,0:T(8,128)(2,1)S(1)} %add_convert_fusion.1.refs_4_), channel_id=1, source_target_pairs={{0,24},{4,28},{8,16},{12,20},{16,8},{20,12},{24,0},{28,4},{1,25},{... | collective-permute-start | bytes 86024 | tf_op jit(solution)/shard_map/ppermute | solution.py:558
  120.1 0.0 collective-permute-start.18
  120.1 2.9 %collective-permute-done.19.refs_7_ = bf16[16,896]{1,0:T(8,128)(2,1)S(1)} collective-permute-done((bf16[16,896]{1,0:T(8,128)(2,1)S(1)}, bf16[16,896]{1,0:T(8,128)(2,1)S(1)}, u32[]{:S(2)}, u32[]{:S(2)}) %collective-permute-start.19) | collective-permute-done | bytes 28704 | tf_op jit(solution)/shard_map/ppermute | solution.py:558
  122.9 1.1 collective-permute-start.17
  124.0 0.8 collective-permute-done.18.refs_6_
  124.8 2.0 %collective-permute-done.17.refs_5_ = bf16[16,896]{1,0:T(8,128)(2,1)S(1)} collective-permute-done((bf16[16,896]{1,0:T(8,128)(2,1)S(1)}, bf16[16,896]{1,0:T(8,128)(2,1)S(1)}, u32[]{:S(2)}, u32[]{:S(2)}) %collective-permute-start.17) | collective-permute-done | bytes 28704 | tf_op jit(solution)/shard_map/ppermute | solution.py:558
  126.8 0.0 collective-permute-done.12.refs_3_
  126.8 0.0 collective-permute-done.11.refs_2_
  126.8 0.0 collective-permute-done.10.refs_1_
  126.8 0.7 finish_outputs.1
  (21 shorter events, 0.1 us)
Async XLA Ops:
  0.6 3.5 %collective-permute-start.2 = (bf16[512,896]{1,0:T(8,128)(2,1)}, bf16[512,896]{1,0:T(8,128)(2,1)S(1)}, u32[]{:S(2)}, u32[]{:S(2)}) collective-permute-start(bf16[512,896]{1,0:T(8,128)(2,1)} %memory_ref.1), channel_id=1, source_target_pairs={{0,1},{1,0},{2,3},{3,2},{4,5},{5,4},{6,7},{7,6},{8,9},{9,8},{10,11... | collective-permute-start | bytes 2752520 | tf_op jit(solution)/shard_map/ppermute | solution.py:558
  1.1 8.3 %collective-permute-start = (bf16[512,896]{1,0:T(8,128)(2,1)}, bf16[512,896]{1,0:T(8,128)(2,1)S(1)}, u32[]{:S(2)}, u32[]{:S(2)}) collective-permute-start(bf16[512,896]{1,0:T(8,128)(2,1)} %slab_ref.1), channel_id=1, source_target_pairs={{0,1},{1,0},{2,3},{3,2},{4,5},{5,4},{6,7},{7,6},{8,9},{9,8},{10,11... | collective-permute-start | bytes 2752520 | tf_op jit(solution)/shard_map/ppermute | solution.py:558
  1.2 23.7 %collective-permute-start.3 = (bf16[512,896]{1,0:T(8,128)(2,1)}, bf16[512,896]{1,0:T(8,128)(2,1)S(1)}, u32[]{:S(2)}, u32[]{:S(2)}) collective-permute-start(bf16[512,896]{1,0:T(8,128)(2,1)} %memory_ref.1), channel_id=1, source_target_pairs={{0,2},{1,3},{2,0},{3,1},{4,6},{5,7},{6,4},{7,5},{8,10},{9,11},{10,... | collective-permute-start | bytes 2752520 | tf_op jit(solution)/shard_map/ppermute | solution.py:558
  4.2 0.9 copy-start.7
  9.4 18.2 %copy-start.11 = (s32[8]{0:T(128)S(1)}, s32[8]{0:T(128)}, u32[]{:S(2)}) copy-start(s32[8]{0:T(128)} %get-tuple-element.23.refs_7_) | copy-start | bytes 100
  9.5 0.9 copy-start.6
  25.0 0.9 copy-start.5
  25.9 14.6 %collective-permute-start.4 = (bf16[512,896]{1,0:T(8,128)(2,1)}, bf16[512,896]{1,0:T(8,128)(2,1)S(1)}, u32[]{:S(2)}, u32[]{:S(2)}) collective-permute-start(bf16[512,896]{1,0:T(8,128)(2,1)} %in_order.2.refs_2_), channel_id=1, source_target_pairs={{0,1},{1,0},{2,3},{3,2},{4,5},{5,4},{6,7},{7,6},{8,9},{9,8},{10,11... | collective-permute-start | bytes 2752520 | tf_op jit(solution)/shard_map/ppermute | solution.py:558
  25.9 24.5 %collective-permute-start.1 = (bf16[512,896]{1,0:T(8,128)(2,1)}, bf16[512,896]{1,0:T(8,128)(2,1)S(1)}, u32[]{:S(2)}, u32[]{:S(2)}) collective-permute-start(bf16[512,896]{1,0:T(8,128)(2,1)} %copy-done.6), channel_id=1, source_target_pairs={{0,2},{1,3},{2,0},{3,1},{4,6},{5,7},{6,4},{7,5},{8,10},{9,11},{10,... | collective-permute-start | bytes 2752520 | tf_op jit(solution)/shard_map/ppermute | solution.py:558
  40.5 0.9 copy-start.8
  46.6 18.0 %all-to-all-start.1 = ((bf16[8,272,128]{2,1,0:T(8,128)(2,1)}), bf16[8,272,128]{2,1,0:T(8,128)(2,1)S(1)}, u32[]{:S(2)}, u32[]{:S(2)}) async-start(bf16[8,272,128]{2,1,0:T(8,128)(2,1)} %memory_pairs.1.dep_ref), calls=%async_computation.1 | async-start | bytes 1114112 | tf_op jit(solution)/shard_map/all_to_all | solution.py:692
  50.4 0.9 copy-start.9
  51.3 2.7 %collective-permute-start.5 = (bf16[512,896]{1,0:T(8,128)(2,1)}, bf16[512,896]{1,0:T(8,128)(2,1)S(1)}, u32[]{:S(2)}, u32[]{:S(2)}) collective-permute-start(bf16[512,896]{1,0:T(8,128)(2,1)} %in_order.3.refs_2_), channel_id=1, source_target_pairs={{0,1},{1,0},{2,3},{3,2},{4,5},{5,4},{6,7},{7,6},{8,9},{9,8},{10,11... | collective-permute-start | bytes 2752520 | tf_op jit(solution)/shard_map/ppermute | solution.py:558
  54.0 10.6 %copy-start.12 = (bf16[512,896]{1,0:T(8,128)(2,1)}, bf16[512,896]{1,0:T(8,128)(2,1)S(1)}, u32[]{:S(2)}) copy-start(bf16[512,896]{1,0:T(8,128)(2,1)S(1)} %collective-permute-done.5.refs_3_) | copy-start | bytes 2752516
  64.6 0.8 copy-start.10
  65.4 37.7 %copy-start.4 = (s32[8]{0:T(128)S(1)}, s32[8]{0:T(128)}, u32[]{:S(2)}) copy-start(s32[8]{0:T(128)} %reduce.refs_1_.refs_0_) | copy-start | bytes 100
  65.4 38.3 %copy-start = (bf16[512,896]{1,0:T(8,128)(2,1)S(1)}, bf16[512,896]{1,0:T(8,128)(2,1)}, u32[]{:S(2)}) copy-start(bf16[512,896]{1,0:T(8,128)(2,1)} %slab_ref.1) | copy-start | bytes 2752516
  65.4 46.0 %copy-start.1 = (bf16[512,896]{1,0:T(8,128)(2,1)S(1)}, bf16[512,896]{1,0:T(8,128)(2,1)}, u32[]{:S(2)}) copy-start(bf16[512,896]{1,0:T(8,128)(2,1)} %memory_ref.1) | copy-start | bytes 2752516
  92.6 10.5 %all-to-all-start.2 = ((f32[8,16,128]{2,1,0:T(8,128)}), f32[8,16,128]{2,1,0:T(8,128)S(1)}, u32[]{:S(2)}, u32[]{:S(2)}) async-start(f32[8,16,128]{2,1,0:T(8,128)} %get-tuple-element.33), calls=%async_computation.2 | async-start | bytes 131072 | tf_op jit(solution)/shard_map/all_to_all | solution.py:736
  96.2 7.5 %collective-permute-start.8 = (f32[40,512]{1,0:T(8,128)}, f32[40,512]{1,0:T(8,128)S(1)}, u32[]{:S(2)}, u32[]{:S(2)}) collective-permute-start(f32[40,512]{1,0:T(8,128)} %get-tuple-element.31.c0), channel_id=1, source_target_pairs={{0,3},{1,2},{2,1},{3,0},{4,7},{5,6},{6,5},{7,4},{8,11},{9,10},{10,... | collective-permute-start | bytes 245768 | tf_op jit(solution)/shard_map/ppermute | solution.py:558
  96.2 7.5 %collective-permute-start.7 = (f32[40,512]{1,0:T(8,128)}, f32[40,512]{1,0:T(8,128)S(1)}, u32[]{:S(2)}, u32[]{:S(2)}) collective-permute-start(f32[40,512]{1,0:T(8,128)} %get-tuple-element.31.c0), channel_id=1, source_target_pairs={{0,2},{1,3},{2,0},{3,1},{4,6},{5,7},{6,4},{7,5},{8,10},{9,11},{10,... | collective-permute-start | bytes 245768 | tf_op jit(solution)/shard_map/ppermute | solution.py:558
  97.0 6.8 %collective-permute-start.6 = (f32[40,512]{1,0:T(8,128)}, f32[40,512]{1,0:T(8,128)S(1)}, u32[]{:S(2)}, u32[]{:S(2)}) collective-permute-start(f32[40,512]{1,0:T(8,128)} %get-tuple-element.31.c0), channel_id=1, source_target_pairs={{0,1},{1,0},{2,3},{3,2},{4,5},{5,4},{6,7},{7,6},{8,9},{9,8},{10,11... | collective-permute-start | bytes 245768 | tf_op jit(solution)/shard_map/ppermute | solution.py:558
  103.8 0.9 copy-start.2
  104.7 0.8 copy-start.3
  106.2 6.4 %collective-permute-start.9 = (f32[16,1920]{1,0:T(8,128)S(1)}, f32[16,1920]{1,0:T(8,128)S(1)}, u32[]{:S(2)}, u32[]{:S(2)}) collective-permute-start(f32[16,1920]{1,0:T(8,128)S(1)} %get-tuple-element.35), channel_id=1, source_target_pairs={{0,4},{4,0},{8,12},{12,8},{16,20},{20,16},{24,28},{28,24},{1,5},{5... | collective-permute-start | bytes 368648 | tf_op jit(solution)/shard_map/ppermute | solution.py:558
  106.6 3.6 %collective-permute-start.15 = (f32[16,512]{1,0:T(8,128)S(1)}, f32[16,512]{1,0:T(8,128)S(1)}, u32[]{:S(2)}, u32[]{:S(2)}) collective-permute-start(f32[16,512]{1,0:T(8,128)S(1)} %owned_cotangent.1.dep_ref.c0), channel_id=1, source_target_pairs={{0,3},{1,2},{2,1},{3,0},{4,7},{5,6},{6,5},{7,4},{8,11},{9,10},{10,... | collective-permute-start | bytes 98312 | tf_op jit(solution)/shard_map/ppermute | solution.py:558
  107.3 4.0 %collective-permute-start.14 = (f32[16,512]{1,0:T(8,128)S(1)}, f32[16,512]{1,0:T(8,128)S(1)}, u32[]{:S(2)}, u32[]{:S(2)}) collective-permute-start(f32[16,512]{1,0:T(8,128)S(1)} %owned_cotangent.1.dep_ref.c0), channel_id=1, source_target_pairs={{0,2},{1,3},{2,0},{3,1},{4,6},{5,7},{6,4},{7,5},{8,10},{9,11},{10,... | collective-permute-start | bytes 98312 | tf_op jit(solution)/shard_map/ppermute | solution.py:558
  108.0 3.4 %collective-permute-start.13 = (f32[16,512]{1,0:T(8,128)S(1)}, f32[16,512]{1,0:T(8,128)S(1)}, u32[]{:S(2)}, u32[]{:S(2)}) collective-permute-start(f32[16,512]{1,0:T(8,128)S(1)} %owned_cotangent.1.dep_ref.c0), channel_id=1, source_target_pairs={{0,1},{1,0},{2,3},{3,2},{4,5},{5,4},{6,7},{7,6},{8,9},{9,8},{10,11... | collective-permute-start | bytes 98312 | tf_op jit(solution)/shard_map/ppermute | solution.py:558
  111.6 5.5 %collective-permute-start.16 = (f32[16,896]{1,0:T(8,128)S(1)}, f32[16,896]{1,0:T(8,128)S(1)}, u32[]{:S(2)}, u32[]{:S(2)}) collective-permute-start(f32[16,896]{1,0:T(8,128)S(1)} %second_down.1), channel_id=1, source_target_pairs={{0,4},{4,0},{8,12},{12,8},{16,20},{20,16},{24,28},{28,24},{1,5},{5... | collective-permute-start | bytes 172040 | tf_op jit(solution)/shard_map/ppermute | solution.py:558
  112.6 14.2 %collective-permute-start.12 = (bf16[16,1920]{1,0:T(8,128)(2,1)S(1)}, bf16[16,1920]{1,0:T(8,128)(2,1)S(1)}, u32[]{:S(2)}, u32[]{:S(2)}) collective-permute-start(bf16[16,1920]{1,0:T(8,128)(2,1)S(1)} %add_convert_fusion.refs_0_), channel_id=1, source_target_pairs={{0,24},{4,28},{8,16},{12,20},{16,8},{20,12},{24,0},{28,4},{1,25},{... | collective-permute-start | bytes 184328 | tf_op jit(solution)/shard_map/ppermute | solution.py:558
  115.6 11.2 %collective-permute-start.11 = (bf16[16,1920]{1,0:T(8,128)(2,1)S(1)}, bf16[16,1920]{1,0:T(8,128)(2,1)S(1)}, u32[]{:S(2)}, u32[]{:S(2)}) collective-permute-start(bf16[16,1920]{1,0:T(8,128)(2,1)S(1)} %add_convert_fusion.refs_0_), channel_id=1, source_target_pairs={{0,16},{4,20},{8,24},{12,28},{16,0},{20,4},{24,8},{28,12},{1,17},{... | collective-permute-start | bytes 184328 | tf_op jit(solution)/shard_map/ppermute | solution.py:558
  115.6 11.2 %collective-permute-start.10 = (bf16[16,1920]{1,0:T(8,128)(2,1)S(1)}, bf16[16,1920]{1,0:T(8,128)(2,1)S(1)}, u32[]{:S(2)}, u32[]{:S(2)}) collective-permute-start(bf16[16,1920]{1,0:T(8,128)(2,1)S(1)} %add_convert_fusion.refs_0_), channel_id=1, source_target_pairs={{0,8},{4,12},{8,0},{12,4},{16,24},{20,28},{24,16},{28,20},{1,9},{5... | collective-permute-start | bytes 184328 | tf_op jit(solution)/shard_map/ppermute | solution.py:558
  117.1 5.8 %collective-permute-start.19 = (bf16[16,896]{1,0:T(8,128)(2,1)S(1)}, bf16[16,896]{1,0:T(8,128)(2,1)S(1)}, u32[]{:S(2)}, u32[]{:S(2)}) collective-permute-start(bf16[16,896]{1,0:T(8,128)(2,1)S(1)} %add_convert_fusion.1.refs_4_), channel_id=1, source_target_pairs={{0,24},{4,28},{8,16},{12,20},{16,8},{20,12},{24,0},{28,4},{1,25},{... | collective-permute-start | bytes 86024 | tf_op jit(solution)/shard_map/ppermute | solution.py:558
  120.1 4.8 %collective-permute-start.18 = (bf16[16,896]{1,0:T(8,128)(2,1)S(1)}, bf16[16,896]{1,0:T(8,128)(2,1)S(1)}, u32[]{:S(2)}, u32[]{:S(2)}) collective-permute-start(bf16[16,896]{1,0:T(8,128)(2,1)S(1)} %add_convert_fusion.1.refs_4_), channel_id=1, source_target_pairs={{0,16},{4,20},{8,24},{12,28},{16,0},{20,4},{24,8},{28,12},{1,17},{... | collective-permute-start | bytes 86024 | tf_op jit(solution)/shard_map/ppermute | solution.py:558
  122.9 3.9 %collective-permute-start.17 = (bf16[16,896]{1,0:T(8,128)(2,1)S(1)}, bf16[16,896]{1,0:T(8,128)(2,1)S(1)}, u32[]{:S(2)}, u32[]{:S(2)}) collective-permute-start(bf16[16,896]{1,0:T(8,128)(2,1)S(1)} %add_convert_fusion.1.refs_4_), channel_id=1, source_target_pairs={{0,8},{4,12},{8,0},{12,4},{16,24},{20,28},{24,16},{28,20},{1,9},{5... | collective-permute-start | bytes 86024 | tf_op jit(solution)/shard_map/ppermute | solution.py:558

commit v2 on v1

--- a/solution.py
+++ b/solution.py
@@ -230,7 +230,7 @@
 STRIP = 16
 PAIR = 2
 MIB = 1024 * 1024
-ROOM = 60
+ROOM = 63
 
 
 def dot_nt(a, b, precision=None):
@@ -296,19 +296,28 @@
             low_ref[...] += low_term
 
 
-def memory_kernel(peers, place_ref, asked_ref, x2, x3, acc_hbm, low_hbm, *refs):
+def memory_middle_kernel(place_ref, x2, acc_hbm, low_hbm, *refs):
+    hbm, acc_ref, low_ref, scratch, sems = refs[:3], refs[3], refs[4], refs[5:9], refs[9]
+    acc_s, low_s, acc_sems = refs[10:13]
+    groups = memory_pieces(place_ref, (2,), (x2,), hbm, scratch, sems)
+    sums = start_copies([(acc_hbm, acc_s), (low_hbm, low_s)], acc_sems)
+    wait_all(groups[0])
+    term, low_term = memory_terms(0, scratch)
+    wait_all(sums)
+    acc_ref[...] = acc_s[...] + term
+    low_ref[...] = low_s[...] + low_term
+
+
+def memory_kernel(peers, place_ref, asked_ref, x3, acc_hbm, low_hbm, *refs):
     hbm, up_ref, out_ref = refs[:3], refs[3], refs[4]
     scratch, sems, acc_s, low_s, acc_sems, pair_ref = refs[5:9], refs[9], refs[10], refs[11], refs[12], refs[13]
+    groups = memory_pieces(place_ref, (3,), (x3,), hbm, scratch, sems)
     sums = start_copies([(acc_hbm, acc_s), (low_hbm, low_s)], acc_sems)
-    groups = memory_pieces(place_ref, (2, 3), (x2, x3), hbm, scratch, sems)
+    wait_all(groups[0])
+    term, low_term = memory_terms(0, scratch)
     wait_all(sums)
-    acc = acc_s[...]
-    low = low_s[...]
-    for n in range(2):
-        wait_all(groups[n])
-        term, low_term = memory_terms(n, scratch)
-        acc = acc + term
-        low = low + low_term
+    acc = acc_s[...] + term
+    low = low_s[...] + low_term
     values = (acc[:, HD:] + dot_nn(low.astype(jnp.bfloat16), up_ref[...])).astype(jnp.bfloat16)
     keys = acc[:, :HD].astype(jnp.bfloat16)
     low_t = jnp.transpose(low).astype(jnp.bfloat16)
@@ -380,14 +389,26 @@
                 ref[...] += term
 
 
-def attention_kernel(peers, heads, place_ref, bound_ref, x3, x2, *refs):
+def project_middle_kernel(place_ref, x3, *refs):
+    hbm, early, outs, scratch, sems = refs[:5], refs[5:8], refs[8:11], refs[11:17], refs[17]
+    sum_refs, sum_sems = refs[18:21], refs[21]
+    groups = project_pieces(place_ref, (3,), (x3,), hbm, scratch, sems)
+    loads = start_copies(list(zip(early, sum_refs)), sum_sems)
+    wait_all(groups[0])
+    terms = project_terms(0, scratch)
+    wait_all(loads)
+    for out, ref, term in zip(outs, sum_refs, terms):
+        out[...] = ref[...] + term
+
+
+def attention_kernel(peers, heads, place_ref, bound_ref, x2, *refs):
     hbm, early, got, grad_hbm, grad_t_hbm = refs[:5], refs[5:8], refs[8], refs[9], refs[10]
     qup_ref, vup_ref, tag_ref, cot_ref, up_ref, mcot_ref = refs[11:17]
     scratch, sems, sum_refs = refs[17:23], refs[23], refs[24:27]
-    (q_s, k_own, v_own, low_s, low_m_s, grad_ref, grad_t_ref, k_all, v_all, kt_all, vt_all, kt_own, vt_own, bias_s, s_s, e_s, dp_s,
+    (q_s, k_own, v_own, low_s, low_m_s, grad_ref, grad_t_ref, k_all, v_all, kt_all, vt_all, kt_own, vt_own, bias_s, s_s, dp_s,
      p_s, ds_s, att_s, dq_s, dv_s, more_sems) = refs[27:]
     seen = peers * BLK
-    groups = project_pieces(place_ref, (3, 2), (x3, x2), hbm, scratch, sems)
+    groups = project_pieces(place_ref, (2,), (x2,), hbm, scratch, sems)
     pairs = list(zip(early, sum_refs))
     for b in range(peers):
         at = slice(b * BLK, (b + 1) * BLK)
@@ -397,12 +418,8 @@
     pairs += [(grad_hbm, grad_ref), (grad_t_hbm, grad_t_ref)]
     copies = start_copies(pairs, more_sems)
     wait_all(groups[0])
-    for ref, term in zip(sum_refs, project_terms(0, scratch)):
-        if ref is sum_refs[0]:
-            wait_all(copies[:3])
-        ref[...] += term
-    wait_all(groups[1])
-    q_acc, kv_acc, low_acc = [ref[...] + term for ref, term in zip(sum_refs, project_terms(1, scratch))]
+    wait_all(copies[:3])
+    q_acc, kv_acc, low_acc = [ref[...] + term for ref, term in zip(sum_refs, project_terms(0, scratch))]
     low = low_acc.astype(jnp.bfloat16)
     q_s[...] = (q_acc + dot_nn(low[:, :RANK], qup_ref[...])).astype(jnp.bfloat16)
     k_own[...] = kv_acc[:, :HD].astype(jnp.bfloat16)
@@ -453,44 +470,36 @@
             times_keys(s_s.at[h % 2], q_s, h, kt_all, kt_own)
 
         def prob_grads(h):
-            times_keys(dp_s.at[h % 3], grad_ref, h, vt_all, vt_own)
-
-        def softmax(h):
+            times_keys(dp_s.at[h % 2], grad_ref, h, vt_all, vt_own)
+
+        def strips(h):
             for r in range(0, PAIR * BLK, STRIP):
                 at = slice(r, r + STRIP)
                 s = s_s[h % 2, at, :]
                 s = jnp.concatenate([s[:, :seen], s[:, seen:] + bias_s[at, :]], 1) * (scale * LOG2E)
                 w = jnp.exp2(s - jnp.max(s, axis=1, keepdims=True))
                 probs = w * (1.0 / jnp.sum(w, axis=1, keepdims=True))
-                e_s[h % 2, at, :] = probs
+                probs_low = probs.astype(jnp.bfloat16)
                 first = h * PAIR * BLK + r
-                p_s[first : first + STRIP, :] = probs.astype(jnp.bfloat16)
-
-        def attend_head(h):
+                p_s[first : first + STRIP, :] = probs_low
+                dp = dp_s[h % 2, at, :]
+                dot = jnp.sum(probs_low.astype(jnp.float32) * dp, axis=1, keepdims=True)
+                ds_s[h % 2, at, :] = (probs * ((dp - dot) * scale)).astype(jnp.bfloat16)
+
+        def finish_head(h):
             att_s[:, head_cols(h)] = over_keys(p_s, h * PAIR * BLK, v_all, v_own)
-
-        def score_grads(h):
-            for r in range(0, PAIR * BLK, STRIP):
-                at = slice(r, r + STRIP)
-                g = grad_ref[pl.ds(pl.multiple_of(base + r, STRIP), STRIP), head_cols(h)]
-                dot = jnp.sum(
-                    g.astype(jnp.float32) * att_s[at, head_cols(h)].astype(jnp.float32), axis=1, keepdims=True
-                )
-                ds_s[h % 2, at, :] = (e_s[h % 2, at, :] * ((dp_s[h % 3, at, :] - dot) * scale)).astype(jnp.bfloat16)
             dq_s[:, head_cols(h)] = over_keys(ds_s.at[h % 2], 0, k_all, k_own)
 
         scores(0)
         prob_grads(0)
         for h in range(heads + 1):
-            if h < heads:
-                softmax(h)
             if h + 1 < heads:
                 scores(h + 1)
                 prob_grads(h + 1)
+            if h < heads:
+                strips(h)
             if h > 0:
-                score_grads(h - 1)
-            if h < heads:
-                attend_head(h)
+                finish_head(h - 1)
         g_t = jnp.concatenate([grad_t_ref[h * HD : (h + 1) * HD, rows] for h in range(heads)], 1)
         dv_s[...] += dot_nn(g_t, p_s[:, :seen])
         dv_own = []
@@ -525,7 +534,7 @@
     out_ref[...] = jnp.concatenate([sum_s[m] for m in range(sum_s.shape[0])], 1)
 
 
-def first_down_kernel(c0, c1, c2, c3, slab_ref, up_ref, dep_ref, logit_ref, query_ref, value_ref):
+def first_down_kernel(c0, c1, c2, c3, slab_ref, up_ref, logit_ref, query_ref, value_ref):
     cot = (c0[...] + c1[...]) + (c2[...] + c3[...])
     logit_ref[...] = cot[2 * RANK :]
     both = dot_nn(cot[: 2 * RANK].astype(jnp.bfloat16), slab_ref[...])
@@ -558,15 +567,15 @@
     return lax.ppermute(x, axis, [(i, i ^ bit) for i in range(lax.axis_size(axis))])
 
 
-def after(x, dep):
+def after(x, *deps):
     return pl.pallas_call(
-        lambda x_ref, dep_ref, out_ref: None,
+        lambda *refs: None,
         out_shape=jax.ShapeDtypeStruct(x.shape, x.dtype),
-        in_specs=[anywhere(), anywhere()],
+        in_specs=[anywhere()] * (1 + len(deps)),
         out_specs=anywhere(),
         input_output_aliases={0: 0},
         name="in_order",
-    )(x, dep)
+    )(x, *deps)
 
 
 def anywhere():
@@ -624,25 +633,36 @@
     f32 = jnp.float32
     bf16 = jnp.bfloat16
 
-    def memory_scratch(rows):
+    def memory_scratch(count):
         return [
-            pltpu.VMEM((2, rows, width), bf16),
-            pltpu.VMEM((2, width, HD), bf16),
-            pltpu.VMEM((2, width, HD), bf16),
-            pltpu.VMEM((2, RANK, width), bf16),
-            pltpu.SemaphoreType.DMA((8,)),
+            pltpu.VMEM((count, mem_rows, width), bf16),
+            pltpu.VMEM((count, width, HD), bf16),
+            pltpu.VMEM((count, width, HD), bf16),
+            pltpu.VMEM((count, RANK, width), bf16),
+            pltpu.SemaphoreType.DMA((4 * count,)),
         ]
 
-    def project_scratch(rows):
+    def project_scratch(count):
         return [
-            pltpu.VMEM((2, rows, width), bf16),
-            pltpu.VMEM((2, width, query_width), bf16),
-            pltpu.VMEM((2, width, HD), bf16),
-            pltpu.VMEM((2, width, HD), bf16),
-            pltpu.VMEM((2, RANK, width), bf16),
-            pltpu.VMEM((2, RANK, width), bf16),
-            pltpu.SemaphoreType.DMA((2 * (WQ_CUTS + 5),)),
+            pltpu.VMEM((count, tok_rows, width), bf16),
+            pltpu.VMEM((count, width, query_width), bf16),
+            pltpu.VMEM((count, width, HD), bf16),
+            pltpu.VMEM((count, width, HD), bf16),
+            pltpu.VMEM((count, RANK, width), bf16),
+            pltpu.VMEM((count, RANK, width), bf16),
+            pltpu.SemaphoreType.DMA((count * (WQ_CUTS + 5),)),
         ]
+
+    memory_sums = [
+        pltpu.VMEM((mem_rows, 2 * HD), f32),
+        pltpu.VMEM((mem_rows, RANK), f32),
+        pltpu.SemaphoreType.DMA((2,)),
+    ]
+    project_sums = [
+        pltpu.VMEM((tok_rows, query_width), f32),
+        pltpu.VMEM((tok_rows, 2 * HD), f32),
+        pltpu.VMEM((tok_rows, 2 * RANK), f32),
+    ]
 
     place = lax.axis_index("heads").astype(jnp.int32).reshape(1)
     tag_t = tag_weight.T
@@ -656,7 +676,7 @@
         "memory_near_half",
         (shaped(mem_rows, 2 * HD), shaped(mem_rows, RANK), shaped(peers, dtype=jnp.int32)),
         [smem()] * 2 + [anywhere()] * 5,
-        memory_scratch(mem_rows),
+        memory_scratch(2),
         out_specs=(vmem(), vmem(), smem()),
     )(place, retrieval, memory, mem_near, key_weight, value_weight, value_down)
     asked = lax.all_to_all(wanted, "tm", split_axis=0, concat_axis=0, tiled=True)
@@ -672,26 +692,35 @@
             shaped(query_width, tok_rows, dtype=bf16),
         ),
         [smem()] + [anywhere()] * 7 + [vmem()] * 2 + [smem()],
-        project_scratch(tok_rows),
+        project_scratch(2),
     )(place, slab_tokens, tok_near, *weights, tag_t, grad_tags.T, wanted)
-    mem_far = after(mem_far, early[2])
+    mem_far = after(mem_far, early[2], asked)
     mem_cross = swap(mem_far, 1)
+    mem_weights = (key_weight, value_weight, value_down)
+    mem_acc, mem_low = run(
+        memory_middle_kernel,
+        "memory_far_quarter",
+        (shaped(mem_rows, 2 * HD), shaped(mem_rows, RANK)),
+        [smem()] + [anywhere()] * 6,
+        memory_scratch(1) + memory_sums,
+    )(place, mem_far, mem_acc, mem_low, *mem_weights)
     pairs = run(
         lambda *refs: memory_kernel(peers, *refs),
         "memory_pairs",
         shaped(peers, PACK, HD, dtype=bf16),
-        [smem()] * 2 + [anywhere()] * 7 + [vmem()],
-        memory_scratch(mem_rows)
-        + [
-            pltpu.VMEM((mem_rows, 2 * HD), f32),
-            pltpu.VMEM((mem_rows, RANK), f32),
-            pltpu.SemaphoreType.DMA((2,)),
-            pltpu.VMEM((blocks, PACK, HD), bf16),
-        ],
-    )(place, asked, mem_far, mem_cross, mem_acc, mem_low, key_weight, value_weight, value_down, value_up)
+        [smem()] * 2 + [anywhere()] * 6 + [vmem()],
+        memory_scratch(1) + memory_sums + [pltpu.VMEM((blocks, PACK, HD), bf16)],
+    )(place, asked, mem_cross, mem_acc, mem_low, *mem_weights, value_up)
     got = lax.all_to_all(pairs, "tm", split_axis=0, concat_axis=0, tiled=True)
     tok_far = after(tok_far, pairs)
     tok_cross = swap(tok_far, 1)
+    early = run(
+        project_middle_kernel,
+        "project_far_quarter",
+        (shaped(tok_rows, query_width), shaped(tok_rows, 2 * HD), shaped(tok_rows, 2 * RANK)),
+        [smem()] + [anywhere()] * 9,
+        project_scratch(1) + project_sums + [pltpu.SemaphoreType.DMA((3,))],
+    )(place, tok_far, *weights, *early)
 
     seen = peers * BLK
     total = seen + BLK
@@ -699,12 +728,10 @@
         lambda *refs: attention_kernel(peers, heads, *refs),
         "span_attention",
         (shaped(2 * RANK + tags, tok_rows), shaped(RANK, query_width + HD), shaped(peers, RANK, BLK)),
-        [smem()] * 2 + [anywhere()] * 13 + [vmem()] * 3,
-        project_scratch(tok_rows)
+        [smem()] * 2 + [anywhere()] * 12 + [vmem()] * 3,
+        project_scratch(1)
+        + project_sums
         + [
-            pltpu.VMEM((tok_rows, query_width), f32),
-            pltpu.VMEM((tok_rows, 2 * HD), f32),
-            pltpu.VMEM((tok_rows, 2 * RANK), f32),
             pltpu.VMEM((tok_rows, query_width), bf16),
             pltpu.VMEM((tok_rows, HD), bf16),
             pltpu.VMEM((tok_rows, HD), bf16),
@@ -721,7 +748,6 @@
             pltpu.VMEM((PAIR * BLK, BLK), f32),
             pltpu.VMEM((2, PAIR * BLK, total), f32),
             pltpu.VMEM((2, PAIR * BLK, total), f32),
-            pltpu.VMEM((3, PAIR * BLK, total), f32),
             pltpu.VMEM((heads * PAIR * BLK, total), bf16),
             pltpu.VMEM((2, PAIR * BLK, total), bf16),
             pltpu.VMEM((PAIR * BLK, query_width), bf16),
@@ -731,7 +757,7 @@
         ],
         flops=20 * tok_rows * query_width * total,
         moved=4 * tok_rows * query_width,
-    )(place, boundary, tok_far, tok_cross, *weights, *early, got, grad, grad_t, query_up, value_up, tag_t)
+    )(place, boundary, tok_cross, *weights, *early, got, grad, grad_t, query_up, value_up, tag_t)
 
     back = lax.all_to_all(mcot, "tm", split_axis=0, concat_axis=0, tiled=True)
     cots = [cot] + [swap(cot, d) for d in range(1, 4)]
@@ -747,11 +773,11 @@
         first_down_kernel,
         "first_down",
         (shaped(tags, tok_rows), shaped(RANK, width + ups.shape[1]), shaped(RANK, width)),
-        [vmem()] * 6 + [anywhere()],
+        [vmem()] * 6,
         flops=4 * RANK * tok_rows * width,
         moved=2 * tok_rows * width,
         room=8,
-    )(*cots, slab_tokens, ups, own)
+    )(*cots, slab_tokens, ups)
     owns = [own] + [swap(own, d) for d in range(1, 4)]
     value_sum = run(
         second_down_kernel,

time: 128 us -> 120 us (0.938)
  blocking collectives: 12.1 us -> 0 us
  waiting for transfers between devices: 32.4 us -> 21.4 us
  starting transfers between devices: 26.2 us -> 36.5 us
  Pallas kernels: 47.9 us -> 54.2 us
  local copies, waits for them, and re-layouts: 7.32 us -> 5.44 us
    all_to_all x1 -> x0, blocking collectives: 12.1 us -> none  [fast(): lax.all_to_all(wanted, 'tm', split_axis=0, concat_axis=0, tiled=True)]
    all_to_all x1, waiting for transfers between devices: 10.6 us -> 0.39 us  [fast(): got = lax.all_to_all(pairs, 'tm', split_axis=0, concat_axis=0, tiled=True)]
    pallas_call x2 -> x4, Pallas kernels: 0.01 us -> 8.92 us  [the longest x1 5.89 us: fast(): run(project_middle_kernel, 'project_far_quarter', (shaped(tok_rows, query...]
    all_to_all x0 -> x1, starting transfers between devices: none -> 6.58 us  [fast(): lax.all_to_all(wanted, 'tm', split_axis=0, concat_axis=0, tiled=True)]
    unnamed x26 -> x16, local copies, waits for them, and re-layouts: 7.24 us -> 4.12 us
    all_to_all x1, waiting for transfers between devices: 5.04 us -> 2.47 us  [fast(): back = lax.all_to_all(mcot, 'tm', split_axis=0, concat_axis=0, tiled=True)]
    all_to_all x1, starting transfers between devices: 3.62 us -> 5.99 us  [fast(): back = lax.all_to_all(mcot, 'tm', split_axis=0, concat_axis=0, tiled=True)]
    all_to_all x1, starting transfers between devices: 3.73 us -> 6.01 us  [fast(): got = lax.all_to_all(pairs, 'tm', split_axis=0, concat_axis=0, tiled=True)]
  transfers between devices with their start and end apart: 22 -> 23, of which waited for: 9 -> 8; matrix products, arithmetic and copies ran while one was open for 1% -> 2% of each run, Pallas kernels for 15% -> 23%
where the time goes in v2:
time: 120 us; the launch traced here: 119 us
  Pallas kernels  54.2 us (45%)
  starting transfers between devices  36.5 us (30%)
  waiting for transfers between devices  21.4 us (18%)
  local copies, waits for them, and re-layouts  5.44 us (5%)
    pallas_call x1, Pallas kernels, fast(): run(lambda *refs: attention_kernel(peers, heads, *refs), 'span_attention'...  25.9 us
    ppermute x20, waiting for transfers between devices, swap(): lax.ppermute(x, axis, [(i, i ^ bit) for i in range(lax.axis_size(axis))])  18.5 us
    ppermute x20, starting transfers between devices, swap(): lax.ppermute(x, axis, [(i, i ^ bit) for i in range(lax.axis_size(axis))])  17.9 us
    pallas_call x1, Pallas kernels, fast(): run(project_early_kernel, 'project_near_half', (shaped(tok_rows, query_wi...  9.01 us
    all_to_all x1, starting transfers between devices, fast(): lax.all_to_all(wanted, 'tm', split_axis=0, concat_axis=0, tiled=True)  6.58 us
    all_to_all x1, starting transfers between devices, fast(): got = lax.all_to_all(pairs, 'tm', split_axis=0, concat_axis=0, tiled=True)  6.01 us
    all_to_all x1, starting transfers between devices, fast(): back = lax.all_to_all(mcot, 'tm', split_axis=0, concat_axis=0, tiled=True)  5.99 us
    pallas_call x1, Pallas kernels, fast(): run(project_middle_kernel, 'project_far_quarter', (shaped(tok_rows, query...  5.89 us
  transfers between devices with their start and end apart: 23, of which 8 were waited for; matrix products, arithmetic and copies ran while one was open for 2% of the time, Pallas kernels for 23%

profile of v2, /device:TPU:0, one launch (start us, length us, event | category | flops | bytes accessed | tf_op | source)
XLA Modules:
  0.0 119.1 jit_solution(15670606307876638561)
XLA Ops:
  0.6 0.5 collective-permute-start.2
  1.1 0.1 collective-permute-start
  1.2 2.9 %collective-permute-start.3 = (bf16[512,896]{1,0:T(8,128)(2,1)}, bf16[512,896]{1,0:T(8,128)(2,1)S(1)}, u32[]{:S(2)}, u32[]{:S(2)}) collective-permute-start(bf16[512,896]{1,0:T(8,128)(2,1)} %memory_ref.1), channel_id=1, source_target_pairs={{0,2},{1,3},{2,0},{3,1},{4,6},{5,7},{6,4},{7,5},{8,10},{9,11},{10,... | collective-permute-start | bytes 2752520 | tf_op jit(solution)/shard_map/ppermute | solution.py:567
  4.2 0.0 collective-permute-done.2.refs_3_
  4.2 4.3 %memory_near_half.1 = (f32[512,256]{1,0:T(8,128)}, f32[512,16]{1,0:T(8,128)}, s32[8]{0:T(128)}) custom-call(s32[1]{0:T(128)} %bitcast.refs_0_.place_ref, s32[4,8]{1,0:T(4,128)} %refs_1_.5, bf16[512,896]{1,0:T(8,128)(2,1)} %memory_ref.1, bf16[512,896]{1,0:T(8,128)(2,1)} %collective-permute-done.2.refs_3_, bf16[3584,128]{1,0:T(8,128)(2,1)} %refs_4_.7, ...), custom_call_target="tpu_custom_call" | custom-call | tf_op jit(solution)/shard_map/memory_near_half/pallas_call | solution.py:674
  8.5 1.3 %copy.21 = s32[8,1,1]{2,1,0:T(1,128)} copy(s32[8,1,1]{0,2,1:T(1,128)} %bitcast.8) | data formatting | bytes 64 | tf_op jit(solution)/shard_map/all_to_all | solution.py:682
  9.8 6.6 %all-to-all-start = ((s32[8,1,1]{2,1,0:T(1,128)}), s32[8,1,1]{2,1,0:T(1,128)S(1)}, u32[]{:S(2)}, u32[]{:S(2)}) async-start(s32[8,1,1]{2,1,0:T(1,128)} %copy.21), calls=%async_computation | async-start | bytes 8192 | tf_op jit(solution)/shard_map/all_to_all | solution.py:682
  16.4 0.0 collective-permute-done.x1
  16.4 9.0 %project_near_half.1 = (f32[512,896]{1,0:T(8,128)}, f32[512,256]{1,0:T(8,128)}, f32[512,32]{1,0:T(8,128)}, bf16[512,896]{1,0:T(8,128)(2,1)}, bf16[896,512]{1,0:T(8,128)(2,1)}) custom-call(s32[1]{0:T(128)} %bitcast.refs_0_.place_ref, bf16[512,896]{1,0:T(8,128)(2,1)} %slab_ref.1, bf16[512,896]{1,0:T(8,128)(2,1)} %collective-permute-done.x1, ...), custom_call_target="tpu_custom_call" | custom-call | tf_op jit(solution)/shard_map/project_near_half/pallas_call | solution.py:684
  25.4 0.0 all-to-all-done
  25.4 0.8 reduce.refs_2_.refs_1_.refs_0_
  26.1 0.0 collective-permute-done.3.refs_0_
  26.1 0.9 copy-done.6
  27.1 0.0 collective-permute-start.4
  27.1 1.5 %collective-permute-start.1 = (bf16[512,896]{1,0:T(8,128)(2,1)}, bf16[512,896]{1,0:T(8,128)(2,1)S(1)}, u32[]{:S(2)}, u32[]{:S(2)}) collective-permute-start(bf16[512,896]{1,0:T(8,128)(2,1)} %collective-permute-done.x1), channel_id=1, source_target_pairs={{0,2},{1,3},{2,0},{3,1},{4,6},{5,7},{6,4},{7,5},{8,10},{9,11},{10,... | collective-permute-start | bytes 2752520 | tf_op jit(solution)/shard_map/ppermute | solution.py:567
  28.6 3.0 %memory_far_quarter.1 = (f32[512,256]{1,0:T(8,128)}, f32[512,16]{1,0:T(8,128)}) custom-call(s32[1]{0:T(128)} %bitcast.refs_0_.place_ref, bf16[512,896]{1,0:T(8,128)(2,1)} %in_order.2.x2, f32[512,256]{1,0:T(8,128)} %get-tuple-element.30.acc_hbm, f32[512,16]{1,0:T(8,128)} %get-tuple-element.31.low_hbm, bf16[3584,128]{1,0:T(8,128)(2,1)} %refs_4_.7, ...), custom_call_target="tpu_custom_call" | custom-call | tf_op jit(solution)/shard_map/memory_far_quarter/pallas_call | solution.py:700
  31.6 0.0 collective-permute-done.4.refs_2_
  31.7 3.8 %memory_pairs.1.refs_1_ = bf16[8,272,128]{2,1,0:T(8,128)(2,1)} custom-call(s32[1]{0:T(128)} %bitcast.refs_0_.place_ref, s32[8]{0:T(128)} %reduce.refs_2_.refs_1_.refs_0_, bf16[512,896]{1,0:T(8,128)(2,1)} %collective-permute-done.4.refs_2_, f32[512,256]{1,0:T(8,128)} %get-tuple-element.32.refs_3_, f32[512,16]{1,0:T(8,128)} %get-tuple-element.33.refs_4_, ...), custom_call_target="tpu_custom_call" | custom-call | tf_op jit(solution)/shard_map/memory_pairs/pallas_call | solution.py:707
  35.5 6.0 %all-to-all-start.1 = ((bf16[8,272,128]{2,1,0:T(8,128)(2,1)}), bf16[8,272,128]{2,1,0:T(8,128)(2,1)}, u32[]{:S(2)}, u32[]{:S(2)}) async-start(bf16[8,272,128]{2,1,0:T(8,128)(2,1)} %memory_pairs.1.refs_1_), calls=%async_computation.1 | async-start | bytes 1114112 | tf_op jit(solution)/shard_map/all_to_all | solution.py:714
  41.5 8.6 %collective-permute-done.1.refs_0_ = bf16[512,896]{1,0:T(8,128)(2,1)S(1)} collective-permute-done((bf16[512,896]{1,0:T(8,128)(2,1)}, bf16[512,896]{1,0:T(8,128)(2,1)S(1)}, u32[]{:S(2)}, u32[]{:S(2)}) %collective-permute-start.1) | collective-permute-done | bytes 917536 | tf_op jit(solution)/shard_map/ppermute | solution.py:567
  50.1 0.9 copy-done.5
  51.0 0.0 collective-permute-start.5
  51.0 5.9 %project_far_quarter.1 = (f32[512,896]{1,0:T(8,128)}, f32[512,256]{1,0:T(8,128)}, f32[512,32]{1,0:T(8,128)}) custom-call(s32[1]{0:T(128)} %bitcast.refs_0_.place_ref, bf16[512,896]{1,0:T(8,128)(2,1)} %in_order.3.x3, bf16[3584,896]{1,0:T(8,128)(2,1)} %refs_3_.5, bf16[3584,128]{1,0:T(8,128)(2,1)} %refs_4_.7, bf16[3584,128]{1,0:T(8,128)(2,1)} %refs_5_.5, ...), custom_call_target="tpu_custom_call" | custom-call | tf_op jit(solution)/shard_map/project_far_quarter/pallas_call | solution.py:717
  56.9 0.0 collective-permute-done.5.refs_2_
  56.9 0.4 all-to-all-done.1.refs_11_
  57.3 0.5 copy-done.7
  57.8 25.9 %span_attention.1 = (f32[40,512]{1,0:T(8,128)}, f32[16,1024]{1,0:T(8,128)}, f32[8,16,128]{2,1,0:T(8,128)}) custom-call(s32[1]{0:T(128)} %bitcast.refs_0_.place_ref, s32[4]{0:T(128)} %refs_1_.9, bf16[512,896]{1,0:T(8,128)(2,1)} %copy-done.7, bf16[3584,896]{1,0:T(8,128)(2,1)} %refs_3_.5, bf16[3584,128]{1,0:T(8,128)(2,1)} %refs_4_.7, ...), custom_call_target="tpu_custom_call" | custom-call | flops 10569646080 | bytes 1835008 | tf_op jit(solution)/shard_map/span_attention/pallas_call | solution.py:727
  83.7 0.0 copy-start.1
  83.7 1.5 %collective-permute-start.8 = (f32[40,512]{1,0:T(8,128)}, f32[40,512]{1,0:T(8,128)S(1)}, u32[]{:S(2)}, u32[]{:S(2)}) collective-permute-start(f32[40,512]{1,0:T(8,128)} %get-tuple-element.41.c0), channel_id=1, source_target_pairs={{0,3},{1,2},{2,1},{3,0},{4,7},{5,6},{6,5},{7,4},{8,11},{9,10},{10,... | collective-permute-start | bytes 245768 | tf_op jit(solution)/shard_map/ppermute | solution.py:567
  85.3 0.5 collective-permute-start.7
  85.8 0.0 collective-permute-start.6
  85.8 6.0 %all-to-all-start.2 = ((f32[8,16,128]{2,1,0:T(8,128)}), f32[8,16,128]{2,1,0:T(8,128)S(1)}, u32[]{:S(2)}, u32[]{:S(2)}) async-start(f32[8,16,128]{2,1,0:T(8,128)} %get-tuple-element.45), calls=%async_computation.2 | async-start | bytes 131072 | tf_op jit(solution)/shard_map/all_to_all | solution.py:762
  91.8 0.0 collective-permute-done.8.c3
  91.8 0.0 collective-permute-done.7.c2
  91.8 0.0 collective-permute-done.6.c1
  91.9 0.9 copy-done.2
  92.7 0.8 copy-done.3
  93.6 0.8 first_down.1
  94.3 2.0 %collective-permute-start.9 = (f32[16,1920]{1,0:T(8,128)S(1)}, f32[16,1920]{1,0:T(8,128)S(1)}, u32[]{:S(2)}, u32[]{:S(2)}) collective-permute-start(f32[16,1920]{1,0:T(8,128)S(1)} %get-tuple-element.44), channel_id=1, source_target_pairs={{0,4},{4,0},{8,12},{12,8},{16,20},{20,16},{24,28},{28,24},{1,5},{5... | collective-permute-start | bytes 368648 | tf_op jit(solution)/shard_map/ppermute | solution.py:567
  96.4 2.5 %all-to-all-done.2.refs_1_ = f32[8,16,128]{2,1,0:T(8,128)S(1)} async-done(((f32[8,16,128]{2,1,0:T(8,128)}), f32[8,16,128]{2,1,0:T(8,128)S(1)}, u32[]{:S(2)}, u32[]{:S(2)}) %all-to-all-start.2) | async-done | bytes 65568 | tf_op jit(solution)/shard_map/all_to_all | solution.py:762
  98.8 0.6 owned_cotangent.1.c0
  99.4 0.1 collective-permute-start.15
  99.5 1.5 %collective-permute-start.14 = (f32[16,512]{1,0:T(8,128)S(1)}, f32[16,512]{1,0:T(8,128)S(1)}, u32[]{:S(2)}, u32[]{:S(2)}) collective-permute-start(f32[16,512]{1,0:T(8,128)S(1)} %owned_cotangent.1.c0), channel_id=1, source_target_pairs={{0,2},{1,3},{2,0},{3,1},{4,6},{5,7},{6,4},{7,5},{8,10},{9,11},{10,... | collective-permute-start | bytes 98312 | tf_op jit(solution)/shard_map/ppermute | solution.py:567
  101.0 0.3 collective-permute-start.13
  101.3 1.8 %collective-permute-done.15.c3 = f32[16,512]{1,0:T(8,128)S(1)} collective-permute-done((f32[16,512]{1,0:T(8,128)S(1)}, f32[16,512]{1,0:T(8,128)S(1)}, u32[]{:S(2)}, u32[]{:S(2)}) %collective-permute-start.15) | collective-permute-done | bytes 32800 | tf_op jit(solution)/shard_map/ppermute | solution.py:567
  103.1 0.4 collective-permute-done.14.c2
  103.5 0.0 collective-permute-done.13.c1
  103.5 0.2 second_down.1
  103.8 0.5 collective-permute-start.16
  104.3 0.0 collective-permute-done.9
  104.3 1.8 %collective-permute-start.12 = (bf16[16,1920]{1,0:T(8,128)(2,1)S(1)}, bf16[16,1920]{1,0:T(8,128)(2,1)S(1)}, u32[]{:S(2)}, u32[]{:S(2)}) collective-permute-start(bf16[16,1920]{1,0:T(8,128)(2,1)S(1)} %add_convert_fusion.refs_0_), channel_id=1, source_target_pairs={{0,24},{4,28},{8,16},{12,20},{16,8},{20,12},{24,0},{28,4},{1,25},{... | collective-permute-start | bytes 184328 | tf_op jit(solution)/shard_map/ppermute | solution.py:567
  106.1 0.4 collective-permute-start.11
  106.5 2.3 %collective-permute-start.10 = (bf16[16,1920]{1,0:T(8,128)(2,1)S(1)}, bf16[16,1920]{1,0:T(8,128)(2,1)S(1)}, u32[]{:S(2)}, u32[]{:S(2)}) collective-permute-start(bf16[16,1920]{1,0:T(8,128)(2,1)S(1)} %add_convert_fusion.refs_0_), channel_id=1, source_target_pairs={{0,8},{4,12},{8,0},{12,4},{16,24},{20,28},{24,16},{28,20},{1,9},{5... | collective-permute-start | bytes 184328 | tf_op jit(solution)/shard_map/ppermute | solution.py:567
  108.7 0.0 collective-permute-done.16
  108.8 1.8 %collective-permute-start.19 = (bf16[16,896]{1,0:T(8,128)(2,1)S(1)}, bf16[16,896]{1,0:T(8,128)(2,1)S(1)}, u32[]{:S(2)}, u32[]{:S(2)}) collective-permute-start(bf16[16,896]{1,0:T(8,128)(2,1)S(1)} %add_convert_fusion.1.refs_4_), channel_id=1, source_target_pairs={{0,24},{4,28},{8,16},{12,20},{16,8},{20,12},{24,0},{28,4},{1,25},{... | collective-permute-start | bytes 86024 | tf_op jit(solution)/shard_map/ppermute | solution.py:567
  110.6 0.0 collective-permute-start.18
  110.6 3.9 %collective-permute-done.19.refs_7_ = bf16[16,896]{1,0:T(8,128)(2,1)S(1)} collective-permute-done((bf16[16,896]{1,0:T(8,128)(2,1)S(1)}, bf16[16,896]{1,0:T(8,128)(2,1)S(1)}, u32[]{:S(2)}, u32[]{:S(2)}) %collective-permute-start.19) | collective-permute-done | bytes 28704 | tf_op jit(solution)/shard_map/ppermute | solution.py:567
  114.5 0.1 collective-permute-start.17
  114.6 0.8 collective-permute-done.18.refs_6_
  115.3 3.0 %collective-permute-done.17.refs_5_ = bf16[16,896]{1,0:T(8,128)(2,1)S(1)} collective-permute-done((bf16[16,896]{1,0:T(8,128)(2,1)S(1)}, bf16[16,896]{1,0:T(8,128)(2,1)S(1)}, u32[]{:S(2)}, u32[]{:S(2)}) %collective-permute-start.17) | collective-permute-done | bytes 28704 | tf_op jit(solution)/shard_map/ppermute | solution.py:567
  118.4 0.0 collective-permute-done.12.refs_3_
  118.4 0.0 collective-permute-done.11.refs_2_
  118.4 0.0 collective-permute-done.10.refs_1_
  118.4 0.7 finish_outputs.1
  (14 shorter events, 0.0 us)
Async XLA Ops:
  0.6 3.5 %collective-permute-start.2 = (bf16[512,896]{1,0:T(8,128)(2,1)}, bf16[512,896]{1,0:T(8,128)(2,1)}, u32[]{:S(2)}, u32[]{:S(2)}) collective-permute-start(bf16[512,896]{1,0:T(8,128)(2,1)} %memory_ref.1), channel_id=1, source_target_pairs={{0,1},{1,0},{2,3},{3,2},{4,5},{5,4},{6,7},{7,6},{8,9},{9,8},{10,11... | collective-permute-start | bytes 2752520 | tf_op jit(solution)/shard_map/ppermute | solution.py:567
  1.1 15.2 %collective-permute-start = (bf16[512,896]{1,0:T(8,128)(2,1)}, bf16[512,896]{1,0:T(8,128)(2,1)}, u32[]{:S(2)}, u32[]{:S(2)}) collective-permute-start(bf16[512,896]{1,0:T(8,128)(2,1)} %slab_ref.1), channel_id=1, source_target_pairs={{0,1},{1,0},{2,3},{3,2},{4,5},{5,4},{6,7},{7,6},{8,9},{9,8},{10,11... | collective-permute-start | bytes 2752520 | tf_op jit(solution)/shard_map/ppermute | solution.py:567
  1.2 24.9 %collective-permute-start.3 = (bf16[512,896]{1,0:T(8,128)(2,1)}, bf16[512,896]{1,0:T(8,128)(2,1)S(1)}, u32[]{:S(2)}, u32[]{:S(2)}) collective-permute-start(bf16[512,896]{1,0:T(8,128)(2,1)} %memory_ref.1), channel_id=1, source_target_pairs={{0,2},{1,3},{2,0},{3,1},{4,6},{5,7},{6,4},{7,5},{8,10},{9,11},{10,... | collective-permute-start | bytes 2752520 | tf_op jit(solution)/shard_map/ppermute | solution.py:567
  9.8 15.6 %all-to-all-start = ((s32[8,1,1]{2,1,0:T(1,128)}), s32[8,1,1]{2,1,0:T(1,128)S(1)}, u32[]{:S(2)}, u32[]{:S(2)}) async-start(s32[8,1,1]{2,1,0:T(1,128)} %copy.21), calls=%async_computation | async-start | bytes 8192 | tf_op jit(solution)/shard_map/all_to_all | solution.py:682
  26.1 0.9 copy-start.6
  27.1 4.6 %collective-permute-start.4 = (bf16[512,896]{1,0:T(8,128)(2,1)}, bf16[512,896]{1,0:T(8,128)(2,1)}, u32[]{:S(2)}, u32[]{:S(2)}) collective-permute-start(bf16[512,896]{1,0:T(8,128)(2,1)} %in_order.2.x2), channel_id=1, source_target_pairs={{0,1},{1,0},{2,3},{3,2},{4,5},{5,4},{6,7},{7,6},{8,9},{9,8},{10,11... | collective-permute-start | bytes 2752520 | tf_op jit(solution)/shard_map/ppermute | solution.py:567
  27.1 23.0 %collective-permute-start.1 = (bf16[512,896]{1,0:T(8,128)(2,1)}, bf16[512,896]{1,0:T(8,128)(2,1)S(1)}, u32[]{:S(2)}, u32[]{:S(2)}) collective-permute-start(bf16[512,896]{1,0:T(8,128)(2,1)} %collective-permute-done.x1), channel_id=1, source_target_pairs={{0,2},{1,3},{2,0},{3,1},{4,6},{5,7},{6,4},{7,5},{8,10},{9,11},{10,... | collective-permute-start | bytes 2752520 | tf_op jit(solution)/shard_map/ppermute | solution.py:567
  35.5 21.8 %all-to-all-start.1 = ((bf16[8,272,128]{2,1,0:T(8,128)(2,1)}), bf16[8,272,128]{2,1,0:T(8,128)(2,1)}, u32[]{:S(2)}, u32[]{:S(2)}) async-start(bf16[8,272,128]{2,1,0:T(8,128)(2,1)} %memory_pairs.1.refs_1_), calls=%async_computation.1 | async-start | bytes 1114112 | tf_op jit(solution)/shard_map/all_to_all | solution.py:714
  50.1 0.9 copy-start.5
  51.0 5.9 %collective-permute-start.5 = (bf16[512,896]{1,0:T(8,128)(2,1)}, bf16[512,896]{1,0:T(8,128)(2,1)S(1)}, u32[]{:S(2)}, u32[]{:S(2)}) collective-permute-start(bf16[512,896]{1,0:T(8,128)(2,1)} %in_order.3.x3), channel_id=1, source_target_pairs={{0,1},{1,0},{2,3},{3,2},{4,5},{5,4},{6,7},{7,6},{8,9},{9,8},{10,11... | collective-permute-start | bytes 2752520 | tf_op jit(solution)/shard_map/ppermute | solution.py:567
  56.9 0.9 copy-start.7
  57.8 34.0 %copy-start = (bf16[512,896]{1,0:T(8,128)(2,1)S(1)}, bf16[512,896]{1,0:T(8,128)(2,1)}, u32[]{:S(2)}) copy-start(bf16[512,896]{1,0:T(8,128)(2,1)} %slab_ref.1) | copy-start | bytes 2752516
  57.8 41.0 %copy-start.4 = (s32[8]{0:T(128)S(1)}, s32[8]{0:T(128)}, u32[]{:S(2)}) copy-start(s32[8]{0:T(128)} %reduce.refs_2_.refs_1_.refs_0_) | copy-start | bytes 100
  83.7 19.8 %copy-start.1 = (bf16[512,896]{1,0:T(8,128)(2,1)S(1)}, bf16[512,896]{1,0:T(8,128)(2,1)}, u32[]{:S(2)}) copy-start(bf16[512,896]{1,0:T(8,128)(2,1)} %memory_ref.1) | copy-start | bytes 2752516
  83.7 8.1 %collective-permute-start.8 = (f32[40,512]{1,0:T(8,128)}, f32[40,512]{1,0:T(8,128)S(1)}, u32[]{:S(2)}, u32[]{:S(2)}) collective-permute-start(f32[40,512]{1,0:T(8,128)} %get-tuple-element.41.c0), channel_id=1, source_target_pairs={{0,3},{1,2},{2,1},{3,0},{4,7},{5,6},{6,5},{7,4},{8,11},{9,10},{10,... | collective-permute-start | bytes 245768 | tf_op jit(solution)/shard_map/ppermute | solution.py:567
  85.3 6.5 %collective-permute-start.7 = (f32[40,512]{1,0:T(8,128)}, f32[40,512]{1,0:T(8,128)S(1)}, u32[]{:S(2)}, u32[]{:S(2)}) collective-permute-start(f32[40,512]{1,0:T(8,128)} %get-tuple-element.41.c0), channel_id=1, source_target_pairs={{0,2},{1,3},{2,0},{3,1},{4,6},{5,7},{6,4},{7,5},{8,10},{9,11},{10,... | collective-permute-start | bytes 245768 | tf_op jit(solution)/shard_map/ppermute | solution.py:567
  85.8 6.0 %collective-permute-start.6 = (f32[40,512]{1,0:T(8,128)}, f32[40,512]{1,0:T(8,128)S(1)}, u32[]{:S(2)}, u32[]{:S(2)}) collective-permute-start(f32[40,512]{1,0:T(8,128)} %get-tuple-element.41.c0), channel_id=1, source_target_pairs={{0,1},{1,0},{2,3},{3,2},{4,5},{5,4},{6,7},{7,6},{8,9},{9,8},{10,11... | collective-permute-start | bytes 245768 | tf_op jit(solution)/shard_map/ppermute | solution.py:567
  85.8 13.0 %all-to-all-start.2 = ((f32[8,16,128]{2,1,0:T(8,128)}), f32[8,16,128]{2,1,0:T(8,128)S(1)}, u32[]{:S(2)}, u32[]{:S(2)}) async-start(f32[8,16,128]{2,1,0:T(8,128)} %get-tuple-element.45), calls=%async_computation.2 | async-start | bytes 131072 | tf_op jit(solution)/shard_map/all_to_all | solution.py:762
  91.9 0.9 copy-start.2
  92.7 0.8 copy-start.3
  94.3 9.9 %collective-permute-start.9 = (f32[16,1920]{1,0:T(8,128)S(1)}, f32[16,1920]{1,0:T(8,128)S(1)}, u32[]{:S(2)}, u32[]{:S(2)}) collective-permute-start(f32[16,1920]{1,0:T(8,128)S(1)} %get-tuple-element.44), channel_id=1, source_target_pairs={{0,4},{4,0},{8,12},{12,8},{16,20},{20,16},{24,28},{28,24},{1,5},{5... | collective-permute-start | bytes 368648 | tf_op jit(solution)/shard_map/ppermute | solution.py:567
  99.4 3.7 %collective-permute-start.15 = (f32[16,512]{1,0:T(8,128)S(1)}, f32[16,512]{1,0:T(8,128)S(1)}, u32[]{:S(2)}, u32[]{:S(2)}) collective-permute-start(f32[16,512]{1,0:T(8,128)S(1)} %owned_cotangent.1.c0), channel_id=1, source_target_pairs={{0,3},{1,2},{2,1},{3,0},{4,7},{5,6},{6,5},{7,4},{8,11},{9,10},{10,... | collective-permute-start | bytes 98312 | tf_op jit(solution)/shard_map/ppermute | solution.py:567
  99.5 4.0 %collective-permute-start.14 = (f32[16,512]{1,0:T(8,128)S(1)}, f32[16,512]{1,0:T(8,128)S(1)}, u32[]{:S(2)}, u32[]{:S(2)}) collective-permute-start(f32[16,512]{1,0:T(8,128)S(1)} %owned_cotangent.1.c0), channel_id=1, source_target_pairs={{0,2},{1,3},{2,0},{3,1},{4,6},{5,7},{6,4},{7,5},{8,10},{9,11},{10,... | collective-permute-start | bytes 98312 | tf_op jit(solution)/shard_map/ppermute | solution.py:567
  101.0 2.5 %collective-permute-start.13 = (f32[16,512]{1,0:T(8,128)S(1)}, f32[16,512]{1,0:T(8,128)S(1)}, u32[]{:S(2)}, u32[]{:S(2)}) collective-permute-start(f32[16,512]{1,0:T(8,128)S(1)} %owned_cotangent.1.c0), channel_id=1, source_target_pairs={{0,1},{1,0},{2,3},{3,2},{4,5},{5,4},{6,7},{7,6},{8,9},{9,8},{10,11... | collective-permute-start | bytes 98312 | tf_op jit(solution)/shard_map/ppermute | solution.py:567
  103.8 5.0 %collective-permute-start.16 = (f32[16,896]{1,0:T(8,128)S(1)}, f32[16,896]{1,0:T(8,128)S(1)}, u32[]{:S(2)}, u32[]{:S(2)}) collective-permute-start(f32[16,896]{1,0:T(8,128)S(1)} %second_down.1), channel_id=1, source_target_pairs={{0,4},{4,0},{8,12},{12,8},{16,20},{20,16},{24,28},{28,24},{1,5},{5... | collective-permute-start | bytes 172040 | tf_op jit(solution)/shard_map/ppermute | solution.py:567
  104.3 14.1 %collective-permute-start.12 = (bf16[16,1920]{1,0:T(8,128)(2,1)S(1)}, bf16[16,1920]{1,0:T(8,128)(2,1)S(1)}, u32[]{:S(2)}, u32[]{:S(2)}) collective-permute-start(bf16[16,1920]{1,0:T(8,128)(2,1)S(1)} %add_convert_fusion.refs_0_), channel_id=1, source_target_pairs={{0,24},{4,28},{8,16},{12,20},{16,8},{20,12},{24,0},{28,4},{1,25},{... | collective-permute-start | bytes 184328 | tf_op jit(solution)/shard_map/ppermute | solution.py:567
  106.1 12.3 %collective-permute-start.11 = (bf16[16,1920]{1,0:T(8,128)(2,1)S(1)}, bf16[16,1920]{1,0:T(8,128)(2,1)S(1)}, u32[]{:S(2)}, u32[]{:S(2)}) collective-permute-start(bf16[16,1920]{1,0:T(8,128)(2,1)S(1)} %add_convert_fusion.refs_0_), channel_id=1, source_target_pairs={{0,16},{4,20},{8,24},{12,28},{16,0},{20,4},{24,8},{28,12},{1,17},{... | collective-permute-start | bytes 184328 | tf_op jit(solution)/shard_map/ppermute | solution.py:567
  106.5 11.9 %collective-permute-start.10 = (bf16[16,1920]{1,0:T(8,128)(2,1)S(1)}, bf16[16,1920]{1,0:T(8,128)(2,1)S(1)}, u32[]{:S(2)}, u32[]{:S(2)}) collective-permute-start(bf16[16,1920]{1,0:T(8,128)(2,1)S(1)} %add_convert_fusion.refs_0_), channel_id=1, source_target_pairs={{0,8},{4,12},{8,0},{12,4},{16,24},{20,28},{24,16},{28,20},{1,9},{5... | collective-permute-start | bytes 184328 | tf_op jit(solution)/shard_map/ppermute | solution.py:567
  108.8 5.7 %collective-permute-start.19 = (bf16[16,896]{1,0:T(8,128)(2,1)S(1)}, bf16[16,896]{1,0:T(8,128)(2,1)S(1)}, u32[]{:S(2)}, u32[]{:S(2)}) collective-permute-start(bf16[16,896]{1,0:T(8,128)(2,1)S(1)} %add_convert_fusion.1.refs_4_), channel_id=1, source_target_pairs={{0,24},{4,28},{8,16},{12,20},{16,8},{20,12},{24,0},{28,4},{1,25},{... | collective-permute-start | bytes 86024 | tf_op jit(solution)/shard_map/ppermute | solution.py:567
  110.6 4.8 %collective-permute-start.18 = (bf16[16,896]{1,0:T(8,128)(2,1)S(1)}, bf16[16,896]{1,0:T(8,128)(2,1)S(1)}, u32[]{:S(2)}, u32[]{:S(2)}) collective-permute-start(bf16[16,896]{1,0:T(8,128)(2,1)S(1)} %add_convert_fusion.1.refs_4_), channel_id=1, source_target_pairs={{0,16},{4,20},{8,24},{12,28},{16,0},{20,4},{24,8},{28,12},{1,17},{... | collective-permute-start | bytes 86024 | tf_op jit(solution)/shard_map/ppermute | solution.py:567
  114.5 3.9 %collective-permute-start.17 = (bf16[16,896]{1,0:T(8,128)(2,1)S(1)}, bf16[16,896]{1,0:T(8,128)(2,1)S(1)}, u32[]{:S(2)}, u32[]{:S(2)}) collective-permute-start(bf16[16,896]{1,0:T(8,128)(2,1)S(1)} %add_convert_fusion.1.refs_4_), channel_id=1, source_target_pairs={{0,8},{4,12},{8,0},{12,4},{16,24},{20,28},{24,16},{28,20},{1,9},{5... | collective-permute-start | bytes 86024 | tf_op jit(solution)/shard_map/ppermute | solution.py:567

commit v3 on v2

--- a/solution.py
+++ b/solution.py
@@ -230,6 +230,7 @@
 STRIP = 16
 PAIR = 2
 MIB = 1024 * 1024
+FLAG = jax.ShapeDtypeStruct((1,), jnp.int32)
 ROOM = 63
 
 
@@ -250,6 +251,11 @@
     for copy in copies:
         copy.start()
     return copies
+
+
+def in_parts(src, dst, parts=4):
+    step = dst.shape[0] // parts
+    return [(src.at[pl.ds(n * step, step), :], dst.at[pl.ds(n * step, step), :]) for n in range(parts)]
 
 
 def wait_all(copies):
@@ -263,13 +269,12 @@
     groups = []
     for n, j in enumerate(js):
         here = piece_rows(place_ref, j, width)
-        pairs = [
-            (xs[n], x_s.at[n]),
+        pairs = in_parts(xs[n], x_s.at[n]) + [
             (hbm[0].at[here, :], wk_s.at[n]),
             (hbm[1].at[here, :], wv_s.at[n]),
             (hbm[2].at[:, here], down_s.at[n]),
         ]
-        groups.append(start_copies(pairs, sems, 4 * n))
+        groups.append(start_copies(pairs, sems, 7 * n))
     return groups
 
 
@@ -309,8 +314,9 @@
 
 
 def memory_kernel(peers, place_ref, asked_ref, x3, acc_hbm, low_hbm, *refs):
-    hbm, up_ref, out_ref = refs[:3], refs[3], refs[4]
-    scratch, sems, acc_s, low_s, acc_sems, pair_ref = refs[5:9], refs[9], refs[10], refs[11], refs[12], refs[13]
+    hbm, up_ref, out_ref, flag_ref = refs[:3], refs[3], refs[4], refs[5]
+    scratch, sems, acc_s, low_s, acc_sems, pair_ref = refs[6:10], refs[10], refs[11], refs[12], refs[13], refs[14]
+    flag_ref[0] = 0
     groups = memory_pieces(place_ref, (3,), (x3,), hbm, scratch, sems)
     sums = start_copies([(acc_hbm, acc_s), (low_hbm, low_s)], acc_sems)
     wait_all(groups[0])
@@ -342,7 +348,7 @@
     for n, j in enumerate(js):
         here = piece_rows(place_ref, j, width)
         start = lax.bitwise_xor(place_ref[0], j) * width
-        pairs = [(xs[n], x_s.at[n])]
+        pairs = in_parts(xs[n], x_s.at[n])
         for m in range(WQ_CUTS):
             rows = pl.ds(pl.multiple_of(start + m * part, part), part)
             pairs.append((wq_hbm.at[rows, :], wq_s.at[n, pl.ds(m * part, part), :]))
@@ -367,9 +373,20 @@
 
 
 def project_early_kernel(place_ref, x0, x1, *refs):
-    hbm, (tag_ref, tags_t_ref), outs, (grad_ref, grad_t_ref) = refs[:5], refs[5:7], refs[8:11], refs[11:13]
-    scratch, sems = refs[13:19], refs[19]
+    hbm, outs, flag_ref, scratch, sems = refs[:5], refs[6:9], refs[9], refs[10:16], refs[16]
+    flag_ref[0] = 0
     groups = project_pieces(place_ref, (0, 1), (x0, x1), hbm, scratch, sems)
+    for n in range(2):
+        wait_all(groups[n])
+        for ref, term in zip(outs, project_terms(n, scratch)):
+            if n == 0:
+                ref[...] = term
+            else:
+                ref[...] += term
+
+
+def grad_kernel(tag_ref, tags_t_ref, dep_ref, grad_ref, grad_t_ref, flag_ref):
+    flag_ref[0] = 0
     first = (((0,), (0,)), ((), ()))
     tag = tag_ref[...].astype(jnp.float32)
     tags_t = tags_t_ref[...]
@@ -380,20 +397,13 @@
     grad_t_ref[...] = lax.dot_general(
         tag, tags_t, first, precision=HIGHEST, preferred_element_type=f32
     ).astype(jnp.bfloat16)
-    for n in range(2):
-        wait_all(groups[n])
-        for ref, term in zip(outs, project_terms(n, scratch)):
-            if n == 0:
-                ref[...] = term
-            else:
-                ref[...] += term
 
 
 def project_middle_kernel(place_ref, x3, *refs):
     hbm, early, outs, scratch, sems = refs[:5], refs[5:8], refs[8:11], refs[11:17], refs[17]
     sum_refs, sum_sems = refs[18:21], refs[21]
     groups = project_pieces(place_ref, (3,), (x3,), hbm, scratch, sems)
-    loads = start_copies(list(zip(early, sum_refs)), sum_sems)
+    loads = start_copies(in_parts(early[0], sum_refs[0]) + list(zip(early[1:], sum_refs[1:])), sum_sems)
     wait_all(groups[0])
     terms = project_terms(0, scratch)
     wait_all(loads)
@@ -401,31 +411,31 @@
         out[...] = ref[...] + term
 
 
-def attention_kernel(peers, heads, place_ref, bound_ref, x2, *refs):
+def attention_kernel(peers, heads, place_ref, me_ref, bound_ref, x2, *refs):
     hbm, early, got, grad_hbm, grad_t_hbm = refs[:5], refs[5:8], refs[8], refs[9], refs[10]
-    qup_ref, vup_ref, tag_ref, cot_ref, up_ref, mcot_ref = refs[11:17]
-    scratch, sems, sum_refs = refs[17:23], refs[23], refs[24:27]
+    qup_ref, vup_ref, tag_ref, cot_ref, up_ref, same_ref, other_ref = refs[11:18]
+    scratch, sems, sum_refs = refs[18:24], refs[24], refs[25:28]
     (q_s, k_own, v_own, low_s, low_m_s, grad_ref, grad_t_ref, k_all, v_all, kt_all, vt_all, kt_own, vt_own, bias_s, s_s, dp_s,
-     p_s, ds_s, att_s, dq_s, dv_s, more_sems) = refs[27:]
+     p_s, ds_s, att_s, dq_s, dv_s, mcot_s, more_sems) = refs[28:]
     seen = peers * BLK
     groups = project_pieces(place_ref, (2,), (x2,), hbm, scratch, sems)
-    pairs = list(zip(early, sum_refs))
+    pairs = in_parts(early[0], sum_refs[0]) + list(zip(early[1:], sum_refs[1:]))
     for b in range(peers):
         at = slice(b * BLK, (b + 1) * BLK)
         pairs.append((got.at[b, pl.ds(0, BLK), :], k_all.at[at, :]))
         pairs.append((got.at[b, pl.ds(BLK, BLK), :], v_all.at[at, :]))
         pairs.append((got.at[b, pl.ds(2 * BLK, RANK), :], low_m_s.at[b]))
-    pairs += [(grad_hbm, grad_ref), (grad_t_hbm, grad_t_ref)]
+    pairs += in_parts(grad_hbm, grad_ref) + in_parts(grad_t_hbm, grad_t_ref)
     copies = start_copies(pairs, more_sems)
     wait_all(groups[0])
-    wait_all(copies[:3])
+    wait_all(copies[:6])
     q_acc, kv_acc, low_acc = [ref[...] + term for ref, term in zip(sum_refs, project_terms(0, scratch))]
     low = low_acc.astype(jnp.bfloat16)
     q_s[...] = (q_acc + dot_nn(low[:, :RANK], qup_ref[...])).astype(jnp.bfloat16)
     k_own[...] = kv_acc[:, :HD].astype(jnp.bfloat16)
     v_own[...] = (kv_acc[:, HD:] + dot_nn(low[:, RANK:], vup_ref[...])).astype(jnp.bfloat16)
     low_s[...] = jnp.transpose(low_acc).astype(jnp.bfloat16)
-    wait_all(copies[3:])
+    wait_all(copies[6:])
     for b in range(peers):
         at = slice(b * BLK, (b + 1) * BLK)
         kt_all[:, at] = jnp.transpose(k_all[at, :])
@@ -523,19 +533,28 @@
     low_m = jnp.concatenate([low_m_s[b] for b in range(peers)], 1).astype(jnp.float32)
     up_ref[:, query_width:] += dot_nt(low_m, dv, HIGHEST)
     for b in range(peers):
-        mcot_ref[b] = mcot[:, b * BLK : (b + 1) * BLK]
-
-
-def own_kernel(peers, asked_ref, back_ref, out_ref, sum_s):
+        mcot_s[b] = mcot[:, b * BLK : (b + 1) * BLK]
+    for n in range(peers // 2):
+        same_ref[n] = mcot_s[lax.bitwise_xor(me_ref[0], 2 * n)]
+        other_ref[n] = mcot_s[lax.bitwise_xor(me_ref[0], 2 * n + 1)]
+
+
+def mix_kernel(same_ref, other_ref, *outs):
+    for n, out in enumerate(outs):
+        out[0] = same_ref[n]
+        out[1] = other_ref[n]
+
+
+def first_down_kernel(steps, me_ref, asked_ref, *refs):
+    pieces, cots, slab_ref, up_ref = refs[:steps], refs[steps : steps + 4], refs[steps + 4], refs[steps + 5]
+    logit_ref, query_ref, value_ref, own_ref, sum_s = refs[steps + 6 :]
     sum_s[...] = jnp.zeros_like(sum_s)
-    for r in range(peers):
-        block = asked_ref[r]
-        sum_s[block] = sum_s[block] + back_ref[r]
-    out_ref[...] = jnp.concatenate([sum_s[m] for m in range(sum_s.shape[0])], 1)
-
-
-def first_down_kernel(c0, c1, c2, c3, slab_ref, up_ref, logit_ref, query_ref, value_ref):
-    cot = (c0[...] + c1[...]) + (c2[...] + c3[...])
+    for n, piece in enumerate(pieces):
+        for side in range(2):
+            block = asked_ref[lax.bitwise_xor(me_ref[0], 2 * n + side)]
+            sum_s[block] = sum_s[block] + piece[side]
+    own_ref[...] = jnp.concatenate([sum_s[m] for m in range(sum_s.shape[0])], 1)
+    cot = (cots[0][...] + cots[1][...]) + (cots[2][...] + cots[3][...])
     logit_ref[...] = cot[2 * RANK :]
     both = dot_nn(cot[: 2 * RANK].astype(jnp.bfloat16), slab_ref[...])
     width = both.shape[1]
@@ -567,15 +586,15 @@
     return lax.ppermute(x, axis, [(i, i ^ bit) for i in range(lax.axis_size(axis))])
 
 
-def after(x, *deps):
+def after(x, *flags):
     return pl.pallas_call(
         lambda *refs: None,
         out_shape=jax.ShapeDtypeStruct(x.shape, x.dtype),
-        in_specs=[anywhere()] * (1 + len(deps)),
+        in_specs=[anywhere()] + [smem()] * len(flags),
         out_specs=anywhere(),
         input_output_aliases={0: 0},
         name="in_order",
-    )(x, *deps)
+    )(x, *flags)
 
 
 def anywhere():
@@ -639,7 +658,7 @@
             pltpu.VMEM((count, width, HD), bf16),
             pltpu.VMEM((count, width, HD), bf16),
             pltpu.VMEM((count, RANK, width), bf16),
-            pltpu.SemaphoreType.DMA((4 * count,)),
+            pltpu.SemaphoreType.DMA((7 * count,)),
         ]
 
     def project_scratch(count):
@@ -650,7 +669,7 @@
             pltpu.VMEM((count, width, HD), bf16),
             pltpu.VMEM((count, RANK, width), bf16),
             pltpu.VMEM((count, RANK, width), bf16),
-            pltpu.SemaphoreType.DMA((count * (WQ_CUTS + 5),)),
+            pltpu.SemaphoreType.DMA((count * (WQ_CUTS + 8),)),
         ]
 
     memory_sums = [
@@ -665,6 +684,7 @@
     ]
 
     place = lax.axis_index("heads").astype(jnp.int32).reshape(1)
+    me = lax.axis_index("tm").astype(jnp.int32).reshape(1)
     tag_t = tag_weight.T
     tags = tag_t.shape[0]
     mem_far = swap(memory, 2)
@@ -681,20 +701,15 @@
     )(place, retrieval, memory, mem_near, key_weight, value_weight, value_down)
     asked = lax.all_to_all(wanted, "tm", split_axis=0, concat_axis=0, tiled=True)
     weights = (query_weight, key_weight, value_weight, query_down, value_down)
-    *early, grad, grad_t = run(
+    *early, near_flag = run(
         project_early_kernel,
         "project_near_half",
-        (
-            shaped(tok_rows, query_width),
-            shaped(tok_rows, 2 * HD),
-            shaped(tok_rows, 2 * RANK),
-            shaped(tok_rows, query_width, dtype=bf16),
-            shaped(query_width, tok_rows, dtype=bf16),
-        ),
-        [smem()] + [anywhere()] * 7 + [vmem()] * 2 + [smem()],
+        (shaped(tok_rows, query_width), shaped(tok_rows, 2 * HD), shaped(tok_rows, 2 * RANK), FLAG),
+        [smem()] + [anywhere()] * 7 + [smem()],
         project_scratch(2),
-    )(place, slab_tokens, tok_near, *weights, tag_t, grad_tags.T, wanted)
-    mem_far = after(mem_far, early[2], asked)
+        out_specs=(vmem(), vmem(), vmem(), smem()),
+    )(place, slab_tokens, tok_near, *weights, wanted)
+    mem_far = after(mem_far, near_flag, asked)
     mem_cross = swap(mem_far, 1)
     mem_weights = (key_weight, value_weight, value_down)
     mem_acc, mem_low = run(
@@ -704,31 +719,40 @@
         [smem()] + [anywhere()] * 6,
         memory_scratch(1) + memory_sums,
     )(place, mem_far, mem_acc, mem_low, *mem_weights)
-    pairs = run(
+    pairs, pair_flag = run(
         lambda *refs: memory_kernel(peers, *refs),
         "memory_pairs",
-        shaped(peers, PACK, HD, dtype=bf16),
+        (shaped(peers, PACK, HD, dtype=bf16), FLAG),
         [smem()] * 2 + [anywhere()] * 6 + [vmem()],
         memory_scratch(1) + memory_sums + [pltpu.VMEM((blocks, PACK, HD), bf16)],
+        out_specs=(vmem(), smem()),
     )(place, asked, mem_cross, mem_acc, mem_low, *mem_weights, value_up)
     got = lax.all_to_all(pairs, "tm", split_axis=0, concat_axis=0, tiled=True)
-    tok_far = after(tok_far, pairs)
+    grad, grad_t, grad_flag = run(
+        grad_kernel,
+        "attended_cotangent",
+        (shaped(tok_rows, query_width, dtype=bf16), shaped(query_width, tok_rows, dtype=bf16), FLAG),
+        [vmem()] * 2 + [smem()],
+        out_specs=(vmem(), vmem(), smem()),
+    )(tag_t, grad_tags.T, pair_flag)
+    tok_far = after(tok_far, grad_flag)
     tok_cross = swap(tok_far, 1)
     early = run(
         project_middle_kernel,
         "project_far_quarter",
         (shaped(tok_rows, query_width), shaped(tok_rows, 2 * HD), shaped(tok_rows, 2 * RANK)),
         [smem()] + [anywhere()] * 9,
-        project_scratch(1) + project_sums + [pltpu.SemaphoreType.DMA((3,))],
+        project_scratch(1) + project_sums + [pltpu.SemaphoreType.DMA((6,))],
     )(place, tok_far, *weights, *early)
 
     seen = peers * BLK
     total = seen + BLK
-    cot, ups, mcot = run(
+    cot, ups, same, other = run(
         lambda *refs: attention_kernel(peers, heads, *refs),
         "span_attention",
-        (shaped(2 * RANK + tags, tok_rows), shaped(RANK, query_width + HD), shaped(peers, RANK, BLK)),
-        [smem()] * 2 + [anywhere()] * 12 + [vmem()] * 3,
+        (shaped(2 * RANK + tags, tok_rows), shaped(RANK, query_width + HD))
+        + (shaped(peers // 2, RANK, BLK),) * 2,
+        [smem()] * 3 + [anywhere()] * 12 + [vmem()] * 3,
         project_scratch(1)
         + project_sums
         + [
@@ -753,31 +777,36 @@
             pltpu.VMEM((PAIR * BLK, query_width), bf16),
             pltpu.VMEM((PAIR * BLK, query_width), bf16),
             pltpu.VMEM((HD, seen), f32),
-            pltpu.SemaphoreType.DMA((3 * peers + 5,)),
+            pltpu.VMEM((peers, RANK, BLK), f32),
+            pltpu.SemaphoreType.DMA((3 * peers + 14,)),
         ],
         flops=20 * tok_rows * query_width * total,
         moved=4 * tok_rows * query_width,
-    )(place, boundary, tok_cross, *weights, *early, got, grad, grad_t, query_up, value_up, tag_t)
-
-    back = lax.all_to_all(mcot, "tm", split_axis=0, concat_axis=0, tiled=True)
+    )(place, me, boundary, tok_cross, *weights, *early, got, grad, grad_t, query_up, value_up, tag_t)
+
+    steps = peers // 2
+    mixed = run(
+        mix_kernel,
+        "both_sides",
+        (shaped(2, RANK, BLK),) * steps,
+        [vmem()] * 2,
+        room=8,
+    )(same, swap(other, 1, "tm"))
+    back = [mixed[0]] + [swap(mixed[n], 2 * n, "tm") for n in range(1, steps)]
     cots = [cot] + [swap(cot, d) for d in range(1, 4)]
-    own = run(
-        lambda *refs: own_kernel(peers, *refs),
-        "owned_cotangent",
-        shaped(RANK, mem_rows),
-        [smem()] + [vmem()],
+    logits, query_sum, value_part, own = run(
+        lambda *refs: first_down_kernel(steps, *refs),
+        "first_down",
+        (
+            shaped(tags, tok_rows),
+            shaped(RANK, width + ups.shape[1]),
+            shaped(RANK, width),
+            shaped(RANK, mem_rows),
+        ),
+        [smem()] * 2 + [vmem()] * (steps + 6),
         [pltpu.VMEM((blocks, RANK, BLK), f32)],
         room=8,
-    )(asked, back)
-    logits, query_sum, value_part = run(
-        first_down_kernel,
-        "first_down",
-        (shaped(tags, tok_rows), shaped(RANK, width + ups.shape[1]), shaped(RANK, width)),
-        [vmem()] * 6,
-        flops=4 * RANK * tok_rows * width,
-        moved=2 * tok_rows * width,
-        room=8,
-    )(*cots, slab_tokens, ups)
+    )(me, asked, *back, *cots, slab_tokens, ups)
     owns = [own] + [swap(own, d) for d in range(1, 4)]
     value_sum = run(
         second_down_kernel,

time: 120 us -> 127 us (1.058)
  Pallas kernels: 54.2 us -> 60.8 us
  waiting for transfers between devices: 21.4 us -> 16.6 us
  starting transfers between devices: 36.5 us -> 41 us
    ppermute x20 -> x24, starting transfers between devices: 17.9 us -> 28.6 us  [swap(): lax.ppermute(x, axis, [(i, i ^ bit) for i in range(lax.axis_size(axis))])]
    all_to_all x1 -> x0, starting transfers between devices: 5.99 us -> none  [fast(): back = lax.all_to_all(mcot, 'tm', split_axis=0, concat_axis=0, tiled=True)]
    pallas_call x3 -> x4, Pallas kernels: 5.17 us -> 10.7 us  [the longest x1 5.42 us: fast(): run(grad_kernel, 'attended_cotangent', (shaped(tok_rows, query_width, dty...]
    all_to_all x1 -> x0, waiting for transfers between devices: 2.47 us -> none  [fast(): back = lax.all_to_all(mcot, 'tm', split_axis=0, concat_axis=0, tiled=True)]
    pallas_call x2, Pallas kernels: 0.01 us -> 1.95 us  [after(): pl.pallas_call(lambda *refs: None, out_shape=jax.ShapeDtypeStruct(x.shape...]
    ppermute x20 -> x24, waiting for transfers between devices: 18.5 us -> 16.6 us  [swap(): lax.ppermute(x, axis, [(i, i ^ bit) for i in range(lax.axis_size(axis))])]
    pallas_call x1, Pallas kernels: 9.01 us -> 7.29 us  [fast(): run(project_early_kernel, 'project_near_half', (shaped(tok_rows, query_wi...]
    unnamed x16 -> x18, local copies, waits for them, and re-layouts: 4.12 us -> 5.27 us
  transfers between devices with their start and end apart: 23 -> 26, of which waited for: 8 -> 9; matrix products, arithmetic and copies ran while one was open for 2% -> 2% of each run, Pallas kernels for 23% -> 25%
where the time goes in v3:
time: 127 us
  Pallas kernels  60.8 us (48%)
  starting transfers between devices  41 us (32%)
  waiting for transfers between devices  16.6 us (13%)
  local copies, waits for them, and re-layouts  6.59 us (5%)
    ppermute x24, starting transfers between devices, swap(): lax.ppermute(x, axis, [(i, i ^ bit) for i in range(lax.axis_size(axis))])  28.6 us
    pallas_call x1, Pallas kernels, fast(): run(lambda *refs: attention_kernel(peers, heads, *refs), 'span_attention'...  26.4 us
    ppermute x24, waiting for transfers between devices, swap(): lax.ppermute(x, axis, [(i, i ^ bit) for i in range(lax.axis_size(axis))])  16.6 us
    pallas_call x1, Pallas kernels, fast(): run(project_early_kernel, 'project_near_half', (shaped(tok_rows, query_wi...  7.29 us
    all_to_all x1, starting transfers between devices, fast(): lax.all_to_all(wanted, 'tm', split_axis=0, concat_axis=0, tiled=True)  6.58 us
    pallas_call x1, Pallas kernels, fast(): run(project_middle_kernel, 'project_far_quarter', (shaped(tok_rows, query...  5.99 us
    all_to_all x1, starting transfers between devices, fast(): got = lax.all_to_all(pairs, 'tm', split_axis=0, concat_axis=0, tiled=True)  5.82 us
    pallas_call x1, Pallas kernels, fast(): run(grad_kernel, 'attended_cotangent', (shaped(tok_rows, query_width, dty...  5.42 us
  transfers between devices with their start and end apart: 26, of which 9 were waited for; matrix products, arithmetic and copies ran while one was open for 2% of the time, Pallas kernels for 25%

profile of v3, /device:TPU:0, one launch (start us, length us, event | category | flops | bytes accessed | tf_op | source)
XLA Modules:
  0.0 126.6 jit_solution(16847940559835773829)
XLA Ops:
  0.6 0.5 collective-permute-start
  1.1 0.1 collective-permute-start.1
  1.2 2.9 %collective-permute-start.3 = (bf16[512,896]{1,0:T(8,128)(2,1)}, bf16[512,896]{1,0:T(8,128)(2,1)S(1)}, u32[]{:S(2)}, u32[]{:S(2)}) collective-permute-start(bf16[512,896]{1,0:T(8,128)(2,1)} %memory_ref.1), channel_id=1, source_target_pairs={{0,2},{1,3},{2,0},{3,1},{4,6},{5,7},{6,4},{7,5},{8,10},{9,11},{10,... | collective-permute-start | bytes 2752520 | tf_op jit(solution)/shard_map/ppermute | solution.py:586
  4.2 0.0 collective-permute-done.refs_3_
  4.2 4.5 %memory_near_half.1 = (f32[512,256]{1,0:T(8,128)}, f32[512,16]{1,0:T(8,128)}, s32[8]{0:T(128)}) custom-call(s32[1]{0:T(128)} %bitcast.1.refs_0_.place_ref, s32[4,8]{1,0:T(4,128)} %refs_1_.4, bf16[512,896]{1,0:T(8,128)(2,1)} %memory_ref.1, bf16[512,896]{1,0:T(8,128)(2,1)} %collective-permute-done.refs_3_, bf16[3584,128]{1,0:T(8,128)(2,1)} %refs_5_.5, ...), custom_call_target="tpu_custom_call" | custom-call | tf_op jit(solution)/shard_map/memory_near_half/pallas_call | solution.py:694
  8.7 1.3 %copy.21 = s32[8,1,1]{2,1,0:T(1,128)} copy(s32[8,1,1]{0,2,1:T(1,128)} %bitcast.9) | data formatting | bytes 64 | tf_op jit(solution)/shard_map/all_to_all | solution.py:702
  10.0 6.6 %all-to-all-start = ((s32[8,1,1]{2,1,0:T(1,128)}), s32[8,1,1]{2,1,0:T(1,128)S(1)}, u32[]{:S(2)}, u32[]{:S(2)}) async-start(s32[8,1,1]{2,1,0:T(1,128)} %copy.21), calls=%async_computation | async-start | bytes 8192 | tf_op jit(solution)/shard_map/all_to_all | solution.py:702
  16.6 7.3 %project_near_half.1 = (f32[512,896]{1,0:T(8,128)}, f32[512,256]{1,0:T(8,128)}, f32[512,32]{1,0:T(8,128)}, s32[1]{0:T(128)}) custom-call(s32[1]{0:T(128)} %bitcast.1.refs_0_.place_ref, bf16[512,896]{1,0:T(8,128)(2,1)} %refs_10_.1, bf16[512,896]{1,0:T(8,128)(2,1)} %collective-permute-done.1.x1, bf16[3584,896]{1,0:T(8,128)(2,1)} %refs_4_.7, ...), custom_call_target="tpu_custom_call" | custom-call | tf_op jit(solution)/shard_map/project_near_half/pallas_call | solution.py:704
  23.9 0.8 reduce.refs_2_.refs_1_
  24.7 0.3 collective-permute-done.3.refs_0_
  25.0 0.9 copy-done.7
  25.9 1.3 %in_order.2.x2 = bf16[512,896]{1,0:T(8,128)(2,1)} custom-call(bf16[512,896]{1,0:T(8,128)(2,1)} %copy-done.7, s32[1]{0:T(128)} %get-tuple-element.39.refs_1_, s32[8]{0:T(128)} %reduce.refs_2_.refs_1_), custom_call_target="tpu_custom_call", output_to_operand_aliasing={{}: (0, {})} | custom-call | tf_op jit(solution)/shard_map/in_order/pallas_call | solution.py:590
  27.2 0.1 collective-permute-start.4
  27.3 1.8 %collective-permute-start.2 = (bf16[512,896]{1,0:T(8,128)(2,1)}, bf16[512,896]{1,0:T(8,128)(2,1)S(1)}, u32[]{:S(2)}, u32[]{:S(2)}) collective-permute-start(bf16[512,896]{1,0:T(8,128)(2,1)} %collective-permute-done.1.x1), channel_id=1, source_target_pairs={{0,2},{1,3},{2,0},{3,1},{4,6},{5,7},{6,4},{7,5},{8,10},{9,11},{10,... | collective-permute-start | bytes 2752520 | tf_op jit(solution)/shard_map/ppermute | solution.py:586
  29.1 3.1 %memory_far_quarter.1 = (f32[512,256]{1,0:T(8,128)}, f32[512,16]{1,0:T(8,128)}) custom-call(s32[1]{0:T(128)} %bitcast.1.refs_0_.place_ref, bf16[512,896]{1,0:T(8,128)(2,1)} %in_order.2.x2, f32[512,256]{1,0:T(8,128)} %get-tuple-element.40.acc_hbm, f32[512,16]{1,0:T(8,128)} %get-tuple-element.41.low_hbm, bf16[3584,128]{1,0:T(8,128)(2,1)} %refs_5_.5, ...), custom_call_target="tpu_custom_call" | custom-call | tf_op jit(solution)/shard_map/memory_far_quarter/pallas_call | solution.py:715
  32.3 0.0 collective-permute-done.4.refs_2_
  32.3 4.0 %memory_pairs.1 = (bf16[8,272,128]{2,1,0:T(8,128)(2,1)}, s32[1]{0:T(128)}) custom-call(s32[1]{0:T(128)} %bitcast.1.refs_0_.place_ref, s32[8]{0:T(128)} %reduce.refs_2_.refs_1_, bf16[512,896]{1,0:T(8,128)(2,1)} %collective-permute-done.4.refs_2_, f32[512,256]{1,0:T(8,128)} %get-tuple-element.42.refs_3_, f32[512,16]{1,0:T(8,128)} %get-tuple-element.43.refs_4_, ...), custom_call_target="tpu_custom_call" | custom-call | tf_op jit(solution)/shard_map/memory_pairs/pallas_call | solution.py:722
  36.3 5.8 %all-to-all-start.1 = ((bf16[8,272,128]{2,1,0:T(8,128)(2,1)}), bf16[8,272,128]{2,1,0:T(8,128)(2,1)}, u32[]{:S(2)}, u32[]{:S(2)}) async-start(bf16[8,272,128]{2,1,0:T(8,128)(2,1)} %get-tuple-element.52), calls=%async_computation.1 | async-start | bytes 1114112 | tf_op jit(solution)/shard_map/all_to_all | solution.py:730
  42.1 5.4 %attended_cotangent.1 = (bf16[512,896]{1,0:T(8,128)(2,1)}, bf16[896,512]{1,0:T(8,128)(2,1)}, s32[1]{0:T(128)}) custom-call(bf16[8,896]{1,0:T(8,128)(2,1)} %bitcast.7, f32[8,512]{1,0:T(8,128)} %bitcast.6, s32[1]{0:T(128)} %get-tuple-element.44.dep_ref), custom_call_target="tpu_custom_call" | custom-call | tf_op jit(solution)/shard_map/attended_cotangent/pallas_call | solution.py:731
  47.5 2.8 %collective-permute-done.2.refs_0_ = bf16[512,896]{1,0:T(8,128)(2,1)S(1)} collective-permute-done((bf16[512,896]{1,0:T(8,128)(2,1)}, bf16[512,896]{1,0:T(8,128)(2,1)S(1)}, u32[]{:S(2)}, u32[]{:S(2)}) %collective-permute-start.2) | collective-permute-done | bytes 917536 | tf_op jit(solution)/shard_map/ppermute | solution.py:586
  50.3 0.9 copy-done.6
  51.2 0.6 in_order.3.x3
  51.9 0.1 collective-permute-start.5
  51.9 6.0 %project_far_quarter.1 = (f32[512,896]{1,0:T(8,128)}, f32[512,256]{1,0:T(8,128)}, f32[512,32]{1,0:T(8,128)}) custom-call(s32[1]{0:T(128)} %bitcast.1.refs_0_.place_ref, bf16[512,896]{1,0:T(8,128)(2,1)} %in_order.3.x3, bf16[3584,896]{1,0:T(8,128)(2,1)} %refs_4_.7, bf16[3584,128]{1,0:T(8,128)(2,1)} %refs_5_.5, bf16[3584,128]{1,0:T(8,128)(2,1)} %refs_6_.5, ...), custom_call_target="tpu_custom_call" | custom-call | tf_op jit(solution)/shard_map/project_far_quarter/pallas_call | solution.py:740
  57.9 0.0 collective-permute-done.5.refs_3_
  58.0 0.9 copy-done.8
  58.9 26.4 %span_attention.1 = (f32[40,512]{1,0:T(8,128)}, f32[16,1024]{1,0:T(8,128)}, f32[4,16,128]{2,1,0:T(8,128)}, f32[4,16,128]{2,1,0:T(8,128)}) custom-call(s32[1]{0:T(128)} %bitcast.1.refs_0_.place_ref, s32[1]{0:T(128)} %bitcast.refs_1_.refs_0_, s32[4]{0:T(128)} %refs_2_.9, bf16[512,896]{1,0:T(8,128)(2,1)} %copy-done.8, bf16[3584,896]{1,0:T(8,128)(2,1)} %refs_4_.7, ...), custom_call_target="tpu_custom_call" | custom-call | flops 10569646080 | bytes 1835008 | tf_op jit(solution)/shard_map/span_attention/pallas_call | solution.py:750
  85.3 0.0 copy-start
  85.3 1.9 %collective-permute-start.12 = (f32[40,512]{1,0:T(8,128)}, f32[40,512]{1,0:T(8,128)S(1)}, u32[]{:S(2)}, u32[]{:S(2)}) collective-permute-start(f32[40,512]{1,0:T(8,128)} %get-tuple-element.61.refs_6_), channel_id=1, source_target_pairs={{0,3},{1,2},{2,1},{3,0},{4,7},{5,6},{6,5},{7,4},{8,11},{9,10},{10,... | collective-permute-start | bytes 245768 | tf_op jit(solution)/shard_map/ppermute | solution.py:586
  87.2 0.3 collective-permute-start.11
  87.4 0.0 collective-permute-start.10
  87.4 1.7 %collective-permute-start.6 = (f32[4,16,128]{2,1,0:T(8,128)}, f32[4,16,128]{2,1,0:T(8,128)S(1)}, u32[]{:S(2)}, u32[]{:S(2)}) collective-permute-start(f32[4,16,128]{2,1,0:T(8,128)} %get-tuple-element.56), channel_id=1, source_target_pairs={{0,4},{4,0},{8,12},{12,8},{16,20},{20,16},{24,28},{28,24},{1,5},{5... | collective-permute-start | bytes 98312 | tf_op jit(solution)/shard_map/ppermute | solution.py:586
  89.1 2.4 %collective-permute-done.6.other_ref = f32[4,16,128]{2,1,0:T(8,128)S(1)} collective-permute-done((f32[4,16,128]{2,1,0:T(8,128)}, f32[4,16,128]{2,1,0:T(8,128)S(1)}, u32[]{:S(2)}, u32[]{:S(2)}) %collective-permute-start.6) | collective-permute-done | bytes 32800 | tf_op jit(solution)/shard_map/ppermute | solution.py:586
  91.6 0.8 copy-done.4
  92.3 1.8 %collective-permute-start.7 = (f32[2,16,128]{2,1,0:T(8,128)S(1)}, f32[2,16,128]{2,1,0:T(8,128)S(1)}, u32[]{:S(2)}, u32[]{:S(2)}) collective-permute-start(f32[2,16,128]{2,1,0:T(8,128)S(1)} %get-tuple-element.58), channel_id=1, source_target_pairs={{0,8},{4,12},{8,0},{12,4},{16,24},{20,28},{24,16},{28,20},{1,9},{5... | collective-permute-start | bytes 49160 | tf_op jit(solution)/shard_map/ppermute | solution.py:586
  94.1 2.6 %collective-permute-start.8 = (f32[2,16,128]{2,1,0:T(8,128)S(1)}, f32[2,16,128]{2,1,0:T(8,128)S(1)}, u32[]{:S(2)}, u32[]{:S(2)}) collective-permute-start(f32[2,16,128]{2,1,0:T(8,128)S(1)} %get-tuple-element.59), channel_id=1, source_target_pairs={{0,16},{4,20},{8,24},{12,28},{16,0},{20,4},{24,8},{28,12},{1,17},{... | collective-permute-start | bytes 49160 | tf_op jit(solution)/shard_map/ppermute | solution.py:586
  96.7 3.2 %collective-permute-start.9 = (f32[2,16,128]{2,1,0:T(8,128)S(1)}, f32[2,16,128]{2,1,0:T(8,128)S(1)}, u32[]{:S(2)}, u32[]{:S(2)}) collective-permute-start(f32[2,16,128]{2,1,0:T(8,128)S(1)} %get-tuple-element.60), channel_id=1, source_target_pairs={{0,24},{4,28},{8,16},{12,20},{16,8},{20,12},{24,0},{28,4},{1,25},{... | collective-permute-start | bytes 49160 | tf_op jit(solution)/shard_map/ppermute | solution.py:586
  99.9 2.4 %collective-permute-done.9.refs_5_ = f32[2,16,128]{2,1,0:T(8,128)S(1)} collective-permute-done((f32[2,16,128]{2,1,0:T(8,128)S(1)}, f32[2,16,128]{2,1,0:T(8,128)S(1)}, u32[]{:S(2)}, u32[]{:S(2)}) %collective-permute-start.9) | collective-permute-done | bytes 16416 | tf_op jit(solution)/shard_map/ppermute | solution.py:586
  102.2 0.0 collective-permute-done.12.refs_9_
  102.2 0.0 collective-permute-done.11.refs_8_
  102.2 0.0 collective-permute-done.10.refs_7_
  102.3 0.9 copy-done.2
  103.2 0.8 copy-done.3
  104.0 1.3 %first_down.1 = (f32[8,512]{1,0:T(8,128)}, f32[16,1920]{1,0:T(8,128)S(1)}, f32[16,896]{1,0:T(8,128)S(1)}, f32[16,512]{1,0:T(8,128)S(1)}) custom-call(s32[1]{0:T(128)} %bitcast.refs_1_.refs_0_, s32[8]{0:T(128)S(1)} %copy-done.5, f32[2,16,128]{2,1,0:T(8,128)S(1)} %get-tuple-element.57.refs_2_, f32[2,16,128]{2,1,0:T(8,128)S(1)} %collective-permute-done.7.refs_3_, ...), custom_call_target="tpu_custom_call" | custom-call | tf_op jit(solution)/shard_map/first_down/pallas_call | solution.py:797
  105.3 1.5 %collective-permute-start.13 = (f32[16,1920]{1,0:T(8,128)S(1)}, f32[16,1920]{1,0:T(8,128)S(1)}, u32[]{:S(2)}, u32[]{:S(2)}) collective-permute-start(f32[16,1920]{1,0:T(8,128)S(1)} %get-tuple-element.64), channel_id=1, source_target_pairs={{0,4},{4,0},{8,12},{12,8},{16,20},{20,16},{24,28},{28,24},{1,5},{5... | collective-permute-start | bytes 368648 | tf_op jit(solution)/shard_map/ppermute | solution.py:586
  106.8 0.0 collective-permute-start.19
  106.8 1.6 %collective-permute-start.18 = (f32[16,512]{1,0:T(8,128)S(1)}, f32[16,512]{1,0:T(8,128)S(1)}, u32[]{:S(2)}, u32[]{:S(2)}) collective-permute-start(f32[16,512]{1,0:T(8,128)S(1)} %get-tuple-element.65.c0), channel_id=1, source_target_pairs={{0,2},{1,3},{2,0},{3,1},{4,6},{5,7},{6,4},{7,5},{8,10},{9,11},{10,... | collective-permute-start | bytes 98312 | tf_op jit(solution)/shard_map/ppermute | solution.py:586
  108.4 0.3 collective-permute-start.17
  108.7 1.7 %collective-permute-done.19.c3 = f32[16,512]{1,0:T(8,128)S(1)} collective-permute-done((f32[16,512]{1,0:T(8,128)S(1)}, f32[16,512]{1,0:T(8,128)S(1)}, u32[]{:S(2)}, u32[]{:S(2)}) %collective-permute-start.19) | collective-permute-done | bytes 32800 | tf_op jit(solution)/shard_map/ppermute | solution.py:586
  110.4 0.4 collective-permute-done.18.c2
  110.8 0.2 second_down.1
  111.1 0.6 collective-permute-start.20
  111.7 0.0 collective-permute-done.13
  111.7 3.2 %collective-permute-start.16 = (bf16[16,1920]{1,0:T(8,128)(2,1)S(1)}, bf16[16,1920]{1,0:T(8,128)(2,1)S(1)}, u32[]{:S(2)}, u32[]{:S(2)}) collective-permute-start(bf16[16,1920]{1,0:T(8,128)(2,1)S(1)} %add_convert_fusion.refs_0_), channel_id=1, source_target_pairs={{0,24},{4,28},{8,16},{12,20},{16,8},{20,12},{24,0},{28,4},{1,25},{... | collective-permute-start | bytes 184328 | tf_op jit(solution)/shard_map/ppermute | solution.py:586
  114.9 0.0 collective-permute-start.15
  114.9 1.2 collective-permute-start.14
  116.1 0.0 collective-permute-done.20
  116.2 3.2 %collective-permute-start.23 = (bf16[16,896]{1,0:T(8,128)(2,1)S(1)}, bf16[16,896]{1,0:T(8,128)(2,1)S(1)}, u32[]{:S(2)}, u32[]{:S(2)}) collective-permute-start(bf16[16,896]{1,0:T(8,128)(2,1)S(1)} %add_convert_fusion.1.refs_4_), channel_id=1, source_target_pairs={{0,24},{4,28},{8,16},{12,20},{16,8},{20,12},{24,0},{28,4},{1,25},{... | collective-permute-start | bytes 86024 | tf_op jit(solution)/shard_map/ppermute | solution.py:586
  119.4 0.0 collective-permute-start.22
  119.4 2.6 %collective-permute-done.23.refs_7_ = bf16[16,896]{1,0:T(8,128)(2,1)S(1)} collective-permute-done((bf16[16,896]{1,0:T(8,128)(2,1)S(1)}, bf16[16,896]{1,0:T(8,128)(2,1)S(1)}, u32[]{:S(2)}, u32[]{:S(2)}) %collective-permute-start.23) | collective-permute-done | bytes 28704 | tf_op jit(solution)/shard_map/ppermute | solution.py:586
  122.0 0.0 collective-permute-start.21
  122.0 2.1 %collective-permute-done.22.refs_6_ = bf16[16,896]{1,0:T(8,128)(2,1)S(1)} collective-permute-done((bf16[16,896]{1,0:T(8,128)(2,1)S(1)}, bf16[16,896]{1,0:T(8,128)(2,1)S(1)}, u32[]{:S(2)}, u32[]{:S(2)}) %collective-permute-start.22) | collective-permute-done | bytes 28704 | tf_op jit(solution)/shard_map/ppermute | solution.py:586
  124.2 1.7 %collective-permute-done.21.refs_5_ = bf16[16,896]{1,0:T(8,128)(2,1)S(1)} collective-permute-done((bf16[16,896]{1,0:T(8,128)(2,1)S(1)}, bf16[16,896]{1,0:T(8,128)(2,1)S(1)}, u32[]{:S(2)}, u32[]{:S(2)}) %collective-permute-start.21) | collective-permute-done | bytes 28704 | tf_op jit(solution)/shard_map/ppermute | solution.py:586
  125.9 0.7 finish_outputs.1
  (23 shorter events, 0.1 us)
Async XLA Ops:
  0.6 3.5 %collective-permute-start = (bf16[512,896]{1,0:T(8,128)(2,1)}, bf16[512,896]{1,0:T(8,128)(2,1)}, u32[]{:S(2)}, u32[]{:S(2)}) collective-permute-start(bf16[512,896]{1,0:T(8,128)(2,1)} %memory_ref.1), channel_id=1, source_target_pairs={{0,1},{1,0},{2,3},{3,2},{4,5},{5,4},{6,7},{7,6},{8,9},{9,8},{10,11... | collective-permute-start | bytes 2752520 | tf_op jit(solution)/shard_map/ppermute | solution.py:586
  1.1 15.4 %collective-permute-start.1 = (bf16[512,896]{1,0:T(8,128)(2,1)}, bf16[512,896]{1,0:T(8,128)(2,1)}, u32[]{:S(2)}, u32[]{:S(2)}) collective-permute-start(bf16[512,896]{1,0:T(8,128)(2,1)} %refs_10_.1), channel_id=1, source_target_pairs={{0,1},{1,0},{2,3},{3,2},{4,5},{5,4},{6,7},{7,6},{8,9},{9,8},{10,11... | collective-permute-start | bytes 2752520 | tf_op jit(solution)/shard_map/ppermute | solution.py:586
  1.2 23.7 %collective-permute-start.3 = (bf16[512,896]{1,0:T(8,128)(2,1)}, bf16[512,896]{1,0:T(8,128)(2,1)S(1)}, u32[]{:S(2)}, u32[]{:S(2)}) collective-permute-start(bf16[512,896]{1,0:T(8,128)(2,1)} %memory_ref.1), channel_id=1, source_target_pairs={{0,2},{1,3},{2,0},{3,1},{4,6},{5,7},{6,4},{7,5},{8,10},{9,11},{10,... | collective-permute-start | bytes 2752520 | tf_op jit(solution)/shard_map/ppermute | solution.py:586
  10.0 13.9 %all-to-all-start = ((s32[8,1,1]{2,1,0:T(1,128)}), s32[8,1,1]{2,1,0:T(1,128)S(1)}, u32[]{:S(2)}, u32[]{:S(2)}) async-start(s32[8,1,1]{2,1,0:T(1,128)} %copy.21), calls=%async_computation | async-start | bytes 8192 | tf_op jit(solution)/shard_map/all_to_all | solution.py:702
  25.0 0.9 copy-start.7
  27.2 5.0 %collective-permute-start.4 = (bf16[512,896]{1,0:T(8,128)(2,1)}, bf16[512,896]{1,0:T(8,128)(2,1)}, u32[]{:S(2)}, u32[]{:S(2)}) collective-permute-start(bf16[512,896]{1,0:T(8,128)(2,1)} %in_order.2.x2), channel_id=1, source_target_pairs={{0,1},{1,0},{2,3},{3,2},{4,5},{5,4},{6,7},{7,6},{8,9},{9,8},{10,11... | collective-permute-start | bytes 2752520 | tf_op jit(solution)/shard_map/ppermute | solution.py:586
  27.3 23.0 %collective-permute-start.2 = (bf16[512,896]{1,0:T(8,128)(2,1)}, bf16[512,896]{1,0:T(8,128)(2,1)S(1)}, u32[]{:S(2)}, u32[]{:S(2)}) collective-permute-start(bf16[512,896]{1,0:T(8,128)(2,1)} %collective-permute-done.1.x1), channel_id=1, source_target_pairs={{0,2},{1,3},{2,0},{3,1},{4,6},{5,7},{6,4},{7,5},{8,10},{9,11},{10,... | collective-permute-start | bytes 2752520 | tf_op jit(solution)/shard_map/ppermute | solution.py:586
  36.3 21.7 %all-to-all-start.1 = ((bf16[8,272,128]{2,1,0:T(8,128)(2,1)}), bf16[8,272,128]{2,1,0:T(8,128)(2,1)}, u32[]{:S(2)}, u32[]{:S(2)}) async-start(bf16[8,272,128]{2,1,0:T(8,128)(2,1)} %get-tuple-element.52), calls=%async_computation.1 | async-start | bytes 1114112 | tf_op jit(solution)/shard_map/all_to_all | solution.py:730
  50.3 0.9 copy-start.6
  51.9 6.1 %collective-permute-start.5 = (bf16[512,896]{1,0:T(8,128)(2,1)}, bf16[512,896]{1,0:T(8,128)(2,1)S(1)}, u32[]{:S(2)}, u32[]{:S(2)}) collective-permute-start(bf16[512,896]{1,0:T(8,128)(2,1)} %in_order.3.x3), channel_id=1, source_target_pairs={{0,1},{1,0},{2,3},{3,2},{4,5},{5,4},{6,7},{7,6},{8,9},{9,8},{10,11... | collective-permute-start | bytes 2752520 | tf_op jit(solution)/shard_map/ppermute | solution.py:586
  58.0 0.9 copy-start.8
  58.9 43.4 %copy-start.1 = (bf16[512,896]{1,0:T(8,128)(2,1)S(1)}, bf16[512,896]{1,0:T(8,128)(2,1)}, u32[]{:S(2)}) copy-start(bf16[512,896]{1,0:T(8,128)(2,1)} %refs_10_.1) | copy-start | bytes 2752516
  58.9 43.4 %copy-start.5 = (s32[8]{0:T(128)S(1)}, s32[8]{0:T(128)}, u32[]{:S(2)}) copy-start(s32[8]{0:T(128)} %reduce.refs_2_.refs_1_) | copy-start | bytes 100
  85.3 25.6 %copy-start = (bf16[512,896]{1,0:T(8,128)(2,1)S(1)}, bf16[512,896]{1,0:T(8,128)(2,1)}, u32[]{:S(2)}) copy-start(bf16[512,896]{1,0:T(8,128)(2,1)} %memory_ref.1) | copy-start | bytes 2752516
  85.3 17.0 %collective-permute-start.12 = (f32[40,512]{1,0:T(8,128)}, f32[40,512]{1,0:T(8,128)S(1)}, u32[]{:S(2)}, u32[]{:S(2)}) collective-permute-start(f32[40,512]{1,0:T(8,128)} %get-tuple-element.61.refs_6_), channel_id=1, source_target_pairs={{0,3},{1,2},{2,1},{3,0},{4,7},{5,6},{6,5},{7,4},{8,11},{9,10},{10,... | collective-permute-start | bytes 245768 | tf_op jit(solution)/shard_map/ppermute | solution.py:586
  87.2 15.1 %collective-permute-start.11 = (f32[40,512]{1,0:T(8,128)}, f32[40,512]{1,0:T(8,128)S(1)}, u32[]{:S(2)}, u32[]{:S(2)}) collective-permute-start(f32[40,512]{1,0:T(8,128)} %get-tuple-element.61.refs_6_), channel_id=1, source_target_pairs={{0,2},{1,3},{2,0},{3,1},{4,6},{5,7},{6,4},{7,5},{8,10},{9,11},{10,... | collective-permute-start | bytes 245768 | tf_op jit(solution)/shard_map/ppermute | solution.py:586
  87.4 14.8 %collective-permute-start.10 = (f32[40,512]{1,0:T(8,128)}, f32[40,512]{1,0:T(8,128)S(1)}, u32[]{:S(2)}, u32[]{:S(2)}) collective-permute-start(f32[40,512]{1,0:T(8,128)} %get-tuple-element.61.refs_6_), channel_id=1, source_target_pairs={{0,1},{1,0},{2,3},{3,2},{4,5},{5,4},{6,7},{7,6},{8,9},{9,8},{10,11... | collective-permute-start | bytes 245768 | tf_op jit(solution)/shard_map/ppermute | solution.py:586
  87.4 4.1 %collective-permute-start.6 = (f32[4,16,128]{2,1,0:T(8,128)}, f32[4,16,128]{2,1,0:T(8,128)S(1)}, u32[]{:S(2)}, u32[]{:S(2)}) collective-permute-start(f32[4,16,128]{2,1,0:T(8,128)} %get-tuple-element.56), channel_id=1, source_target_pairs={{0,4},{4,0},{8,12},{12,8},{16,20},{20,16},{24,28},{28,24},{1,5},{5... | collective-permute-start | bytes 98312 | tf_op jit(solution)/shard_map/ppermute | solution.py:586
  91.6 0.8 copy-start.4
  92.3 4.4 %collective-permute-start.7 = (f32[2,16,128]{2,1,0:T(8,128)S(1)}, f32[2,16,128]{2,1,0:T(8,128)S(1)}, u32[]{:S(2)}, u32[]{:S(2)}) collective-permute-start(f32[2,16,128]{2,1,0:T(8,128)S(1)} %get-tuple-element.58), channel_id=1, source_target_pairs={{0,8},{4,12},{8,0},{12,4},{16,24},{20,28},{24,16},{28,20},{1,9},{5... | collective-permute-start | bytes 49160 | tf_op jit(solution)/shard_map/ppermute | solution.py:586
  94.1 5.8 %collective-permute-start.8 = (f32[2,16,128]{2,1,0:T(8,128)S(1)}, f32[2,16,128]{2,1,0:T(8,128)S(1)}, u32[]{:S(2)}, u32[]{:S(2)}) collective-permute-start(f32[2,16,128]{2,1,0:T(8,128)S(1)} %get-tuple-element.59), channel_id=1, source_target_pairs={{0,16},{4,20},{8,24},{12,28},{16,0},{20,4},{24,8},{28,12},{1,17},{... | collective-permute-start | bytes 49160 | tf_op jit(solution)/shard_map/ppermute | solution.py:586
  96.7 5.5 %collective-permute-start.9 = (f32[2,16,128]{2,1,0:T(8,128)S(1)}, f32[2,16,128]{2,1,0:T(8,128)S(1)}, u32[]{:S(2)}, u32[]{:S(2)}) collective-permute-start(f32[2,16,128]{2,1,0:T(8,128)S(1)} %get-tuple-element.60), channel_id=1, source_target_pairs={{0,24},{4,28},{8,16},{12,20},{16,8},{20,12},{24,0},{28,4},{1,25},{... | collective-permute-start | bytes 49160 | tf_op jit(solution)/shard_map/ppermute | solution.py:586
  102.3 0.9 copy-start.2
  103.2 0.8 copy-start.3
  105.3 6.4 %collective-permute-start.13 = (f32[16,1920]{1,0:T(8,128)S(1)}, f32[16,1920]{1,0:T(8,128)S(1)}, u32[]{:S(2)}, u32[]{:S(2)}) collective-permute-start(f32[16,1920]{1,0:T(8,128)S(1)} %get-tuple-element.64), channel_id=1, source_target_pairs={{0,4},{4,0},{8,12},{12,8},{16,20},{20,16},{24,28},{28,24},{1,5},{5... | collective-permute-start | bytes 368648 | tf_op jit(solution)/shard_map/ppermute | solution.py:586
  106.8 3.6 %collective-permute-start.19 = (f32[16,512]{1,0:T(8,128)S(1)}, f32[16,512]{1,0:T(8,128)S(1)}, u32[]{:S(2)}, u32[]{:S(2)}) collective-permute-start(f32[16,512]{1,0:T(8,128)S(1)} %get-tuple-element.65.c0), channel_id=1, source_target_pairs={{0,3},{1,2},{2,1},{3,0},{4,7},{5,6},{6,5},{7,4},{8,11},{9,10},{10,... | collective-permute-start | bytes 98312 | tf_op jit(solution)/shard_map/ppermute | solution.py:586
  106.8 4.0 %collective-permute-start.18 = (f32[16,512]{1,0:T(8,128)S(1)}, f32[16,512]{1,0:T(8,128)S(1)}, u32[]{:S(2)}, u32[]{:S(2)}) collective-permute-start(f32[16,512]{1,0:T(8,128)S(1)} %get-tuple-element.65.c0), channel_id=1, source_target_pairs={{0,2},{1,3},{2,0},{3,1},{4,6},{5,7},{6,4},{7,5},{8,10},{9,11},{10,... | collective-permute-start | bytes 98312 | tf_op jit(solution)/shard_map/ppermute | solution.py:586
  108.4 2.5 %collective-permute-start.17 = (f32[16,512]{1,0:T(8,128)S(1)}, f32[16,512]{1,0:T(8,128)S(1)}, u32[]{:S(2)}, u32[]{:S(2)}) collective-permute-start(f32[16,512]{1,0:T(8,128)S(1)} %get-tuple-element.65.c0), channel_id=1, source_target_pairs={{0,1},{1,0},{2,3},{3,2},{4,5},{5,4},{6,7},{7,6},{8,9},{9,8},{10,11... | collective-permute-start | bytes 98312 | tf_op jit(solution)/shard_map/ppermute | solution.py:586
  111.1 5.1 %collective-permute-start.20 = (f32[16,896]{1,0:T(8,128)S(1)}, f32[16,896]{1,0:T(8,128)S(1)}, u32[]{:S(2)}, u32[]{:S(2)}) collective-permute-start(f32[16,896]{1,0:T(8,128)S(1)} %second_down.1), channel_id=1, source_target_pairs={{0,4},{4,0},{8,12},{12,8},{16,20},{20,16},{24,28},{28,24},{1,5},{5... | collective-permute-start | bytes 172040 | tf_op jit(solution)/shard_map/ppermute | solution.py:586
  111.7 14.2 %collective-permute-start.16 = (bf16[16,1920]{1,0:T(8,128)(2,1)S(1)}, bf16[16,1920]{1,0:T(8,128)(2,1)S(1)}, u32[]{:S(2)}, u32[]{:S(2)}) collective-permute-start(bf16[16,1920]{1,0:T(8,128)(2,1)S(1)} %add_convert_fusion.refs_0_), channel_id=1, source_target_pairs={{0,24},{4,28},{8,16},{12,20},{16,8},{20,12},{24,0},{28,4},{1,25},{... | collective-permute-start | bytes 184328 | tf_op jit(solution)/shard_map/ppermute | solution.py:586
  114.9 11.0 %collective-permute-start.15 = (bf16[16,1920]{1,0:T(8,128)(2,1)S(1)}, bf16[16,1920]{1,0:T(8,128)(2,1)S(1)}, u32[]{:S(2)}, u32[]{:S(2)}) collective-permute-start(bf16[16,1920]{1,0:T(8,128)(2,1)S(1)} %add_convert_fusion.refs_0_), channel_id=1, source_target_pairs={{0,16},{4,20},{8,24},{12,28},{16,0},{20,4},{24,8},{28,12},{1,17},{... | collective-permute-start | bytes 184328 | tf_op jit(solution)/shard_map/ppermute | solution.py:586
  114.9 11.0 %collective-permute-start.14 = (bf16[16,1920]{1,0:T(8,128)(2,1)S(1)}, bf16[16,1920]{1,0:T(8,128)(2,1)S(1)}, u32[]{:S(2)}, u32[]{:S(2)}) collective-permute-start(bf16[16,1920]{1,0:T(8,128)(2,1)S(1)} %add_convert_fusion.refs_0_), channel_id=1, source_target_pairs={{0,8},{4,12},{8,0},{12,4},{16,24},{20,28},{24,16},{28,20},{1,9},{5... | collective-permute-start | bytes 184328 | tf_op jit(solution)/shard_map/ppermute | solution.py:586
  116.2 5.9 %collective-permute-start.23 = (bf16[16,896]{1,0:T(8,128)(2,1)S(1)}, bf16[16,896]{1,0:T(8,128)(2,1)S(1)}, u32[]{:S(2)}, u32[]{:S(2)}) collective-permute-start(bf16[16,896]{1,0:T(8,128)(2,1)S(1)} %add_convert_fusion.1.refs_4_), channel_id=1, source_target_pairs={{0,24},{4,28},{8,16},{12,20},{16,8},{20,12},{24,0},{28,4},{1,25},{... | collective-permute-start | bytes 86024 | tf_op jit(solution)/shard_map/ppermute | solution.py:586
  119.4 4.8 %collective-permute-start.22 = (bf16[16,896]{1,0:T(8,128)(2,1)S(1)}, bf16[16,896]{1,0:T(8,128)(2,1)S(1)}, u32[]{:S(2)}, u32[]{:S(2)}) collective-permute-start(bf16[16,896]{1,0:T(8,128)(2,1)S(1)} %add_convert_fusion.1.refs_4_), channel_id=1, source_target_pairs={{0,16},{4,20},{8,24},{12,28},{16,0},{20,4},{24,8},{28,12},{1,17},{... | collective-permute-start | bytes 86024 | tf_op jit(solution)/shard_map/ppermute | solution.py:586
  122.0 3.9 %collective-permute-start.21 = (bf16[16,896]{1,0:T(8,128)(2,1)S(1)}, bf16[16,896]{1,0:T(8,128)(2,1)S(1)}, u32[]{:S(2)}, u32[]{:S(2)}) collective-permute-start(bf16[16,896]{1,0:T(8,128)(2,1)S(1)} %add_convert_fusion.1.refs_4_), channel_id=1, source_target_pairs={{0,8},{4,12},{8,0},{12,4},{16,24},{20,28},{24,16},{28,20},{1,9},{5... | collective-permute-start | bytes 86024 | tf_op jit(solution)/shard_map/ppermute | solution.py:586

commit v4 on v2

--- a/solution.py
+++ b/solution.py
@@ -230,7 +230,7 @@
 STRIP = 16
 PAIR = 2
 MIB = 1024 * 1024
-ROOM = 63
+ROOM = 63.5
 
 
 def dot_nt(a, b, precision=None):
@@ -389,47 +389,45 @@
                 ref[...] += term
 
 
-def project_middle_kernel(place_ref, x3, *refs):
-    hbm, early, outs, scratch, sems = refs[:5], refs[5:8], refs[8:11], refs[11:17], refs[17]
-    sum_refs, sum_sems = refs[18:21], refs[21]
-    groups = project_pieces(place_ref, (3,), (x3,), hbm, scratch, sems)
+def project_far_kernel(place_ref, x3, x2, *refs):
+    hbm, early, (qup_ref, vup_ref), (q_ref, k_ref, v_ref, low_ref) = refs[:5], refs[5:8], refs[8:10], refs[10:14]
+    scratch, sems, sum_refs, sum_sems = refs[14:20], refs[20], refs[21:24], refs[24]
+    groups = project_pieces(place_ref, (3, 2), (x3, x2), hbm, scratch, sems)
     loads = start_copies(list(zip(early, sum_refs)), sum_sems)
     wait_all(groups[0])
     terms = project_terms(0, scratch)
     wait_all(loads)
-    for out, ref, term in zip(outs, sum_refs, terms):
-        out[...] = ref[...] + term
-
-
-def attention_kernel(peers, heads, place_ref, bound_ref, x2, *refs):
-    hbm, early, got, grad_hbm, grad_t_hbm = refs[:5], refs[5:8], refs[8], refs[9], refs[10]
-    qup_ref, vup_ref, tag_ref, cot_ref, up_ref, mcot_ref = refs[11:17]
-    scratch, sems, sum_refs = refs[17:23], refs[23], refs[24:27]
+    for ref, term in zip(sum_refs, terms):
+        ref[...] += term
+    wait_all(groups[1])
+    q_acc, kv_acc, low_acc = [ref[...] + term for ref, term in zip(sum_refs, project_terms(1, scratch))]
+    low = low_acc.astype(jnp.bfloat16)
+    q_ref[...] = (q_acc + dot_nn(low[:, :RANK], qup_ref[...])).astype(jnp.bfloat16)
+    k_ref[...] = kv_acc[:, :HD].astype(jnp.bfloat16)
+    v_ref[...] = (kv_acc[:, HD:] + dot_nn(low[:, RANK:], vup_ref[...])).astype(jnp.bfloat16)
+    low_ref[...] = jnp.transpose(low_acc).astype(jnp.bfloat16)
+
+
+def attention_kernel(peers, heads, bound_ref, *refs):
+    parts, got, grad_hbm, grad_t_hbm = refs[:4], refs[4], refs[5], refs[6]
+    qup_ref, vup_ref, tag_ref, cot_ref, up_ref, mcot_ref = refs[7:13]
     (q_s, k_own, v_own, low_s, low_m_s, grad_ref, grad_t_ref, k_all, v_all, kt_all, vt_all, kt_own, vt_own, bias_s, s_s, dp_s,
-     p_s, ds_s, att_s, dq_s, dv_s, more_sems) = refs[27:]
+     p_s, ds_s, att_s, dq_s, dv_s, more_sems) = refs[13:]
     seen = peers * BLK
-    groups = project_pieces(place_ref, (2,), (x2,), hbm, scratch, sems)
-    pairs = list(zip(early, sum_refs))
+    pairs = []
     for b in range(peers):
         at = slice(b * BLK, (b + 1) * BLK)
         pairs.append((got.at[b, pl.ds(0, BLK), :], k_all.at[at, :]))
         pairs.append((got.at[b, pl.ds(BLK, BLK), :], v_all.at[at, :]))
         pairs.append((got.at[b, pl.ds(2 * BLK, RANK), :], low_m_s.at[b]))
-    pairs += [(grad_hbm, grad_ref), (grad_t_hbm, grad_t_ref)]
+    pairs += list(zip(parts, (q_s, k_own, v_own, low_s))) + [(grad_hbm, grad_ref), (grad_t_hbm, grad_t_ref)]
     copies = start_copies(pairs, more_sems)
-    wait_all(groups[0])
-    wait_all(copies[:3])
-    q_acc, kv_acc, low_acc = [ref[...] + term for ref, term in zip(sum_refs, project_terms(0, scratch))]
-    low = low_acc.astype(jnp.bfloat16)
-    q_s[...] = (q_acc + dot_nn(low[:, :RANK], qup_ref[...])).astype(jnp.bfloat16)
-    k_own[...] = kv_acc[:, :HD].astype(jnp.bfloat16)
-    v_own[...] = (kv_acc[:, HD:] + dot_nn(low[:, RANK:], vup_ref[...])).astype(jnp.bfloat16)
-    low_s[...] = jnp.transpose(low_acc).astype(jnp.bfloat16)
-    wait_all(copies[3:])
+    wait_all(copies[: 3 * peers])
     for b in range(peers):
         at = slice(b * BLK, (b + 1) * BLK)
         kt_all[:, at] = jnp.transpose(k_all[at, :])
         vt_all[:, at] = jnp.transpose(v_all[at, :])
+    wait_all(copies[3 * peers :])
     dv_s[...] = jnp.zeros_like(dv_s)
     up_ref[...] = jnp.zeros_like(up_ref)
     scale = HD ** (-0.5)
@@ -526,15 +524,12 @@
         mcot_ref[b] = mcot[:, b * BLK : (b + 1) * BLK]
 
 
-def own_kernel(peers, asked_ref, back_ref, out_ref, sum_s):
+def first_down_kernel(peers, asked_ref, back_ref, c0, c1, c2, c3, slab_ref, up_ref, logit_ref, query_ref, value_ref, own_ref, sum_s):
     sum_s[...] = jnp.zeros_like(sum_s)
     for r in range(peers):
         block = asked_ref[r]
         sum_s[block] = sum_s[block] + back_ref[r]
-    out_ref[...] = jnp.concatenate([sum_s[m] for m in range(sum_s.shape[0])], 1)
-
-
-def first_down_kernel(c0, c1, c2, c3, slab_ref, up_ref, logit_ref, query_ref, value_ref):
+    own_ref[...] = jnp.concatenate([sum_s[m] for m in range(sum_s.shape[0])], 1)
     cot = (c0[...] + c1[...]) + (c2[...] + c3[...])
     logit_ref[...] = cot[2 * RANK :]
     both = dot_nn(cot[: 2 * RANK].astype(jnp.bfloat16), slab_ref[...])
@@ -602,7 +597,7 @@
         in_specs=in_specs,
         out_specs=out_specs or (tuple(vmem() for _ in out_shape) if many else vmem()),
         scratch_shapes=list(scratch),
-        compiler_params=pltpu.CompilerParams(vmem_limit_bytes=room * MIB),
+        compiler_params=pltpu.CompilerParams(vmem_limit_bytes=int(room * MIB)),
         cost_estimate=pl.CostEstimate(flops=flops, bytes_accessed=moved, transcendentals=0),
         name=name,
     )
@@ -681,20 +676,7 @@
     )(place, retrieval, memory, mem_near, key_weight, value_weight, value_down)
     asked = lax.all_to_all(wanted, "tm", split_axis=0, concat_axis=0, tiled=True)
     weights = (query_weight, key_weight, value_weight, query_down, value_down)
-    *early, grad, grad_t = run(
-        project_early_kernel,
-        "project_near_half",
-        (
-            shaped(tok_rows, query_width),
-            shaped(tok_rows, 2 * HD),
-            shaped(tok_rows, 2 * RANK),
-            shaped(tok_rows, query_width, dtype=bf16),
-            shaped(query_width, tok_rows, dtype=bf16),
-        ),
-        [smem()] + [anywhere()] * 7 + [vmem()] * 2 + [smem()],
-        project_scratch(2),
-    )(place, slab_tokens, tok_near, *weights, tag_t, grad_tags.T, wanted)
-    mem_far = after(mem_far, early[2], asked)
+    mem_far = after(mem_far, asked)
     mem_cross = swap(mem_far, 1)
     mem_weights = (key_weight, value_weight, value_down)
     mem_acc, mem_low = run(
@@ -712,15 +694,33 @@
         memory_scratch(1) + memory_sums + [pltpu.VMEM((blocks, PACK, HD), bf16)],
     )(place, asked, mem_cross, mem_acc, mem_low, *mem_weights, value_up)
     got = lax.all_to_all(pairs, "tm", split_axis=0, concat_axis=0, tiled=True)
-    tok_far = after(tok_far, pairs)
+    *early, grad, grad_t = run(
+        project_early_kernel,
+        "project_near_half",
+        (
+            shaped(tok_rows, query_width),
+            shaped(tok_rows, 2 * HD),
+            shaped(tok_rows, 2 * RANK),
+            shaped(tok_rows, query_width, dtype=bf16),
+            shaped(query_width, tok_rows, dtype=bf16),
+        ),
+        [smem()] + [anywhere()] * 7 + [vmem()] * 2 + [anywhere()],
+        project_scratch(2),
+    )(place, slab_tokens, tok_near, *weights, tag_t, grad_tags.T, pairs)
+    tok_far = after(tok_far, early[2])
     tok_cross = swap(tok_far, 1)
-    early = run(
-        project_middle_kernel,
-        "project_far_quarter",
-        (shaped(tok_rows, query_width), shaped(tok_rows, 2 * HD), shaped(tok_rows, 2 * RANK)),
-        [smem()] + [anywhere()] * 9,
-        project_scratch(1) + project_sums + [pltpu.SemaphoreType.DMA((3,))],
-    )(place, tok_far, *weights, *early)
+    parts = run(
+        project_far_kernel,
+        "project_far_half",
+        (
+            shaped(tok_rows, query_width, dtype=bf16),
+            shaped(tok_rows, HD, dtype=bf16),
+            shaped(tok_rows, HD, dtype=bf16),
+            shaped(2 * RANK, tok_rows, dtype=bf16),
+        ),
+        [smem()] + [anywhere()] * 10 + [vmem()] * 2,
+        project_scratch(2) + project_sums + [pltpu.SemaphoreType.DMA((3,))],
+    )(place, tok_far, tok_cross, *weights, *early, query_up, value_up)
 
     seen = peers * BLK
     total = seen + BLK
@@ -728,10 +728,8 @@
         lambda *refs: attention_kernel(peers, heads, *refs),
         "span_attention",
         (shaped(2 * RANK + tags, tok_rows), shaped(RANK, query_width + HD), shaped(peers, RANK, BLK)),
-        [smem()] * 2 + [anywhere()] * 12 + [vmem()] * 3,
-        project_scratch(1)
-        + project_sums
-        + [
+        [smem()] + [anywhere()] * 7 + [vmem()] * 3,
+        [
             pltpu.VMEM((tok_rows, query_width), bf16),
             pltpu.VMEM((tok_rows, HD), bf16),
             pltpu.VMEM((tok_rows, HD), bf16),
@@ -753,31 +751,28 @@
             pltpu.VMEM((PAIR * BLK, query_width), bf16),
             pltpu.VMEM((PAIR * BLK, query_width), bf16),
             pltpu.VMEM((HD, seen), f32),
-            pltpu.SemaphoreType.DMA((3 * peers + 5,)),
+            pltpu.SemaphoreType.DMA((3 * peers + 6,)),
         ],
         flops=20 * tok_rows * query_width * total,
         moved=4 * tok_rows * query_width,
-    )(place, boundary, tok_cross, *weights, *early, got, grad, grad_t, query_up, value_up, tag_t)
+        room=60,
+    )(boundary, *parts, got, grad, grad_t, query_up, value_up, tag_t)
 
     back = lax.all_to_all(mcot, "tm", split_axis=0, concat_axis=0, tiled=True)
     cots = [cot] + [swap(cot, d) for d in range(1, 4)]
-    own = run(
-        lambda *refs: own_kernel(peers, *refs),
-        "owned_cotangent",
-        shaped(RANK, mem_rows),
-        [smem()] + [vmem()],
+    logits, query_sum, value_part, own = run(
+        lambda *refs: first_down_kernel(peers, *refs),
+        "first_down",
+        (
+            shaped(tags, tok_rows),
+            shaped(RANK, width + ups.shape[1]),
+            shaped(RANK, width),
+            shaped(RANK, mem_rows),
+        ),
+        [smem()] + [vmem()] * 7,
         [pltpu.VMEM((blocks, RANK, BLK), f32)],
         room=8,
-    )(asked, back)
-    logits, query_sum, value_part = run(
-        first_down_kernel,
-        "first_down",
-        (shaped(tags, tok_rows), shaped(RANK, width + ups.shape[1]), shaped(RANK, width)),
-        [vmem()] * 6,
-        flops=4 * RANK * tok_rows * width,
-        moved=2 * tok_rows * width,
-        room=8,
-    )(*cots, slab_tokens, ups)
+    )(asked, back, *cots, slab_tokens, ups)
     owns = [own] + [swap(own, d) for d in range(1, 4)]
     value_sum = run(
         second_down_kernel,

time: 120 us -> 120 us (level)
  blocking collectives: 0 us -> 13.1 us
  starting transfers between devices: 36.5 us -> 31.3 us
  waiting for transfers between devices: 21.4 us -> 18.3 us
  local copies, waits for them, and re-layouts: 5.44 us -> 2.48 us
  Pallas kernels: 54.2 us -> 52.7 us
    all_to_all x0 -> x1, blocking collectives: none -> 13.1 us  [fast(): lax.all_to_all(wanted, 'tm', split_axis=0, concat_axis=0, tiled=True)]
    all_to_all x1 -> x0, starting transfers between devices: 6.58 us -> none  [fast(): lax.all_to_all(wanted, 'tm', split_axis=0, concat_axis=0, tiled=True)]
    pallas_call x1, Pallas kernels: 25.9 us -> 22.6 us  [fast(): run(lambda *refs: attention_kernel(peers, heads, *refs), 'span_attention'...]
    unnamed x16 -> x10, local copies, waits for them, and re-layouts: 4.12 us -> 1.75 us
    all_to_all x1, waiting for transfers between devices: 2.47 us -> 0.19 us  [fast(): back = lax.all_to_all(mcot, 'tm', split_axis=0, concat_axis=0, tiled=True)]
    pallas_call x3 -> x2, Pallas kernels: 7.24 us -> 9.03 us  [the longest x1 7.73 us: fast(): run(project_far_kernel, 'project_far_half', (shaped(tok_rows, query_width...]
    ppermute x20, starting transfers between devices: 17.9 us -> 19.5 us  [swap(): lax.ppermute(x, axis, [(i, i ^ bit) for i in range(lax.axis_size(axis))])]
  transfers between devices with their start and end apart: 23 -> 22, of which waited for: 8 -> 10; matrix products, arithmetic and copies ran while one was open for 2% -> 1% of each run, Pallas kernels for 23% -> 24%
where the time goes in v4:
time: 120 us
  Pallas kernels  52.7 us (44%)
  starting transfers between devices  31.3 us (26%)
  waiting for transfers between devices  18.3 us (15%)
  blocking collectives  13.1 us (11%)
  local copies, waits for them, and re-layouts  2.48 us (2%)
    pallas_call x1, Pallas kernels, fast(): run(lambda *refs: attention_kernel(peers, heads, *refs), 'span_attention'...  22.6 us
    ppermute x20, starting transfers between devices, swap(): lax.ppermute(x, axis, [(i, i ^ bit) for i in range(lax.axis_size(axis))])  19.5 us
    ppermute x20, waiting for transfers between devices, swap(): lax.ppermute(x, axis, [(i, i ^ bit) for i in range(lax.axis_size(axis))])  18.1 us
    all_to_all x1, blocking collectives, fast(): lax.all_to_all(wanted, 'tm', split_axis=0, concat_axis=0, tiled=True)  13.1 us
    pallas_call x1, Pallas kernels, fast(): run(project_early_kernel, 'project_near_half', (shaped(tok_rows, query_wi...  9.04 us
    pallas_call x1, Pallas kernels, fast(): run(project_far_kernel, 'project_far_half', (shaped(tok_rows, query_width...  7.73 us
    all_to_all x1, starting transfers between devices, fast(): back = lax.all_to_all(mcot, 'tm', split_axis=0, concat_axis=0, tiled=True)  6.02 us
    all_to_all x1, starting transfers between devices, fast(): got = lax.all_to_all(pairs, 'tm', split_axis=0, concat_axis=0, tiled=True)  5.82 us
  transfers between devices with their start and end apart: 22, of which 10 were waited for; matrix products, arithmetic and copies ran while one was open for 1% of the time, Pallas kernels for 24%

profile of v4, /device:TPU:0, one launch (start us, length us, event | category | flops | bytes accessed | tf_op | source)
XLA Modules:
  0.0 119.5 jit_solution(16425691190957540197)
XLA Ops:
  0.6 0.5 collective-permute-start
  1.1 2.6 %collective-permute-start.3 = (bf16[512,896]{1,0:T(8,128)(2,1)}, bf16[512,896]{1,0:T(8,128)(2,1)}, u32[]{:S(2)}, u32[]{:S(2)}) collective-permute-start(bf16[512,896]{1,0:T(8,128)(2,1)} %memory_ref.1), channel_id=1, source_target_pairs={{0,2},{1,3},{2,0},{3,1},{4,6},{5,7},{6,4},{7,5},{8,10},{9,11},{10,... | collective-permute-start | bytes 2752520 | tf_op jit(solution)/shard_map/ppermute | solution.py:562
  3.7 0.2 collective-permute-start.1
  3.9 0.0 collective-permute-done.refs_3_
  3.9 4.3 %memory_near_half.1 = (f32[512,256]{1,0:T(8,128)}, f32[512,16]{1,0:T(8,128)}, s32[8]{0:T(128)}) custom-call(s32[1]{0:T(128)} %bitcast.refs_0_.place_ref, s32[4,8]{1,0:T(4,128)} %refs_1_.4, bf16[512,896]{1,0:T(8,128)(2,1)} %memory_ref.1, bf16[512,896]{1,0:T(8,128)(2,1)} %collective-permute-done.refs_3_, bf16[3584,128]{1,0:T(8,128)(2,1)} %refs_1_.7, ...), custom_call_target="tpu_custom_call" | custom-call | tf_op jit(solution)/shard_map/memory_near_half/pallas_call | solution.py:669
  8.2 0.7 copy.21
  8.9 13.1 %all_to_all.21 = s32[8,1,1]{2,1,0:T(1,128)S(1)} all-to-all(s32[8,1,1]{2,1,0:T(1,128)S(1)} %copy.21), channel_id=1, replica_groups=mesh['tm'=8,'heads'=4] {'tm'}, dimensions={0} | all-to-all | bytes 64 | tf_op jit(solution)/shard_map/all_to_all | solution.py:677
  22.0 0.8 reduce.refs_1_.refs_0_
  22.8 2.2 %collective-permute-done.3.refs_0_ = bf16[512,896]{1,0:T(8,128)(2,1)} collective-permute-done((bf16[512,896]{1,0:T(8,128)(2,1)}, bf16[512,896]{1,0:T(8,128)(2,1)}, u32[]{:S(2)}, u32[]{:S(2)}) %collective-permute-start.3) | collective-permute-done | bytes 917536 | tf_op jit(solution)/shard_map/ppermute | solution.py:562
  25.0 0.0 collective-permute-start.4
  25.0 0.0 collective-permute-done.1.x1
  25.0 1.8 %collective-permute-start.2 = (bf16[512,896]{1,0:T(8,128)(2,1)}, bf16[512,896]{1,0:T(8,128)(2,1)}, u32[]{:S(2)}, u32[]{:S(2)}) collective-permute-start(bf16[512,896]{1,0:T(8,128)(2,1)} %collective-permute-done.1.x1), channel_id=1, source_target_pairs={{0,2},{1,3},{2,0},{3,1},{4,6},{5,7},{6,4},{7,5},{8,10},{9,11},{10,... | collective-permute-start | bytes 2752520 | tf_op jit(solution)/shard_map/ppermute | solution.py:562
  26.8 3.0 %memory_far_quarter.1 = (f32[512,256]{1,0:T(8,128)}, f32[512,16]{1,0:T(8,128)}) custom-call(s32[1]{0:T(128)} %bitcast.refs_0_.place_ref, bf16[512,896]{1,0:T(8,128)(2,1)} %in_order.2.x2, f32[512,256]{1,0:T(8,128)} %get-tuple-element.31.acc_hbm, f32[512,16]{1,0:T(8,128)} %get-tuple-element.32.low_hbm, bf16[3584,128]{1,0:T(8,128)(2,1)} %refs_1_.7, ...), custom_call_target="tpu_custom_call" | custom-call | tf_op jit(solution)/shard_map/memory_far_quarter/pallas_call | solution.py:682
  29.8 0.0 collective-permute-done.4.refs_2_
  29.9 3.8 %memory_pairs.1.refs_7_ = bf16[8,272,128]{2,1,0:T(8,128)(2,1)} custom-call(s32[1]{0:T(128)} %bitcast.refs_0_.place_ref, s32[8]{0:T(128)} %reduce.refs_1_.refs_0_, bf16[512,896]{1,0:T(8,128)(2,1)} %collective-permute-done.4.refs_2_, f32[512,256]{1,0:T(8,128)} %get-tuple-element.33.refs_3_, f32[512,16]{1,0:T(8,128)} %get-tuple-element.34.refs_4_, ...), custom_call_target="tpu_custom_call" | custom-call | tf_op jit(solution)/shard_map/memory_pairs/pallas_call | solution.py:689
  33.7 5.8 %all-to-all-start.1 = ((bf16[8,272,128]{2,1,0:T(8,128)(2,1)}), bf16[8,272,128]{2,1,0:T(8,128)(2,1)}, u32[]{:S(2)}, u32[]{:S(2)}) async-start(bf16[8,272,128]{2,1,0:T(8,128)(2,1)} %memory_pairs.1.refs_7_), calls=%async_computation.1 | async-start | bytes 1114112 | tf_op jit(solution)/shard_map/all_to_all | solution.py:696
  39.5 9.0 %project_near_half.1 = (f32[512,896]{1,0:T(8,128)}, f32[512,256]{1,0:T(8,128)}, f32[512,32]{1,0:T(8,128)}, bf16[512,896]{1,0:T(8,128)(2,1)}, bf16[896,512]{1,0:T(8,128)(2,1)}) custom-call(s32[1]{0:T(128)} %bitcast.refs_0_.place_ref, bf16[512,896]{1,0:T(8,128)(2,1)} %refs_6_.5, bf16[512,896]{1,0:T(8,128)(2,1)} %collective-permute-done.1.x1, ...), custom_call_target="tpu_custom_call" | custom-call | tf_op jit(solution)/shard_map/project_near_half/pallas_call | solution.py:697
  48.6 0.0 collective-permute-done.2.refs_0_
  48.6 0.1 collective-permute-start.5
  48.7 2.8 %collective-permute-done.5.x2 = bf16[512,896]{1,0:T(8,128)(2,1)} collective-permute-done((bf16[512,896]{1,0:T(8,128)(2,1)}, bf16[512,896]{1,0:T(8,128)(2,1)}, u32[]{:S(2)}, u32[]{:S(2)}) %collective-permute-start.5) | collective-permute-done | bytes 917536 | tf_op jit(solution)/shard_map/ppermute | solution.py:562
  51.5 7.7 %project_far_half.1 = (bf16[512,896]{1,0:T(8,128)(2,1)}, bf16[512,128]{1,0:T(8,128)(2,1)}, bf16[512,128]{1,0:T(8,128)(2,1)}, bf16[32,512]{1,0:T(8,128)(2,1)}) custom-call(s32[1]{0:T(128)} %bitcast.refs_0_.place_ref, bf16[512,896]{1,0:T(8,128)(2,1)} %in_order.3.x3, bf16[512,896]{1,0:T(8,128)(2,1)} %collective-permute-done.5.x2, bf16[3584,896]{1,0:T(8,128)(2,1)} %refs_0_.6, ...), custom_call_target="tpu_custom_call" | custom-call | tf_op jit(solution)/shard_map/project_far_half/pallas_call | solution.py:712
  59.2 0.0 all-to-all-done.1.refs_5_
  59.2 0.0 copy-start
  59.2 0.0 copy-start.4
  59.2 0.0 copy-start.1
  59.2 22.6 %span_attention.1 = (f32[40,512]{1,0:T(8,128)}, f32[16,1024]{1,0:T(8,128)}, f32[8,16,128]{2,1,0:T(8,128)}) custom-call(s32[4]{0:T(128)} %refs_0_.7, bf16[512,896]{1,0:T(8,128)(2,1)} %get-tuple-element.38.refs_1_, bf16[512,128]{1,0:T(8,128)(2,1)} %get-tuple-element.39.refs_2_, bf16[512,128]{1,0:T(8,128)(2,1)} %get-tuple-element.40.refs_3_, ...), custom_call_target="tpu_custom_call" | custom-call | flops 10569646080 | bytes 1835008 | tf_op jit(solution)/shard_map/span_attention/pallas_call | solution.py:727
  81.9 6.0 %all-to-all-start.2 = ((f32[8,16,128]{2,1,0:T(8,128)}), f32[8,16,128]{2,1,0:T(8,128)S(1)}, u32[]{:S(2)}, u32[]{:S(2)}) async-start(f32[8,16,128]{2,1,0:T(8,128)} %get-tuple-element.44), calls=%async_computation.2 | async-start | bytes 131072 | tf_op jit(solution)/shard_map/all_to_all | solution.py:761
  87.9 0.5 collective-permute-start.8
  88.4 1.0 collective-permute-start.7
  89.4 0.4 collective-permute-start.6
  89.8 3.1 %collective-permute-done.8.refs_5_ = f32[40,512]{1,0:T(8,128)S(1)} collective-permute-done((f32[40,512]{1,0:T(8,128)}, f32[40,512]{1,0:T(8,128)S(1)}, u32[]{:S(2)}, u32[]{:S(2)}) %collective-permute-start.8) | collective-permute-done | bytes 81952 | tf_op jit(solution)/shard_map/ppermute | solution.py:562
  92.9 1.8 %collective-permute-done.7.refs_4_ = f32[40,512]{1,0:T(8,128)S(1)} collective-permute-done((f32[40,512]{1,0:T(8,128)}, f32[40,512]{1,0:T(8,128)S(1)}, u32[]{:S(2)}, u32[]{:S(2)}) %collective-permute-start.7) | collective-permute-done | bytes 81952 | tf_op jit(solution)/shard_map/ppermute | solution.py:562
  94.6 0.0 collective-permute-done.6.refs_3_
  94.6 0.2 all-to-all-done.2.refs_1_
  94.8 0.0 copy-done
  94.8 0.0 copy-done.4
  94.8 0.9 copy-done.2
  95.7 0.8 copy-done.3
  96.6 1.3 %first_down.1 = (f32[8,512]{1,0:T(8,128)}, f32[16,1920]{1,0:T(8,128)S(1)}, f32[16,896]{1,0:T(8,128)S(1)}, f32[16,512]{1,0:T(8,128)S(1)}) custom-call(s32[8]{0:T(128)S(1)} %copy-done.4, f32[8,16,128]{2,1,0:T(8,128)S(1)} %all-to-all-done.2.refs_1_, f32[40,512]{1,0:T(8,128)S(1)} %copy-done.2, f32[40,512]{1,0:T(8,128)S(1)} %collective-permute-done.6.refs_3_, ...), custom_call_target="tpu_custom_call" | custom-call | tf_op jit(solution)/shard_map/first_down/pallas_call | solution.py:763
  97.9 1.3 %collective-permute-start.9 = (f32[16,1920]{1,0:T(8,128)S(1)}, f32[16,1920]{1,0:T(8,128)S(1)}, u32[]{:S(2)}, u32[]{:S(2)}) collective-permute-start(f32[16,1920]{1,0:T(8,128)S(1)} %get-tuple-element.48), channel_id=1, source_target_pairs={{0,4},{4,0},{8,12},{12,8},{16,20},{20,16},{24,28},{28,24},{1,5},{5... | collective-permute-start | bytes 368648 | tf_op jit(solution)/shard_map/ppermute | solution.py:562
  99.2 0.5 collective-permute-start.15
  99.6 1.0 collective-permute-start.14
  100.6 0.4 collective-permute-start.13
  101.0 1.8 %collective-permute-done.15.c3 = f32[16,512]{1,0:T(8,128)S(1)} collective-permute-done((f32[16,512]{1,0:T(8,128)S(1)}, f32[16,512]{1,0:T(8,128)S(1)}, u32[]{:S(2)}, u32[]{:S(2)}) %collective-permute-start.15) | collective-permute-done | bytes 32800 | tf_op jit(solution)/shard_map/ppermute | solution.py:562
  102.8 0.8 collective-permute-done.14.c2
  103.6 0.0 collective-permute-done.13.c1
  103.6 0.0 copy-done.1
  103.6 0.2 second_down.1
  103.9 0.8 collective-permute-start.16
  104.6 0.0 collective-permute-done.9
  104.6 3.2 %collective-permute-start.12 = (bf16[16,1920]{1,0:T(8,128)(2,1)S(1)}, bf16[16,1920]{1,0:T(8,128)(2,1)S(1)}, u32[]{:S(2)}, u32[]{:S(2)}) collective-permute-start(bf16[16,1920]{1,0:T(8,128)(2,1)S(1)} %add_convert_fusion.refs_0_), channel_id=1, source_target_pairs={{0,24},{4,28},{8,16},{12,20},{16,8},{20,12},{24,0},{28,4},{1,25},{... | collective-permute-start | bytes 184328 | tf_op jit(solution)/shard_map/ppermute | solution.py:562
  107.8 0.0 collective-permute-start.11
  107.8 1.3 %collective-permute-start.10 = (bf16[16,1920]{1,0:T(8,128)(2,1)S(1)}, bf16[16,1920]{1,0:T(8,128)(2,1)S(1)}, u32[]{:S(2)}, u32[]{:S(2)}) collective-permute-start(bf16[16,1920]{1,0:T(8,128)(2,1)S(1)} %add_convert_fusion.refs_0_), channel_id=1, source_target_pairs={{0,8},{4,12},{8,0},{12,4},{16,24},{20,28},{24,16},{28,20},{1,9},{5... | collective-permute-start | bytes 184328 | tf_op jit(solution)/shard_map/ppermute | solution.py:562
  109.1 0.0 collective-permute-done.16
  109.1 3.2 %collective-permute-start.19 = (bf16[16,896]{1,0:T(8,128)(2,1)S(1)}, bf16[16,896]{1,0:T(8,128)(2,1)S(1)}, u32[]{:S(2)}, u32[]{:S(2)}) collective-permute-start(bf16[16,896]{1,0:T(8,128)(2,1)S(1)} %add_convert_fusion.1.refs_4_), channel_id=1, source_target_pairs={{0,24},{4,28},{8,16},{12,20},{16,8},{20,12},{24,0},{28,4},{1,25},{... | collective-permute-start | bytes 86024 | tf_op jit(solution)/shard_map/ppermute | solution.py:562
  112.3 0.0 collective-permute-start.18
  112.3 2.7 %collective-permute-done.19.refs_7_ = bf16[16,896]{1,0:T(8,128)(2,1)S(1)} collective-permute-done((bf16[16,896]{1,0:T(8,128)(2,1)S(1)}, bf16[16,896]{1,0:T(8,128)(2,1)S(1)}, u32[]{:S(2)}, u32[]{:S(2)}) %collective-permute-start.19) | collective-permute-done | bytes 28704 | tf_op jit(solution)/shard_map/ppermute | solution.py:562
  114.9 0.9 collective-permute-start.17
  115.8 1.2 %collective-permute-done.18.refs_6_ = bf16[16,896]{1,0:T(8,128)(2,1)S(1)} collective-permute-done((bf16[16,896]{1,0:T(8,128)(2,1)S(1)}, bf16[16,896]{1,0:T(8,128)(2,1)S(1)}, u32[]{:S(2)}, u32[]{:S(2)}) %collective-permute-start.18) | collective-permute-done | bytes 28704 | tf_op jit(solution)/shard_map/ppermute | solution.py:562
  117.0 1.8 %collective-permute-done.17.refs_5_ = bf16[16,896]{1,0:T(8,128)(2,1)S(1)} collective-permute-done((bf16[16,896]{1,0:T(8,128)(2,1)S(1)}, bf16[16,896]{1,0:T(8,128)(2,1)S(1)}, u32[]{:S(2)}, u32[]{:S(2)}) %collective-permute-start.17) | collective-permute-done | bytes 28704 | tf_op jit(solution)/shard_map/ppermute | solution.py:562
  118.8 0.0 collective-permute-done.12.refs_3_
  118.8 0.0 collective-permute-done.11.refs_2_
  118.8 0.0 collective-permute-done.10.refs_1_
  118.8 0.7 finish_outputs.1
  (6 shorter events, 0.0 us)
Async XLA Ops:
  0.6 3.3 %collective-permute-start = (bf16[512,896]{1,0:T(8,128)(2,1)}, bf16[512,896]{1,0:T(8,128)(2,1)}, u32[]{:S(2)}, u32[]{:S(2)}) collective-permute-start(bf16[512,896]{1,0:T(8,128)(2,1)} %memory_ref.1), channel_id=1, source_target_pairs={{0,1},{1,0},{2,3},{3,2},{4,5},{5,4},{6,7},{7,6},{8,9},{9,8},{10,11... | collective-permute-start | bytes 2752520 | tf_op jit(solution)/shard_map/ppermute | solution.py:562
  1.1 23.9 %collective-permute-start.3 = (bf16[512,896]{1,0:T(8,128)(2,1)}, bf16[512,896]{1,0:T(8,128)(2,1)}, u32[]{:S(2)}, u32[]{:S(2)}) collective-permute-start(bf16[512,896]{1,0:T(8,128)(2,1)} %memory_ref.1), channel_id=1, source_target_pairs={{0,2},{1,3},{2,0},{3,1},{4,6},{5,7},{6,4},{7,5},{8,10},{9,11},{10,... | collective-permute-start | bytes 2752520 | tf_op jit(solution)/shard_map/ppermute | solution.py:562
  3.7 21.3 %collective-permute-start.1 = (bf16[512,896]{1,0:T(8,128)(2,1)}, bf16[512,896]{1,0:T(8,128)(2,1)}, u32[]{:S(2)}, u32[]{:S(2)}) collective-permute-start(bf16[512,896]{1,0:T(8,128)(2,1)} %refs_6_.5), channel_id=1, source_target_pairs={{0,1},{1,0},{2,3},{3,2},{4,5},{5,4},{6,7},{7,6},{8,9},{9,8},{10,11... | collective-permute-start | bytes 2752520 | tf_op jit(solution)/shard_map/ppermute | solution.py:562
  25.0 4.8 %collective-permute-start.4 = (bf16[512,896]{1,0:T(8,128)(2,1)}, bf16[512,896]{1,0:T(8,128)(2,1)}, u32[]{:S(2)}, u32[]{:S(2)}) collective-permute-start(bf16[512,896]{1,0:T(8,128)(2,1)} %in_order.2.x2), channel_id=1, source_target_pairs={{0,1},{1,0},{2,3},{3,2},{4,5},{5,4},{6,7},{7,6},{8,9},{9,8},{10,11... | collective-permute-start | bytes 2752520 | tf_op jit(solution)/shard_map/ppermute | solution.py:562
  25.0 23.6 %collective-permute-start.2 = (bf16[512,896]{1,0:T(8,128)(2,1)}, bf16[512,896]{1,0:T(8,128)(2,1)}, u32[]{:S(2)}, u32[]{:S(2)}) collective-permute-start(bf16[512,896]{1,0:T(8,128)(2,1)} %collective-permute-done.1.x1), channel_id=1, source_target_pairs={{0,2},{1,3},{2,0},{3,1},{4,6},{5,7},{6,4},{7,5},{8,10},{9,11},{10,... | collective-permute-start | bytes 2752520 | tf_op jit(solution)/shard_map/ppermute | solution.py:562
  33.7 25.5 %all-to-all-start.1 = ((bf16[8,272,128]{2,1,0:T(8,128)(2,1)}), bf16[8,272,128]{2,1,0:T(8,128)(2,1)}, u32[]{:S(2)}, u32[]{:S(2)}) async-start(bf16[8,272,128]{2,1,0:T(8,128)(2,1)} %memory_pairs.1.refs_7_), calls=%async_computation.1 | async-start | bytes 1114112 | tf_op jit(solution)/shard_map/all_to_all | solution.py:696
  48.6 2.9 %collective-permute-start.5 = (bf16[512,896]{1,0:T(8,128)(2,1)}, bf16[512,896]{1,0:T(8,128)(2,1)}, u32[]{:S(2)}, u32[]{:S(2)}) collective-permute-start(bf16[512,896]{1,0:T(8,128)(2,1)} %in_order.3.x3), channel_id=1, source_target_pairs={{0,1},{1,0},{2,3},{3,2},{4,5},{5,4},{6,7},{7,6},{8,9},{9,8},{10,11... | collective-permute-start | bytes 2752520 | tf_op jit(solution)/shard_map/ppermute | solution.py:562
  59.2 35.6 %copy-start = (bf16[512,896]{1,0:T(8,128)(2,1)S(1)}, bf16[512,896]{1,0:T(8,128)(2,1)}, u32[]{:S(2)}) copy-start(bf16[512,896]{1,0:T(8,128)(2,1)} %refs_6_.5) | copy-start | bytes 2752516
  59.2 35.6 %copy-start.4 = (s32[8]{0:T(128)S(1)}, s32[8]{0:T(128)}, u32[]{:S(2)}) copy-start(s32[8]{0:T(128)} %reduce.refs_1_.refs_0_) | copy-start | bytes 100
  59.2 44.4 %copy-start.1 = (bf16[512,896]{1,0:T(8,128)(2,1)S(1)}, bf16[512,896]{1,0:T(8,128)(2,1)}, u32[]{:S(2)}) copy-start(bf16[512,896]{1,0:T(8,128)(2,1)} %memory_ref.1) | copy-start | bytes 2752516
  81.9 12.9 %all-to-all-start.2 = ((f32[8,16,128]{2,1,0:T(8,128)}), f32[8,16,128]{2,1,0:T(8,128)S(1)}, u32[]{:S(2)}, u32[]{:S(2)}) async-start(f32[8,16,128]{2,1,0:T(8,128)} %get-tuple-element.44), calls=%async_computation.2 | async-start | bytes 131072 | tf_op jit(solution)/shard_map/all_to_all | solution.py:761
  87.9 4.9 %collective-permute-start.8 = (f32[40,512]{1,0:T(8,128)}, f32[40,512]{1,0:T(8,128)S(1)}, u32[]{:S(2)}, u32[]{:S(2)}) collective-permute-start(f32[40,512]{1,0:T(8,128)} %get-tuple-element.45.refs_2_), channel_id=1, source_target_pairs={{0,3},{1,2},{2,1},{3,0},{4,7},{5,6},{6,5},{7,4},{8,11},{9,10},{10,... | collective-permute-start | bytes 245768 | tf_op jit(solution)/shard_map/ppermute | solution.py:562
  88.4 6.2 %collective-permute-start.7 = (f32[40,512]{1,0:T(8,128)}, f32[40,512]{1,0:T(8,128)S(1)}, u32[]{:S(2)}, u32[]{:S(2)}) collective-permute-start(f32[40,512]{1,0:T(8,128)} %get-tuple-element.45.refs_2_), channel_id=1, source_target_pairs={{0,2},{1,3},{2,0},{3,1},{4,6},{5,7},{6,4},{7,5},{8,10},{9,11},{10,... | collective-permute-start | bytes 245768 | tf_op jit(solution)/shard_map/ppermute | solution.py:562
  89.4 5.2 %collective-permute-start.6 = (f32[40,512]{1,0:T(8,128)}, f32[40,512]{1,0:T(8,128)S(1)}, u32[]{:S(2)}, u32[]{:S(2)}) collective-permute-start(f32[40,512]{1,0:T(8,128)} %get-tuple-element.45.refs_2_), channel_id=1, source_target_pairs={{0,1},{1,0},{2,3},{3,2},{4,5},{5,4},{6,7},{7,6},{8,9},{9,8},{10,11... | collective-permute-start | bytes 245768 | tf_op jit(solution)/shard_map/ppermute | solution.py:562
  94.8 0.9 copy-start.2
  95.7 0.8 copy-start.3
  97.9 6.8 %collective-permute-start.9 = (f32[16,1920]{1,0:T(8,128)S(1)}, f32[16,1920]{1,0:T(8,128)S(1)}, u32[]{:S(2)}, u32[]{:S(2)}) collective-permute-start(f32[16,1920]{1,0:T(8,128)S(1)} %get-tuple-element.48), channel_id=1, source_target_pairs={{0,4},{4,0},{8,12},{12,8},{16,20},{20,16},{24,28},{28,24},{1,5},{5... | collective-permute-start | bytes 368648 | tf_op jit(solution)/shard_map/ppermute | solution.py:562
  99.2 3.7 %collective-permute-start.15 = (f32[16,512]{1,0:T(8,128)S(1)}, f32[16,512]{1,0:T(8,128)S(1)}, u32[]{:S(2)}, u32[]{:S(2)}) collective-permute-start(f32[16,512]{1,0:T(8,128)S(1)} %get-tuple-element.49.c0), channel_id=1, source_target_pairs={{0,3},{1,2},{2,1},{3,0},{4,7},{5,6},{6,5},{7,4},{8,11},{9,10},{10,... | collective-permute-start | bytes 98312 | tf_op jit(solution)/shard_map/ppermute | solution.py:562
  99.6 4.0 %collective-permute-start.14 = (f32[16,512]{1,0:T(8,128)S(1)}, f32[16,512]{1,0:T(8,128)S(1)}, u32[]{:S(2)}, u32[]{:S(2)}) collective-permute-start(f32[16,512]{1,0:T(8,128)S(1)} %get-tuple-element.49.c0), channel_id=1, source_target_pairs={{0,2},{1,3},{2,0},{3,1},{4,6},{5,7},{6,4},{7,5},{8,10},{9,11},{10,... | collective-permute-start | bytes 98312 | tf_op jit(solution)/shard_map/ppermute | solution.py:562
  100.6 3.0 %collective-permute-start.13 = (f32[16,512]{1,0:T(8,128)S(1)}, f32[16,512]{1,0:T(8,128)S(1)}, u32[]{:S(2)}, u32[]{:S(2)}) collective-permute-start(f32[16,512]{1,0:T(8,128)S(1)} %get-tuple-element.49.c0), channel_id=1, source_target_pairs={{0,1},{1,0},{2,3},{3,2},{4,5},{5,4},{6,7},{7,6},{8,9},{9,8},{10,11... | collective-permute-start | bytes 98312 | tf_op jit(solution)/shard_map/ppermute | solution.py:562
  103.9 5.2 %collective-permute-start.16 = (f32[16,896]{1,0:T(8,128)S(1)}, f32[16,896]{1,0:T(8,128)S(1)}, u32[]{:S(2)}, u32[]{:S(2)}) collective-permute-start(f32[16,896]{1,0:T(8,128)S(1)} %second_down.1), channel_id=1, source_target_pairs={{0,4},{4,0},{8,12},{12,8},{16,20},{20,16},{24,28},{28,24},{1,5},{5... | collective-permute-start | bytes 172040 | tf_op jit(solution)/shard_map/ppermute | solution.py:562
  104.6 14.2 %collective-permute-start.12 = (bf16[16,1920]{1,0:T(8,128)(2,1)S(1)}, bf16[16,1920]{1,0:T(8,128)(2,1)S(1)}, u32[]{:S(2)}, u32[]{:S(2)}) collective-permute-start(bf16[16,1920]{1,0:T(8,128)(2,1)S(1)} %add_convert_fusion.refs_0_), channel_id=1, source_target_pairs={{0,24},{4,28},{8,16},{12,20},{16,8},{20,12},{24,0},{28,4},{1,25},{... | collective-permute-start | bytes 184328 | tf_op jit(solution)/shard_map/ppermute | solution.py:562
  107.8 11.0 %collective-permute-start.11 = (bf16[16,1920]{1,0:T(8,128)(2,1)S(1)}, bf16[16,1920]{1,0:T(8,128)(2,1)S(1)}, u32[]{:S(2)}, u32[]{:S(2)}) collective-permute-start(bf16[16,1920]{1,0:T(8,128)(2,1)S(1)} %add_convert_fusion.refs_0_), channel_id=1, source_target_pairs={{0,16},{4,20},{8,24},{12,28},{16,0},{20,4},{24,8},{28,12},{1,17},{... | collective-permute-start | bytes 184328 | tf_op jit(solution)/shard_map/ppermute | solution.py:562
  107.8 11.0 %collective-permute-start.10 = (bf16[16,1920]{1,0:T(8,128)(2,1)S(1)}, bf16[16,1920]{1,0:T(8,128)(2,1)S(1)}, u32[]{:S(2)}, u32[]{:S(2)}) collective-permute-start(bf16[16,1920]{1,0:T(8,128)(2,1)S(1)} %add_convert_fusion.refs_0_), channel_id=1, source_target_pairs={{0,8},{4,12},{8,0},{12,4},{16,24},{20,28},{24,16},{28,20},{1,9},{5... | collective-permute-start | bytes 184328 | tf_op jit(solution)/shard_map/ppermute | solution.py:562
  109.1 5.8 %collective-permute-start.19 = (bf16[16,896]{1,0:T(8,128)(2,1)S(1)}, bf16[16,896]{1,0:T(8,128)(2,1)S(1)}, u32[]{:S(2)}, u32[]{:S(2)}) collective-permute-start(bf16[16,896]{1,0:T(8,128)(2,1)S(1)} %add_convert_fusion.1.refs_4_), channel_id=1, source_target_pairs={{0,24},{4,28},{8,16},{12,20},{16,8},{20,12},{24,0},{28,4},{1,25},{... | collective-permute-start | bytes 86024 | tf_op jit(solution)/shard_map/ppermute | solution.py:562
  112.3 4.8 %collective-permute-start.18 = (bf16[16,896]{1,0:T(8,128)(2,1)S(1)}, bf16[16,896]{1,0:T(8,128)(2,1)S(1)}, u32[]{:S(2)}, u32[]{:S(2)}) collective-permute-start(bf16[16,896]{1,0:T(8,128)(2,1)S(1)} %add_convert_fusion.1.refs_4_), channel_id=1, source_target_pairs={{0,16},{4,20},{8,24},{12,28},{16,0},{20,4},{24,8},{28,12},{1,17},{... | collective-permute-start | bytes 86024 | tf_op jit(solution)/shard_map/ppermute | solution.py:562
  114.9 3.9 %collective-permute-start.17 = (bf16[16,896]{1,0:T(8,128)(2,1)S(1)}, bf16[16,896]{1,0:T(8,128)(2,1)S(1)}, u32[]{:S(2)}, u32[]{:S(2)}) collective-permute-start(bf16[16,896]{1,0:T(8,128)(2,1)S(1)} %add_convert_fusion.1.refs_4_), channel_id=1, source_target_pairs={{0,8},{4,12},{8,0},{12,4},{16,24},{20,28},{24,16},{28,20},{1,9},{5... | collective-permute-start | bytes 86024 | tf_op jit(solution)/shard_map/ppermute | solution.py:562

commit v5 on v4

--- a/solution.py
+++ b/solution.py
@@ -279,12 +279,15 @@
     return dot_nn(x, jnp.concatenate([wk_s[n], wv_s[n]], 1)), dot_nt(x, down_s[n])
 
 
-def memory_early_kernel(blocks, place_ref, named_ref, x0, x1, *refs):
-    hbm, acc_ref, low_ref, wanted_ref, scratch, sems = refs[:3], refs[3], refs[4], refs[5], refs[6:10], refs[10]
-    groups = memory_pieces(place_ref, (0, 1), (x0, x1), hbm, scratch, sems)
+def wanted_kernel(blocks, named_ref, dep_ref, wanted_ref):
     for slot in range(TOP):
         block = named_ref[0, slot]
         wanted_ref[lax.div(block, blocks)] = lax.rem(block, blocks)
+
+
+def memory_early_kernel(place_ref, x0, x1, *refs):
+    hbm, acc_ref, low_ref, scratch, sems = refs[:3], refs[4], refs[5], refs[6:10], refs[10]
+    groups = memory_pieces(place_ref, (0, 1), (x0, x1), hbm, scratch, sems)
     for n in range(2):
         wait_all(groups[n])
         term, low_term = memory_terms(n, scratch)
@@ -296,38 +299,38 @@
             low_ref[...] += low_term
 
 
-def memory_middle_kernel(place_ref, x2, acc_hbm, low_hbm, *refs):
-    hbm, acc_ref, low_ref, scratch, sems = refs[:3], refs[3], refs[4], refs[5:9], refs[9]
-    acc_s, low_s, acc_sems = refs[10:13]
-    groups = memory_pieces(place_ref, (2,), (x2,), hbm, scratch, sems)
-    sums = start_copies([(acc_hbm, acc_s), (low_hbm, low_s)], acc_sems)
-    wait_all(groups[0])
-    term, low_term = memory_terms(0, scratch)
+def memory_kernel(first, peers, place_ref, asked_ref, x2, x3, acc_hbm, low_hbm, *refs):
+    hbm, up_ref, before, out_ref = refs[:3], refs[3], refs[4], refs[5]
+    scratch, sems, acc_s, low_s, acc_sems = refs[6:10], refs[10], refs[11], refs[12], refs[13]
+    groups = memory_pieces(place_ref, (2, 3), (x2, x3), hbm, scratch, sems)
+    at = pl.ds(first, x2.shape[0])
+    pairs = [(acc_hbm.at[at, :], acc_s), (low_hbm.at[at, :], low_s)]
+    if first:
+        pair_ref = refs[14]
+        offset = before.shape[0]
+        pairs.append((before, pair_ref.at[pl.ds(0, offset)]))
+    else:
+        pair_ref = out_ref
+        offset = 0
+    sums = start_copies(pairs, acc_sems)
+    terms = []
+    for n in range(2):
+        wait_all(groups[n])
+        terms.append(memory_terms(n, scratch))
     wait_all(sums)
-    acc_ref[...] = acc_s[...] + term
-    low_ref[...] = low_s[...] + low_term
-
-
-def memory_kernel(peers, place_ref, asked_ref, x3, acc_hbm, low_hbm, *refs):
-    hbm, up_ref, out_ref = refs[:3], refs[3], refs[4]
-    scratch, sems, acc_s, low_s, acc_sems, pair_ref = refs[5:9], refs[9], refs[10], refs[11], refs[12], refs[13]
-    groups = memory_pieces(place_ref, (3,), (x3,), hbm, scratch, sems)
-    sums = start_copies([(acc_hbm, acc_s), (low_hbm, low_s)], acc_sems)
-    wait_all(groups[0])
-    term, low_term = memory_terms(0, scratch)
-    wait_all(sums)
-    acc = acc_s[...] + term
-    low = low_s[...] + low_term
+    acc = acc_s[...] + terms[0][0] + terms[1][0]
+    low = low_s[...] + terms[0][1] + terms[1][1]
     values = (acc[:, HD:] + dot_nn(low.astype(jnp.bfloat16), up_ref[...])).astype(jnp.bfloat16)
     keys = acc[:, :HD].astype(jnp.bfloat16)
     low_t = jnp.transpose(low).astype(jnp.bfloat16)
     for b in range(acc.shape[0] // BLK):
         at = slice(b * BLK, (b + 1) * BLK)
-        pair_ref[b, 0:BLK, :] = keys[at]
-        pair_ref[b, BLK : 2 * BLK, :] = values[at]
-        pair_ref[b, 2 * BLK : PACK, :] = low_t[:, at]
-    for r in range(peers):
-        out_ref[r] = pair_ref[asked_ref[r]]
+        pair_ref[offset + b, 0:BLK, :] = keys[at]
+        pair_ref[offset + b, BLK : 2 * BLK, :] = values[at]
+        pair_ref[offset + b, 2 * BLK : PACK, :] = low_t[:, at]
+    if first:
+        for r in range(peers):
+            out_ref[r] = pair_ref[asked_ref[r]]
 
 
 WQ_CUTS = 4
@@ -628,9 +631,9 @@
     f32 = jnp.float32
     bf16 = jnp.bfloat16
 
-    def memory_scratch(count):
+    def memory_scratch(count, rows):
         return [
-            pltpu.VMEM((count, mem_rows, width), bf16),
+            pltpu.VMEM((count, rows, width), bf16),
             pltpu.VMEM((count, width, HD), bf16),
             pltpu.VMEM((count, width, HD), bf16),
             pltpu.VMEM((count, RANK, width), bf16),
@@ -648,11 +651,6 @@
             pltpu.SemaphoreType.DMA((count * (WQ_CUTS + 5),)),
         ]
 
-    memory_sums = [
-        pltpu.VMEM((mem_rows, 2 * HD), f32),
-        pltpu.VMEM((mem_rows, RANK), f32),
-        pltpu.SemaphoreType.DMA((2,)),
-    ]
     project_sums = [
         pltpu.VMEM((tok_rows, query_width), f32),
         pltpu.VMEM((tok_rows, 2 * HD), f32),
@@ -662,37 +660,52 @@
     place = lax.axis_index("heads").astype(jnp.int32).reshape(1)
     tag_t = tag_weight.T
     tags = tag_t.shape[0]
-    mem_far = swap(memory, 2)
+    cut_rows = mem_rows // 2
+    mem_far = [swap(m, 2) for m in jnp.split(memory, 2, 0)]
     mem_near = swap(memory, 1)
     tok_near = swap(slab_tokens, 1)
     tok_far = swap(tok_near, 2)
-    mem_acc, mem_low, wanted = run(
-        lambda *refs: memory_early_kernel(blocks, *refs),
-        "memory_near_half",
-        (shaped(mem_rows, 2 * HD), shaped(mem_rows, RANK), shaped(peers, dtype=jnp.int32)),
-        [smem()] * 2 + [anywhere()] * 5,
-        memory_scratch(2),
-        out_specs=(vmem(), vmem(), smem()),
-    )(place, retrieval, memory, mem_near, key_weight, value_weight, value_down)
+    wanted = run(
+        lambda *refs: wanted_kernel(blocks, *refs),
+        "wanted_blocks",
+        shaped(peers, dtype=jnp.int32),
+        [smem(), anywhere()],
+        out_specs=smem(),
+    )(retrieval, mem_near)
     asked = lax.all_to_all(wanted, "tm", split_axis=0, concat_axis=0, tiled=True)
     weights = (query_weight, key_weight, value_weight, query_down, value_down)
-    mem_far = after(mem_far, asked)
-    mem_cross = swap(mem_far, 1)
     mem_weights = (key_weight, value_weight, value_down)
     mem_acc, mem_low = run(
-        memory_middle_kernel,
-        "memory_far_quarter",
+        memory_early_kernel,
+        "memory_near_half",
         (shaped(mem_rows, 2 * HD), shaped(mem_rows, RANK)),
-        [smem()] + [anywhere()] * 6,
-        memory_scratch(1) + memory_sums,
-    )(place, mem_far, mem_acc, mem_low, *mem_weights)
-    pairs = run(
-        lambda *refs: memory_kernel(peers, *refs),
-        "memory_pairs",
-        shaped(peers, PACK, HD, dtype=bf16),
-        [smem()] * 2 + [anywhere()] * 6 + [vmem()],
-        memory_scratch(1) + memory_sums + [pltpu.VMEM((blocks, PACK, HD), bf16)],
-    )(place, asked, mem_cross, mem_acc, mem_low, *mem_weights, value_up)
+        [smem()] + [anywhere()] * 5 + [smem()],
+        memory_scratch(2, mem_rows),
+    )(place, memory, mem_near, *mem_weights, wanted)
+    before = mem_low
+    for t in range(2):
+        if t == 0:
+            far = after(mem_far[0], asked, mem_low)
+            out_shape = shaped(blocks // 2, PACK, HD, dtype=bf16)
+            extra = []
+        else:
+            far = mem_far[1]
+            out_shape = shaped(peers, PACK, HD, dtype=bf16)
+            extra = [pltpu.VMEM((blocks, PACK, HD), bf16)]
+        before = run(
+            lambda *refs, t=t: memory_kernel(t * cut_rows, peers, *refs),
+            "memory_pairs",
+            out_shape,
+            [smem()] * 2 + [anywhere()] * 7 + [vmem(), anywhere()],
+            memory_scratch(2, cut_rows)
+            + [
+                pltpu.VMEM((cut_rows, 2 * HD), f32),
+                pltpu.VMEM((cut_rows, RANK), f32),
+                pltpu.SemaphoreType.DMA((3,)),
+            ]
+            + extra,
+        )(place, asked, far, swap(far, 1), mem_acc, mem_low, *mem_weights, value_up, before)
+    pairs = before
     got = lax.all_to_all(pairs, "tm", split_axis=0, concat_axis=0, tiled=True)
     *early, grad, grad_t = run(
         project_early_kernel,

time: 120 us -> 124 us (1.033)
  blocking collectives: 13.1 us -> 0 us
  starting transfers between devices: 31.3 us -> 38.9 us
  local copies, waits for them, and re-layouts: 2.48 us -> 6.84 us
  waiting for transfers between devices: 18.3 us -> 20.4 us
  Pallas kernels: 52.7 us -> 54.6 us
    all_to_all x1 -> x0, blocking collectives: 13.1 us -> none  [fast(): lax.all_to_all(wanted, 'tm', split_axis=0, concat_axis=0, tiled=True)]
    all_to_all x0 -> x1, starting transfers between devices: none -> 5.81 us  [fast(): lax.all_to_all(wanted, 'tm', split_axis=0, concat_axis=0, tiled=True)]
    all_to_all x0 -> x1, waiting for transfers between devices: none -> 2.24 us  [fast(): lax.all_to_all(wanted, 'tm', split_axis=0, concat_axis=0, tiled=True)]
    split x0 -> x1, local copies, waits for them, and re-layouts: none -> 2.21 us  [fast(): mem_far = [swap(m, 2) for m in jnp.split(memory, 2, 0)]]
    pallas_call x3 -> x4, Pallas kernels: 11.1 us -> 13 us  [the longest x2 7.51 us: fast(): run(lambda *refs, t=t: memory_kernel(t * cut_rows, peers, *refs), 'memory...]
    unnamed x10 -> x14, local copies, waits for them, and re-layouts: 1.75 us -> 3.31 us
    ppermute x20 -> x22, starting transfers between devices: 19.5 us -> 20.8 us  [swap(): lax.ppermute(x, axis, [(i, i ^ bit) for i in range(lax.axis_size(axis))])]
    ppermute x20 -> x22, waiting for transfers between devices: 18.1 us -> 17.9 us  [swap(): lax.ppermute(x, axis, [(i, i ^ bit) for i in range(lax.axis_size(axis))])]
  transfers between devices with their start and end apart: 22 -> 25, of which waited for: 10 -> 11; matrix products, arithmetic and copies ran while one was open for 1% -> 4% of each run, Pallas kernels for 24% -> 24%
where the time goes in v5:
time: 124 us; the launch traced here: 123 us
  Pallas kernels  54.6 us (44%)
  starting transfers between devices  38.9 us (31%)
  waiting for transfers between devices  20.4 us (16%)
  local copies, waits for them, and re-layouts  6.84 us (6%)
  other arithmetic  1.46 us (1%)
    pallas_call x1, Pallas kernels, fast(): run(lambda *refs: attention_kernel(peers, heads, *refs), 'span_attention'...  22.7 us
    ppermute x22, starting transfers between devices, swap(): lax.ppermute(x, axis, [(i, i ^ bit) for i in range(lax.axis_size(axis))])  20.8 us
    ppermute x22, waiting for transfers between devices, swap(): lax.ppermute(x, axis, [(i, i ^ bit) for i in range(lax.axis_size(axis))])  17.9 us
    pallas_call x1, Pallas kernels, fast(): run(project_early_kernel, 'project_near_half', (shaped(tok_rows, query_wi...  8.95 us
    pallas_call x1, Pallas kernels, fast(): run(project_far_kernel, 'project_far_half', (shaped(tok_rows, query_width...  7.73 us
    pallas_call x2, Pallas kernels, fast(): run(lambda *refs, t=t: memory_kernel(t * cut_rows, peers, *refs), 'memory...  7.51 us
    all_to_all x1, starting transfers between devices, fast(): got = lax.all_to_all(pairs, 'tm', split_axis=0, concat_axis=0, tiled=True)  6.36 us
    all_to_all x1, starting transfers between devices, fast(): back = lax.all_to_all(mcot, 'tm', split_axis=0, concat_axis=0, tiled=True)  6.01 us
  transfers between devices with their start and end apart: 25, of which 11 were waited for; matrix products, arithmetic and copies ran while one was open for 4% of the time, Pallas kernels for 24%

profile of v5, /device:TPU:0, one launch (start us, length us, event | category | flops | bytes accessed | tf_op | source)
XLA Modules:
  0.0 123.0 jit_solution(2195123138252640593)
XLA Ops:
  0.6 0.5 collective-permute-start.1
  1.1 0.1 collective-permute-start
  1.2 2.2 %fusion = (bf16[256,896]{1,0:T(8,128)(2,1)}, bf16[256,896]{1,0:T(8,128)(2,1)}) fusion(bf16[512,896]{1,0:T(8,128)(2,1)} %memory_ref.1), kind=kLoop, calls=%fused_computation.2 | loop fusion | bytes 1835008 | tf_op jit(solution)/shard_map/split | solution.py:664
  3.4 2.9 %collective-permute-start.5 = (bf16[256,896]{1,0:T(8,128)(2,1)}, bf16[256,896]{1,0:T(8,128)(2,1)S(1)}, u32[]{:S(2)}, u32[]{:S(2)}) collective-permute-start(bf16[256,896]{1,0:T(8,128)(2,1)} %get-tuple-element.49), channel_id=1, source_target_pairs={{0,2},{1,3},{2,0},{3,1},{4,6},{5,7},{6,4},{7,5},{8,10},{9,11},{10,... | collective-permute-start | bytes 1376264 | tf_op jit(solution)/shard_map/ppermute | solution.py:565
  6.4 0.0 collective-permute-start.3
  6.4 0.0 collective-permute-done.1.x1
  6.4 2.0 %collective-permute-start.2 = (bf16[512,896]{1,0:T(8,128)(2,1)}, bf16[512,896]{1,0:T(8,128)(2,1)}, u32[]{:S(2)}, u32[]{:S(2)}) collective-permute-start(bf16[512,896]{1,0:T(8,128)(2,1)} %collective-permute-done.1.x1), channel_id=1, source_target_pairs={{0,2},{1,3},{2,0},{3,1},{4,6},{5,7},{6,4},{7,5},{8,10},{9,11},{10,... | collective-permute-start | bytes 2752520 | tf_op jit(solution)/shard_map/ppermute | solution.py:565
  8.4 0.0 collective-permute-done.refs_1_.x1
  8.4 1.2 %wanted_blocks.1.refs_3_ = s32[8]{0:T(128)} custom-call(s32[4,8]{1,0:T(4,128)} %refs_0_.5, bf16[512,896]{1,0:T(8,128)(2,1)} %collective-permute-done.refs_1_.x1), custom_call_target="tpu_custom_call" | custom-call | tf_op jit(solution)/shard_map/wanted_blocks/pallas_call | solution.py:668
  9.7 1.3 %copy.21 = s32[8,1,1]{2,1,0:T(1,128)} copy(s32[8,1,1]{0,2,1:T(1,128)} %bitcast.8) | data formatting | bytes 64 | tf_op jit(solution)/shard_map/all_to_all | solution.py:675
  11.0 5.8 %all-to-all-start = ((s32[8,1,1]{2,1,0:T(1,128)}), s32[8,1,1]{2,1,0:T(1,128)}, u32[]{:S(2)}, u32[]{:S(2)}) async-start(s32[8,1,1]{2,1,0:T(1,128)} %copy.21), calls=%async_computation | async-start | bytes 8192 | tf_op jit(solution)/shard_map/all_to_all | solution.py:675
  16.8 4.2 %memory_near_half.1 = (f32[512,256]{1,0:T(8,128)}, f32[512,16]{1,0:T(8,128)}) custom-call(s32[1]{0:T(128)} %bitcast.1.place_ref.refs_0_, bf16[512,896]{1,0:T(8,128)(2,1)} %memory_ref.1, bf16[512,896]{1,0:T(8,128)(2,1)} %collective-permute-done.refs_1_.x1, bf16[3584,128]{1,0:T(8,128)(2,1)} %refs_1_.5, bf16[3584,128]{1,0:T(8,128)(2,1)} %refs_2_.5, ...), custom_call_target="tpu_custom_call" | custom-call | tf_op jit(solution)/shard_map/memory_near_half/pallas_call | solution.py:678
  21.0 2.2 %all-to-all-done = s32[8,1,1]{2,1,0:T(1,128)} async-done(((s32[8,1,1]{2,1,0:T(1,128)}), s32[8,1,1]{2,1,0:T(1,128)}, u32[]{:S(2)}, u32[]{:S(2)}) %all-to-all-start) | async-done | bytes 64 | tf_op jit(solution)/shard_map/all_to_all | solution.py:675
  23.3 1.4 %reduce.refs_1_.refs_0_ = s32[8]{0:T(128)} reduce(s32[8,1,1]{2,1,0:T(1,128)} %all-to-all-done, s32[]{:T(128)} %constant.6), dimensions={1,2}, to_apply=%all_to_all.14.reduce_sub_computation | reduce | bytes 68 | tf_op jit(solution)/shard_map/all_to_all | solution.py:675
  24.7 0.0 collective-permute-done.5.refs_0_
  24.7 0.8 copy-done.5
  25.5 0.0 collective-permute-start.6
  25.5 2.3 %collective-permute-done.3.refs_2_ = bf16[256,896]{1,0:T(8,128)(2,1)} collective-permute-done((bf16[256,896]{1,0:T(8,128)(2,1)}, bf16[256,896]{1,0:T(8,128)(2,1)}, u32[]{:S(2)}, u32[]{:S(2)}) %collective-permute-start.3) | collective-permute-done | bytes 458784 | tf_op jit(solution)/shard_map/ppermute | solution.py:565
  27.9 0.8 copy-done.6
  28.6 3.7 %memory_pairs.2.refs_10_ = bf16[2,272,128]{2,1,0:T(8,128)(2,1)} custom-call(s32[1]{0:T(128)} %bitcast.1.place_ref.refs_0_, s32[8]{0:T(128)} %reduce.refs_1_.refs_0_, bf16[256,896]{1,0:T(8,128)(2,1)} %in_order.2.refs_2_, bf16[256,896]{1,0:T(8,128)(2,1)} %copy-done.6, f32[512,256]{1,0:T(8,128)} %get-tuple-element.27.refs_4_, ...), custom_call_target="tpu_custom_call" | custom-call | tf_op jit(solution)/shard_map/memory_pairs/pallas_call | solution.py:695
  32.3 0.0 collective-permute-done.4.refs_3_
  32.3 3.9 %memory_pairs.3.refs_7_ = bf16[8,272,128]{2,1,0:T(8,128)(2,1)} custom-call(s32[1]{0:T(128)} %bitcast.1.place_ref.refs_0_, s32[8]{0:T(128)} %reduce.refs_1_.refs_0_, bf16[256,896]{1,0:T(8,128)(2,1)} %collective-permute-done.3.refs_2_, bf16[256,896]{1,0:T(8,128)(2,1)} %collective-permute-done.4.refs_3_, f32[512,256]{1,0:T(8,128)} %get-tuple-element.27.refs_4_, ...), custom_call_target="tpu_custom_call" | custom-call | tf_op jit(solution)/shard_map/memory_pairs/pallas_call | solution.py:695
  36.2 6.4 %all-to-all-start.1 = ((bf16[8,272,128]{2,1,0:T(8,128)(2,1)}), bf16[8,272,128]{2,1,0:T(8,128)(2,1)}, u32[]{:S(2)}, u32[]{:S(2)}) async-start(bf16[8,272,128]{2,1,0:T(8,128)(2,1)} %memory_pairs.3.refs_7_), calls=%async_computation.1 | async-start | bytes 1114112 | tf_op jit(solution)/shard_map/all_to_all | solution.py:709
  42.5 9.0 %project_near_half.1 = (f32[512,896]{1,0:T(8,128)}, f32[512,256]{1,0:T(8,128)}, f32[512,32]{1,0:T(8,128)}, bf16[512,896]{1,0:T(8,128)(2,1)}, bf16[896,512]{1,0:T(8,128)(2,1)}) custom-call(s32[1]{0:T(128)} %bitcast.1.place_ref.refs_0_, bf16[512,896]{1,0:T(8,128)(2,1)} %refs_6_.5, bf16[512,896]{1,0:T(8,128)(2,1)} %collective-permute-done.1.x1, ...), custom_call_target="tpu_custom_call" | custom-call | tf_op jit(solution)/shard_map/project_near_half/pallas_call | solution.py:710
  51.5 0.3 collective-permute-start.7
  51.8 2.6 %collective-permute-done.7.x2 = bf16[512,896]{1,0:T(8,128)(2,1)} collective-permute-done((bf16[512,896]{1,0:T(8,128)(2,1)}, bf16[512,896]{1,0:T(8,128)(2,1)}, u32[]{:S(2)}, u32[]{:S(2)}) %collective-permute-start.7) | collective-permute-done | bytes 917536 | tf_op jit(solution)/shard_map/ppermute | solution.py:565
  54.4 7.7 %project_far_half.1 = (bf16[512,896]{1,0:T(8,128)(2,1)}, bf16[512,128]{1,0:T(8,128)(2,1)}, bf16[512,128]{1,0:T(8,128)(2,1)}, bf16[32,512]{1,0:T(8,128)(2,1)}) custom-call(s32[1]{0:T(128)} %bitcast.1.place_ref.refs_0_, bf16[512,896]{1,0:T(8,128)(2,1)} %in_order.3.x3, bf16[512,896]{1,0:T(8,128)(2,1)} %collective-permute-done.7.x2, bf16[3584,896]{1,0:T(8,128)(2,1)} %refs_0_.8, ...), custom_call_target="tpu_custom_call" | custom-call | tf_op jit(solution)/shard_map/project_far_half/pallas_call | solution.py:725
  62.1 0.0 all-to-all-done.1.refs_5_
  62.2 0.0 copy-start.1
  62.2 0.0 copy-start.4
  62.2 0.0 copy-start
  62.2 22.7 %span_attention.1 = (f32[40,512]{1,0:T(8,128)}, f32[16,1024]{1,0:T(8,128)}, f32[8,16,128]{2,1,0:T(8,128)}) custom-call(s32[4]{0:T(128)} %refs_0_.9, bf16[512,896]{1,0:T(8,128)(2,1)} %get-tuple-element.32.refs_1_, bf16[512,128]{1,0:T(8,128)(2,1)} %get-tuple-element.33.refs_2_, bf16[512,128]{1,0:T(8,128)(2,1)} %get-tuple-element.34.refs_3_, ...), custom_call_target="tpu_custom_call" | custom-call | flops 10569646080 | bytes 1835008 | tf_op jit(solution)/shard_map/span_attention/pallas_call | solution.py:740
  84.9 6.0 %all-to-all-start.2 = ((f32[8,16,128]{2,1,0:T(8,128)}), f32[8,16,128]{2,1,0:T(8,128)S(1)}, u32[]{:S(2)}, u32[]{:S(2)}) async-start(f32[8,16,128]{2,1,0:T(8,128)} %get-tuple-element.38), calls=%async_computation.2 | async-start | bytes 131072 | tf_op jit(solution)/shard_map/all_to_all | solution.py:774
  90.9 1.0 collective-permute-start.10
  91.9 0.6 collective-permute-start.9
  92.5 0.3 collective-permute-start.8
  92.8 3.0 %collective-permute-done.10.refs_5_ = f32[40,512]{1,0:T(8,128)S(1)} collective-permute-done((f32[40,512]{1,0:T(8,128)}, f32[40,512]{1,0:T(8,128)S(1)}, u32[]{:S(2)}, u32[]{:S(2)}) %collective-permute-start.10) | collective-permute-done | bytes 81952 | tf_op jit(solution)/shard_map/ppermute | solution.py:565
  95.8 1.8 %collective-permute-done.9.refs_4_ = f32[40,512]{1,0:T(8,128)S(1)} collective-permute-done((f32[40,512]{1,0:T(8,128)}, f32[40,512]{1,0:T(8,128)S(1)}, u32[]{:S(2)}, u32[]{:S(2)}) %collective-permute-start.9) | collective-permute-done | bytes 81952 | tf_op jit(solution)/shard_map/ppermute | solution.py:565
  97.6 0.0 collective-permute-done.8.refs_3_
  97.6 0.2 all-to-all-done.2.refs_1_
  97.8 0.9 copy-done.2
  98.7 0.8 copy-done.3
  99.5 1.3 %first_down.1 = (f32[8,512]{1,0:T(8,128)}, f32[16,1920]{1,0:T(8,128)S(1)}, f32[16,896]{1,0:T(8,128)S(1)}, f32[16,512]{1,0:T(8,128)S(1)}) custom-call(s32[8]{0:T(128)S(1)} %copy-done.4, f32[8,16,128]{2,1,0:T(8,128)S(1)} %all-to-all-done.2.refs_1_, f32[40,512]{1,0:T(8,128)S(1)} %copy-done.2, f32[40,512]{1,0:T(8,128)S(1)} %collective-permute-done.8.refs_3_, ...), custom_call_target="tpu_custom_call" | custom-call | tf_op jit(solution)/shard_map/first_down/pallas_call | solution.py:776
  100.8 1.8 %collective-permute-start.11 = (f32[16,1920]{1,0:T(8,128)S(1)}, f32[16,1920]{1,0:T(8,128)S(1)}, u32[]{:S(2)}, u32[]{:S(2)}) collective-permute-start(f32[16,1920]{1,0:T(8,128)S(1)} %get-tuple-element.42), channel_id=1, source_target_pairs={{0,4},{4,0},{8,12},{12,8},{16,20},{20,16},{24,28},{28,24},{1,5},{5... | collective-permute-start | bytes 368648 | tf_op jit(solution)/shard_map/ppermute | solution.py:565
  102.7 0.5 collective-permute-start.17
  103.2 0.9 collective-permute-start.16
  104.1 0.5 collective-permute-start.15
  104.5 1.8 %collective-permute-done.17.c3 = f32[16,512]{1,0:T(8,128)S(1)} collective-permute-done((f32[16,512]{1,0:T(8,128)S(1)}, f32[16,512]{1,0:T(8,128)S(1)}, u32[]{:S(2)}, u32[]{:S(2)}) %collective-permute-start.17) | collective-permute-done | bytes 32800 | tf_op jit(solution)/shard_map/ppermute | solution.py:565
  106.3 0.8 collective-permute-done.16.c2
  107.1 0.0 collective-permute-done.15.c1
  107.1 0.2 second_down.1
  107.4 0.7 collective-permute-start.18
  108.1 3.2 %collective-permute-start.14 = (bf16[16,1920]{1,0:T(8,128)(2,1)S(1)}, bf16[16,1920]{1,0:T(8,128)(2,1)S(1)}, u32[]{:S(2)}, u32[]{:S(2)}) collective-permute-start(bf16[16,1920]{1,0:T(8,128)(2,1)S(1)} %add_convert_fusion.refs_0_), channel_id=1, source_target_pairs={{0,24},{4,28},{8,16},{12,20},{16,8},{20,12},{24,0},{28,4},{1,25},{... | collective-permute-start | bytes 184328 | tf_op jit(solution)/shard_map/ppermute | solution.py:565
  111.3 1.2 collective-permute-start.12
  112.6 0.0 collective-permute-done.18
  112.6 3.2 %collective-permute-start.21 = (bf16[16,896]{1,0:T(8,128)(2,1)S(1)}, bf16[16,896]{1,0:T(8,128)(2,1)S(1)}, u32[]{:S(2)}, u32[]{:S(2)}) collective-permute-start(bf16[16,896]{1,0:T(8,128)(2,1)S(1)} %add_convert_fusion.1.refs_4_), channel_id=1, source_target_pairs={{0,24},{4,28},{8,16},{12,20},{16,8},{20,12},{24,0},{28,4},{1,25},{... | collective-permute-start | bytes 86024 | tf_op jit(solution)/shard_map/ppermute | solution.py:565
  115.8 2.6 %collective-permute-done.21.refs_7_ = bf16[16,896]{1,0:T(8,128)(2,1)S(1)} collective-permute-done((bf16[16,896]{1,0:T(8,128)(2,1)S(1)}, bf16[16,896]{1,0:T(8,128)(2,1)S(1)}, u32[]{:S(2)}, u32[]{:S(2)}) %collective-permute-start.21) | collective-permute-done | bytes 28704 | tf_op jit(solution)/shard_map/ppermute | solution.py:565
  118.4 0.9 collective-permute-start.19
  119.3 1.2 %collective-permute-done.20.refs_6_ = bf16[16,896]{1,0:T(8,128)(2,1)S(1)} collective-permute-done((bf16[16,896]{1,0:T(8,128)(2,1)S(1)}, bf16[16,896]{1,0:T(8,128)(2,1)S(1)}, u32[]{:S(2)}, u32[]{:S(2)}) %collective-permute-start.20) | collective-permute-done | bytes 28704 | tf_op jit(solution)/shard_map/ppermute | solution.py:565
  120.6 1.7 %collective-permute-done.19.refs_5_ = bf16[16,896]{1,0:T(8,128)(2,1)S(1)} collective-permute-done((bf16[16,896]{1,0:T(8,128)(2,1)S(1)}, bf16[16,896]{1,0:T(8,128)(2,1)S(1)}, u32[]{:S(2)}, u32[]{:S(2)}) %collective-permute-start.19) | collective-permute-done | bytes 28704 | tf_op jit(solution)/shard_map/ppermute | solution.py:565
  122.3 0.0 collective-permute-done.14.refs_3_
  122.3 0.0 collective-permute-done.13.refs_2_
  122.3 0.0 collective-permute-done.12.refs_1_
  122.3 0.7 finish_outputs.1
  (17 shorter events, 0.1 us)
Async XLA Ops:
  0.6 5.8 %collective-permute-start.1 = (bf16[512,896]{1,0:T(8,128)(2,1)}, bf16[512,896]{1,0:T(8,128)(2,1)}, u32[]{:S(2)}, u32[]{:S(2)}) collective-permute-start(bf16[512,896]{1,0:T(8,128)(2,1)} %refs_6_.5), channel_id=1, source_target_pairs={{0,1},{1,0},{2,3},{3,2},{4,5},{5,4},{6,7},{7,6},{8,9},{9,8},{10,11... | collective-permute-start | bytes 2752520 | tf_op jit(solution)/shard_map/ppermute | solution.py:565
  1.1 7.3 %collective-permute-start = (bf16[512,896]{1,0:T(8,128)(2,1)}, bf16[512,896]{1,0:T(8,128)(2,1)}, u32[]{:S(2)}, u32[]{:S(2)}) collective-permute-start(bf16[512,896]{1,0:T(8,128)(2,1)} %memory_ref.1), channel_id=1, source_target_pairs={{0,1},{1,0},{2,3},{3,2},{4,5},{5,4},{6,7},{7,6},{8,9},{9,8},{10,11... | collective-permute-start | bytes 2752520 | tf_op jit(solution)/shard_map/ppermute | solution.py:565
  3.4 21.3 %collective-permute-start.5 = (bf16[256,896]{1,0:T(8,128)(2,1)}, bf16[256,896]{1,0:T(8,128)(2,1)S(1)}, u32[]{:S(2)}, u32[]{:S(2)}) collective-permute-start(bf16[256,896]{1,0:T(8,128)(2,1)} %get-tuple-element.49), channel_id=1, source_target_pairs={{0,2},{1,3},{2,0},{3,1},{4,6},{5,7},{6,4},{7,5},{8,10},{9,11},{10,... | collective-permute-start | bytes 1376264 | tf_op jit(solution)/shard_map/ppermute | solution.py:565
  6.4 21.5 %collective-permute-start.3 = (bf16[256,896]{1,0:T(8,128)(2,1)}, bf16[256,896]{1,0:T(8,128)(2,1)}, u32[]{:S(2)}, u32[]{:S(2)}) collective-permute-start(bf16[256,896]{1,0:T(8,128)(2,1)} %get-tuple-element.50), channel_id=1, source_target_pairs={{0,2},{1,3},{2,0},{3,1},{4,6},{5,7},{6,4},{7,5},{8,10},{9,11},{10,... | collective-permute-start | bytes 1376264 | tf_op jit(solution)/shard_map/ppermute | solution.py:565
  6.4 45.1 %collective-permute-start.2 = (bf16[512,896]{1,0:T(8,128)(2,1)}, bf16[512,896]{1,0:T(8,128)(2,1)}, u32[]{:S(2)}, u32[]{:S(2)}) collective-permute-start(bf16[512,896]{1,0:T(8,128)(2,1)} %collective-permute-done.1.x1), channel_id=1, source_target_pairs={{0,2},{1,3},{2,0},{3,1},{4,6},{5,7},{6,4},{7,5},{8,10},{9,11},{10,... | collective-permute-start | bytes 2752520 | tf_op jit(solution)/shard_map/ppermute | solution.py:565
  11.0 12.3 %all-to-all-start = ((s32[8,1,1]{2,1,0:T(1,128)}), s32[8,1,1]{2,1,0:T(1,128)}, u32[]{:S(2)}, u32[]{:S(2)}) async-start(s32[8,1,1]{2,1,0:T(1,128)} %copy.21), calls=%async_computation | async-start | bytes 8192 | tf_op jit(solution)/shard_map/all_to_all | solution.py:675
  24.7 0.8 copy-start.5
  25.5 2.4 %collective-permute-start.6 = (bf16[256,896]{1,0:T(8,128)(2,1)}, bf16[256,896]{1,0:T(8,128)(2,1)S(1)}, u32[]{:S(2)}, u32[]{:S(2)}) collective-permute-start(bf16[256,896]{1,0:T(8,128)(2,1)} %in_order.2.refs_2_), channel_id=1, source_target_pairs={{0,1},{1,0},{2,3},{3,2},{4,5},{5,4},{6,7},{7,6},{8,9},{9,8},{10,11... | collective-permute-start | bytes 1376264 | tf_op jit(solution)/shard_map/ppermute | solution.py:565
  27.8 4.5 %collective-permute-start.4 = (bf16[256,896]{1,0:T(8,128)(2,1)}, bf16[256,896]{1,0:T(8,128)(2,1)}, u32[]{:S(2)}, u32[]{:S(2)}) collective-permute-start(bf16[256,896]{1,0:T(8,128)(2,1)} %collective-permute-done.3.refs_2_), channel_id=1, source_target_pairs={{0,1},{1,0},{2,3},{3,2},{4,5},{5,4},{6,7},{7,6},{8,9},{9,8},{10,11... | collective-permute-start | bytes 1376264 | tf_op jit(solution)/shard_map/ppermute | solution.py:565
  27.8 0.8 copy-start.6
  36.2 26.0 %all-to-all-start.1 = ((bf16[8,272,128]{2,1,0:T(8,128)(2,1)}), bf16[8,272,128]{2,1,0:T(8,128)(2,1)}, u32[]{:S(2)}, u32[]{:S(2)}) async-start(bf16[8,272,128]{2,1,0:T(8,128)(2,1)} %memory_pairs.3.refs_7_), calls=%async_computation.1 | async-start | bytes 1114112 | tf_op jit(solution)/shard_map/all_to_all | solution.py:709
  51.5 2.9 %collective-permute-start.7 = (bf16[512,896]{1,0:T(8,128)(2,1)}, bf16[512,896]{1,0:T(8,128)(2,1)}, u32[]{:S(2)}, u32[]{:S(2)}) collective-permute-start(bf16[512,896]{1,0:T(8,128)(2,1)} %in_order.3.x3), channel_id=1, source_target_pairs={{0,1},{1,0},{2,3},{3,2},{4,5},{5,4},{6,7},{7,6},{8,9},{9,8},{10,11... | collective-permute-start | bytes 2752520 | tf_op jit(solution)/shard_map/ppermute | solution.py:565
  62.2 35.6 %copy-start.1 = (bf16[512,896]{1,0:T(8,128)(2,1)S(1)}, bf16[512,896]{1,0:T(8,128)(2,1)}, u32[]{:S(2)}) copy-start(bf16[512,896]{1,0:T(8,128)(2,1)} %refs_6_.5) | copy-start | bytes 2752516
  62.2 35.6 %copy-start.4 = (s32[8]{0:T(128)S(1)}, s32[8]{0:T(128)}, u32[]{:S(2)}) copy-start(s32[8]{0:T(128)} %reduce.refs_1_.refs_0_) | copy-start | bytes 100
  62.2 44.9 %copy-start = (bf16[512,896]{1,0:T(8,128)(2,1)S(1)}, bf16[512,896]{1,0:T(8,128)(2,1)}, u32[]{:S(2)}) copy-start(bf16[512,896]{1,0:T(8,128)(2,1)} %memory_ref.1) | copy-start | bytes 2752516
  84.9 12.9 %all-to-all-start.2 = ((f32[8,16,128]{2,1,0:T(8,128)}), f32[8,16,128]{2,1,0:T(8,128)S(1)}, u32[]{:S(2)}, u32[]{:S(2)}) async-start(f32[8,16,128]{2,1,0:T(8,128)} %get-tuple-element.38), calls=%async_computation.2 | async-start | bytes 131072 | tf_op jit(solution)/shard_map/all_to_all | solution.py:774
  90.9 4.9 %collective-permute-start.10 = (f32[40,512]{1,0:T(8,128)}, f32[40,512]{1,0:T(8,128)S(1)}, u32[]{:S(2)}, u32[]{:S(2)}) collective-permute-start(f32[40,512]{1,0:T(8,128)} %get-tuple-element.39.refs_2_), channel_id=1, source_target_pairs={{0,3},{1,2},{2,1},{3,0},{4,7},{5,6},{6,5},{7,4},{8,11},{9,10},{10,... | collective-permute-start | bytes 245768 | tf_op jit(solution)/shard_map/ppermute | solution.py:565
  91.9 5.7 %collective-permute-start.9 = (f32[40,512]{1,0:T(8,128)}, f32[40,512]{1,0:T(8,128)S(1)}, u32[]{:S(2)}, u32[]{:S(2)}) collective-permute-start(f32[40,512]{1,0:T(8,128)} %get-tuple-element.39.refs_2_), channel_id=1, source_target_pairs={{0,2},{1,3},{2,0},{3,1},{4,6},{5,7},{6,4},{7,5},{8,10},{9,11},{10,... | collective-permute-start | bytes 245768 | tf_op jit(solution)/shard_map/ppermute | solution.py:565
  92.5 5.1 %collective-permute-start.8 = (f32[40,512]{1,0:T(8,128)}, f32[40,512]{1,0:T(8,128)S(1)}, u32[]{:S(2)}, u32[]{:S(2)}) collective-permute-start(f32[40,512]{1,0:T(8,128)} %get-tuple-element.39.refs_2_), channel_id=1, source_target_pairs={{0,1},{1,0},{2,3},{3,2},{4,5},{5,4},{6,7},{7,6},{8,9},{9,8},{10,11... | collective-permute-start | bytes 245768 | tf_op jit(solution)/shard_map/ppermute | solution.py:565
  97.8 0.9 copy-start.2
  98.7 0.8 copy-start.3
  100.8 7.3 %collective-permute-start.11 = (f32[16,1920]{1,0:T(8,128)S(1)}, f32[16,1920]{1,0:T(8,128)S(1)}, u32[]{:S(2)}, u32[]{:S(2)}) collective-permute-start(f32[16,1920]{1,0:T(8,128)S(1)} %get-tuple-element.42), channel_id=1, source_target_pairs={{0,4},{4,0},{8,12},{12,8},{16,20},{20,16},{24,28},{28,24},{1,5},{5... | collective-permute-start | bytes 368648 | tf_op jit(solution)/shard_map/ppermute | solution.py:565
  102.7 3.6 %collective-permute-start.17 = (f32[16,512]{1,0:T(8,128)S(1)}, f32[16,512]{1,0:T(8,128)S(1)}, u32[]{:S(2)}, u32[]{:S(2)}) collective-permute-start(f32[16,512]{1,0:T(8,128)S(1)} %get-tuple-element.43.c0), channel_id=1, source_target_pairs={{0,3},{1,2},{2,1},{3,0},{4,7},{5,6},{6,5},{7,4},{8,11},{9,10},{10,... | collective-permute-start | bytes 98312 | tf_op jit(solution)/shard_map/ppermute | solution.py:565
  103.2 4.0 %collective-permute-start.16 = (f32[16,512]{1,0:T(8,128)S(1)}, f32[16,512]{1,0:T(8,128)S(1)}, u32[]{:S(2)}, u32[]{:S(2)}) collective-permute-start(f32[16,512]{1,0:T(8,128)S(1)} %get-tuple-element.43.c0), channel_id=1, source_target_pairs={{0,2},{1,3},{2,0},{3,1},{4,6},{5,7},{6,4},{7,5},{8,10},{9,11},{10,... | collective-permute-start | bytes 98312 | tf_op jit(solution)/shard_map/ppermute | solution.py:565
  104.1 3.1 %collective-permute-start.15 = (f32[16,512]{1,0:T(8,128)S(1)}, f32[16,512]{1,0:T(8,128)S(1)}, u32[]{:S(2)}, u32[]{:S(2)}) collective-permute-start(f32[16,512]{1,0:T(8,128)S(1)} %get-tuple-element.43.c0), channel_id=1, source_target_pairs={{0,1},{1,0},{2,3},{3,2},{4,5},{5,4},{6,7},{7,6},{8,9},{9,8},{10,11... | collective-permute-start | bytes 98312 | tf_op jit(solution)/shard_map/ppermute | solution.py:565
  107.4 5.2 %collective-permute-start.18 = (f32[16,896]{1,0:T(8,128)S(1)}, f32[16,896]{1,0:T(8,128)S(1)}, u32[]{:S(2)}, u32[]{:S(2)}) collective-permute-start(f32[16,896]{1,0:T(8,128)S(1)} %second_down.1), channel_id=1, source_target_pairs={{0,4},{4,0},{8,12},{12,8},{16,20},{20,16},{24,28},{28,24},{1,5},{5... | collective-permute-start | bytes 172040 | tf_op jit(solution)/shard_map/ppermute | solution.py:565
  108.1 14.2 %collective-permute-start.14 = (bf16[16,1920]{1,0:T(8,128)(2,1)S(1)}, bf16[16,1920]{1,0:T(8,128)(2,1)S(1)}, u32[]{:S(2)}, u32[]{:S(2)}) collective-permute-start(bf16[16,1920]{1,0:T(8,128)(2,1)S(1)} %add_convert_fusion.refs_0_), channel_id=1, source_target_pairs={{0,24},{4,28},{8,16},{12,20},{16,8},{20,12},{24,0},{28,4},{1,25},{... | collective-permute-start | bytes 184328 | tf_op jit(solution)/shard_map/ppermute | solution.py:565
  111.3 11.0 %collective-permute-start.13 = (bf16[16,1920]{1,0:T(8,128)(2,1)S(1)}, bf16[16,1920]{1,0:T(8,128)(2,1)S(1)}, u32[]{:S(2)}, u32[]{:S(2)}) collective-permute-start(bf16[16,1920]{1,0:T(8,128)(2,1)S(1)} %add_convert_fusion.refs_0_), channel_id=1, source_target_pairs={{0,16},{4,20},{8,24},{12,28},{16,0},{20,4},{24,8},{28,12},{1,17},{... | collective-permute-start | bytes 184328 | tf_op jit(solution)/shard_map/ppermute | solution.py:565
  111.3 11.0 %collective-permute-start.12 = (bf16[16,1920]{1,0:T(8,128)(2,1)S(1)}, bf16[16,1920]{1,0:T(8,128)(2,1)S(1)}, u32[]{:S(2)}, u32[]{:S(2)}) collective-permute-start(bf16[16,1920]{1,0:T(8,128)(2,1)S(1)} %add_convert_fusion.refs_0_), channel_id=1, source_target_pairs={{0,8},{4,12},{8,0},{12,4},{16,24},{20,28},{24,16},{28,20},{1,9},{5... | collective-permute-start | bytes 184328 | tf_op jit(solution)/shard_map/ppermute | solution.py:565
  112.6 5.8 %collective-permute-start.21 = (bf16[16,896]{1,0:T(8,128)(2,1)S(1)}, bf16[16,896]{1,0:T(8,128)(2,1)S(1)}, u32[]{:S(2)}, u32[]{:S(2)}) collective-permute-start(bf16[16,896]{1,0:T(8,128)(2,1)S(1)} %add_convert_fusion.1.refs_4_), channel_id=1, source_target_pairs={{0,24},{4,28},{8,16},{12,20},{16,8},{20,12},{24,0},{28,4},{1,25},{... | collective-permute-start | bytes 86024 | tf_op jit(solution)/shard_map/ppermute | solution.py:565
  115.8 4.8 %collective-permute-start.20 = (bf16[16,896]{1,0:T(8,128)(2,1)S(1)}, bf16[16,896]{1,0:T(8,128)(2,1)S(1)}, u32[]{:S(2)}, u32[]{:S(2)}) collective-permute-start(bf16[16,896]{1,0:T(8,128)(2,1)S(1)} %add_convert_fusion.1.refs_4_), channel_id=1, source_target_pairs={{0,16},{4,20},{8,24},{12,28},{16,0},{20,4},{24,8},{28,12},{1,17},{... | collective-permute-start | bytes 86024 | tf_op jit(solution)/shard_map/ppermute | solution.py:565
  118.4 3.9 %collective-permute-start.19 = (bf16[16,896]{1,0:T(8,128)(2,1)S(1)}, bf16[16,896]{1,0:T(8,128)(2,1)S(1)}, u32[]{:S(2)}, u32[]{:S(2)}) collective-permute-start(bf16[16,896]{1,0:T(8,128)(2,1)S(1)} %add_convert_fusion.1.refs_4_), channel_id=1, source_target_pairs={{0,8},{4,12},{8,0},{12,4},{16,24},{20,28},{24,16},{28,20},{1,9},{5... | collective-permute-start | bytes 86024 | tf_op jit(solution)/shard_map/ppermute | solution.py:565

commit v6 on v4

--- a/solution.py
+++ b/solution.py
@@ -456,13 +456,13 @@
                 at = slice(b * BLK, (b + 1) * BLK)
                 out_ref[at, seen:] = dot_nn(left_ref[own_rows[b], head_cols(h)], own_t[:, at])
 
-        def over_keys(left_ref, first, all_ref, own_ref):
-            whole = dot_nn(left_ref[first : first + PAIR * BLK, :seen], all_ref[...])
+        def over_keys(right_ref, first, all_t, own_t):
+            whole = dot_nt(all_t[...], right_ref[first : first + PAIR * BLK, :seen])
             mine = [
-                dot_nn(left_ref[first + b * BLK : first + (b + 1) * BLK, seen:], own_ref[own_rows[b], :])
+                dot_nt(own_t[:, b * BLK : (b + 1) * BLK], right_ref[first + b * BLK : first + (b + 1) * BLK, seen:])
                 for b in range(PAIR)
             ]
-            return (whole + jnp.concatenate(mine, 0)).astype(jnp.bfloat16)
+            return (whole + jnp.concatenate(mine, 1)).astype(jnp.bfloat16)
 
         def scores(h):
             times_keys(s_s.at[h % 2], q_s, h, kt_all, kt_own)
@@ -485,8 +485,8 @@
                 ds_s[h % 2, at, :] = (probs * ((dp - dot) * scale)).astype(jnp.bfloat16)
 
         def finish_head(h):
-            att_s[:, head_cols(h)] = over_keys(p_s, h * PAIR * BLK, v_all, v_own)
-            dq_s[:, head_cols(h)] = over_keys(ds_s.at[h % 2], 0, k_all, k_own)
+            att_s[head_cols(h), :] = over_keys(p_s, h * PAIR * BLK, vt_all, vt_own)
+            dq_s[head_cols(h), :] = over_keys(ds_s.at[h % 2], 0, kt_all, kt_own)
 
         scores(0)
         prob_grads(0)
@@ -508,10 +508,10 @@
             dv_own.append(dot_nn(g_b, p_b))
         dv_own = jnp.concatenate(dv_own, 1)
         dq = dq_s[...]
-        cot_ref[0:RANK, rows] = dot_nt(qup_ref[...], dq)
+        cot_ref[0:RANK, rows] = dot_nn(qup_ref[...], dq)
         cot_ref[RANK : 2 * RANK, rows] = dot_nn(up_wide, dv_own, HIGHEST)
-        cot_ref[2 * RANK :, rows] = dot_nt(tag_ref[...], att_s[...])
-        up_ref[:, :query_width] += dot_nn(low_s[0:RANK, rows], dq)
+        cot_ref[2 * RANK :, rows] = dot_nn(tag_ref[...], att_s[...])
+        up_ref[:, :query_width] += dot_nt(low_s[0:RANK, rows], dq)
         up_ref[:, query_width:] += dot_nt(low_s[RANK:, rows].astype(jnp.float32), dv_own, HIGHEST)
         return carry
 
@@ -748,8 +748,8 @@
             pltpu.VMEM((2, PAIR * BLK, total), f32),
             pltpu.VMEM((heads * PAIR * BLK, total), bf16),
             pltpu.VMEM((2, PAIR * BLK, total), bf16),
-            pltpu.VMEM((PAIR * BLK, query_width), bf16),
-            pltpu.VMEM((PAIR * BLK, query_width), bf16),
+            pltpu.VMEM((query_width, PAIR * BLK), bf16),
+            pltpu.VMEM((query_width, PAIR * BLK), bf16),
             pltpu.VMEM((HD, seen), f32),
             pltpu.SemaphoreType.DMA((3 * peers + 6,)),
         ],

time: 120 us -> 121 us (level)
  transfers between devices with their start and end apart: 22 -> 22, of which waited for: 10 -> 10; matrix products, arithmetic and copies ran while one was open for 1% -> 1% of each run, Pallas kernels for 24% -> 23%
where the time goes in v6:
time: 121 us; the launch traced here: 120 us
  Pallas kernels  53.4 us (44%)
  starting transfers between devices  31.4 us (26%)
  waiting for transfers between devices  18.3 us (15%)
  blocking collectives  13.1 us (11%)
  local copies, waits for them, and re-layouts  2.48 us (2%)
    pallas_call x1, Pallas kernels, fast(): run(lambda *refs: attention_kernel(peers, heads, *refs), 'span_attention'...  23.3 us
    ppermute x20, starting transfers between devices, swap(): lax.ppermute(x, axis, [(i, i ^ bit) for i in range(lax.axis_size(axis))])  19.5 us
    ppermute x20, waiting for transfers between devices, swap(): lax.ppermute(x, axis, [(i, i ^ bit) for i in range(lax.axis_size(axis))])  18.1 us
    all_to_all x1, blocking collectives, fast(): lax.all_to_all(wanted, 'tm', split_axis=0, concat_axis=0, tiled=True)  13.1 us
    pallas_call x1, Pallas kernels, fast(): run(project_early_kernel, 'project_near_half', (shaped(tok_rows, query_wi...  9.03 us
    pallas_call x1, Pallas kernels, fast(): run(project_far_kernel, 'project_far_half', (shaped(tok_rows, query_width...  7.73 us
    all_to_all x1, starting transfers between devices, fast(): back = lax.all_to_all(mcot, 'tm', split_axis=0, concat_axis=0, tiled=True)  6.01 us
    all_to_all x1, starting transfers between devices, fast(): got = lax.all_to_all(pairs, 'tm', split_axis=0, concat_axis=0, tiled=True)  5.82 us
  transfers between devices with their start and end apart: 22, of which 10 were waited for; matrix products, arithmetic and copies ran while one was open for 1% of the time, Pallas kernels for 23%

profile of v6, /device:TPU:0, one launch (start us, length us, event | category | flops | bytes accessed | tf_op | source)
XLA Modules:
  0.0 120.1 jit_solution(3867201477755604358)
XLA Ops:
  0.6 0.5 collective-permute-start
  1.1 2.6 %collective-permute-start.3 = (bf16[512,896]{1,0:T(8,128)(2,1)}, bf16[512,896]{1,0:T(8,128)(2,1)}, u32[]{:S(2)}, u32[]{:S(2)}) collective-permute-start(bf16[512,896]{1,0:T(8,128)(2,1)} %memory_ref.1), channel_id=1, source_target_pairs={{0,2},{1,3},{2,0},{3,1},{4,6},{5,7},{6,4},{7,5},{8,10},{9,11},{10,... | collective-permute-start | bytes 2752520 | tf_op jit(solution)/shard_map/ppermute | solution.py:562
  3.7 0.2 collective-permute-start.1
  3.9 0.0 collective-permute-done.refs_3_
  3.9 4.3 %memory_near_half.1 = (f32[512,256]{1,0:T(8,128)}, f32[512,16]{1,0:T(8,128)}, s32[8]{0:T(128)}) custom-call(s32[1]{0:T(128)} %bitcast.refs_0_.place_ref, s32[4,8]{1,0:T(4,128)} %refs_1_.4, bf16[512,896]{1,0:T(8,128)(2,1)} %memory_ref.1, bf16[512,896]{1,0:T(8,128)(2,1)} %collective-permute-done.refs_3_, bf16[3584,128]{1,0:T(8,128)(2,1)} %refs_1_.7, ...), custom_call_target="tpu_custom_call" | custom-call | tf_op jit(solution)/shard_map/memory_near_half/pallas_call | solution.py:669
  8.2 0.7 copy.21
  8.9 13.1 %all_to_all.21 = s32[8,1,1]{2,1,0:T(1,128)S(1)} all-to-all(s32[8,1,1]{2,1,0:T(1,128)S(1)} %copy.21), channel_id=1, replica_groups=mesh['tm'=8,'heads'=4] {'tm'}, dimensions={0} | all-to-all | bytes 64 | tf_op jit(solution)/shard_map/all_to_all | solution.py:677
  22.0 0.8 reduce.refs_1_.refs_0_
  22.8 2.2 %collective-permute-done.3.refs_0_ = bf16[512,896]{1,0:T(8,128)(2,1)} collective-permute-done((bf16[512,896]{1,0:T(8,128)(2,1)}, bf16[512,896]{1,0:T(8,128)(2,1)}, u32[]{:S(2)}, u32[]{:S(2)}) %collective-permute-start.3) | collective-permute-done | bytes 917536 | tf_op jit(solution)/shard_map/ppermute | solution.py:562
  25.0 0.0 collective-permute-start.4
  25.0 0.0 collective-permute-done.1.x1
  25.0 1.8 %collective-permute-start.2 = (bf16[512,896]{1,0:T(8,128)(2,1)}, bf16[512,896]{1,0:T(8,128)(2,1)}, u32[]{:S(2)}, u32[]{:S(2)}) collective-permute-start(bf16[512,896]{1,0:T(8,128)(2,1)} %collective-permute-done.1.x1), channel_id=1, source_target_pairs={{0,2},{1,3},{2,0},{3,1},{4,6},{5,7},{6,4},{7,5},{8,10},{9,11},{10,... | collective-permute-start | bytes 2752520 | tf_op jit(solution)/shard_map/ppermute | solution.py:562
  26.8 3.0 %memory_far_quarter.1 = (f32[512,256]{1,0:T(8,128)}, f32[512,16]{1,0:T(8,128)}) custom-call(s32[1]{0:T(128)} %bitcast.refs_0_.place_ref, bf16[512,896]{1,0:T(8,128)(2,1)} %in_order.2.x2, f32[512,256]{1,0:T(8,128)} %get-tuple-element.31.acc_hbm, f32[512,16]{1,0:T(8,128)} %get-tuple-element.32.low_hbm, bf16[3584,128]{1,0:T(8,128)(2,1)} %refs_1_.7, ...), custom_call_target="tpu_custom_call" | custom-call | tf_op jit(solution)/shard_map/memory_far_quarter/pallas_call | solution.py:682
  29.8 0.0 collective-permute-done.4.refs_2_
  29.9 3.8 %memory_pairs.1.refs_7_ = bf16[8,272,128]{2,1,0:T(8,128)(2,1)} custom-call(s32[1]{0:T(128)} %bitcast.refs_0_.place_ref, s32[8]{0:T(128)} %reduce.refs_1_.refs_0_, bf16[512,896]{1,0:T(8,128)(2,1)} %collective-permute-done.4.refs_2_, f32[512,256]{1,0:T(8,128)} %get-tuple-element.33.refs_3_, f32[512,16]{1,0:T(8,128)} %get-tuple-element.34.refs_4_, ...), custom_call_target="tpu_custom_call" | custom-call | tf_op jit(solution)/shard_map/memory_pairs/pallas_call | solution.py:689
  33.7 5.8 %all-to-all-start.1 = ((bf16[8,272,128]{2,1,0:T(8,128)(2,1)}), bf16[8,272,128]{2,1,0:T(8,128)(2,1)}, u32[]{:S(2)}, u32[]{:S(2)}) async-start(bf16[8,272,128]{2,1,0:T(8,128)(2,1)} %memory_pairs.1.refs_7_), calls=%async_computation.1 | async-start | bytes 1114112 | tf_op jit(solution)/shard_map/all_to_all | solution.py:696
  39.5 9.0 %project_near_half.1 = (f32[512,896]{1,0:T(8,128)}, f32[512,256]{1,0:T(8,128)}, f32[512,32]{1,0:T(8,128)}, bf16[512,896]{1,0:T(8,128)(2,1)}, bf16[896,512]{1,0:T(8,128)(2,1)}) custom-call(s32[1]{0:T(128)} %bitcast.refs_0_.place_ref, bf16[512,896]{1,0:T(8,128)(2,1)} %refs_6_.5, bf16[512,896]{1,0:T(8,128)(2,1)} %collective-permute-done.1.x1, ...), custom_call_target="tpu_custom_call" | custom-call | tf_op jit(solution)/shard_map/project_near_half/pallas_call | solution.py:697
  48.5 0.0 collective-permute-done.2.refs_0_
  48.6 0.1 collective-permute-start.5
  48.6 2.8 %collective-permute-done.5.x2 = bf16[512,896]{1,0:T(8,128)(2,1)} collective-permute-done((bf16[512,896]{1,0:T(8,128)(2,1)}, bf16[512,896]{1,0:T(8,128)(2,1)}, u32[]{:S(2)}, u32[]{:S(2)}) %collective-permute-start.5) | collective-permute-done | bytes 917536 | tf_op jit(solution)/shard_map/ppermute | solution.py:562
  51.4 7.7 %project_far_half.1 = (bf16[512,896]{1,0:T(8,128)(2,1)}, bf16[512,128]{1,0:T(8,128)(2,1)}, bf16[512,128]{1,0:T(8,128)(2,1)}, bf16[32,512]{1,0:T(8,128)(2,1)}) custom-call(s32[1]{0:T(128)} %bitcast.refs_0_.place_ref, bf16[512,896]{1,0:T(8,128)(2,1)} %in_order.3.x3, bf16[512,896]{1,0:T(8,128)(2,1)} %collective-permute-done.5.x2, bf16[3584,896]{1,0:T(8,128)(2,1)} %refs_0_.6, ...), custom_call_target="tpu_custom_call" | custom-call | tf_op jit(solution)/shard_map/project_far_half/pallas_call | solution.py:712
  59.2 0.0 all-to-all-done.1.refs_5_
  59.2 0.0 copy-start
  59.2 0.0 copy-start.4
  59.2 0.0 copy-start.1
  59.2 23.3 %span_attention.1 = (f32[40,512]{1,0:T(8,128)}, f32[16,1024]{1,0:T(8,128)}, f32[8,16,128]{2,1,0:T(8,128)}) custom-call(s32[4]{0:T(128)} %refs_0_.7, bf16[512,896]{1,0:T(8,128)(2,1)} %get-tuple-element.38.refs_1_, bf16[512,128]{1,0:T(8,128)(2,1)} %get-tuple-element.39.refs_2_, bf16[512,128]{1,0:T(8,128)(2,1)} %get-tuple-element.40.refs_3_, ...), custom_call_target="tpu_custom_call" | custom-call | flops 10569646080 | bytes 1835008 | tf_op jit(solution)/shard_map/span_attention/pallas_call | solution.py:727
  82.5 6.0 %all-to-all-start.2 = ((f32[8,16,128]{2,1,0:T(8,128)}), f32[8,16,128]{2,1,0:T(8,128)S(1)}, u32[]{:S(2)}, u32[]{:S(2)}) async-start(f32[8,16,128]{2,1,0:T(8,128)} %get-tuple-element.44), calls=%async_computation.2 | async-start | bytes 131072 | tf_op jit(solution)/shard_map/all_to_all | solution.py:761
  88.5 0.5 collective-permute-start.8
  89.0 1.0 collective-permute-start.7
  90.0 0.4 collective-permute-start.6
  90.4 3.1 %collective-permute-done.8.refs_5_ = f32[40,512]{1,0:T(8,128)S(1)} collective-permute-done((f32[40,512]{1,0:T(8,128)}, f32[40,512]{1,0:T(8,128)S(1)}, u32[]{:S(2)}, u32[]{:S(2)}) %collective-permute-start.8) | collective-permute-done | bytes 81952 | tf_op jit(solution)/shard_map/ppermute | solution.py:562
  93.5 1.8 %collective-permute-done.7.refs_4_ = f32[40,512]{1,0:T(8,128)S(1)} collective-permute-done((f32[40,512]{1,0:T(8,128)}, f32[40,512]{1,0:T(8,128)S(1)}, u32[]{:S(2)}, u32[]{:S(2)}) %collective-permute-start.7) | collective-permute-done | bytes 81952 | tf_op jit(solution)/shard_map/ppermute | solution.py:562
  95.2 0.0 collective-permute-done.6.refs_3_
  95.3 0.2 all-to-all-done.2.refs_1_
  95.4 0.0 copy-done
  95.4 0.0 copy-done.4
  95.5 0.9 copy-done.2
  96.3 0.8 copy-done.3
  97.2 1.3 %first_down.1 = (f32[8,512]{1,0:T(8,128)}, f32[16,1920]{1,0:T(8,128)S(1)}, f32[16,896]{1,0:T(8,128)S(1)}, f32[16,512]{1,0:T(8,128)S(1)}) custom-call(s32[8]{0:T(128)S(1)} %copy-done.4, f32[8,16,128]{2,1,0:T(8,128)S(1)} %all-to-all-done.2.refs_1_, f32[40,512]{1,0:T(8,128)S(1)} %copy-done.2, f32[40,512]{1,0:T(8,128)S(1)} %collective-permute-done.6.refs_3_, ...), custom_call_target="tpu_custom_call" | custom-call | tf_op jit(solution)/shard_map/first_down/pallas_call | solution.py:763
  98.5 1.3 %collective-permute-start.9 = (f32[16,1920]{1,0:T(8,128)S(1)}, f32[16,1920]{1,0:T(8,128)S(1)}, u32[]{:S(2)}, u32[]{:S(2)}) collective-permute-start(f32[16,1920]{1,0:T(8,128)S(1)} %get-tuple-element.48), channel_id=1, source_target_pairs={{0,4},{4,0},{8,12},{12,8},{16,20},{20,16},{24,28},{28,24},{1,5},{5... | collective-permute-start | bytes 368648 | tf_op jit(solution)/shard_map/ppermute | solution.py:562
  99.8 0.5 collective-permute-start.15
  100.3 1.0 collective-permute-start.14
  101.3 0.4 collective-permute-start.13
  101.7 1.8 %collective-permute-done.15.c3 = f32[16,512]{1,0:T(8,128)S(1)} collective-permute-done((f32[16,512]{1,0:T(8,128)S(1)}, f32[16,512]{1,0:T(8,128)S(1)}, u32[]{:S(2)}, u32[]{:S(2)}) %collective-permute-start.15) | collective-permute-done | bytes 32800 | tf_op jit(solution)/shard_map/ppermute | solution.py:562
  103.5 0.8 collective-permute-done.14.c2
  104.2 0.0 collective-permute-done.13.c1
  104.3 0.0 copy-done.1
  104.3 0.2 second_down.1
  104.5 0.7 collective-permute-start.16
  105.2 0.0 collective-permute-done.9
  105.2 3.2 %collective-permute-start.12 = (bf16[16,1920]{1,0:T(8,128)(2,1)S(1)}, bf16[16,1920]{1,0:T(8,128)(2,1)S(1)}, u32[]{:S(2)}, u32[]{:S(2)}) collective-permute-start(bf16[16,1920]{1,0:T(8,128)(2,1)S(1)} %add_convert_fusion.refs_0_), channel_id=1, source_target_pairs={{0,24},{4,28},{8,16},{12,20},{16,8},{20,12},{24,0},{28,4},{1,25},{... | collective-permute-start | bytes 184328 | tf_op jit(solution)/shard_map/ppermute | solution.py:562
  108.5 0.0 collective-permute-start.11
  108.5 1.2 %collective-permute-start.10 = (bf16[16,1920]{1,0:T(8,128)(2,1)S(1)}, bf16[16,1920]{1,0:T(8,128)(2,1)S(1)}, u32[]{:S(2)}, u32[]{:S(2)}) collective-permute-start(bf16[16,1920]{1,0:T(8,128)(2,1)S(1)} %add_convert_fusion.refs_0_), channel_id=1, source_target_pairs={{0,8},{4,12},{8,0},{12,4},{16,24},{20,28},{24,16},{28,20},{1,9},{5... | collective-permute-start | bytes 184328 | tf_op jit(solution)/shard_map/ppermute | solution.py:562
  109.7 0.0 collective-permute-done.16
  109.7 3.2 %collective-permute-start.19 = (bf16[16,896]{1,0:T(8,128)(2,1)S(1)}, bf16[16,896]{1,0:T(8,128)(2,1)S(1)}, u32[]{:S(2)}, u32[]{:S(2)}) collective-permute-start(bf16[16,896]{1,0:T(8,128)(2,1)S(1)} %add_convert_fusion.1.refs_4_), channel_id=1, source_target_pairs={{0,24},{4,28},{8,16},{12,20},{16,8},{20,12},{24,0},{28,4},{1,25},{... | collective-permute-start | bytes 86024 | tf_op jit(solution)/shard_map/ppermute | solution.py:562
  112.9 0.0 collective-permute-start.18
  112.9 2.6 %collective-permute-done.19.refs_7_ = bf16[16,896]{1,0:T(8,128)(2,1)S(1)} collective-permute-done((bf16[16,896]{1,0:T(8,128)(2,1)S(1)}, bf16[16,896]{1,0:T(8,128)(2,1)S(1)}, u32[]{:S(2)}, u32[]{:S(2)}) %collective-permute-start.19) | collective-permute-done | bytes 28704 | tf_op jit(solution)/shard_map/ppermute | solution.py:562
  115.6 0.9 collective-permute-start.17
  116.5 1.2 %collective-permute-done.18.refs_6_ = bf16[16,896]{1,0:T(8,128)(2,1)S(1)} collective-permute-done((bf16[16,896]{1,0:T(8,128)(2,1)S(1)}, bf16[16,896]{1,0:T(8,128)(2,1)S(1)}, u32[]{:S(2)}, u32[]{:S(2)}) %collective-permute-start.18) | collective-permute-done | bytes 28704 | tf_op jit(solution)/shard_map/ppermute | solution.py:562
  117.7 1.7 %collective-permute-done.17.refs_5_ = bf16[16,896]{1,0:T(8,128)(2,1)S(1)} collective-permute-done((bf16[16,896]{1,0:T(8,128)(2,1)S(1)}, bf16[16,896]{1,0:T(8,128)(2,1)S(1)}, u32[]{:S(2)}, u32[]{:S(2)}) %collective-permute-start.17) | collective-permute-done | bytes 28704 | tf_op jit(solution)/shard_map/ppermute | solution.py:562
  119.4 0.0 collective-permute-done.12.refs_3_
  119.4 0.0 collective-permute-done.11.refs_2_
  119.4 0.0 collective-permute-done.10.refs_1_
  119.4 0.7 finish_outputs.1
  (6 shorter events, 0.0 us)
Async XLA Ops:
  0.6 3.3 %collective-permute-start = (bf16[512,896]{1,0:T(8,128)(2,1)}, bf16[512,896]{1,0:T(8,128)(2,1)}, u32[]{:S(2)}, u32[]{:S(2)}) collective-permute-start(bf16[512,896]{1,0:T(8,128)(2,1)} %memory_ref.1), channel_id=1, source_target_pairs={{0,1},{1,0},{2,3},{3,2},{4,5},{5,4},{6,7},{7,6},{8,9},{9,8},{10,11... | collective-permute-start | bytes 2752520 | tf_op jit(solution)/shard_map/ppermute | solution.py:562
  1.1 23.9 %collective-permute-start.3 = (bf16[512,896]{1,0:T(8,128)(2,1)}, bf16[512,896]{1,0:T(8,128)(2,1)}, u32[]{:S(2)}, u32[]{:S(2)}) collective-permute-start(bf16[512,896]{1,0:T(8,128)(2,1)} %memory_ref.1), channel_id=1, source_target_pairs={{0,2},{1,3},{2,0},{3,1},{4,6},{5,7},{6,4},{7,5},{8,10},{9,11},{10,... | collective-permute-start | bytes 2752520 | tf_op jit(solution)/shard_map/ppermute | solution.py:562
  3.7 21.3 %collective-permute-start.1 = (bf16[512,896]{1,0:T(8,128)(2,1)}, bf16[512,896]{1,0:T(8,128)(2,1)}, u32[]{:S(2)}, u32[]{:S(2)}) collective-permute-start(bf16[512,896]{1,0:T(8,128)(2,1)} %refs_6_.5), channel_id=1, source_target_pairs={{0,1},{1,0},{2,3},{3,2},{4,5},{5,4},{6,7},{7,6},{8,9},{9,8},{10,11... | collective-permute-start | bytes 2752520 | tf_op jit(solution)/shard_map/ppermute | solution.py:562
  25.0 4.8 %collective-permute-start.4 = (bf16[512,896]{1,0:T(8,128)(2,1)}, bf16[512,896]{1,0:T(8,128)(2,1)}, u32[]{:S(2)}, u32[]{:S(2)}) collective-permute-start(bf16[512,896]{1,0:T(8,128)(2,1)} %in_order.2.x2), channel_id=1, source_target_pairs={{0,1},{1,0},{2,3},{3,2},{4,5},{5,4},{6,7},{7,6},{8,9},{9,8},{10,11... | collective-permute-start | bytes 2752520 | tf_op jit(solution)/shard_map/ppermute | solution.py:562
  25.0 23.5 %collective-permute-start.2 = (bf16[512,896]{1,0:T(8,128)(2,1)}, bf16[512,896]{1,0:T(8,128)(2,1)}, u32[]{:S(2)}, u32[]{:S(2)}) collective-permute-start(bf16[512,896]{1,0:T(8,128)(2,1)} %collective-permute-done.1.x1), channel_id=1, source_target_pairs={{0,2},{1,3},{2,0},{3,1},{4,6},{5,7},{6,4},{7,5},{8,10},{9,11},{10,... | collective-permute-start | bytes 2752520 | tf_op jit(solution)/shard_map/ppermute | solution.py:562
  33.7 25.5 %all-to-all-start.1 = ((bf16[8,272,128]{2,1,0:T(8,128)(2,1)}), bf16[8,272,128]{2,1,0:T(8,128)(2,1)}, u32[]{:S(2)}, u32[]{:S(2)}) async-start(bf16[8,272,128]{2,1,0:T(8,128)(2,1)} %memory_pairs.1.refs_7_), calls=%async_computation.1 | async-start | bytes 1114112 | tf_op jit(solution)/shard_map/all_to_all | solution.py:696
  48.6 2.9 %collective-permute-start.5 = (bf16[512,896]{1,0:T(8,128)(2,1)}, bf16[512,896]{1,0:T(8,128)(2,1)}, u32[]{:S(2)}, u32[]{:S(2)}) collective-permute-start(bf16[512,896]{1,0:T(8,128)(2,1)} %in_order.3.x3), channel_id=1, source_target_pairs={{0,1},{1,0},{2,3},{3,2},{4,5},{5,4},{6,7},{7,6},{8,9},{9,8},{10,11... | collective-permute-start | bytes 2752520 | tf_op jit(solution)/shard_map/ppermute | solution.py:562
  59.2 36.2 %copy-start = (bf16[512,896]{1,0:T(8,128)(2,1)S(1)}, bf16[512,896]{1,0:T(8,128)(2,1)}, u32[]{:S(2)}) copy-start(bf16[512,896]{1,0:T(8,128)(2,1)} %refs_6_.5) | copy-start | bytes 2752516
  59.2 36.2 %copy-start.4 = (s32[8]{0:T(128)S(1)}, s32[8]{0:T(128)}, u32[]{:S(2)}) copy-start(s32[8]{0:T(128)} %reduce.refs_1_.refs_0_) | copy-start | bytes 100
  59.2 45.0 %copy-start.1 = (bf16[512,896]{1,0:T(8,128)(2,1)S(1)}, bf16[512,896]{1,0:T(8,128)(2,1)}, u32[]{:S(2)}) copy-start(bf16[512,896]{1,0:T(8,128)(2,1)} %memory_ref.1) | copy-start | bytes 2752516
  82.5 12.9 %all-to-all-start.2 = ((f32[8,16,128]{2,1,0:T(8,128)}), f32[8,16,128]{2,1,0:T(8,128)S(1)}, u32[]{:S(2)}, u32[]{:S(2)}) async-start(f32[8,16,128]{2,1,0:T(8,128)} %get-tuple-element.44), calls=%async_computation.2 | async-start | bytes 131072 | tf_op jit(solution)/shard_map/all_to_all | solution.py:761
  88.5 4.9 %collective-permute-start.8 = (f32[40,512]{1,0:T(8,128)}, f32[40,512]{1,0:T(8,128)S(1)}, u32[]{:S(2)}, u32[]{:S(2)}) collective-permute-start(f32[40,512]{1,0:T(8,128)} %get-tuple-element.45.refs_2_), channel_id=1, source_target_pairs={{0,3},{1,2},{2,1},{3,0},{4,7},{5,6},{6,5},{7,4},{8,11},{9,10},{10,... | collective-permute-start | bytes 245768 | tf_op jit(solution)/shard_map/ppermute | solution.py:562
  89.0 6.2 %collective-permute-start.7 = (f32[40,512]{1,0:T(8,128)}, f32[40,512]{1,0:T(8,128)S(1)}, u32[]{:S(2)}, u32[]{:S(2)}) collective-permute-start(f32[40,512]{1,0:T(8,128)} %get-tuple-element.45.refs_2_), channel_id=1, source_target_pairs={{0,2},{1,3},{2,0},{3,1},{4,6},{5,7},{6,4},{7,5},{8,10},{9,11},{10,... | collective-permute-start | bytes 245768 | tf_op jit(solution)/shard_map/ppermute | solution.py:562
  90.0 5.2 %collective-permute-start.6 = (f32[40,512]{1,0:T(8,128)}, f32[40,512]{1,0:T(8,128)S(1)}, u32[]{:S(2)}, u32[]{:S(2)}) collective-permute-start(f32[40,512]{1,0:T(8,128)} %get-tuple-element.45.refs_2_), channel_id=1, source_target_pairs={{0,1},{1,0},{2,3},{3,2},{4,5},{5,4},{6,7},{7,6},{8,9},{9,8},{10,11... | collective-permute-start | bytes 245768 | tf_op jit(solution)/shard_map/ppermute | solution.py:562
  95.4 0.9 copy-start.2
  96.3 0.8 copy-start.3
  98.5 6.8 %collective-permute-start.9 = (f32[16,1920]{1,0:T(8,128)S(1)}, f32[16,1920]{1,0:T(8,128)S(1)}, u32[]{:S(2)}, u32[]{:S(2)}) collective-permute-start(f32[16,1920]{1,0:T(8,128)S(1)} %get-tuple-element.48), channel_id=1, source_target_pairs={{0,4},{4,0},{8,12},{12,8},{16,20},{20,16},{24,28},{28,24},{1,5},{5... | collective-permute-start | bytes 368648 | tf_op jit(solution)/shard_map/ppermute | solution.py:562
  99.8 3.7 %collective-permute-start.15 = (f32[16,512]{1,0:T(8,128)S(1)}, f32[16,512]{1,0:T(8,128)S(1)}, u32[]{:S(2)}, u32[]{:S(2)}) collective-permute-start(f32[16,512]{1,0:T(8,128)S(1)} %get-tuple-element.49.c0), channel_id=1, source_target_pairs={{0,3},{1,2},{2,1},{3,0},{4,7},{5,6},{6,5},{7,4},{8,11},{9,10},{10,... | collective-permute-start | bytes 98312 | tf_op jit(solution)/shard_map/ppermute | solution.py:562
  100.3 4.0 %collective-permute-start.14 = (f32[16,512]{1,0:T(8,128)S(1)}, f32[16,512]{1,0:T(8,128)S(1)}, u32[]{:S(2)}, u32[]{:S(2)}) collective-permute-start(f32[16,512]{1,0:T(8,128)S(1)} %get-tuple-element.49.c0), channel_id=1, source_target_pairs={{0,2},{1,3},{2,0},{3,1},{4,6},{5,7},{6,4},{7,5},{8,10},{9,11},{10,... | collective-permute-start | bytes 98312 | tf_op jit(solution)/shard_map/ppermute | solution.py:562
  101.3 3.0 %collective-permute-start.13 = (f32[16,512]{1,0:T(8,128)S(1)}, f32[16,512]{1,0:T(8,128)S(1)}, u32[]{:S(2)}, u32[]{:S(2)}) collective-permute-start(f32[16,512]{1,0:T(8,128)S(1)} %get-tuple-element.49.c0), channel_id=1, source_target_pairs={{0,1},{1,0},{2,3},{3,2},{4,5},{5,4},{6,7},{7,6},{8,9},{9,8},{10,11... | collective-permute-start | bytes 98312 | tf_op jit(solution)/shard_map/ppermute | solution.py:562
  104.5 5.2 %collective-permute-start.16 = (f32[16,896]{1,0:T(8,128)S(1)}, f32[16,896]{1,0:T(8,128)S(1)}, u32[]{:S(2)}, u32[]{:S(2)}) collective-permute-start(f32[16,896]{1,0:T(8,128)S(1)} %second_down.1), channel_id=1, source_target_pairs={{0,4},{4,0},{8,12},{12,8},{16,20},{20,16},{24,28},{28,24},{1,5},{5... | collective-permute-start | bytes 172040 | tf_op jit(solution)/shard_map/ppermute | solution.py:562
  105.2 14.2 %collective-permute-start.12 = (bf16[16,1920]{1,0:T(8,128)(2,1)S(1)}, bf16[16,1920]{1,0:T(8,128)(2,1)S(1)}, u32[]{:S(2)}, u32[]{:S(2)}) collective-permute-start(bf16[16,1920]{1,0:T(8,128)(2,1)S(1)} %add_convert_fusion.refs_0_), channel_id=1, source_target_pairs={{0,24},{4,28},{8,16},{12,20},{16,8},{20,12},{24,0},{28,4},{1,25},{... | collective-permute-start | bytes 184328 | tf_op jit(solution)/shard_map/ppermute | solution.py:562
  108.5 11.0 %collective-permute-start.11 = (bf16[16,1920]{1,0:T(8,128)(2,1)S(1)}, bf16[16,1920]{1,0:T(8,128)(2,1)S(1)}, u32[]{:S(2)}, u32[]{:S(2)}) collective-permute-start(bf16[16,1920]{1,0:T(8,128)(2,1)S(1)} %add_convert_fusion.refs_0_), channel_id=1, source_target_pairs={{0,16},{4,20},{8,24},{12,28},{16,0},{20,4},{24,8},{28,12},{1,17},{... | collective-permute-start | bytes 184328 | tf_op jit(solution)/shard_map/ppermute | solution.py:562
  108.5 11.0 %collective-permute-start.10 = (bf16[16,1920]{1,0:T(8,128)(2,1)S(1)}, bf16[16,1920]{1,0:T(8,128)(2,1)S(1)}, u32[]{:S(2)}, u32[]{:S(2)}) collective-permute-start(bf16[16,1920]{1,0:T(8,128)(2,1)S(1)} %add_convert_fusion.refs_0_), channel_id=1, source_target_pairs={{0,8},{4,12},{8,0},{12,4},{16,24},{20,28},{24,16},{28,20},{1,9},{5... | collective-permute-start | bytes 184328 | tf_op jit(solution)/shard_map/ppermute | solution.py:562
  109.7 5.8 %collective-permute-start.19 = (bf16[16,896]{1,0:T(8,128)(2,1)S(1)}, bf16[16,896]{1,0:T(8,128)(2,1)S(1)}, u32[]{:S(2)}, u32[]{:S(2)}) collective-permute-start(bf16[16,896]{1,0:T(8,128)(2,1)S(1)} %add_convert_fusion.1.refs_4_), channel_id=1, source_target_pairs={{0,24},{4,28},{8,16},{12,20},{16,8},{20,12},{24,0},{28,4},{1,25},{... | collective-permute-start | bytes 86024 | tf_op jit(solution)/shard_map/ppermute | solution.py:562
  112.9 4.8 %collective-permute-start.18 = (bf16[16,896]{1,0:T(8,128)(2,1)S(1)}, bf16[16,896]{1,0:T(8,128)(2,1)S(1)}, u32[]{:S(2)}, u32[]{:S(2)}) collective-permute-start(bf16[16,896]{1,0:T(8,128)(2,1)S(1)} %add_convert_fusion.1.refs_4_), channel_id=1, source_target_pairs={{0,16},{4,20},{8,24},{12,28},{16,0},{20,4},{24,8},{28,12},{1,17},{... | collective-permute-start | bytes 86024 | tf_op jit(solution)/shard_map/ppermute | solution.py:562
  115.6 3.9 %collective-permute-start.17 = (bf16[16,896]{1,0:T(8,128)(2,1)S(1)}, bf16[16,896]{1,0:T(8,128)(2,1)S(1)}, u32[]{:S(2)}, u32[]{:S(2)}) collective-permute-start(bf16[16,896]{1,0:T(8,128)(2,1)S(1)} %add_convert_fusion.1.refs_4_), channel_id=1, source_target_pairs={{0,8},{4,12},{8,0},{12,4},{16,24},{20,28},{24,16},{28,20},{1,9},{5... | collective-permute-start | bytes 86024 | tf_op jit(solution)/shard_map/ppermute | solution.py:562

commit v7 on v4

--- a/solution.py
+++ b/solution.py
@@ -427,7 +427,7 @@
         at = slice(b * BLK, (b + 1) * BLK)
         kt_all[:, at] = jnp.transpose(k_all[at, :])
         vt_all[:, at] = jnp.transpose(v_all[at, :])
-    wait_all(copies[3 * peers :])
+    wait_all(copies[3 * peers : -1])
     dv_s[...] = jnp.zeros_like(dv_s)
     up_ref[...] = jnp.zeros_like(up_ref)
     scale = HD ** (-0.5)
@@ -498,6 +498,7 @@
                 strips(h)
             if h > 0:
                 finish_head(h - 1)
+        pl.when(c == 0)(copies[-1].wait)
         g_t = jnp.concatenate([grad_t_ref[h * HD : (h + 1) * HD, rows] for h in range(heads)], 1)
         dv_s[...] += dot_nn(g_t, p_s[:, :seen])
         dv_own = []
@@ -524,12 +525,15 @@
         mcot_ref[b] = mcot[:, b * BLK : (b + 1) * BLK]
 
 
-def first_down_kernel(peers, asked_ref, back_ref, c0, c1, c2, c3, slab_ref, up_ref, logit_ref, query_ref, value_ref, own_ref, sum_s):
+def own_kernel(peers, asked_ref, back_ref, out_ref, sum_s):
     sum_s[...] = jnp.zeros_like(sum_s)
     for r in range(peers):
         block = asked_ref[r]
         sum_s[block] = sum_s[block] + back_ref[r]
-    own_ref[...] = jnp.concatenate([sum_s[m] for m in range(sum_s.shape[0])], 1)
+    out_ref[...] = jnp.concatenate([sum_s[m] for m in range(sum_s.shape[0])], 1)
+
+
+def first_down_kernel(c0, c1, c2, c3, slab_ref, up_ref, logit_ref, query_ref, value_ref):
     cot = (c0[...] + c1[...]) + (c2[...] + c3[...])
     logit_ref[...] = cot[2 * RANK :]
     both = dot_nn(cot[: 2 * RANK].astype(jnp.bfloat16), slab_ref[...])
@@ -545,12 +549,10 @@
 
 
 def finish_kernel(*refs):
-    query, value = [
-        (ref[0][...].astype(jnp.float32) + ref[1][...].astype(jnp.float32))
-        + (ref[2][...].astype(jnp.float32) + ref[3][...].astype(jnp.float32))
-        for ref in (refs[:4], refs[4:8])
-    ]
-    query_down_ref, query_up_ref, value_down_ref, value_up_ref = refs[8:]
+    parts = [ref[...].astype(jnp.float32) for ref in refs[:6]]
+    query = parts[0] + parts[1]
+    value = (parts[2] + parts[3]) + (parts[4] + parts[5])
+    query_down_ref, query_up_ref, value_down_ref, value_up_ref = refs[6:]
     value_down_ref[...] = value
     at = 0
     for out_ref in (query_down_ref, query_up_ref, value_up_ref):
@@ -760,19 +762,23 @@
 
     back = lax.all_to_all(mcot, "tm", split_axis=0, concat_axis=0, tiled=True)
     cots = [cot] + [swap(cot, d) for d in range(1, 4)]
-    logits, query_sum, value_part, own = run(
-        lambda *refs: first_down_kernel(peers, *refs),
-        "first_down",
-        (
-            shaped(tags, tok_rows),
-            shaped(RANK, width + ups.shape[1]),
-            shaped(RANK, width),
-            shaped(RANK, mem_rows),
-        ),
-        [smem()] + [vmem()] * 7,
+    own = run(
+        lambda *refs: own_kernel(peers, *refs),
+        "owned_cotangent",
+        shaped(RANK, mem_rows),
+        [smem()] + [vmem()],
         [pltpu.VMEM((blocks, RANK, BLK), f32)],
         room=8,
-    )(asked, back, *cots, slab_tokens, ups)
+    )(asked, back)
+    logits, query_sum, value_part = run(
+        first_down_kernel,
+        "first_down",
+        (shaped(tags, tok_rows), shaped(RANK, width + ups.shape[1]), shaped(RANK, width)),
+        [vmem()] * 6,
+        flops=4 * RANK * tok_rows * width,
+        moved=2 * tok_rows * width,
+        room=8,
+    )(*cots, slab_tokens, ups)
     owns = [own] + [swap(own, d) for d in range(1, 4)]
     value_sum = run(
         second_down_kernel,
@@ -783,15 +789,15 @@
         moved=2 * mem_rows * width,
         room=8,
     )(*owns, memory, value_part)
-    sums = []
-    for part in (query_sum, value_sum):
-        part = (part + swap(part, 1, "tm")).astype(bf16)
-        sums += [part] + [swap(part, bit, "tm") for bit in (2, 4, 6)]
+    query_sum = query_sum + swap(query_sum, 1, "tm")
+    query_sum = (query_sum + swap(query_sum, 2, "tm")).astype(bf16)
+    value_sum = (value_sum + swap(value_sum, 1, "tm")).astype(bf16)
+    sums = [query_sum, swap(query_sum, 4, "tm"), value_sum] + [swap(value_sum, bit, "tm") for bit in (2, 4, 6)]
     query_down_grad, query_up_grad, value_down_grad, value_up_grad = run(
         finish_kernel,
         "finish_outputs",
         (shaped(RANK, width), shaped(RANK, query_width), shaped(RANK, width), shaped(RANK, HD)),
-        [vmem()] * 8,
+        [vmem()] * 6,
         room=8,
     )(*sums)
     return (logits.T, query_down_grad, query_up_grad, value_down_grad, value_up_grad)

time: 120 us -> 122 us (1.017)
  waiting for transfers between devices: 18.3 us -> 22.3 us
  starting transfers between devices: 31.3 us -> 28.9 us
    all_to_all x1, waiting for transfers between devices: 0.19 us -> 4.91 us  [fast(): back = lax.all_to_all(mcot, 'tm', split_axis=0, concat_axis=0, tiled=True)]
    all_to_all x1, starting transfers between devices: 6.02 us -> 4.54 us  [fast(): back = lax.all_to_all(mcot, 'tm', split_axis=0, concat_axis=0, tiled=True)]
    ppermute x20 -> x19, starting transfers between devices: 19.5 us -> 18.5 us  [swap(): lax.ppermute(x, axis, [(i, i ^ bit) for i in range(lax.axis_size(axis))])]
    ppermute x20 -> x19, waiting for transfers between devices: 18.1 us -> 17.4 us  [swap(): lax.ppermute(x, axis, [(i, i ^ bit) for i in range(lax.axis_size(axis))])]
  transfers between devices with their start and end apart: 22 -> 21, of which waited for: 10 -> 10; matrix products, arithmetic and copies ran while one was open for 1% -> 1% of each run, Pallas kernels for 24% -> 24%
where the time goes in v7:
time: 122 us; the launch traced here: 121 us
  Pallas kernels  52.9 us (43%)
  starting transfers between devices  28.9 us (24%)
  waiting for transfers between devices  22.3 us (18%)
  blocking collectives  13.1 us (11%)
  local copies, waits for them, and re-layouts  2.48 us (2%)
    pallas_call x1, Pallas kernels, fast(): run(lambda *refs: attention_kernel(peers, heads, *refs), 'span_attention'...  22.8 us
    ppermute x19, starting transfers between devices, swap(): lax.ppermute(x, axis, [(i, i ^ bit) for i in range(lax.axis_size(axis))])  18.5 us
    ppermute x19, waiting for transfers between devices, swap(): lax.ppermute(x, axis, [(i, i ^ bit) for i in range(lax.axis_size(axis))])  17.4 us
    all_to_all x1, blocking collectives, fast(): lax.all_to_all(wanted, 'tm', split_axis=0, concat_axis=0, tiled=True)  13.1 us
    pallas_call x1, Pallas kernels, fast(): run(project_early_kernel, 'project_near_half', (shaped(tok_rows, query_wi...  9.02 us
    pallas_call x1, Pallas kernels, fast(): run(project_far_kernel, 'project_far_half', (shaped(tok_rows, query_width...  7.74 us
    all_to_all x1, starting transfers between devices, fast(): got = lax.all_to_all(pairs, 'tm', split_axis=0, concat_axis=0, tiled=True)  5.82 us
    all_to_all x1, waiting for transfers between devices, fast(): back = lax.all_to_all(mcot, 'tm', split_axis=0, concat_axis=0, tiled=True)  4.91 us
  transfers between devices with their start and end apart: 21, of which 10 were waited for; matrix products, arithmetic and copies ran while one was open for 1% of the time, Pallas kernels for 24%

profile of v7, /device:TPU:0, one launch (start us, length us, event | category | flops | bytes accessed | tf_op | source)
XLA Modules:
  0.0 121.2 jit_solution(8858703336815514727)
XLA Ops:
  0.6 0.5 collective-permute-start.2
  1.1 2.6 %collective-permute-start.3 = (bf16[512,896]{1,0:T(8,128)(2,1)}, bf16[512,896]{1,0:T(8,128)(2,1)}, u32[]{:S(2)}, u32[]{:S(2)}) collective-permute-start(bf16[512,896]{1,0:T(8,128)(2,1)} %memory_ref.1), channel_id=1, source_target_pairs={{0,2},{1,3},{2,0},{3,1},{4,6},{5,7},{6,4},{7,5},{8,10},{9,11},{10,... | collective-permute-start | bytes 2752520 | tf_op jit(solution)/shard_map/ppermute | solution.py:564
  3.7 0.2 collective-permute-start
  3.9 0.0 collective-permute-done.2.refs_3_
  3.9 4.3 %memory_near_half.1 = (f32[512,256]{1,0:T(8,128)}, f32[512,16]{1,0:T(8,128)}, s32[8]{0:T(128)}) custom-call(s32[1]{0:T(128)} %bitcast.refs_0_.place_ref, s32[4,8]{1,0:T(4,128)} %refs_1_.4, bf16[512,896]{1,0:T(8,128)(2,1)} %memory_ref.1, bf16[512,896]{1,0:T(8,128)(2,1)} %collective-permute-done.2.refs_3_, bf16[3584,128]{1,0:T(8,128)(2,1)} %refs_1_.7, ...), custom_call_target="tpu_custom_call" | custom-call | tf_op jit(solution)/shard_map/memory_near_half/pallas_call | solution.py:671
  8.2 0.7 copy.21
  8.9 13.1 %all_to_all.21 = s32[8,1,1]{2,1,0:T(1,128)S(1)} all-to-all(s32[8,1,1]{2,1,0:T(1,128)S(1)} %copy.21), channel_id=1, replica_groups=mesh['tm'=8,'heads'=4] {'tm'}, dimensions={0} | all-to-all | bytes 64 | tf_op jit(solution)/shard_map/all_to_all | solution.py:679
  22.0 0.8 reduce.refs_1_.refs_0_
  22.8 2.2 %collective-permute-done.3.refs_0_ = bf16[512,896]{1,0:T(8,128)(2,1)} collective-permute-done((bf16[512,896]{1,0:T(8,128)(2,1)}, bf16[512,896]{1,0:T(8,128)(2,1)}, u32[]{:S(2)}, u32[]{:S(2)}) %collective-permute-start.3) | collective-permute-done | bytes 917536 | tf_op jit(solution)/shard_map/ppermute | solution.py:564
  25.0 0.0 collective-permute-start.4
  25.0 0.0 collective-permute-done.x1
  25.0 1.8 %collective-permute-start.1 = (bf16[512,896]{1,0:T(8,128)(2,1)}, bf16[512,896]{1,0:T(8,128)(2,1)}, u32[]{:S(2)}, u32[]{:S(2)}) collective-permute-start(bf16[512,896]{1,0:T(8,128)(2,1)} %collective-permute-done.x1), channel_id=1, source_target_pairs={{0,2},{1,3},{2,0},{3,1},{4,6},{5,7},{6,4},{7,5},{8,10},{9,11},{10,... | collective-permute-start | bytes 2752520 | tf_op jit(solution)/shard_map/ppermute | solution.py:564
  26.8 3.0 %memory_far_quarter.1 = (f32[512,256]{1,0:T(8,128)}, f32[512,16]{1,0:T(8,128)}) custom-call(s32[1]{0:T(128)} %bitcast.refs_0_.place_ref, bf16[512,896]{1,0:T(8,128)(2,1)} %in_order.2.x2, f32[512,256]{1,0:T(8,128)} %get-tuple-element.30.acc_hbm, f32[512,16]{1,0:T(8,128)} %get-tuple-element.31.low_hbm, bf16[3584,128]{1,0:T(8,128)(2,1)} %refs_1_.7, ...), custom_call_target="tpu_custom_call" | custom-call | tf_op jit(solution)/shard_map/memory_far_quarter/pallas_call | solution.py:684
  29.9 0.0 collective-permute-done.4.refs_2_
  29.9 3.8 %memory_pairs.1.refs_7_ = bf16[8,272,128]{2,1,0:T(8,128)(2,1)} custom-call(s32[1]{0:T(128)} %bitcast.refs_0_.place_ref, s32[8]{0:T(128)} %reduce.refs_1_.refs_0_, bf16[512,896]{1,0:T(8,128)(2,1)} %collective-permute-done.4.refs_2_, f32[512,256]{1,0:T(8,128)} %get-tuple-element.32.refs_3_, f32[512,16]{1,0:T(8,128)} %get-tuple-element.33.refs_4_, ...), custom_call_target="tpu_custom_call" | custom-call | tf_op jit(solution)/shard_map/memory_pairs/pallas_call | solution.py:691
  33.7 5.8 %all-to-all-start.1 = ((bf16[8,272,128]{2,1,0:T(8,128)(2,1)}), bf16[8,272,128]{2,1,0:T(8,128)(2,1)}, u32[]{:S(2)}, u32[]{:S(2)}) async-start(bf16[8,272,128]{2,1,0:T(8,128)(2,1)} %memory_pairs.1.refs_7_), calls=%async_computation.1 | async-start | bytes 1114112 | tf_op jit(solution)/shard_map/all_to_all | solution.py:698
  39.5 9.0 %project_near_half.1 = (f32[512,896]{1,0:T(8,128)}, f32[512,256]{1,0:T(8,128)}, f32[512,32]{1,0:T(8,128)}, bf16[512,896]{1,0:T(8,128)(2,1)}, bf16[896,512]{1,0:T(8,128)(2,1)}) custom-call(s32[1]{0:T(128)} %bitcast.refs_0_.place_ref, bf16[512,896]{1,0:T(8,128)(2,1)} %slab_ref.1, bf16[512,896]{1,0:T(8,128)(2,1)} %collective-permute-done.x1, ...), custom_call_target="tpu_custom_call" | custom-call | tf_op jit(solution)/shard_map/project_near_half/pallas_call | solution.py:699
  48.6 0.0 collective-permute-done.1.refs_0_
  48.6 0.1 collective-permute-start.5
  48.7 2.8 %collective-permute-done.5.x2 = bf16[512,896]{1,0:T(8,128)(2,1)} collective-permute-done((bf16[512,896]{1,0:T(8,128)(2,1)}, bf16[512,896]{1,0:T(8,128)(2,1)}, u32[]{:S(2)}, u32[]{:S(2)}) %collective-permute-start.5) | collective-permute-done | bytes 917536 | tf_op jit(solution)/shard_map/ppermute | solution.py:564
  51.5 7.7 %project_far_half.1 = (bf16[512,896]{1,0:T(8,128)(2,1)}, bf16[512,128]{1,0:T(8,128)(2,1)}, bf16[512,128]{1,0:T(8,128)(2,1)}, bf16[32,512]{1,0:T(8,128)(2,1)}) custom-call(s32[1]{0:T(128)} %bitcast.refs_0_.place_ref, bf16[512,896]{1,0:T(8,128)(2,1)} %in_order.3.x3, bf16[512,896]{1,0:T(8,128)(2,1)} %collective-permute-done.5.x2, bf16[3584,896]{1,0:T(8,128)(2,1)} %refs_0_.6, ...), custom_call_target="tpu_custom_call" | custom-call | tf_op jit(solution)/shard_map/project_far_half/pallas_call | solution.py:714
  59.2 0.0 all-to-all-done.1.refs_5_
  59.2 0.0 copy-start
  59.2 0.0 copy-start.4
  59.2 0.0 copy-start.1
  59.2 22.8 %span_attention.1 = (f32[40,512]{1,0:T(8,128)}, f32[16,1024]{1,0:T(8,128)}, f32[8,16,128]{2,1,0:T(8,128)}) custom-call(s32[4]{0:T(128)} %refs_0_.7, bf16[512,896]{1,0:T(8,128)(2,1)} %get-tuple-element.37.refs_1_, bf16[512,128]{1,0:T(8,128)(2,1)} %get-tuple-element.38.refs_2_, bf16[512,128]{1,0:T(8,128)(2,1)} %get-tuple-element.39.refs_3_, ...), custom_call_target="tpu_custom_call" | custom-call | flops 10569646080 | bytes 1835008 | tf_op jit(solution)/shard_map/span_attention/pallas_call | solution.py:729
  82.0 1.0 collective-permute-start.8
  83.0 0.8 collective-permute-start.7
  83.9 0.1 collective-permute-start.6
  83.9 2.8 %collective-permute-done.8.c3 = f32[40,512]{1,0:T(8,128)S(1)} collective-permute-done((f32[40,512]{1,0:T(8,128)}, f32[40,512]{1,0:T(8,128)S(1)}, u32[]{:S(2)}, u32[]{:S(2)}) %collective-permute-start.8) | collective-permute-done | bytes 81952 | tf_op jit(solution)/shard_map/ppermute | solution.py:564
  86.7 2.1 %collective-permute-done.7.c2 = f32[40,512]{1,0:T(8,128)S(1)} collective-permute-done((f32[40,512]{1,0:T(8,128)}, f32[40,512]{1,0:T(8,128)S(1)}, u32[]{:S(2)}, u32[]{:S(2)}) %collective-permute-start.7) | collective-permute-done | bytes 81952 | tf_op jit(solution)/shard_map/ppermute | solution.py:564
  88.8 0.0 collective-permute-done.6.c1
  88.8 0.0 copy-done
  88.8 0.0 copy-start.2
  88.8 0.9 copy-done.2
  89.7 0.8 copy-done.3
  90.5 0.8 first_down.1
  91.3 2.0 %collective-permute-start.9 = (f32[16,1920]{1,0:T(8,128)S(1)}, f32[16,1920]{1,0:T(8,128)S(1)}, u32[]{:S(2)}, u32[]{:S(2)}) collective-permute-start(f32[16,1920]{1,0:T(8,128)S(1)} %get-tuple-element.46), channel_id=1, source_target_pairs={{0,4},{4,0},{8,12},{12,8},{16,20},{20,16},{24,28},{28,24},{1,5},{5... | collective-permute-start | bytes 368648 | tf_op jit(solution)/shard_map/ppermute | solution.py:564
  93.3 4.5 %all-to-all-start.2 = ((f32[8,16,128]{2,1,0:T(8,128)}), f32[8,16,128]{2,1,0:T(8,128)S(1)}, u32[]{:S(2)}, u32[]{:S(2)}) async-start(f32[8,16,128]{2,1,0:T(8,128)} %get-tuple-element.47), calls=%async_computation.2 | async-start | bytes 131072 | tf_op jit(solution)/shard_map/all_to_all | solution.py:763
  97.8 0.0 collective-permute-done.9
  97.9 2.1 %collective-permute-start.10 = (f32[16,1920]{1,0:T(8,128)S(1)}, f32[16,1920]{1,0:T(8,128)S(1)}, u32[]{:S(2)}, u32[]{:S(2)}) collective-permute-start(f32[16,1920]{1,0:T(8,128)S(1)} %add.9), channel_id=1, source_target_pairs={{0,8},{4,12},{8,0},{12,4},{16,24},{20,28},{24,16},{28,20},{1,9},{5... | collective-permute-start | bytes 368648 | tf_op jit(solution)/shard_map/ppermute | solution.py:564
  100.0 4.9 %all-to-all-done.2.refs_1_ = f32[8,16,128]{2,1,0:T(8,128)S(1)} async-done(((f32[8,16,128]{2,1,0:T(8,128)}), f32[8,16,128]{2,1,0:T(8,128)S(1)}, u32[]{:S(2)}, u32[]{:S(2)}) %all-to-all-start.2) | async-done | bytes 65568 | tf_op jit(solution)/shard_map/all_to_all | solution.py:763
  104.9 0.0 copy-done.4
  104.9 0.6 owned_cotangent.1.c0
  105.4 0.1 collective-permute-start.14
  105.5 1.1 collective-permute-start.13
  106.6 0.8 collective-permute-start.12
  107.4 1.5 %collective-permute-done.14.c3 = f32[16,512]{1,0:T(8,128)S(1)} collective-permute-done((f32[16,512]{1,0:T(8,128)S(1)}, f32[16,512]{1,0:T(8,128)S(1)}, u32[]{:S(2)}, u32[]{:S(2)}) %collective-permute-start.14) | collective-permute-done | bytes 32800 | tf_op jit(solution)/shard_map/ppermute | solution.py:564
  108.8 0.9 collective-permute-done.13.c2
  109.8 0.0 collective-permute-done.12.c1
  109.8 0.0 copy-done.1
  109.8 0.2 second_down.1
  110.0 0.4 collective-permute-start.15
  110.5 0.0 collective-permute-done.10
  110.5 0.5 collective-permute-start.11
  111.0 3.2 %collective-permute-done.15 = f32[16,896]{1,0:T(8,128)S(1)} collective-permute-done((f32[16,896]{1,0:T(8,128)S(1)}, f32[16,896]{1,0:T(8,128)S(1)}, u32[]{:S(2)}, u32[]{:S(2)}) %collective-permute-start.15) | collective-permute-done | bytes 57376 | tf_op jit(solution)/shard_map/ppermute | solution.py:564
  114.3 0.7 collective-permute-start.18
  115.0 1.0 collective-permute-start.17
  116.0 2.7 %collective-permute-start.16 = (bf16[16,896]{1,0:T(8,128)(2,1)S(1)}, bf16[16,896]{1,0:T(8,128)(2,1)S(1)}, u32[]{:S(2)}, u32[]{:S(2)}) collective-permute-start(bf16[16,896]{1,0:T(8,128)(2,1)S(1)} %add_convert_fusion.1.refs_2_), channel_id=1, source_target_pairs={{0,8},{4,12},{8,0},{12,4},{16,24},{20,28},{24,16},{28,20},{1,9},{5... | collective-permute-start | bytes 86024 | tf_op jit(solution)/shard_map/ppermute | solution.py:564
  118.7 1.3 %collective-permute-done.18.refs_5_ = bf16[16,896]{1,0:T(8,128)(2,1)S(1)} collective-permute-done((bf16[16,896]{1,0:T(8,128)(2,1)S(1)}, bf16[16,896]{1,0:T(8,128)(2,1)S(1)}, u32[]{:S(2)}, u32[]{:S(2)}) %collective-permute-start.18) | collective-permute-done | bytes 28704 | tf_op jit(solution)/shard_map/ppermute | solution.py:564
  120.0 0.0 collective-permute-done.17.refs_4_
  120.1 0.5 collective-permute-done.16.refs_3_
  120.6 0.0 collective-permute-done.11.refs_1_
  120.6 0.7 finish_outputs.1
  (6 shorter events, 0.0 us)
Async XLA Ops:
  0.6 3.3 %collective-permute-start.2 = (bf16[512,896]{1,0:T(8,128)(2,1)}, bf16[512,896]{1,0:T(8,128)(2,1)}, u32[]{:S(2)}, u32[]{:S(2)}) collective-permute-start(bf16[512,896]{1,0:T(8,128)(2,1)} %memory_ref.1), channel_id=1, source_target_pairs={{0,1},{1,0},{2,3},{3,2},{4,5},{5,4},{6,7},{7,6},{8,9},{9,8},{10,11... | collective-permute-start | bytes 2752520 | tf_op jit(solution)/shard_map/ppermute | solution.py:564
  1.1 23.9 %collective-permute-start.3 = (bf16[512,896]{1,0:T(8,128)(2,1)}, bf16[512,896]{1,0:T(8,128)(2,1)}, u32[]{:S(2)}, u32[]{:S(2)}) collective-permute-start(bf16[512,896]{1,0:T(8,128)(2,1)} %memory_ref.1), channel_id=1, source_target_pairs={{0,2},{1,3},{2,0},{3,1},{4,6},{5,7},{6,4},{7,5},{8,10},{9,11},{10,... | collective-permute-start | bytes 2752520 | tf_op jit(solution)/shard_map/ppermute | solution.py:564
  3.7 21.3 %collective-permute-start = (bf16[512,896]{1,0:T(8,128)(2,1)}, bf16[512,896]{1,0:T(8,128)(2,1)}, u32[]{:S(2)}, u32[]{:S(2)}) collective-permute-start(bf16[512,896]{1,0:T(8,128)(2,1)} %slab_ref.1), channel_id=1, source_target_pairs={{0,1},{1,0},{2,3},{3,2},{4,5},{5,4},{6,7},{7,6},{8,9},{9,8},{10,11... | collective-permute-start | bytes 2752520 | tf_op jit(solution)/shard_map/ppermute | solution.py:564
  25.0 4.9 %collective-permute-start.4 = (bf16[512,896]{1,0:T(8,128)(2,1)}, bf16[512,896]{1,0:T(8,128)(2,1)}, u32[]{:S(2)}, u32[]{:S(2)}) collective-permute-start(bf16[512,896]{1,0:T(8,128)(2,1)} %in_order.2.x2), channel_id=1, source_target_pairs={{0,1},{1,0},{2,3},{3,2},{4,5},{5,4},{6,7},{7,6},{8,9},{9,8},{10,11... | collective-permute-start | bytes 2752520 | tf_op jit(solution)/shard_map/ppermute | solution.py:564
  25.0 23.5 %collective-permute-start.1 = (bf16[512,896]{1,0:T(8,128)(2,1)}, bf16[512,896]{1,0:T(8,128)(2,1)}, u32[]{:S(2)}, u32[]{:S(2)}) collective-permute-start(bf16[512,896]{1,0:T(8,128)(2,1)} %collective-permute-done.x1), channel_id=1, source_target_pairs={{0,2},{1,3},{2,0},{3,1},{4,6},{5,7},{6,4},{7,5},{8,10},{9,11},{10,... | collective-permute-start | bytes 2752520 | tf_op jit(solution)/shard_map/ppermute | solution.py:564
  33.7 25.5 %all-to-all-start.1 = ((bf16[8,272,128]{2,1,0:T(8,128)(2,1)}), bf16[8,272,128]{2,1,0:T(8,128)(2,1)}, u32[]{:S(2)}, u32[]{:S(2)}) async-start(bf16[8,272,128]{2,1,0:T(8,128)(2,1)} %memory_pairs.1.refs_7_), calls=%async_computation.1 | async-start | bytes 1114112 | tf_op jit(solution)/shard_map/all_to_all | solution.py:698
  48.6 2.9 %collective-permute-start.5 = (bf16[512,896]{1,0:T(8,128)(2,1)}, bf16[512,896]{1,0:T(8,128)(2,1)}, u32[]{:S(2)}, u32[]{:S(2)}) collective-permute-start(bf16[512,896]{1,0:T(8,128)(2,1)} %in_order.3.x3), channel_id=1, source_target_pairs={{0,1},{1,0},{2,3},{3,2},{4,5},{5,4},{6,7},{7,6},{8,9},{9,8},{10,11... | collective-permute-start | bytes 2752520 | tf_op jit(solution)/shard_map/ppermute | solution.py:564
  59.2 29.6 %copy-start = (bf16[512,896]{1,0:T(8,128)(2,1)S(1)}, bf16[512,896]{1,0:T(8,128)(2,1)}, u32[]{:S(2)}) copy-start(bf16[512,896]{1,0:T(8,128)(2,1)} %slab_ref.1) | copy-start | bytes 2752516
  59.2 45.6 %copy-start.4 = (s32[8]{0:T(128)S(1)}, s32[8]{0:T(128)}, u32[]{:S(2)}) copy-start(s32[8]{0:T(128)} %reduce.refs_1_.refs_0_) | copy-start | bytes 100
  59.2 50.6 %copy-start.1 = (bf16[512,896]{1,0:T(8,128)(2,1)S(1)}, bf16[512,896]{1,0:T(8,128)(2,1)}, u32[]{:S(2)}) copy-start(bf16[512,896]{1,0:T(8,128)(2,1)} %memory_ref.1) | copy-start | bytes 2752516
  82.0 4.7 %collective-permute-start.8 = (f32[40,512]{1,0:T(8,128)}, f32[40,512]{1,0:T(8,128)S(1)}, u32[]{:S(2)}, u32[]{:S(2)}) collective-permute-start(f32[40,512]{1,0:T(8,128)} %get-tuple-element.43.c0), channel_id=1, source_target_pairs={{0,3},{1,2},{2,1},{3,0},{4,7},{5,6},{6,5},{7,4},{8,11},{9,10},{10,... | collective-permute-start | bytes 245768 | tf_op jit(solution)/shard_map/ppermute | solution.py:564
  83.0 5.8 %collective-permute-start.7 = (f32[40,512]{1,0:T(8,128)}, f32[40,512]{1,0:T(8,128)S(1)}, u32[]{:S(2)}, u32[]{:S(2)}) collective-permute-start(f32[40,512]{1,0:T(8,128)} %get-tuple-element.43.c0), channel_id=1, source_target_pairs={{0,2},{1,3},{2,0},{3,1},{4,6},{5,7},{6,4},{7,5},{8,10},{9,11},{10,... | collective-permute-start | bytes 245768 | tf_op jit(solution)/shard_map/ppermute | solution.py:564
  83.9 4.9 %collective-permute-start.6 = (f32[40,512]{1,0:T(8,128)}, f32[40,512]{1,0:T(8,128)S(1)}, u32[]{:S(2)}, u32[]{:S(2)}) collective-permute-start(f32[40,512]{1,0:T(8,128)} %get-tuple-element.43.c0), channel_id=1, source_target_pairs={{0,1},{1,0},{2,3},{3,2},{4,5},{5,4},{6,7},{7,6},{8,9},{9,8},{10,11... | collective-permute-start | bytes 245768 | tf_op jit(solution)/shard_map/ppermute | solution.py:564
  88.8 0.9 copy-start.2
  89.7 0.8 copy-start.3
  91.3 6.6 %collective-permute-start.9 = (f32[16,1920]{1,0:T(8,128)S(1)}, f32[16,1920]{1,0:T(8,128)S(1)}, u32[]{:S(2)}, u32[]{:S(2)}) collective-permute-start(f32[16,1920]{1,0:T(8,128)S(1)} %get-tuple-element.46), channel_id=1, source_target_pairs={{0,4},{4,0},{8,12},{12,8},{16,20},{20,16},{24,28},{28,24},{1,5},{5... | collective-permute-start | bytes 368648 | tf_op jit(solution)/shard_map/ppermute | solution.py:564
  93.3 11.6 %all-to-all-start.2 = ((f32[8,16,128]{2,1,0:T(8,128)}), f32[8,16,128]{2,1,0:T(8,128)S(1)}, u32[]{:S(2)}, u32[]{:S(2)}) async-start(f32[8,16,128]{2,1,0:T(8,128)} %get-tuple-element.47), calls=%async_computation.2 | async-start | bytes 131072 | tf_op jit(solution)/shard_map/all_to_all | solution.py:763
  97.9 12.6 %collective-permute-start.10 = (f32[16,1920]{1,0:T(8,128)S(1)}, f32[16,1920]{1,0:T(8,128)S(1)}, u32[]{:S(2)}, u32[]{:S(2)}) collective-permute-start(f32[16,1920]{1,0:T(8,128)S(1)} %add.9), channel_id=1, source_target_pairs={{0,8},{4,12},{8,0},{12,4},{16,24},{20,28},{24,16},{28,20},{1,9},{5... | collective-permute-start | bytes 368648 | tf_op jit(solution)/shard_map/ppermute | solution.py:564
  105.4 3.4 %collective-permute-start.14 = (f32[16,512]{1,0:T(8,128)S(1)}, f32[16,512]{1,0:T(8,128)S(1)}, u32[]{:S(2)}, u32[]{:S(2)}) collective-permute-start(f32[16,512]{1,0:T(8,128)S(1)} %owned_cotangent.1.c0), channel_id=1, source_target_pairs={{0,3},{1,2},{2,1},{3,0},{4,7},{5,6},{6,5},{7,4},{8,11},{9,10},{10,... | collective-permute-start | bytes 98312 | tf_op jit(solution)/shard_map/ppermute | solution.py:564
  105.5 4.3 %collective-permute-start.13 = (f32[16,512]{1,0:T(8,128)S(1)}, f32[16,512]{1,0:T(8,128)S(1)}, u32[]{:S(2)}, u32[]{:S(2)}) collective-permute-start(f32[16,512]{1,0:T(8,128)S(1)} %owned_cotangent.1.c0), channel_id=1, source_target_pairs={{0,2},{1,3},{2,0},{3,1},{4,6},{5,7},{6,4},{7,5},{8,10},{9,11},{10,... | collective-permute-start | bytes 98312 | tf_op jit(solution)/shard_map/ppermute | solution.py:564
  106.6 3.2 %collective-permute-start.12 = (f32[16,512]{1,0:T(8,128)S(1)}, f32[16,512]{1,0:T(8,128)S(1)}, u32[]{:S(2)}, u32[]{:S(2)}) collective-permute-start(f32[16,512]{1,0:T(8,128)S(1)} %owned_cotangent.1.c0), channel_id=1, source_target_pairs={{0,1},{1,0},{2,3},{3,2},{4,5},{5,4},{6,7},{7,6},{8,9},{9,8},{10,11... | collective-permute-start | bytes 98312 | tf_op jit(solution)/shard_map/ppermute | solution.py:564
  110.0 4.2 %collective-permute-start.15 = (f32[16,896]{1,0:T(8,128)S(1)}, f32[16,896]{1,0:T(8,128)S(1)}, u32[]{:S(2)}, u32[]{:S(2)}) collective-permute-start(f32[16,896]{1,0:T(8,128)S(1)} %second_down.1), channel_id=1, source_target_pairs={{0,4},{4,0},{8,12},{12,8},{16,20},{20,16},{24,28},{28,24},{1,5},{5... | collective-permute-start | bytes 172040 | tf_op jit(solution)/shard_map/ppermute | solution.py:564
  110.5 10.1 %collective-permute-start.11 = (bf16[16,1920]{1,0:T(8,128)(2,1)S(1)}, bf16[16,1920]{1,0:T(8,128)(2,1)S(1)}, u32[]{:S(2)}, u32[]{:S(2)}) collective-permute-start(bf16[16,1920]{1,0:T(8,128)(2,1)S(1)} %add_convert_fusion.refs_0_), channel_id=1, source_target_pairs={{0,16},{4,20},{8,24},{12,28},{16,0},{20,4},{24,8},{28,12},{1,17},{... | collective-permute-start | bytes 184328 | tf_op jit(solution)/shard_map/ppermute | solution.py:564
  114.3 5.8 %collective-permute-start.18 = (bf16[16,896]{1,0:T(8,128)(2,1)S(1)}, bf16[16,896]{1,0:T(8,128)(2,1)S(1)}, u32[]{:S(2)}, u32[]{:S(2)}) collective-permute-start(bf16[16,896]{1,0:T(8,128)(2,1)S(1)} %add_convert_fusion.1.refs_2_), channel_id=1, source_target_pairs={{0,24},{4,28},{8,16},{12,20},{16,8},{20,12},{24,0},{28,4},{1,25},{... | collective-permute-start | bytes 86024 | tf_op jit(solution)/shard_map/ppermute | solution.py:564
  115.0 5.1 %collective-permute-start.17 = (bf16[16,896]{1,0:T(8,128)(2,1)S(1)}, bf16[16,896]{1,0:T(8,128)(2,1)S(1)}, u32[]{:S(2)}, u32[]{:S(2)}) collective-permute-start(bf16[16,896]{1,0:T(8,128)(2,1)S(1)} %add_convert_fusion.1.refs_2_), channel_id=1, source_target_pairs={{0,16},{4,20},{8,24},{12,28},{16,0},{20,4},{24,8},{28,12},{1,17},{... | collective-permute-start | bytes 86024 | tf_op jit(solution)/shard_map/ppermute | solution.py:564
  116.0 4.6 %collective-permute-start.16 = (bf16[16,896]{1,0:T(8,128)(2,1)S(1)}, bf16[16,896]{1,0:T(8,128)(2,1)S(1)}, u32[]{:S(2)}, u32[]{:S(2)}) collective-permute-start(bf16[16,896]{1,0:T(8,128)(2,1)S(1)} %add_convert_fusion.1.refs_2_), channel_id=1, source_target_pairs={{0,8},{4,12},{8,0},{12,4},{16,24},{20,28},{24,16},{28,20},{1,9},{5... | collective-permute-start | bytes 86024 | tf_op jit(solution)/shard_map/ppermute | solution.py:564

commit v8 on v7

--- a/solution.py
+++ b/solution.py
@@ -410,9 +410,9 @@
 
 def attention_kernel(peers, heads, bound_ref, *refs):
     parts, got, grad_hbm, grad_t_hbm = refs[:4], refs[4], refs[5], refs[6]
-    qup_ref, vup_ref, tag_ref, cot_ref, up_ref, mcot_ref = refs[7:13]
+    qup_ref, vup_ref, tag_ref, cot_ref, mine_ref, mcot_ref = refs[7:13]
     (q_s, k_own, v_own, low_s, low_m_s, grad_ref, grad_t_ref, k_all, v_all, kt_all, vt_all, kt_own, vt_own, bias_s, s_s, dp_s,
-     p_s, ds_s, att_s, dq_s, dv_s, more_sems) = refs[13:]
+     p_s, ds_s, att_s, dq_s, dv_s, up_ref, more_sems) = refs[13:]
     seen = peers * BLK
     pairs = []
     for b in range(peers):
@@ -523,6 +523,11 @@
     up_ref[:, query_width:] += dot_nt(low_m, dv, HIGHEST)
     for b in range(peers):
         mcot_ref[b] = mcot[:, b * BLK : (b + 1) * BLK]
+    at, wide = cot_ref.shape
+    mine_ref[:at, :] = cot_ref[...]
+    for n in range(0, up_ref.shape[1], wide):
+        mine_ref[at : at + RANK, :] = up_ref[:, n : n + wide]
+        at += RANK
 
 
 def own_kernel(peers, asked_ref, back_ref, out_ref, sum_s):
@@ -533,17 +538,20 @@
     out_ref[...] = jnp.concatenate([sum_s[m] for m in range(sum_s.shape[0])], 1)
 
 
-def first_down_kernel(c0, c1, c2, c3, slab_ref, up_ref, logit_ref, query_ref, value_ref):
-    cot = (c0[...] + c1[...]) + (c2[...] + c3[...])
+def first_down_kernel(mine_ref, c1, c2, c3, slab_ref, dep_ref, logit_ref, query_ref, value_ref):
+    own, wide = c1.shape
+    cot = (mine_ref[:own, :] + c1[...]) + (c2[...] + c3[...])
     logit_ref[...] = cot[2 * RANK :]
     both = dot_nn(cot[: 2 * RANK].astype(jnp.bfloat16), slab_ref[...])
     width = both.shape[1]
     query_ref[:, :width] = both[:RANK]
-    query_ref[:, width:] = up_ref[...]
+    for n, at in enumerate(range(own, mine_ref.shape[0], RANK)):
+        query_ref[:, width + n * wide : width + (n + 1) * wide] = mine_ref[at : at + RANK, :]
     value_ref[...] = both[RANK:]
 
 
-def second_down_kernel(c0, c1, c2, c3, memory_ref, value_ref, out_ref):
+def second_down_kernel(c0, c1, c2, c3, memory_ref, value_ref, q0, q1, out_ref, query_ref):
+    query_ref[...] = q0[...] + q1[...]
     cot = (c0[...] + c1[...]) + (c2[...] + c3[...])
     out_ref[...] = value_ref[...] + dot_nn(cot.astype(jnp.bfloat16), memory_ref[...])
 
@@ -726,10 +734,14 @@
 
     seen = peers * BLK
     total = seen + BLK
-    cot, ups, mcot = run(
+    cot, mine, mcot = run(
         lambda *refs: attention_kernel(peers, heads, *refs),
         "span_attention",
-        (shaped(2 * RANK + tags, tok_rows), shaped(RANK, query_width + HD), shaped(peers, RANK, BLK)),
+        (
+            shaped(2 * RANK + tags, tok_rows),
+            shaped(2 * RANK + tags + RANK * (query_width + HD) // tok_rows, tok_rows),
+            shaped(peers, RANK, BLK),
+        ),
         [smem()] + [anywhere()] * 7 + [vmem()] * 3,
         [
             pltpu.VMEM((tok_rows, query_width), bf16),
@@ -753,6 +765,7 @@
             pltpu.VMEM((PAIR * BLK, query_width), bf16),
             pltpu.VMEM((PAIR * BLK, query_width), bf16),
             pltpu.VMEM((HD, seen), f32),
+            pltpu.VMEM((RANK, query_width + HD), f32),
             pltpu.SemaphoreType.DMA((3 * peers + 6,)),
         ],
         flops=20 * tok_rows * query_width * total,
@@ -761,7 +774,7 @@
     )(boundary, *parts, got, grad, grad_t, query_up, value_up, tag_t)
 
     back = lax.all_to_all(mcot, "tm", split_axis=0, concat_axis=0, tiled=True)
-    cots = [cot] + [swap(cot, d) for d in range(1, 4)]
+    cots = [mine] + [swap(cot, d) for d in range(1, 4)]
     own = run(
         lambda *refs: own_kernel(peers, *refs),
         "owned_cotangent",
@@ -773,23 +786,22 @@
     logits, query_sum, value_part = run(
         first_down_kernel,
         "first_down",
-        (shaped(tags, tok_rows), shaped(RANK, width + ups.shape[1]), shaped(RANK, width)),
-        [vmem()] * 6,
+        (shaped(tags, tok_rows), shaped(RANK, width + query_width + HD), shaped(RANK, width)),
+        [vmem()] * 5 + [anywhere()],
         flops=4 * RANK * tok_rows * width,
         moved=2 * tok_rows * width,
         room=8,
-    )(*cots, slab_tokens, ups)
+    )(*cots, slab_tokens, own)
     owns = [own] + [swap(own, d) for d in range(1, 4)]
-    value_sum = run(
+    value_sum, query_sum = run(
         second_down_kernel,
         "second_down",
-        shaped(RANK, width),
-        [vmem()] * 6,
+        (shaped(RANK, width), shaped(*query_sum.shape)),
+        [vmem()] * 8,
         flops=2 * RANK * mem_rows * width,
         moved=2 * mem_rows * width,
         room=8,
-    )(*owns, memory, value_part)
-    query_sum = query_sum + swap(query_sum, 1, "tm")
+    )(*owns, memory, value_part, query_sum, swap(query_sum, 1, "tm"))
     query_sum = (query_sum + swap(query_sum, 2, "tm")).astype(bf16)
     value_sum = (value_sum + swap(value_sum, 1, "tm")).astype(bf16)
     sums = [query_sum, swap(query_sum, 4, "tm"), value_sum] + [swap(value_sum, bit, "tm") for bit in (2, 4, 6)]

time: 122 us -> 118 us (0.967)
  waiting for transfers between devices: 22.3 us -> 17.7 us
  starting transfers between devices: 28.9 us -> 30.7 us
    ppermute x19, waiting for transfers between devices: 17.4 us -> 12.7 us  [swap(): lax.ppermute(x, axis, [(i, i ^ bit) for i in range(lax.axis_size(axis))])]
    all_to_all x1, starting transfers between devices: 4.54 us -> 5.99 us  [fast(): back = lax.all_to_all(mcot, 'tm', split_axis=0, concat_axis=0, tiled=True)]
  transfers between devices with their start and end apart: 21 -> 21, of which waited for: 10 -> 9; matrix products, arithmetic and copies ran while one was open for 1% -> 1% of each run, Pallas kernels for 24% -> 24%
where the time goes in v8:
time: 118 us
  Pallas kernels  53 us (45%)
  starting transfers between devices  30.7 us (26%)
  waiting for transfers between devices  17.7 us (15%)
  blocking collectives  13.1 us (11%)
  local copies, waits for them, and re-layouts  1.65 us (1%)
    pallas_call x1, Pallas kernels, fast(): run(lambda *refs: attention_kernel(peers, heads, *refs), 'span_attention'...  22.8 us
    ppermute x19, starting transfers between devices, swap(): lax.ppermute(x, axis, [(i, i ^ bit) for i in range(lax.axis_size(axis))])  18.9 us
    all_to_all x1, blocking collectives, fast(): lax.all_to_all(wanted, 'tm', split_axis=0, concat_axis=0, tiled=True)  13.1 us
    ppermute x19, waiting for transfers between devices, swap(): lax.ppermute(x, axis, [(i, i ^ bit) for i in range(lax.axis_size(axis))])  12.7 us
    pallas_call x1, Pallas kernels, fast(): run(project_early_kernel, 'project_near_half', (shaped(tok_rows, query_wi...  9.03 us
    pallas_call x1, Pallas kernels, fast(): run(project_far_kernel, 'project_far_half', (shaped(tok_rows, query_width...  7.74 us
    all_to_all x1, starting transfers between devices, fast(): back = lax.all_to_all(mcot, 'tm', split_axis=0, concat_axis=0, tiled=True)  5.99 us
    all_to_all x1, starting transfers between devices, fast(): got = lax.all_to_all(pairs, 'tm', split_axis=0, concat_axis=0, tiled=True)  5.82 us
  transfers between devices with their start and end apart: 21, of which 9 were waited for; matrix products, arithmetic and copies ran while one was open for 1% of the time, Pallas kernels for 24%

profile of v8, /device:TPU:0, one launch (start us, length us, event | category | flops | bytes accessed | tf_op | source)
XLA Modules:
  0.0 117.8 jit_solution(10651457449710857570)
XLA Ops:
  0.6 0.5 collective-permute-start.2
  1.1 2.6 %collective-permute-start.3 = (bf16[512,896]{1,0:T(8,128)(2,1)}, bf16[512,896]{1,0:T(8,128)(2,1)}, u32[]{:S(2)}, u32[]{:S(2)}) collective-permute-start(bf16[512,896]{1,0:T(8,128)(2,1)} %memory_ref.1), channel_id=1, source_target_pairs={{0,2},{1,3},{2,0},{3,1},{4,6},{5,7},{6,4},{7,5},{8,10},{9,11},{10,... | collective-permute-start | bytes 2752520 | tf_op jit(solution)/shard_map/ppermute | solution.py:572
  3.7 0.2 collective-permute-start
  3.9 0.0 collective-permute-done.2.refs_3_
  3.9 4.3 %memory_near_half.1 = (f32[512,256]{1,0:T(8,128)}, f32[512,16]{1,0:T(8,128)}, s32[8]{0:T(128)}) custom-call(s32[1]{0:T(128)} %bitcast.refs_0_.place_ref, s32[4,8]{1,0:T(4,128)} %refs_1_.4, bf16[512,896]{1,0:T(8,128)(2,1)} %memory_ref.1, bf16[512,896]{1,0:T(8,128)(2,1)} %collective-permute-done.2.refs_3_, bf16[3584,128]{1,0:T(8,128)(2,1)} %refs_1_.7, ...), custom_call_target="tpu_custom_call" | custom-call | tf_op jit(solution)/shard_map/memory_near_half/pallas_call | solution.py:679
  8.2 0.7 copy.21
  8.9 13.1 %all_to_all.21 = s32[8,1,1]{2,1,0:T(1,128)S(1)} all-to-all(s32[8,1,1]{2,1,0:T(1,128)S(1)} %copy.21), channel_id=1, replica_groups=mesh['tm'=8,'heads'=4] {'tm'}, dimensions={0} | all-to-all | bytes 64 | tf_op jit(solution)/shard_map/all_to_all | solution.py:687
  22.0 0.8 reduce.refs_1_.refs_0_
  22.8 2.2 %collective-permute-done.3.refs_0_ = bf16[512,896]{1,0:T(8,128)(2,1)} collective-permute-done((bf16[512,896]{1,0:T(8,128)(2,1)}, bf16[512,896]{1,0:T(8,128)(2,1)}, u32[]{:S(2)}, u32[]{:S(2)}) %collective-permute-start.3) | collective-permute-done | bytes 917536 | tf_op jit(solution)/shard_map/ppermute | solution.py:572
  25.0 0.0 collective-permute-start.4
  25.0 0.0 collective-permute-done.x1
  25.0 1.8 %collective-permute-start.1 = (bf16[512,896]{1,0:T(8,128)(2,1)}, bf16[512,896]{1,0:T(8,128)(2,1)}, u32[]{:S(2)}, u32[]{:S(2)}) collective-permute-start(bf16[512,896]{1,0:T(8,128)(2,1)} %collective-permute-done.x1), channel_id=1, source_target_pairs={{0,2},{1,3},{2,0},{3,1},{4,6},{5,7},{6,4},{7,5},{8,10},{9,11},{10,... | collective-permute-start | bytes 2752520 | tf_op jit(solution)/shard_map/ppermute | solution.py:572
  26.8 3.0 %memory_far_quarter.1 = (f32[512,256]{1,0:T(8,128)}, f32[512,16]{1,0:T(8,128)}) custom-call(s32[1]{0:T(128)} %bitcast.refs_0_.place_ref, bf16[512,896]{1,0:T(8,128)(2,1)} %in_order.2.x2, f32[512,256]{1,0:T(8,128)} %get-tuple-element.32.acc_hbm, f32[512,16]{1,0:T(8,128)} %get-tuple-element.33.low_hbm, bf16[3584,128]{1,0:T(8,128)(2,1)} %refs_1_.7, ...), custom_call_target="tpu_custom_call" | custom-call | tf_op jit(solution)/shard_map/memory_far_quarter/pallas_call | solution.py:692
  29.9 0.0 collective-permute-done.4.refs_2_
  29.9 3.8 %memory_pairs.1.refs_7_ = bf16[8,272,128]{2,1,0:T(8,128)(2,1)} custom-call(s32[1]{0:T(128)} %bitcast.refs_0_.place_ref, s32[8]{0:T(128)} %reduce.refs_1_.refs_0_, bf16[512,896]{1,0:T(8,128)(2,1)} %collective-permute-done.4.refs_2_, f32[512,256]{1,0:T(8,128)} %get-tuple-element.34.refs_3_, f32[512,16]{1,0:T(8,128)} %get-tuple-element.35.refs_4_, ...), custom_call_target="tpu_custom_call" | custom-call | tf_op jit(solution)/shard_map/memory_pairs/pallas_call | solution.py:699
  33.7 5.8 %all-to-all-start.1 = ((bf16[8,272,128]{2,1,0:T(8,128)(2,1)}), bf16[8,272,128]{2,1,0:T(8,128)(2,1)}, u32[]{:S(2)}, u32[]{:S(2)}) async-start(bf16[8,272,128]{2,1,0:T(8,128)(2,1)} %memory_pairs.1.refs_7_), calls=%async_computation.1 | async-start | bytes 1114112 | tf_op jit(solution)/shard_map/all_to_all | solution.py:706
  39.5 9.0 %project_near_half.1 = (f32[512,896]{1,0:T(8,128)}, f32[512,256]{1,0:T(8,128)}, f32[512,32]{1,0:T(8,128)}, bf16[512,896]{1,0:T(8,128)(2,1)}, bf16[896,512]{1,0:T(8,128)(2,1)}) custom-call(s32[1]{0:T(128)} %bitcast.refs_0_.place_ref, bf16[512,896]{1,0:T(8,128)(2,1)} %slab_ref.1, bf16[512,896]{1,0:T(8,128)(2,1)} %collective-permute-done.x1, ...), custom_call_target="tpu_custom_call" | custom-call | tf_op jit(solution)/shard_map/project_near_half/pallas_call | solution.py:707
  48.6 0.0 collective-permute-done.1.refs_0_
  48.6 0.1 collective-permute-start.5
  48.7 2.8 %collective-permute-done.5.x2 = bf16[512,896]{1,0:T(8,128)(2,1)} collective-permute-done((bf16[512,896]{1,0:T(8,128)(2,1)}, bf16[512,896]{1,0:T(8,128)(2,1)}, u32[]{:S(2)}, u32[]{:S(2)}) %collective-permute-start.5) | collective-permute-done | bytes 917536 | tf_op jit(solution)/shard_map/ppermute | solution.py:572
  51.5 7.7 %project_far_half.1 = (bf16[512,896]{1,0:T(8,128)(2,1)}, bf16[512,128]{1,0:T(8,128)(2,1)}, bf16[512,128]{1,0:T(8,128)(2,1)}, bf16[32,512]{1,0:T(8,128)(2,1)}) custom-call(s32[1]{0:T(128)} %bitcast.refs_0_.place_ref, bf16[512,896]{1,0:T(8,128)(2,1)} %in_order.3.x3, bf16[512,896]{1,0:T(8,128)(2,1)} %collective-permute-done.5.x2, bf16[3584,896]{1,0:T(8,128)(2,1)} %refs_0_.6, ...), custom_call_target="tpu_custom_call" | custom-call | tf_op jit(solution)/shard_map/project_far_half/pallas_call | solution.py:722
  59.2 0.0 all-to-all-done.1.refs_5_
  59.2 0.0 copy-start.3
  59.2 0.0 copy-start
  59.2 0.0 copy-start.1
  59.2 22.8 %span_attention.1 = (f32[40,512]{1,0:T(8,128)}, f32[72,512]{1,0:T(8,128)}, f32[8,16,128]{2,1,0:T(8,128)}) custom-call(s32[4]{0:T(128)} %refs_0_.7, bf16[512,896]{1,0:T(8,128)(2,1)} %get-tuple-element.39.refs_1_, bf16[512,128]{1,0:T(8,128)(2,1)} %get-tuple-element.40.refs_2_, bf16[512,128]{1,0:T(8,128)(2,1)} %get-tuple-element.41.refs_3_, ...), custom_call_target="tpu_custom_call" | custom-call | flops 10569646080 | bytes 1835008 | tf_op jit(solution)/shard_map/span_attention/pallas_call | solution.py:737
  82.1 6.0 %all-to-all-start.2 = ((f32[8,16,128]{2,1,0:T(8,128)}), f32[8,16,128]{2,1,0:T(8,128)S(1)}, u32[]{:S(2)}, u32[]{:S(2)}) async-start(f32[8,16,128]{2,1,0:T(8,128)} %get-tuple-element.47), calls=%async_computation.2 | async-start | bytes 131072 | tf_op jit(solution)/shard_map/all_to_all | solution.py:776
  88.1 0.5 collective-permute-start.8
  88.5 1.0 collective-permute-start.7
  89.5 0.4 collective-permute-start.6
  89.9 5.0 %all-to-all-done.2.refs_1_ = f32[8,16,128]{2,1,0:T(8,128)S(1)} async-done(((f32[8,16,128]{2,1,0:T(8,128)}), f32[8,16,128]{2,1,0:T(8,128)S(1)}, u32[]{:S(2)}, u32[]{:S(2)}) %all-to-all-start.2) | async-done | bytes 65568 | tf_op jit(solution)/shard_map/all_to_all | solution.py:776
  95.0 0.0 copy-done.3
  95.0 0.6 owned_cotangent.1.dep_ref.c0
  95.6 0.0 collective-permute-done.8.c3
  95.6 0.0 collective-permute-done.7.c2
  95.6 0.0 collective-permute-done.6.c1
  95.6 0.0 copy-done
  95.6 0.0 copy-start.2
  95.6 0.9 copy-done.2
  96.5 0.8 first_down.1
  97.3 0.7 collective-permute-start.12
  98.0 0.4 collective-permute-start.11
  98.4 1.0 collective-permute-start.10
  99.5 0.4 collective-permute-start.9
  99.8 1.8 %collective-permute-done.11.c3 = f32[16,512]{1,0:T(8,128)S(1)} collective-permute-done((f32[16,512]{1,0:T(8,128)S(1)}, f32[16,512]{1,0:T(8,128)S(1)}, u32[]{:S(2)}, u32[]{:S(2)}) %collective-permute-start.11) | collective-permute-done | bytes 32800 | tf_op jit(solution)/shard_map/ppermute | solution.py:572
  101.7 0.7 collective-permute-done.10.c2
  102.4 0.0 collective-permute-done.9.c1
  102.4 0.0 collective-permute-done.12.q1
  102.4 0.0 copy-done.1
  102.4 0.3 second_down.1
  102.7 1.5 %collective-permute-start.13 = (f32[16,1920]{1,0:T(8,128)S(1)}, f32[16,1920]{1,0:T(8,128)S(1)}, u32[]{:S(2)}, u32[]{:S(2)}) collective-permute-start(f32[16,1920]{1,0:T(8,128)S(1)} %get-tuple-element.51), channel_id=1, source_target_pairs={{0,8},{4,12},{8,0},{12,4},{16,24},{20,28},{24,16},{28,20},{1,9},{5... | collective-permute-start | bytes 368648 | tf_op jit(solution)/shard_map/ppermute | solution.py:572
  104.2 0.9 collective-permute-start.15
  105.1 2.7 %collective-permute-done.13 = f32[16,1920]{1,0:T(8,128)S(1)} collective-permute-done((f32[16,1920]{1,0:T(8,128)S(1)}, f32[16,1920]{1,0:T(8,128)S(1)}, u32[]{:S(2)}, u32[]{:S(2)}) %collective-permute-start.13) | collective-permute-done | bytes 122912 | tf_op jit(solution)/shard_map/ppermute | solution.py:572
  107.8 2.4 %collective-permute-start.14 = (bf16[16,1920]{1,0:T(8,128)(2,1)S(1)}, bf16[16,1920]{1,0:T(8,128)(2,1)S(1)}, u32[]{:S(2)}, u32[]{:S(2)}) collective-permute-start(bf16[16,1920]{1,0:T(8,128)(2,1)S(1)} %add_convert_fusion.refs_0_), channel_id=1, source_target_pairs={{0,16},{4,20},{8,24},{12,28},{16,0},{20,4},{24,8},{28,12},{1,17},{... | collective-permute-start | bytes 184328 | tf_op jit(solution)/shard_map/ppermute | solution.py:572
  110.2 0.0 collective-permute-done.15
  110.2 1.5 %collective-permute-start.18 = (bf16[16,896]{1,0:T(8,128)(2,1)S(1)}, bf16[16,896]{1,0:T(8,128)(2,1)S(1)}, u32[]{:S(2)}, u32[]{:S(2)}) collective-permute-start(bf16[16,896]{1,0:T(8,128)(2,1)S(1)} %add_convert_fusion.1.refs_2_), channel_id=1, source_target_pairs={{0,24},{4,28},{8,16},{12,20},{16,8},{20,12},{24,0},{28,4},{1,25},{... | collective-permute-start | bytes 86024 | tf_op jit(solution)/shard_map/ppermute | solution.py:572
  111.7 1.5 %collective-permute-start.17 = (bf16[16,896]{1,0:T(8,128)(2,1)S(1)}, bf16[16,896]{1,0:T(8,128)(2,1)S(1)}, u32[]{:S(2)}, u32[]{:S(2)}) collective-permute-start(bf16[16,896]{1,0:T(8,128)(2,1)S(1)} %add_convert_fusion.1.refs_2_), channel_id=1, source_target_pairs={{0,16},{4,20},{8,24},{12,28},{16,0},{20,4},{24,8},{28,12},{1,17},{... | collective-permute-start | bytes 86024 | tf_op jit(solution)/shard_map/ppermute | solution.py:572
  113.2 1.5 %collective-permute-start.16 = (bf16[16,896]{1,0:T(8,128)(2,1)S(1)}, bf16[16,896]{1,0:T(8,128)(2,1)S(1)}, u32[]{:S(2)}, u32[]{:S(2)}) collective-permute-start(bf16[16,896]{1,0:T(8,128)(2,1)S(1)} %add_convert_fusion.1.refs_2_), channel_id=1, source_target_pairs={{0,8},{4,12},{8,0},{12,4},{16,24},{20,28},{24,16},{28,20},{1,9},{5... | collective-permute-start | bytes 86024 | tf_op jit(solution)/shard_map/ppermute | solution.py:572
  114.7 1.3 %collective-permute-done.18.refs_5_ = bf16[16,896]{1,0:T(8,128)(2,1)S(1)} collective-permute-done((bf16[16,896]{1,0:T(8,128)(2,1)S(1)}, bf16[16,896]{1,0:T(8,128)(2,1)S(1)}, u32[]{:S(2)}, u32[]{:S(2)}) %collective-permute-start.18) | collective-permute-done | bytes 28704 | tf_op jit(solution)/shard_map/ppermute | solution.py:572
  115.9 0.6 collective-permute-done.17.refs_4_
  116.6 0.5 collective-permute-done.16.refs_3_
  117.1 0.0 collective-permute-done.14.refs_1_
  117.1 0.7 finish_outputs.1
  (4 shorter events, 0.0 us)
Async XLA Ops:
  0.6 3.3 %collective-permute-start.2 = (bf16[512,896]{1,0:T(8,128)(2,1)}, bf16[512,896]{1,0:T(8,128)(2,1)}, u32[]{:S(2)}, u32[]{:S(2)}) collective-permute-start(bf16[512,896]{1,0:T(8,128)(2,1)} %memory_ref.1), channel_id=1, source_target_pairs={{0,1},{1,0},{2,3},{3,2},{4,5},{5,4},{6,7},{7,6},{8,9},{9,8},{10,11... | collective-permute-start | bytes 2752520 | tf_op jit(solution)/shard_map/ppermute | solution.py:572
  1.1 23.9 %collective-permute-start.3 = (bf16[512,896]{1,0:T(8,128)(2,1)}, bf16[512,896]{1,0:T(8,128)(2,1)}, u32[]{:S(2)}, u32[]{:S(2)}) collective-permute-start(bf16[512,896]{1,0:T(8,128)(2,1)} %memory_ref.1), channel_id=1, source_target_pairs={{0,2},{1,3},{2,0},{3,1},{4,6},{5,7},{6,4},{7,5},{8,10},{9,11},{10,... | collective-permute-start | bytes 2752520 | tf_op jit(solution)/shard_map/ppermute | solution.py:572
  3.7 21.3 %collective-permute-start = (bf16[512,896]{1,0:T(8,128)(2,1)}, bf16[512,896]{1,0:T(8,128)(2,1)}, u32[]{:S(2)}, u32[]{:S(2)}) collective-permute-start(bf16[512,896]{1,0:T(8,128)(2,1)} %slab_ref.1), channel_id=1, source_target_pairs={{0,1},{1,0},{2,3},{3,2},{4,5},{5,4},{6,7},{7,6},{8,9},{9,8},{10,11... | collective-permute-start | bytes 2752520 | tf_op jit(solution)/shard_map/ppermute | solution.py:572
  25.0 4.9 %collective-permute-start.4 = (bf16[512,896]{1,0:T(8,128)(2,1)}, bf16[512,896]{1,0:T(8,128)(2,1)}, u32[]{:S(2)}, u32[]{:S(2)}) collective-permute-start(bf16[512,896]{1,0:T(8,128)(2,1)} %in_order.2.x2), channel_id=1, source_target_pairs={{0,1},{1,0},{2,3},{3,2},{4,5},{5,4},{6,7},{7,6},{8,9},{9,8},{10,11... | collective-permute-start | bytes 2752520 | tf_op jit(solution)/shard_map/ppermute | solution.py:572
  25.0 23.5 %collective-permute-start.1 = (bf16[512,896]{1,0:T(8,128)(2,1)}, bf16[512,896]{1,0:T(8,128)(2,1)}, u32[]{:S(2)}, u32[]{:S(2)}) collective-permute-start(bf16[512,896]{1,0:T(8,128)(2,1)} %collective-permute-done.x1), channel_id=1, source_target_pairs={{0,2},{1,3},{2,0},{3,1},{4,6},{5,7},{6,4},{7,5},{8,10},{9,11},{10,... | collective-permute-start | bytes 2752520 | tf_op jit(solution)/shard_map/ppermute | solution.py:572
  33.7 25.5 %all-to-all-start.1 = ((bf16[8,272,128]{2,1,0:T(8,128)(2,1)}), bf16[8,272,128]{2,1,0:T(8,128)(2,1)}, u32[]{:S(2)}, u32[]{:S(2)}) async-start(bf16[8,272,128]{2,1,0:T(8,128)(2,1)} %memory_pairs.1.refs_7_), calls=%async_computation.1 | async-start | bytes 1114112 | tf_op jit(solution)/shard_map/all_to_all | solution.py:706
  48.6 2.9 %collective-permute-start.5 = (bf16[512,896]{1,0:T(8,128)(2,1)}, bf16[512,896]{1,0:T(8,128)(2,1)}, u32[]{:S(2)}, u32[]{:S(2)}) collective-permute-start(bf16[512,896]{1,0:T(8,128)(2,1)} %in_order.3.x3), channel_id=1, source_target_pairs={{0,1},{1,0},{2,3},{3,2},{4,5},{5,4},{6,7},{7,6},{8,9},{9,8},{10,11... | collective-permute-start | bytes 2752520 | tf_op jit(solution)/shard_map/ppermute | solution.py:572
  59.2 35.8 %copy-start.3 = (s32[8]{0:T(128)S(1)}, s32[8]{0:T(128)}, u32[]{:S(2)}) copy-start(s32[8]{0:T(128)} %reduce.refs_1_.refs_0_) | copy-start | bytes 100
  59.2 36.4 %copy-start = (bf16[512,896]{1,0:T(8,128)(2,1)S(1)}, bf16[512,896]{1,0:T(8,128)(2,1)}, u32[]{:S(2)}) copy-start(bf16[512,896]{1,0:T(8,128)(2,1)} %slab_ref.1) | copy-start | bytes 2752516
  59.2 43.2 %copy-start.1 = (bf16[512,896]{1,0:T(8,128)(2,1)S(1)}, bf16[512,896]{1,0:T(8,128)(2,1)}, u32[]{:S(2)}) copy-start(bf16[512,896]{1,0:T(8,128)(2,1)} %memory_ref.1) | copy-start | bytes 2752516
  82.1 12.9 %all-to-all-start.2 = ((f32[8,16,128]{2,1,0:T(8,128)}), f32[8,16,128]{2,1,0:T(8,128)S(1)}, u32[]{:S(2)}, u32[]{:S(2)}) async-start(f32[8,16,128]{2,1,0:T(8,128)} %get-tuple-element.47), calls=%async_computation.2 | async-start | bytes 131072 | tf_op jit(solution)/shard_map/all_to_all | solution.py:776
  88.1 7.5 %collective-permute-start.8 = (f32[40,512]{1,0:T(8,128)}, f32[40,512]{1,0:T(8,128)S(1)}, u32[]{:S(2)}, u32[]{:S(2)}) collective-permute-start(f32[40,512]{1,0:T(8,128)} %get-tuple-element.46), channel_id=1, source_target_pairs={{0,3},{1,2},{2,1},{3,0},{4,7},{5,6},{6,5},{7,4},{8,11},{9,10},{10,... | collective-permute-start | bytes 245768 | tf_op jit(solution)/shard_map/ppermute | solution.py:572
  88.5 7.0 %collective-permute-start.7 = (f32[40,512]{1,0:T(8,128)}, f32[40,512]{1,0:T(8,128)S(1)}, u32[]{:S(2)}, u32[]{:S(2)}) collective-permute-start(f32[40,512]{1,0:T(8,128)} %get-tuple-element.46), channel_id=1, source_target_pairs={{0,2},{1,3},{2,0},{3,1},{4,6},{5,7},{6,4},{7,5},{8,10},{9,11},{10,... | collective-permute-start | bytes 245768 | tf_op jit(solution)/shard_map/ppermute | solution.py:572
  89.5 6.0 %collective-permute-start.6 = (f32[40,512]{1,0:T(8,128)}, f32[40,512]{1,0:T(8,128)S(1)}, u32[]{:S(2)}, u32[]{:S(2)}) collective-permute-start(f32[40,512]{1,0:T(8,128)} %get-tuple-element.46), channel_id=1, source_target_pairs={{0,1},{1,0},{2,3},{3,2},{4,5},{5,4},{6,7},{7,6},{8,9},{9,8},{10,11... | collective-permute-start | bytes 245768 | tf_op jit(solution)/shard_map/ppermute | solution.py:572
  95.6 0.9 copy-start.2
  97.3 5.1 %collective-permute-start.12 = (f32[16,1920]{1,0:T(8,128)S(1)}, f32[16,1920]{1,0:T(8,128)S(1)}, u32[]{:S(2)}, u32[]{:S(2)}) collective-permute-start(f32[16,1920]{1,0:T(8,128)S(1)} %get-tuple-element.50.q0), channel_id=1, source_target_pairs={{0,4},{4,0},{8,12},{12,8},{16,20},{20,16},{24,28},{28,24},{1,5},{5... | collective-permute-start | bytes 368648 | tf_op jit(solution)/shard_map/ppermute | solution.py:572
  98.0 3.7 %collective-permute-start.11 = (f32[16,512]{1,0:T(8,128)S(1)}, f32[16,512]{1,0:T(8,128)S(1)}, u32[]{:S(2)}, u32[]{:S(2)}) collective-permute-start(f32[16,512]{1,0:T(8,128)S(1)} %owned_cotangent.1.dep_ref.c0), channel_id=1, source_target_pairs={{0,3},{1,2},{2,1},{3,0},{4,7},{5,6},{6,5},{7,4},{8,11},{9,10},{10,... | collective-permute-start | bytes 98312 | tf_op jit(solution)/shard_map/ppermute | solution.py:572
  98.4 4.0 %collective-permute-start.10 = (f32[16,512]{1,0:T(8,128)S(1)}, f32[16,512]{1,0:T(8,128)S(1)}, u32[]{:S(2)}, u32[]{:S(2)}) collective-permute-start(f32[16,512]{1,0:T(8,128)S(1)} %owned_cotangent.1.dep_ref.c0), channel_id=1, source_target_pairs={{0,2},{1,3},{2,0},{3,1},{4,6},{5,7},{6,4},{7,5},{8,10},{9,11},{10,... | collective-permute-start | bytes 98312 | tf_op jit(solution)/shard_map/ppermute | solution.py:572
  99.5 2.9 %collective-permute-start.9 = (f32[16,512]{1,0:T(8,128)S(1)}, f32[16,512]{1,0:T(8,128)S(1)}, u32[]{:S(2)}, u32[]{:S(2)}) collective-permute-start(f32[16,512]{1,0:T(8,128)S(1)} %owned_cotangent.1.dep_ref.c0), channel_id=1, source_target_pairs={{0,1},{1,0},{2,3},{3,2},{4,5},{5,4},{6,7},{7,6},{8,9},{9,8},{10,11... | collective-permute-start | bytes 98312 | tf_op jit(solution)/shard_map/ppermute | solution.py:572
  102.7 5.1 %collective-permute-start.13 = (f32[16,1920]{1,0:T(8,128)S(1)}, f32[16,1920]{1,0:T(8,128)S(1)}, u32[]{:S(2)}, u32[]{:S(2)}) collective-permute-start(f32[16,1920]{1,0:T(8,128)S(1)} %get-tuple-element.51), channel_id=1, source_target_pairs={{0,8},{4,12},{8,0},{12,4},{16,24},{20,28},{24,16},{28,20},{1,9},{5... | collective-permute-start | bytes 368648 | tf_op jit(solution)/shard_map/ppermute | solution.py:572
  104.2 6.0 %collective-permute-start.15 = (f32[16,896]{1,0:T(8,128)S(1)}, f32[16,896]{1,0:T(8,128)S(1)}, u32[]{:S(2)}, u32[]{:S(2)}) collective-permute-start(f32[16,896]{1,0:T(8,128)S(1)} %get-tuple-element.52), channel_id=1, source_target_pairs={{0,4},{4,0},{8,12},{12,8},{16,20},{20,16},{24,28},{28,24},{1,5},{5... | collective-permute-start | bytes 172040 | tf_op jit(solution)/shard_map/ppermute | solution.py:572
  107.8 9.3 %collective-permute-start.14 = (bf16[16,1920]{1,0:T(8,128)(2,1)S(1)}, bf16[16,1920]{1,0:T(8,128)(2,1)S(1)}, u32[]{:S(2)}, u32[]{:S(2)}) collective-permute-start(bf16[16,1920]{1,0:T(8,128)(2,1)S(1)} %add_convert_fusion.refs_0_), channel_id=1, source_target_pairs={{0,16},{4,20},{8,24},{12,28},{16,0},{20,4},{24,8},{28,12},{1,17},{... | collective-permute-start | bytes 184328 | tf_op jit(solution)/shard_map/ppermute | solution.py:572
  110.2 5.7 %collective-permute-start.18 = (bf16[16,896]{1,0:T(8,128)(2,1)S(1)}, bf16[16,896]{1,0:T(8,128)(2,1)S(1)}, u32[]{:S(2)}, u32[]{:S(2)}) collective-permute-start(bf16[16,896]{1,0:T(8,128)(2,1)S(1)} %add_convert_fusion.1.refs_2_), channel_id=1, source_target_pairs={{0,24},{4,28},{8,16},{12,20},{16,8},{20,12},{24,0},{28,4},{1,25},{... | collective-permute-start | bytes 86024 | tf_op jit(solution)/shard_map/ppermute | solution.py:572
  111.7 4.8 %collective-permute-start.17 = (bf16[16,896]{1,0:T(8,128)(2,1)S(1)}, bf16[16,896]{1,0:T(8,128)(2,1)S(1)}, u32[]{:S(2)}, u32[]{:S(2)}) collective-permute-start(bf16[16,896]{1,0:T(8,128)(2,1)S(1)} %add_convert_fusion.1.refs_2_), channel_id=1, source_target_pairs={{0,16},{4,20},{8,24},{12,28},{16,0},{20,4},{24,8},{28,12},{1,17},{... | collective-permute-start | bytes 86024 | tf_op jit(solution)/shard_map/ppermute | solution.py:572
  113.2 3.9 %collective-permute-start.16 = (bf16[16,896]{1,0:T(8,128)(2,1)S(1)}, bf16[16,896]{1,0:T(8,128)(2,1)S(1)}, u32[]{:S(2)}, u32[]{:S(2)}) collective-permute-start(bf16[16,896]{1,0:T(8,128)(2,1)S(1)} %add_convert_fusion.1.refs_2_), channel_id=1, source_target_pairs={{0,8},{4,12},{8,0},{12,4},{16,24},{20,28},{24,16},{28,20},{1,9},{5... | collective-permute-start | bytes 86024 | tf_op jit(solution)/shard_map/ppermute | solution.py:572

commit v9 on v8

--- a/solution.py
+++ b/solution.py
@@ -389,45 +389,49 @@
                 ref[...] += term
 
 
-def project_far_kernel(place_ref, x3, x2, *refs):
-    hbm, early, (qup_ref, vup_ref), (q_ref, k_ref, v_ref, low_ref) = refs[:5], refs[5:8], refs[8:10], refs[10:14]
-    scratch, sems, sum_refs, sum_sems = refs[14:20], refs[20], refs[21:24], refs[24]
-    groups = project_pieces(place_ref, (3, 2), (x3, x2), hbm, scratch, sems)
+def project_middle_kernel(place_ref, x3, *refs):
+    hbm, early, outs, scratch, sems = refs[:5], refs[5:8], refs[8:11], refs[11:17], refs[17]
+    sum_refs, sum_sems = refs[18:21], refs[21]
+    groups = project_pieces(place_ref, (3,), (x3,), hbm, scratch, sems)
     loads = start_copies(list(zip(early, sum_refs)), sum_sems)
     wait_all(groups[0])
     terms = project_terms(0, scratch)
     wait_all(loads)
-    for ref, term in zip(sum_refs, terms):
-        ref[...] += term
-    wait_all(groups[1])
-    q_acc, kv_acc, low_acc = [ref[...] + term for ref, term in zip(sum_refs, project_terms(1, scratch))]
-    low = low_acc.astype(jnp.bfloat16)
-    q_ref[...] = (q_acc + dot_nn(low[:, :RANK], qup_ref[...])).astype(jnp.bfloat16)
-    k_ref[...] = kv_acc[:, :HD].astype(jnp.bfloat16)
-    v_ref[...] = (kv_acc[:, HD:] + dot_nn(low[:, RANK:], vup_ref[...])).astype(jnp.bfloat16)
-    low_ref[...] = jnp.transpose(low_acc).astype(jnp.bfloat16)
-
-
-def attention_kernel(peers, heads, bound_ref, *refs):
-    parts, got, grad_hbm, grad_t_hbm = refs[:4], refs[4], refs[5], refs[6]
-    qup_ref, vup_ref, tag_ref, cot_ref, mine_ref, mcot_ref = refs[7:13]
+    for out, ref, term in zip(outs, sum_refs, terms):
+        out[...] = ref[...] + term
+
+
+def attention_kernel(peers, heads, place_ref, bound_ref, x2, *refs):
+    hbm, early, got, grad_hbm, grad_t_hbm = refs[:5], refs[5:8], refs[8], refs[9], refs[10]
+    qup_ref, vup_ref, tag_ref, cot_ref, mine_ref, mcot_ref = refs[11:17]
+    scratch, sems, sum_refs = refs[17:23], refs[23], refs[24:27]
     (q_s, k_own, v_own, low_s, low_m_s, grad_ref, grad_t_ref, k_all, v_all, kt_all, vt_all, kt_own, vt_own, bias_s, s_s, dp_s,
-     p_s, ds_s, att_s, dq_s, dv_s, up_ref, more_sems) = refs[13:]
+     p_s, ds_s, att_s, dq_s, dv_s, up_ref, more_sems) = refs[27:]
     seen = peers * BLK
-    pairs = []
+    groups = project_pieces(place_ref, (2,), (x2,), hbm, scratch, sems)
+    pairs = list(zip(early, sum_refs))
     for b in range(peers):
         at = slice(b * BLK, (b + 1) * BLK)
         pairs.append((got.at[b, pl.ds(0, BLK), :], k_all.at[at, :]))
         pairs.append((got.at[b, pl.ds(BLK, BLK), :], v_all.at[at, :]))
         pairs.append((got.at[b, pl.ds(2 * BLK, RANK), :], low_m_s.at[b]))
-    pairs += list(zip(parts, (q_s, k_own, v_own, low_s))) + [(grad_hbm, grad_ref), (grad_t_hbm, grad_t_ref)]
+    pairs += [(grad_hbm, grad_ref), (grad_t_hbm, grad_t_ref)]
     copies = start_copies(pairs, more_sems)
-    wait_all(copies[: 3 * peers])
+    wait_all(groups[0])
+    terms = project_terms(0, scratch)
+    wait_all(copies[:3])
+    q_acc, kv_acc, low_acc = [ref[...] + term for ref, term in zip(sum_refs, terms)]
+    low = low_acc.astype(jnp.bfloat16)
+    q_s[...] = (q_acc + dot_nn(low[:, :RANK], qup_ref[...])).astype(jnp.bfloat16)
+    k_own[...] = kv_acc[:, :HD].astype(jnp.bfloat16)
+    v_own[...] = (kv_acc[:, HD:] + dot_nn(low[:, RANK:], vup_ref[...])).astype(jnp.bfloat16)
+    low_s[...] = jnp.transpose(low_acc).astype(jnp.bfloat16)
+    wait_all(copies[3 : 3 + 3 * peers])
     for b in range(peers):
         at = slice(b * BLK, (b + 1) * BLK)
         kt_all[:, at] = jnp.transpose(k_all[at, :])
         vt_all[:, at] = jnp.transpose(v_all[at, :])
-    wait_all(copies[3 * peers : -1])
+    wait_all(copies[3 + 3 * peers : -1])
     dv_s[...] = jnp.zeros_like(dv_s)
     up_ref[...] = jnp.zeros_like(up_ref)
     scale = HD ** (-0.5)
@@ -719,18 +723,13 @@
     )(place, slab_tokens, tok_near, *weights, tag_t, grad_tags.T, pairs)
     tok_far = after(tok_far, early[2])
     tok_cross = swap(tok_far, 1)
-    parts = run(
-        project_far_kernel,
-        "project_far_half",
-        (
-            shaped(tok_rows, query_width, dtype=bf16),
-            shaped(tok_rows, HD, dtype=bf16),
-            shaped(tok_rows, HD, dtype=bf16),
-            shaped(2 * RANK, tok_rows, dtype=bf16),
-        ),
-        [smem()] + [anywhere()] * 10 + [vmem()] * 2,
-        project_scratch(2) + project_sums + [pltpu.SemaphoreType.DMA((3,))],
-    )(place, tok_far, tok_cross, *weights, *early, query_up, value_up)
+    early = run(
+        project_middle_kernel,
+        "project_far_quarter",
+        (shaped(tok_rows, query_width), shaped(tok_rows, 2 * HD), shaped(tok_rows, 2 * RANK)),
+        [smem()] + [anywhere()] * 9,
+        project_scratch(1) + project_sums + [pltpu.SemaphoreType.DMA((3,))],
+    )(place, tok_far, *weights, *early)
 
     seen = peers * BLK
     total = seen + BLK
@@ -742,8 +741,10 @@
             shaped(2 * RANK + tags + RANK * (query_width + HD) // tok_rows, tok_rows),
             shaped(peers, RANK, BLK),
         ),
-        [smem()] + [anywhere()] * 7 + [vmem()] * 3,
-        [
+        [smem()] * 2 + [anywhere()] * 12 + [vmem()] * 3,
+        project_scratch(1)
+        + project_sums
+        + [
             pltpu.VMEM((tok_rows, query_width), bf16),
             pltpu.VMEM((tok_rows, HD), bf16),
             pltpu.VMEM((tok_rows, HD), bf16),
@@ -766,12 +767,12 @@
             pltpu.VMEM((PAIR * BLK, query_width), bf16),
             pltpu.VMEM((HD, seen), f32),
             pltpu.VMEM((RANK, query_width + HD), f32),
-            pltpu.SemaphoreType.DMA((3 * peers + 6,)),
+            pltpu.SemaphoreType.DMA((3 * peers + 5,)),
         ],
         flops=20 * tok_rows * query_width * total,
         moved=4 * tok_rows * query_width,
         room=60,
-    )(boundary, *parts, got, grad, grad_t, query_up, value_up, tag_t)
+    )(place, boundary, tok_cross, *weights, *early, got, grad, grad_t, query_up, value_up, tag_t)
 
     back = lax.all_to_all(mcot, "tm", split_axis=0, concat_axis=0, tiled=True)
     cots = [mine] + [swap(cot, d) for d in range(1, 4)]

time: 118 us -> 118 us (level)
  Pallas kernels: 53 us -> 54.6 us
  waiting for transfers between devices: 17.7 us -> 16.4 us
    pallas_call x1, Pallas kernels: 22.8 us -> 26.5 us  [fast(): run(lambda *refs: attention_kernel(peers, heads, *refs), 'span_attention'...]
    ppermute x19, waiting for transfers between devices: 12.7 us -> 10.5 us  [swap(): lax.ppermute(x, axis, [(i, i ^ bit) for i in range(lax.axis_size(axis))])]
    pallas_call x1, Pallas kernels: 7.74 us -> 5.77 us  [fast(): run(project_middle_kernel, 'project_far_quarter', (shaped(tok_rows, query...]
  transfers between devices with their start and end apart: 21 -> 21, of which waited for: 9 -> 9; matrix products, arithmetic and copies ran while one was open for 1% -> 1% of each run, Pallas kernels for 24% -> 22%
where the time goes in v9:
time: 118 us
  Pallas kernels  54.6 us (46%)
  starting transfers between devices  30.2 us (26%)
  waiting for transfers between devices  16.4 us (14%)
  blocking collectives  13.1 us (11%)
  local copies, waits for them, and re-layouts  1.65 us (1%)
    pallas_call x1, Pallas kernels, fast(): run(lambda *refs: attention_kernel(peers, heads, *refs), 'span_attention'...  26.5 us
    ppermute x19, starting transfers between devices, swap(): lax.ppermute(x, axis, [(i, i ^ bit) for i in range(lax.axis_size(axis))])  19.1 us
    all_to_all x1, blocking collectives, fast(): lax.all_to_all(wanted, 'tm', split_axis=0, concat_axis=0, tiled=True)  13.1 us
    ppermute x19, waiting for transfers between devices, swap(): lax.ppermute(x, axis, [(i, i ^ bit) for i in range(lax.axis_size(axis))])  10.5 us
    pallas_call x1, Pallas kernels, fast(): run(project_early_kernel, 'project_near_half', (shaped(tok_rows, query_wi...  8.9 us
    all_to_all x1, starting transfers between devices, fast(): got = lax.all_to_all(pairs, 'tm', split_axis=0, concat_axis=0, tiled=True)  5.82 us
    pallas_call x1, Pallas kernels, fast(): run(project_middle_kernel, 'project_far_quarter', (shaped(tok_rows, query...  5.77 us
    all_to_all x1, starting transfers between devices, fast(): back = lax.all_to_all(mcot, 'tm', split_axis=0, concat_axis=0, tiled=True)  5.31 us
  transfers between devices with their start and end apart: 21, of which 9 were waited for; matrix products, arithmetic and copies ran while one was open for 1% of the time, Pallas kernels for 22%

profile of v9, /device:TPU:0, one launch (start us, length us, event | category | flops | bytes accessed | tf_op | source)
XLA Modules:
  0.0 117.5 jit_solution(9625829469984002358)
XLA Ops:
  0.6 0.5 collective-permute-start.2
  1.1 2.6 %collective-permute-start.3 = (bf16[512,896]{1,0:T(8,128)(2,1)}, bf16[512,896]{1,0:T(8,128)(2,1)}, u32[]{:S(2)}, u32[]{:S(2)}) collective-permute-start(bf16[512,896]{1,0:T(8,128)(2,1)} %memory_ref.1), channel_id=1, source_target_pairs={{0,2},{1,3},{2,0},{3,1},{4,6},{5,7},{6,4},{7,5},{8,10},{9,11},{10,... | collective-permute-start | bytes 2752520 | tf_op jit(solution)/shard_map/ppermute | solution.py:576
  3.7 0.2 collective-permute-start
  3.9 0.0 collective-permute-done.2.refs_3_
  3.9 4.3 %memory_near_half.1 = (f32[512,256]{1,0:T(8,128)}, f32[512,16]{1,0:T(8,128)}, s32[8]{0:T(128)}) custom-call(s32[1]{0:T(128)} %bitcast.refs_0_.place_ref, s32[4,8]{1,0:T(4,128)} %refs_1_.5, bf16[512,896]{1,0:T(8,128)(2,1)} %memory_ref.1, bf16[512,896]{1,0:T(8,128)(2,1)} %collective-permute-done.2.refs_3_, bf16[3584,128]{1,0:T(8,128)(2,1)} %refs_4_.7, ...), custom_call_target="tpu_custom_call" | custom-call | tf_op jit(solution)/shard_map/memory_near_half/pallas_call | solution.py:683
  8.2 0.7 copy.21
  8.9 13.1 %all_to_all.21 = s32[8,1,1]{2,1,0:T(1,128)S(1)} all-to-all(s32[8,1,1]{2,1,0:T(1,128)S(1)} %copy.21), channel_id=1, replica_groups=mesh['tm'=8,'heads'=4] {'tm'}, dimensions={0} | all-to-all | bytes 64 | tf_op jit(solution)/shard_map/all_to_all | solution.py:691
  22.0 0.8 reduce.refs_1_.refs_0_
  22.8 2.2 %collective-permute-done.3.refs_0_ = bf16[512,896]{1,0:T(8,128)(2,1)} collective-permute-done((bf16[512,896]{1,0:T(8,128)(2,1)}, bf16[512,896]{1,0:T(8,128)(2,1)}, u32[]{:S(2)}, u32[]{:S(2)}) %collective-permute-start.3) | collective-permute-done | bytes 917536 | tf_op jit(solution)/shard_map/ppermute | solution.py:576
  25.0 0.0 collective-permute-start.4
  25.0 0.0 collective-permute-done.x1
  25.0 1.8 %collective-permute-start.1 = (bf16[512,896]{1,0:T(8,128)(2,1)}, bf16[512,896]{1,0:T(8,128)(2,1)}, u32[]{:S(2)}, u32[]{:S(2)}) collective-permute-start(bf16[512,896]{1,0:T(8,128)(2,1)} %collective-permute-done.x1), channel_id=1, source_target_pairs={{0,2},{1,3},{2,0},{3,1},{4,6},{5,7},{6,4},{7,5},{8,10},{9,11},{10,... | collective-permute-start | bytes 2752520 | tf_op jit(solution)/shard_map/ppermute | solution.py:576
  26.8 3.0 %memory_far_quarter.1 = (f32[512,256]{1,0:T(8,128)}, f32[512,16]{1,0:T(8,128)}) custom-call(s32[1]{0:T(128)} %bitcast.refs_0_.place_ref, bf16[512,896]{1,0:T(8,128)(2,1)} %in_order.2.x2, f32[512,256]{1,0:T(8,128)} %get-tuple-element.31.acc_hbm, f32[512,16]{1,0:T(8,128)} %get-tuple-element.32.low_hbm, bf16[3584,128]{1,0:T(8,128)(2,1)} %refs_4_.7, ...), custom_call_target="tpu_custom_call" | custom-call | tf_op jit(solution)/shard_map/memory_far_quarter/pallas_call | solution.py:696
  29.8 0.0 collective-permute-done.4.refs_2_
  29.9 3.9 %memory_pairs.1.refs_7_ = bf16[8,272,128]{2,1,0:T(8,128)(2,1)} custom-call(s32[1]{0:T(128)} %bitcast.refs_0_.place_ref, s32[8]{0:T(128)} %reduce.refs_1_.refs_0_, bf16[512,896]{1,0:T(8,128)(2,1)} %collective-permute-done.4.refs_2_, f32[512,256]{1,0:T(8,128)} %get-tuple-element.33.refs_3_, f32[512,16]{1,0:T(8,128)} %get-tuple-element.34.refs_4_, ...), custom_call_target="tpu_custom_call" | custom-call | tf_op jit(solution)/shard_map/memory_pairs/pallas_call | solution.py:703
  33.7 5.8 %all-to-all-start.1 = ((bf16[8,272,128]{2,1,0:T(8,128)(2,1)}), bf16[8,272,128]{2,1,0:T(8,128)(2,1)}, u32[]{:S(2)}, u32[]{:S(2)}) async-start(bf16[8,272,128]{2,1,0:T(8,128)(2,1)} %memory_pairs.1.refs_7_), calls=%async_computation.1 | async-start | bytes 1114112 | tf_op jit(solution)/shard_map/all_to_all | solution.py:710
  39.5 8.9 %project_near_half.1 = (f32[512,896]{1,0:T(8,128)}, f32[512,256]{1,0:T(8,128)}, f32[512,32]{1,0:T(8,128)}, bf16[512,896]{1,0:T(8,128)(2,1)}, bf16[896,512]{1,0:T(8,128)(2,1)}) custom-call(s32[1]{0:T(128)} %bitcast.refs_0_.place_ref, bf16[512,896]{1,0:T(8,128)(2,1)} %slab_ref.1, bf16[512,896]{1,0:T(8,128)(2,1)} %collective-permute-done.x1, ...), custom_call_target="tpu_custom_call" | custom-call | tf_op jit(solution)/shard_map/project_near_half/pallas_call | solution.py:711
  48.5 0.0 collective-permute-done.1.refs_0_
  48.5 0.1 collective-permute-start.5
  48.6 5.8 %project_far_quarter.1 = (f32[512,896]{1,0:T(8,128)}, f32[512,256]{1,0:T(8,128)}, f32[512,32]{1,0:T(8,128)}) custom-call(s32[1]{0:T(128)} %bitcast.refs_0_.place_ref, bf16[512,896]{1,0:T(8,128)(2,1)} %in_order.3.x3, bf16[3584,896]{1,0:T(8,128)(2,1)} %refs_3_.5, bf16[3584,128]{1,0:T(8,128)(2,1)} %refs_4_.7, bf16[3584,128]{1,0:T(8,128)(2,1)} %refs_5_.5, ...), custom_call_target="tpu_custom_call" | custom-call | tf_op jit(solution)/shard_map/project_far_quarter/pallas_call | solution.py:726
  54.3 0.0 collective-permute-done.5.refs_2_
  54.3 0.9 all-to-all-done.1.refs_11_
  55.2 0.0 copy-start.3
  55.2 0.0 copy-start
  55.2 26.5 %span_attention.1 = (f32[40,512]{1,0:T(8,128)}, f32[72,512]{1,0:T(8,128)}, f32[8,16,128]{2,1,0:T(8,128)}) custom-call(s32[1]{0:T(128)} %bitcast.refs_0_.place_ref, s32[4]{0:T(128)} %refs_1_.9, bf16[512,896]{1,0:T(8,128)(2,1)} %collective-permute-done.5.refs_2_, bf16[3584,896]{1,0:T(8,128)(2,1)} %refs_3_.5, bf16[3584,128]{1,0:T(8,128)(2,1)} %refs_4_.7, ...), custom_call_target="tpu_custom_call" | custom-call | flops 10569646080 | bytes 1835008 | tf_op jit(solution)/shard_map/span_attention/pallas_call | solution.py:736
  81.7 0.0 copy-start.1
  81.7 5.3 %all-to-all-start.2 = ((f32[8,16,128]{2,1,0:T(8,128)}), f32[8,16,128]{2,1,0:T(8,128)S(1)}, u32[]{:S(2)}, u32[]{:S(2)}) async-start(f32[8,16,128]{2,1,0:T(8,128)} %get-tuple-element.45), calls=%async_computation.2 | async-start | bytes 131072 | tf_op jit(solution)/shard_map/all_to_all | solution.py:777
  87.0 1.0 collective-permute-start.8
  88.0 0.9 collective-permute-start.7
  88.9 0.0 collective-permute-start.6
  88.9 5.0 %all-to-all-done.2.refs_1_ = f32[8,16,128]{2,1,0:T(8,128)S(1)} async-done(((f32[8,16,128]{2,1,0:T(8,128)}), f32[8,16,128]{2,1,0:T(8,128)S(1)}, u32[]{:S(2)}, u32[]{:S(2)}) %all-to-all-start.2) | async-done | bytes 65568 | tf_op jit(solution)/shard_map/all_to_all | solution.py:777
  93.9 0.0 copy-done.3
  93.9 0.6 owned_cotangent.1.dep_ref.c0
  94.5 0.0 collective-permute-done.8.c3
  94.5 0.0 collective-permute-done.7.c2
  94.5 0.0 collective-permute-done.6.c1
  94.5 0.0 copy-done
  94.5 0.0 copy-start.2
  94.5 0.9 copy-done.2
  95.4 0.8 first_down.1
  96.2 1.2 %collective-permute-start.12 = (f32[16,1920]{1,0:T(8,128)S(1)}, f32[16,1920]{1,0:T(8,128)S(1)}, u32[]{:S(2)}, u32[]{:S(2)}) collective-permute-start(f32[16,1920]{1,0:T(8,128)S(1)} %get-tuple-element.48.q0), channel_id=1, source_target_pairs={{0,4},{4,0},{8,12},{12,8},{16,20},{20,16},{24,28},{28,24},{1,5},{5... | collective-permute-start | bytes 368648 | tf_op jit(solution)/shard_map/ppermute | solution.py:576
  97.4 0.5 collective-permute-start.11
  97.9 0.8 collective-permute-start.10
  98.7 0.6 collective-permute-start.9
  99.3 1.7 %collective-permute-done.11.c3 = f32[16,512]{1,0:T(8,128)S(1)} collective-permute-done((f32[16,512]{1,0:T(8,128)S(1)}, f32[16,512]{1,0:T(8,128)S(1)}, u32[]{:S(2)}, u32[]{:S(2)}) %collective-permute-start.11) | collective-permute-done | bytes 32800 | tf_op jit(solution)/shard_map/ppermute | solution.py:576
  100.9 1.1 collective-permute-done.10.c2
  102.0 0.0 collective-permute-done.9.c1
  102.0 0.0 collective-permute-done.12.q1
  102.0 0.0 copy-done.1
  102.0 0.3 second_down.1
  102.3 1.5 %collective-permute-start.13 = (f32[16,1920]{1,0:T(8,128)S(1)}, f32[16,1920]{1,0:T(8,128)S(1)}, u32[]{:S(2)}, u32[]{:S(2)}) collective-permute-start(f32[16,1920]{1,0:T(8,128)S(1)} %get-tuple-element.49), channel_id=1, source_target_pairs={{0,8},{4,12},{8,0},{12,4},{16,24},{20,28},{24,16},{28,20},{1,9},{5... | collective-permute-start | bytes 368648 | tf_op jit(solution)/shard_map/ppermute | solution.py:576
  103.8 0.6 collective-permute-start.15
  104.4 3.2 %collective-permute-done.13 = f32[16,1920]{1,0:T(8,128)S(1)} collective-permute-done((f32[16,1920]{1,0:T(8,128)S(1)}, f32[16,1920]{1,0:T(8,128)S(1)}, u32[]{:S(2)}, u32[]{:S(2)}) %collective-permute-start.13) | collective-permute-done | bytes 122912 | tf_op jit(solution)/shard_map/ppermute | solution.py:576
  107.5 2.4 %collective-permute-start.14 = (bf16[16,1920]{1,0:T(8,128)(2,1)S(1)}, bf16[16,1920]{1,0:T(8,128)(2,1)S(1)}, u32[]{:S(2)}, u32[]{:S(2)}) collective-permute-start(bf16[16,1920]{1,0:T(8,128)(2,1)S(1)} %add_convert_fusion.refs_0_), channel_id=1, source_target_pairs={{0,16},{4,20},{8,24},{12,28},{16,0},{20,4},{24,8},{28,12},{1,17},{... | collective-permute-start | bytes 184328 | tf_op jit(solution)/shard_map/ppermute | solution.py:576
  110.0 0.0 collective-permute-done.15
  110.0 1.5 %collective-permute-start.18 = (bf16[16,896]{1,0:T(8,128)(2,1)S(1)}, bf16[16,896]{1,0:T(8,128)(2,1)S(1)}, u32[]{:S(2)}, u32[]{:S(2)}) collective-permute-start(bf16[16,896]{1,0:T(8,128)(2,1)S(1)} %add_convert_fusion.1.refs_2_), channel_id=1, source_target_pairs={{0,24},{4,28},{8,16},{12,20},{16,8},{20,12},{24,0},{28,4},{1,25},{... | collective-permute-start | bytes 86024 | tf_op jit(solution)/shard_map/ppermute | solution.py:576
  111.5 1.5 %collective-permute-start.17 = (bf16[16,896]{1,0:T(8,128)(2,1)S(1)}, bf16[16,896]{1,0:T(8,128)(2,1)S(1)}, u32[]{:S(2)}, u32[]{:S(2)}) collective-permute-start(bf16[16,896]{1,0:T(8,128)(2,1)S(1)} %add_convert_fusion.1.refs_2_), channel_id=1, source_target_pairs={{0,16},{4,20},{8,24},{12,28},{16,0},{20,4},{24,8},{28,12},{1,17},{... | collective-permute-start | bytes 86024 | tf_op jit(solution)/shard_map/ppermute | solution.py:576
  113.0 1.5 %collective-permute-start.16 = (bf16[16,896]{1,0:T(8,128)(2,1)S(1)}, bf16[16,896]{1,0:T(8,128)(2,1)S(1)}, u32[]{:S(2)}, u32[]{:S(2)}) collective-permute-start(bf16[16,896]{1,0:T(8,128)(2,1)S(1)} %add_convert_fusion.1.refs_2_), channel_id=1, source_target_pairs={{0,8},{4,12},{8,0},{12,4},{16,24},{20,28},{24,16},{28,20},{1,9},{5... | collective-permute-start | bytes 86024 | tf_op jit(solution)/shard_map/ppermute | solution.py:576
  114.4 1.3 %collective-permute-done.18.refs_5_ = bf16[16,896]{1,0:T(8,128)(2,1)S(1)} collective-permute-done((bf16[16,896]{1,0:T(8,128)(2,1)S(1)}, bf16[16,896]{1,0:T(8,128)(2,1)S(1)}, u32[]{:S(2)}, u32[]{:S(2)}) %collective-permute-start.18) | collective-permute-done | bytes 28704 | tf_op jit(solution)/shard_map/ppermute | solution.py:576
  115.7 0.6 collective-permute-done.17.refs_4_
  116.3 0.5 collective-permute-done.16.refs_3_
  116.8 0.0 collective-permute-done.14.refs_1_
  116.8 0.7 finish_outputs.1
  (4 shorter events, 0.0 us)
Async XLA Ops:
  0.6 3.3 %collective-permute-start.2 = (bf16[512,896]{1,0:T(8,128)(2,1)}, bf16[512,896]{1,0:T(8,128)(2,1)}, u32[]{:S(2)}, u32[]{:S(2)}) collective-permute-start(bf16[512,896]{1,0:T(8,128)(2,1)} %memory_ref.1), channel_id=1, source_target_pairs={{0,1},{1,0},{2,3},{3,2},{4,5},{5,4},{6,7},{7,6},{8,9},{9,8},{10,11... | collective-permute-start | bytes 2752520 | tf_op jit(solution)/shard_map/ppermute | solution.py:576
  1.1 23.9 %collective-permute-start.3 = (bf16[512,896]{1,0:T(8,128)(2,1)}, bf16[512,896]{1,0:T(8,128)(2,1)}, u32[]{:S(2)}, u32[]{:S(2)}) collective-permute-start(bf16[512,896]{1,0:T(8,128)(2,1)} %memory_ref.1), channel_id=1, source_target_pairs={{0,2},{1,3},{2,0},{3,1},{4,6},{5,7},{6,4},{7,5},{8,10},{9,11},{10,... | collective-permute-start | bytes 2752520 | tf_op jit(solution)/shard_map/ppermute | solution.py:576
  3.7 21.3 %collective-permute-start = (bf16[512,896]{1,0:T(8,128)(2,1)}, bf16[512,896]{1,0:T(8,128)(2,1)}, u32[]{:S(2)}, u32[]{:S(2)}) collective-permute-start(bf16[512,896]{1,0:T(8,128)(2,1)} %slab_ref.1), channel_id=1, source_target_pairs={{0,1},{1,0},{2,3},{3,2},{4,5},{5,4},{6,7},{7,6},{8,9},{9,8},{10,11... | collective-permute-start | bytes 2752520 | tf_op jit(solution)/shard_map/ppermute | solution.py:576
  25.0 4.8 %collective-permute-start.4 = (bf16[512,896]{1,0:T(8,128)(2,1)}, bf16[512,896]{1,0:T(8,128)(2,1)}, u32[]{:S(2)}, u32[]{:S(2)}) collective-permute-start(bf16[512,896]{1,0:T(8,128)(2,1)} %in_order.2.x2), channel_id=1, source_target_pairs={{0,1},{1,0},{2,3},{3,2},{4,5},{5,4},{6,7},{7,6},{8,9},{9,8},{10,11... | collective-permute-start | bytes 2752520 | tf_op jit(solution)/shard_map/ppermute | solution.py:576
  25.0 23.4 %collective-permute-start.1 = (bf16[512,896]{1,0:T(8,128)(2,1)}, bf16[512,896]{1,0:T(8,128)(2,1)}, u32[]{:S(2)}, u32[]{:S(2)}) collective-permute-start(bf16[512,896]{1,0:T(8,128)(2,1)} %collective-permute-done.x1), channel_id=1, source_target_pairs={{0,2},{1,3},{2,0},{3,1},{4,6},{5,7},{6,4},{7,5},{8,10},{9,11},{10,... | collective-permute-start | bytes 2752520 | tf_op jit(solution)/shard_map/ppermute | solution.py:576
  33.7 21.5 %all-to-all-start.1 = ((bf16[8,272,128]{2,1,0:T(8,128)(2,1)}), bf16[8,272,128]{2,1,0:T(8,128)(2,1)}, u32[]{:S(2)}, u32[]{:S(2)}) async-start(bf16[8,272,128]{2,1,0:T(8,128)(2,1)} %memory_pairs.1.refs_7_), calls=%async_computation.1 | async-start | bytes 1114112 | tf_op jit(solution)/shard_map/all_to_all | solution.py:710
  48.5 5.9 %collective-permute-start.5 = (bf16[512,896]{1,0:T(8,128)(2,1)}, bf16[512,896]{1,0:T(8,128)(2,1)}, u32[]{:S(2)}, u32[]{:S(2)}) collective-permute-start(bf16[512,896]{1,0:T(8,128)(2,1)} %in_order.3.x3), channel_id=1, source_target_pairs={{0,1},{1,0},{2,3},{3,2},{4,5},{5,4},{6,7},{7,6},{8,9},{9,8},{10,11... | collective-permute-start | bytes 2752520 | tf_op jit(solution)/shard_map/ppermute | solution.py:576
  55.2 38.7 %copy-start.3 = (s32[8]{0:T(128)S(1)}, s32[8]{0:T(128)}, u32[]{:S(2)}) copy-start(s32[8]{0:T(128)} %reduce.refs_1_.refs_0_) | copy-start | bytes 100
  55.2 39.3 %copy-start = (bf16[512,896]{1,0:T(8,128)(2,1)S(1)}, bf16[512,896]{1,0:T(8,128)(2,1)}, u32[]{:S(2)}) copy-start(bf16[512,896]{1,0:T(8,128)(2,1)} %slab_ref.1) | copy-start | bytes 2752516
  81.7 20.3 %copy-start.1 = (bf16[512,896]{1,0:T(8,128)(2,1)S(1)}, bf16[512,896]{1,0:T(8,128)(2,1)}, u32[]{:S(2)}) copy-start(bf16[512,896]{1,0:T(8,128)(2,1)} %memory_ref.1) | copy-start | bytes 2752516
  81.7 12.2 %all-to-all-start.2 = ((f32[8,16,128]{2,1,0:T(8,128)}), f32[8,16,128]{2,1,0:T(8,128)S(1)}, u32[]{:S(2)}, u32[]{:S(2)}) async-start(f32[8,16,128]{2,1,0:T(8,128)} %get-tuple-element.45), calls=%async_computation.2 | async-start | bytes 131072 | tf_op jit(solution)/shard_map/all_to_all | solution.py:777
  87.0 7.5 %collective-permute-start.8 = (f32[40,512]{1,0:T(8,128)}, f32[40,512]{1,0:T(8,128)S(1)}, u32[]{:S(2)}, u32[]{:S(2)}) collective-permute-start(f32[40,512]{1,0:T(8,128)} %get-tuple-element.44), channel_id=1, source_target_pairs={{0,3},{1,2},{2,1},{3,0},{4,7},{5,6},{6,5},{7,4},{8,11},{9,10},{10,... | collective-permute-start | bytes 245768 | tf_op jit(solution)/shard_map/ppermute | solution.py:576
  88.0 6.5 %collective-permute-start.7 = (f32[40,512]{1,0:T(8,128)}, f32[40,512]{1,0:T(8,128)S(1)}, u32[]{:S(2)}, u32[]{:S(2)}) collective-permute-start(f32[40,512]{1,0:T(8,128)} %get-tuple-element.44), channel_id=1, source_target_pairs={{0,2},{1,3},{2,0},{3,1},{4,6},{5,7},{6,4},{7,5},{8,10},{9,11},{10,... | collective-permute-start | bytes 245768 | tf_op jit(solution)/shard_map/ppermute | solution.py:576
  88.9 5.6 %collective-permute-start.6 = (f32[40,512]{1,0:T(8,128)}, f32[40,512]{1,0:T(8,128)S(1)}, u32[]{:S(2)}, u32[]{:S(2)}) collective-permute-start(f32[40,512]{1,0:T(8,128)} %get-tuple-element.44), channel_id=1, source_target_pairs={{0,1},{1,0},{2,3},{3,2},{4,5},{5,4},{6,7},{7,6},{8,9},{9,8},{10,11... | collective-permute-start | bytes 245768 | tf_op jit(solution)/shard_map/ppermute | solution.py:576
  94.5 0.9 copy-start.2
  96.2 5.8 %collective-permute-start.12 = (f32[16,1920]{1,0:T(8,128)S(1)}, f32[16,1920]{1,0:T(8,128)S(1)}, u32[]{:S(2)}, u32[]{:S(2)}) collective-permute-start(f32[16,1920]{1,0:T(8,128)S(1)} %get-tuple-element.48.q0), channel_id=1, source_target_pairs={{0,4},{4,0},{8,12},{12,8},{16,20},{20,16},{24,28},{28,24},{1,5},{5... | collective-permute-start | bytes 368648 | tf_op jit(solution)/shard_map/ppermute | solution.py:576
  97.4 3.5 %collective-permute-start.11 = (f32[16,512]{1,0:T(8,128)S(1)}, f32[16,512]{1,0:T(8,128)S(1)}, u32[]{:S(2)}, u32[]{:S(2)}) collective-permute-start(f32[16,512]{1,0:T(8,128)S(1)} %owned_cotangent.1.dep_ref.c0), channel_id=1, source_target_pairs={{0,3},{1,2},{2,1},{3,0},{4,7},{5,6},{6,5},{7,4},{8,11},{9,10},{10,... | collective-permute-start | bytes 98312 | tf_op jit(solution)/shard_map/ppermute | solution.py:576
  97.9 4.1 %collective-permute-start.10 = (f32[16,512]{1,0:T(8,128)S(1)}, f32[16,512]{1,0:T(8,128)S(1)}, u32[]{:S(2)}, u32[]{:S(2)}) collective-permute-start(f32[16,512]{1,0:T(8,128)S(1)} %owned_cotangent.1.dep_ref.c0), channel_id=1, source_target_pairs={{0,2},{1,3},{2,0},{3,1},{4,6},{5,7},{6,4},{7,5},{8,10},{9,11},{10,... | collective-permute-start | bytes 98312 | tf_op jit(solution)/shard_map/ppermute | solution.py:576
  98.7 3.3 %collective-permute-start.9 = (f32[16,512]{1,0:T(8,128)S(1)}, f32[16,512]{1,0:T(8,128)S(1)}, u32[]{:S(2)}, u32[]{:S(2)}) collective-permute-start(f32[16,512]{1,0:T(8,128)S(1)} %owned_cotangent.1.dep_ref.c0), channel_id=1, source_target_pairs={{0,1},{1,0},{2,3},{3,2},{4,5},{5,4},{6,7},{7,6},{8,9},{9,8},{10,11... | collective-permute-start | bytes 98312 | tf_op jit(solution)/shard_map/ppermute | solution.py:576
  102.3 5.2 %collective-permute-start.13 = (f32[16,1920]{1,0:T(8,128)S(1)}, f32[16,1920]{1,0:T(8,128)S(1)}, u32[]{:S(2)}, u32[]{:S(2)}) collective-permute-start(f32[16,1920]{1,0:T(8,128)S(1)} %get-tuple-element.49), channel_id=1, source_target_pairs={{0,8},{4,12},{8,0},{12,4},{16,24},{20,28},{24,16},{28,20},{1,9},{5... | collective-permute-start | bytes 368648 | tf_op jit(solution)/shard_map/ppermute | solution.py:576
  103.8 6.2 %collective-permute-start.15 = (f32[16,896]{1,0:T(8,128)S(1)}, f32[16,896]{1,0:T(8,128)S(1)}, u32[]{:S(2)}, u32[]{:S(2)}) collective-permute-start(f32[16,896]{1,0:T(8,128)S(1)} %get-tuple-element.50), channel_id=1, source_target_pairs={{0,4},{4,0},{8,12},{12,8},{16,20},{20,16},{24,28},{28,24},{1,5},{5... | collective-permute-start | bytes 172040 | tf_op jit(solution)/shard_map/ppermute | solution.py:576
  107.5 9.3 %collective-permute-start.14 = (bf16[16,1920]{1,0:T(8,128)(2,1)S(1)}, bf16[16,1920]{1,0:T(8,128)(2,1)S(1)}, u32[]{:S(2)}, u32[]{:S(2)}) collective-permute-start(bf16[16,1920]{1,0:T(8,128)(2,1)S(1)} %add_convert_fusion.refs_0_), channel_id=1, source_target_pairs={{0,16},{4,20},{8,24},{12,28},{16,0},{20,4},{24,8},{28,12},{1,17},{... | collective-permute-start | bytes 184328 | tf_op jit(solution)/shard_map/ppermute | solution.py:576
  110.0 5.7 %collective-permute-start.18 = (bf16[16,896]{1,0:T(8,128)(2,1)S(1)}, bf16[16,896]{1,0:T(8,128)(2,1)S(1)}, u32[]{:S(2)}, u32[]{:S(2)}) collective-permute-start(bf16[16,896]{1,0:T(8,128)(2,1)S(1)} %add_convert_fusion.1.refs_2_), channel_id=1, source_target_pairs={{0,24},{4,28},{8,16},{12,20},{16,8},{20,12},{24,0},{28,4},{1,25},{... | collective-permute-start | bytes 86024 | tf_op jit(solution)/shard_map/ppermute | solution.py:576
  111.5 4.8 %collective-permute-start.17 = (bf16[16,896]{1,0:T(8,128)(2,1)S(1)}, bf16[16,896]{1,0:T(8,128)(2,1)S(1)}, u32[]{:S(2)}, u32[]{:S(2)}) collective-permute-start(bf16[16,896]{1,0:T(8,128)(2,1)S(1)} %add_convert_fusion.1.refs_2_), channel_id=1, source_target_pairs={{0,16},{4,20},{8,24},{12,28},{16,0},{20,4},{24,8},{28,12},{1,17},{... | collective-permute-start | bytes 86024 | tf_op jit(solution)/shard_map/ppermute | solution.py:576
  113.0 3.9 %collective-permute-start.16 = (bf16[16,896]{1,0:T(8,128)(2,1)S(1)}, bf16[16,896]{1,0:T(8,128)(2,1)S(1)}, u32[]{:S(2)}, u32[]{:S(2)}) collective-permute-start(bf16[16,896]{1,0:T(8,128)(2,1)S(1)} %add_convert_fusion.1.refs_2_), channel_id=1, source_target_pairs={{0,8},{4,12},{8,0},{12,4},{16,24},{20,28},{24,16},{28,20},{1,9},{5... | collective-permute-start | bytes 86024 | tf_op jit(solution)/shard_map/ppermute | solution.py:576

commit v10 on v9

--- a/solution.py
+++ b/solution.py
@@ -560,12 +560,22 @@
     out_ref[...] = value_ref[...] + dot_nn(cot.astype(jnp.bfloat16), memory_ref[...])
 
 
-def finish_kernel(*refs):
-    parts = [ref[...].astype(jnp.float32) for ref in refs[:6]]
-    query = parts[0] + parts[1]
-    value = (parts[2] + parts[3]) + (parts[4] + parts[5])
-    query_down_ref, query_up_ref, value_down_ref, value_up_ref = refs[6:]
-    value_down_ref[...] = value
+def pack_kernel(q0, q1, v0, v1, both_ref, value_ref):
+    split = q0.shape[1]
+    value = (v0[...] + v1[...]).astype(jnp.bfloat16)
+    both_ref[:, :split] = (q0[...] + q1[...]).astype(jnp.bfloat16)
+    both_ref[:, split:] = value
+    value_ref[...] = value
+
+
+def finish_kernel(here_ref, there_ref, v1, v3, query_down_ref, query_up_ref, value_down_ref, value_up_ref):
+    here = here_ref[...].astype(jnp.float32)
+    there = there_ref[...].astype(jnp.float32)
+    split = here.shape[1] - value_down_ref.shape[1]
+    value_down_ref[...] = (here[:, split:] + v1[...].astype(jnp.float32)) + (
+        there[:, split:] + v3[...].astype(jnp.float32)
+    )
+    query = here[:, :split] + there[:, :split]
     at = 0
     for out_ref in (query_down_ref, query_up_ref, value_up_ref):
         out_ref[...] = query[:, at : at + out_ref.shape[1]]
@@ -803,14 +813,20 @@
         moved=2 * mem_rows * width,
         room=8,
     )(*owns, memory, value_part, query_sum, swap(query_sum, 1, "tm"))
-    query_sum = (query_sum + swap(query_sum, 2, "tm")).astype(bf16)
-    value_sum = (value_sum + swap(value_sum, 1, "tm")).astype(bf16)
-    sums = [query_sum, swap(query_sum, 4, "tm"), value_sum] + [swap(value_sum, bit, "tm") for bit in (2, 4, 6)]
+    split = query_sum.shape[1]
+    both, value_low = run(
+        pack_kernel,
+        "pack_sums",
+        (shaped(RANK, split + width, dtype=bf16), shaped(RANK, width, dtype=bf16)),
+        [vmem()] * 4,
+        room=8,
+    )(query_sum, swap(query_sum, 2, "tm"), value_sum, swap(value_sum, 1, "tm"))
+    sums = [both, swap(both, 4, "tm"), swap(value_low, 2, "tm"), swap(value_low, 6, "tm")]
     query_down_grad, query_up_grad, value_down_grad, value_up_grad = run(
         finish_kernel,
         "finish_outputs",
         (shaped(RANK, width), shaped(RANK, query_width), shaped(RANK, width), shaped(RANK, HD)),
-        [vmem()] * 6,
+        [vmem()] * 4,
         room=8,
     )(*sums)
     return (logits.T, query_down_grad, query_up_grad, value_down_grad, value_up_grad)

time: 118 us -> 117 us (level)
  starting transfers between devices: 30.2 us -> 26.9 us
  waiting for transfers between devices: 16.4 us -> 19 us
    ppermute x19 -> x18, starting transfers between devices: 19.1 us -> 15.8 us  [swap(): lax.ppermute(x, axis, [(i, i ^ bit) for i in range(lax.axis_size(axis))])]
    ppermute x19 -> x18, waiting for transfers between devices: 10.5 us -> 13.1 us  [swap(): lax.ppermute(x, axis, [(i, i ^ bit) for i in range(lax.axis_size(axis))])]
  transfers between devices with their start and end apart: 21 -> 20, of which waited for: 9 -> 7; matrix products, arithmetic and copies ran while one was open for 1% -> 1% of each run, Pallas kernels for 22% -> 23%
where the time goes in v10:
time: 117 us
  Pallas kernels  54.6 us (47%)
  starting transfers between devices  26.9 us (23%)
  waiting for transfers between devices  19 us (16%)
  blocking collectives  13.1 us (11%)
  local copies, waits for them, and re-layouts  1.65 us (1%)
    pallas_call x1, Pallas kernels, fast(): run(lambda *refs: attention_kernel(peers, heads, *refs), 'span_attention'...  26.5 us
    ppermute x18, starting transfers between devices, swap(): lax.ppermute(x, axis, [(i, i ^ bit) for i in range(lax.axis_size(axis))])  15.8 us
    ppermute x18, waiting for transfers between devices, swap(): lax.ppermute(x, axis, [(i, i ^ bit) for i in range(lax.axis_size(axis))])  13.1 us
    all_to_all x1, blocking collectives, fast(): lax.all_to_all(wanted, 'tm', split_axis=0, concat_axis=0, tiled=True)  13.1 us
    pallas_call x1, Pallas kernels, fast(): run(project_early_kernel, 'project_near_half', (shaped(tok_rows, query_wi...  8.9 us
    all_to_all x1, starting transfers between devices, fast(): got = lax.all_to_all(pairs, 'tm', split_axis=0, concat_axis=0, tiled=True)  5.82 us
    pallas_call x1, Pallas kernels, fast(): run(project_middle_kernel, 'project_far_quarter', (shaped(tok_rows, query...  5.77 us
    all_to_all x1, starting transfers between devices, fast(): back = lax.all_to_all(mcot, 'tm', split_axis=0, concat_axis=0, tiled=True)  5.32 us
  transfers between devices with their start and end apart: 20, of which 7 were waited for; matrix products, arithmetic and copies ran while one was open for 1% of the time, Pallas kernels for 23%

profile of v10, /device:TPU:0, one launch (start us, length us, event | category | flops | bytes accessed | tf_op | source)
XLA Modules:
  0.0 116.8 jit_solution(16696434560524566676)
XLA Ops:
  0.6 0.5 collective-permute-start.2
  1.1 2.6 %collective-permute-start.3 = (bf16[512,896]{1,0:T(8,128)(2,1)}, bf16[512,896]{1,0:T(8,128)(2,1)}, u32[]{:S(2)}, u32[]{:S(2)}) collective-permute-start(bf16[512,896]{1,0:T(8,128)(2,1)} %memory_ref.1), channel_id=1, source_target_pairs={{0,2},{1,3},{2,0},{3,1},{4,6},{5,7},{6,4},{7,5},{8,10},{9,11},{10,... | collective-permute-start | bytes 2752520 | tf_op jit(solution)/shard_map/ppermute | solution.py:586
  3.7 0.2 collective-permute-start
  3.9 0.0 collective-permute-done.2.refs_3_
  3.9 4.3 %memory_near_half.1 = (f32[512,256]{1,0:T(8,128)}, f32[512,16]{1,0:T(8,128)}, s32[8]{0:T(128)}) custom-call(s32[1]{0:T(128)} %bitcast.refs_0_.place_ref, s32[4,8]{1,0:T(4,128)} %refs_1_.5, bf16[512,896]{1,0:T(8,128)(2,1)} %memory_ref.1, bf16[512,896]{1,0:T(8,128)(2,1)} %collective-permute-done.2.refs_3_, bf16[3584,128]{1,0:T(8,128)(2,1)} %refs_4_.7, ...), custom_call_target="tpu_custom_call" | custom-call | tf_op jit(solution)/shard_map/memory_near_half/pallas_call | solution.py:693
  8.2 0.7 copy.21
  8.9 13.1 %all_to_all.21 = s32[8,1,1]{2,1,0:T(1,128)S(1)} all-to-all(s32[8,1,1]{2,1,0:T(1,128)S(1)} %copy.21), channel_id=1, replica_groups=mesh['tm'=8,'heads'=4] {'tm'}, dimensions={0} | all-to-all | bytes 64 | tf_op jit(solution)/shard_map/all_to_all | solution.py:701
  22.0 0.8 reduce.refs_1_.refs_0_
  22.8 2.2 %collective-permute-done.3.refs_0_ = bf16[512,896]{1,0:T(8,128)(2,1)} collective-permute-done((bf16[512,896]{1,0:T(8,128)(2,1)}, bf16[512,896]{1,0:T(8,128)(2,1)}, u32[]{:S(2)}, u32[]{:S(2)}) %collective-permute-start.3) | collective-permute-done | bytes 917536 | tf_op jit(solution)/shard_map/ppermute | solution.py:586
  25.0 0.0 collective-permute-start.4
  25.0 0.0 collective-permute-done.x1
  25.0 1.8 %collective-permute-start.1 = (bf16[512,896]{1,0:T(8,128)(2,1)}, bf16[512,896]{1,0:T(8,128)(2,1)}, u32[]{:S(2)}, u32[]{:S(2)}) collective-permute-start(bf16[512,896]{1,0:T(8,128)(2,1)} %collective-permute-done.x1), channel_id=1, source_target_pairs={{0,2},{1,3},{2,0},{3,1},{4,6},{5,7},{6,4},{7,5},{8,10},{9,11},{10,... | collective-permute-start | bytes 2752520 | tf_op jit(solution)/shard_map/ppermute | solution.py:586
  26.8 3.0 %memory_far_quarter.1 = (f32[512,256]{1,0:T(8,128)}, f32[512,16]{1,0:T(8,128)}) custom-call(s32[1]{0:T(128)} %bitcast.refs_0_.place_ref, bf16[512,896]{1,0:T(8,128)(2,1)} %in_order.2.x2, f32[512,256]{1,0:T(8,128)} %get-tuple-element.33.acc_hbm, f32[512,16]{1,0:T(8,128)} %get-tuple-element.34.low_hbm, bf16[3584,128]{1,0:T(8,128)(2,1)} %refs_4_.7, ...), custom_call_target="tpu_custom_call" | custom-call | tf_op jit(solution)/shard_map/memory_far_quarter/pallas_call | solution.py:706
  29.8 0.0 collective-permute-done.4.refs_2_
  29.9 3.9 %memory_pairs.1.refs_7_ = bf16[8,272,128]{2,1,0:T(8,128)(2,1)} custom-call(s32[1]{0:T(128)} %bitcast.refs_0_.place_ref, s32[8]{0:T(128)} %reduce.refs_1_.refs_0_, bf16[512,896]{1,0:T(8,128)(2,1)} %collective-permute-done.4.refs_2_, f32[512,256]{1,0:T(8,128)} %get-tuple-element.35.refs_3_, f32[512,16]{1,0:T(8,128)} %get-tuple-element.36.refs_4_, ...), custom_call_target="tpu_custom_call" | custom-call | tf_op jit(solution)/shard_map/memory_pairs/pallas_call | solution.py:713
  33.7 5.8 %all-to-all-start.1 = ((bf16[8,272,128]{2,1,0:T(8,128)(2,1)}), bf16[8,272,128]{2,1,0:T(8,128)(2,1)}, u32[]{:S(2)}, u32[]{:S(2)}) async-start(bf16[8,272,128]{2,1,0:T(8,128)(2,1)} %memory_pairs.1.refs_7_), calls=%async_computation.1 | async-start | bytes 1114112 | tf_op jit(solution)/shard_map/all_to_all | solution.py:720
  39.5 8.9 %project_near_half.1 = (f32[512,896]{1,0:T(8,128)}, f32[512,256]{1,0:T(8,128)}, f32[512,32]{1,0:T(8,128)}, bf16[512,896]{1,0:T(8,128)(2,1)}, bf16[896,512]{1,0:T(8,128)(2,1)}) custom-call(s32[1]{0:T(128)} %bitcast.refs_0_.place_ref, bf16[512,896]{1,0:T(8,128)(2,1)} %slab_ref.1, bf16[512,896]{1,0:T(8,128)(2,1)} %collective-permute-done.x1, ...), custom_call_target="tpu_custom_call" | custom-call | tf_op jit(solution)/shard_map/project_near_half/pallas_call | solution.py:721
  48.5 0.0 collective-permute-done.1.refs_0_
  48.5 0.1 collective-permute-start.5
  48.6 5.8 %project_far_quarter.1 = (f32[512,896]{1,0:T(8,128)}, f32[512,256]{1,0:T(8,128)}, f32[512,32]{1,0:T(8,128)}) custom-call(s32[1]{0:T(128)} %bitcast.refs_0_.place_ref, bf16[512,896]{1,0:T(8,128)(2,1)} %in_order.3.x3, bf16[3584,896]{1,0:T(8,128)(2,1)} %refs_3_.5, bf16[3584,128]{1,0:T(8,128)(2,1)} %refs_4_.7, bf16[3584,128]{1,0:T(8,128)(2,1)} %refs_5_.5, ...), custom_call_target="tpu_custom_call" | custom-call | tf_op jit(solution)/shard_map/project_far_quarter/pallas_call | solution.py:736
  54.3 0.0 collective-permute-done.5.refs_2_
  54.3 0.9 all-to-all-done.1.refs_11_
  55.2 0.0 copy-start.3
  55.2 0.0 copy-start
  55.2 26.5 %span_attention.1 = (f32[40,512]{1,0:T(8,128)}, f32[72,512]{1,0:T(8,128)}, f32[8,16,128]{2,1,0:T(8,128)}) custom-call(s32[1]{0:T(128)} %bitcast.refs_0_.place_ref, s32[4]{0:T(128)} %refs_1_.9, bf16[512,896]{1,0:T(8,128)(2,1)} %collective-permute-done.5.refs_2_, bf16[3584,896]{1,0:T(8,128)(2,1)} %refs_3_.5, bf16[3584,128]{1,0:T(8,128)(2,1)} %refs_4_.7, ...), custom_call_target="tpu_custom_call" | custom-call | flops 10569646080 | bytes 1835008 | tf_op jit(solution)/shard_map/span_attention/pallas_call | solution.py:746
  81.7 0.0 copy-start.1
  81.7 5.3 %all-to-all-start.2 = ((f32[8,16,128]{2,1,0:T(8,128)}), f32[8,16,128]{2,1,0:T(8,128)S(1)}, u32[]{:S(2)}, u32[]{:S(2)}) async-start(f32[8,16,128]{2,1,0:T(8,128)} %get-tuple-element.47), calls=%async_computation.2 | async-start | bytes 131072 | tf_op jit(solution)/shard_map/all_to_all | solution.py:787
  87.0 1.0 collective-permute-start.8
  88.0 0.9 collective-permute-start.7
  89.0 0.0 collective-permute-start.6
  89.0 5.0 %all-to-all-done.2.refs_1_ = f32[8,16,128]{2,1,0:T(8,128)S(1)} async-done(((f32[8,16,128]{2,1,0:T(8,128)}), f32[8,16,128]{2,1,0:T(8,128)S(1)}, u32[]{:S(2)}, u32[]{:S(2)}) %all-to-all-start.2) | async-done | bytes 65568 | tf_op jit(solution)/shard_map/all_to_all | solution.py:787
  93.9 0.0 copy-done.3
  93.9 0.6 owned_cotangent.1.dep_ref.c0
  94.5 0.0 collective-permute-done.8.c3
  94.5 0.0 collective-permute-done.7.c2
  94.5 0.0 collective-permute-done.6.c1
  94.5 0.0 copy-done
  94.6 0.0 copy-start.2
  94.6 0.9 copy-done.2
  95.5 0.8 first_down.1
  96.2 1.2 %collective-permute-start.12 = (f32[16,1920]{1,0:T(8,128)S(1)}, f32[16,1920]{1,0:T(8,128)S(1)}, u32[]{:S(2)}, u32[]{:S(2)}) collective-permute-start(f32[16,1920]{1,0:T(8,128)S(1)} %get-tuple-element.50.q0), channel_id=1, source_target_pairs={{0,4},{4,0},{8,12},{12,8},{16,20},{20,16},{24,28},{28,24},{1,5},{5... | collective-permute-start | bytes 368648 | tf_op jit(solution)/shard_map/ppermute | solution.py:586
  97.4 0.5 collective-permute-start.11
  97.9 0.8 collective-permute-start.10
  98.7 0.6 collective-permute-start.9
  99.3 1.6 %collective-permute-done.11.c3 = f32[16,512]{1,0:T(8,128)S(1)} collective-permute-done((f32[16,512]{1,0:T(8,128)S(1)}, f32[16,512]{1,0:T(8,128)S(1)}, u32[]{:S(2)}, u32[]{:S(2)}) %collective-permute-start.11) | collective-permute-done | bytes 32800 | tf_op jit(solution)/shard_map/ppermute | solution.py:586
  100.9 1.1 collective-permute-done.10.c2
  102.0 0.0 collective-permute-done.9.c1
  102.0 0.0 collective-permute-done.12.q1
  102.0 0.0 copy-done.1
  102.0 0.3 second_down.1
  102.3 1.5 %collective-permute-start.13 = (f32[16,1920]{1,0:T(8,128)S(1)}, f32[16,1920]{1,0:T(8,128)S(1)}, u32[]{:S(2)}, u32[]{:S(2)}) collective-permute-start(f32[16,1920]{1,0:T(8,128)S(1)} %get-tuple-element.51.q0), channel_id=1, source_target_pairs={{0,8},{4,12},{8,0},{12,4},{16,24},{20,28},{24,16},{28,20},{1,9},{5... | collective-permute-start | bytes 368648 | tf_op jit(solution)/shard_map/ppermute | solution.py:586
  103.8 0.6 collective-permute-start.14
  104.4 3.6 %collective-permute-done.14.v1 = f32[16,896]{1,0:T(8,128)S(1)} collective-permute-done((f32[16,896]{1,0:T(8,128)S(1)}, f32[16,896]{1,0:T(8,128)S(1)}, u32[]{:S(2)}, u32[]{:S(2)}) %collective-permute-start.14) | collective-permute-done | bytes 57376 | tf_op jit(solution)/shard_map/ppermute | solution.py:586
  108.0 0.0 collective-permute-done.13.q1
  108.0 2.4 %collective-permute-start.15 = (bf16[16,2816]{1,0:T(8,128)(2,1)S(1)}, bf16[16,2816]{1,0:T(8,128)(2,1)S(1)}, u32[]{:S(2)}, u32[]{:S(2)}) collective-permute-start(bf16[16,2816]{1,0:T(8,128)(2,1)S(1)} %get-tuple-element.53.here_ref), channel_id=1, source_target_pairs={{0,16},{4,20},{8,24},{12,28},{16,0},{20,4},{24,8},{28,12},{1,17},{... | collective-permute-start | bytes 270344 | tf_op jit(solution)/shard_map/ppermute | solution.py:586
  110.4 1.0 collective-permute-start.17
  111.4 0.1 collective-permute-start.16
  111.6 4.5 %collective-permute-done.17.v3 = bf16[16,896]{1,0:T(8,128)(2,1)S(1)} collective-permute-done((bf16[16,896]{1,0:T(8,128)(2,1)S(1)}, bf16[16,896]{1,0:T(8,128)(2,1)S(1)}, u32[]{:S(2)}, u32[]{:S(2)}) %collective-permute-start.17) | collective-permute-done | bytes 28704 | tf_op jit(solution)/shard_map/ppermute | solution.py:586
  116.1 0.0 collective-permute-done.16.v1
  116.1 0.0 collective-permute-done.15.there_ref
  116.1 0.7 finish_outputs.1
  (3 shorter events, 0.0 us)
Async XLA Ops:
  0.6 3.3 %collective-permute-start.2 = (bf16[512,896]{1,0:T(8,128)(2,1)}, bf16[512,896]{1,0:T(8,128)(2,1)}, u32[]{:S(2)}, u32[]{:S(2)}) collective-permute-start(bf16[512,896]{1,0:T(8,128)(2,1)} %memory_ref.1), channel_id=1, source_target_pairs={{0,1},{1,0},{2,3},{3,2},{4,5},{5,4},{6,7},{7,6},{8,9},{9,8},{10,11... | collective-permute-start | bytes 2752520 | tf_op jit(solution)/shard_map/ppermute | solution.py:586
  1.1 23.9 %collective-permute-start.3 = (bf16[512,896]{1,0:T(8,128)(2,1)}, bf16[512,896]{1,0:T(8,128)(2,1)}, u32[]{:S(2)}, u32[]{:S(2)}) collective-permute-start(bf16[512,896]{1,0:T(8,128)(2,1)} %memory_ref.1), channel_id=1, source_target_pairs={{0,2},{1,3},{2,0},{3,1},{4,6},{5,7},{6,4},{7,5},{8,10},{9,11},{10,... | collective-permute-start | bytes 2752520 | tf_op jit(solution)/shard_map/ppermute | solution.py:586
  3.7 21.3 %collective-permute-start = (bf16[512,896]{1,0:T(8,128)(2,1)}, bf16[512,896]{1,0:T(8,128)(2,1)}, u32[]{:S(2)}, u32[]{:S(2)}) collective-permute-start(bf16[512,896]{1,0:T(8,128)(2,1)} %slab_ref.1), channel_id=1, source_target_pairs={{0,1},{1,0},{2,3},{3,2},{4,5},{5,4},{6,7},{7,6},{8,9},{9,8},{10,11... | collective-permute-start | bytes 2752520 | tf_op jit(solution)/shard_map/ppermute | solution.py:586
  25.0 4.8 %collective-permute-start.4 = (bf16[512,896]{1,0:T(8,128)(2,1)}, bf16[512,896]{1,0:T(8,128)(2,1)}, u32[]{:S(2)}, u32[]{:S(2)}) collective-permute-start(bf16[512,896]{1,0:T(8,128)(2,1)} %in_order.2.x2), channel_id=1, source_target_pairs={{0,1},{1,0},{2,3},{3,2},{4,5},{5,4},{6,7},{7,6},{8,9},{9,8},{10,11... | collective-permute-start | bytes 2752520 | tf_op jit(solution)/shard_map/ppermute | solution.py:586
  25.0 23.4 %collective-permute-start.1 = (bf16[512,896]{1,0:T(8,128)(2,1)}, bf16[512,896]{1,0:T(8,128)(2,1)}, u32[]{:S(2)}, u32[]{:S(2)}) collective-permute-start(bf16[512,896]{1,0:T(8,128)(2,1)} %collective-permute-done.x1), channel_id=1, source_target_pairs={{0,2},{1,3},{2,0},{3,1},{4,6},{5,7},{6,4},{7,5},{8,10},{9,11},{10,... | collective-permute-start | bytes 2752520 | tf_op jit(solution)/shard_map/ppermute | solution.py:586
  33.7 21.5 %all-to-all-start.1 = ((bf16[8,272,128]{2,1,0:T(8,128)(2,1)}), bf16[8,272,128]{2,1,0:T(8,128)(2,1)}, u32[]{:S(2)}, u32[]{:S(2)}) async-start(bf16[8,272,128]{2,1,0:T(8,128)(2,1)} %memory_pairs.1.refs_7_), calls=%async_computation.1 | async-start | bytes 1114112 | tf_op jit(solution)/shard_map/all_to_all | solution.py:720
  48.5 5.9 %collective-permute-start.5 = (bf16[512,896]{1,0:T(8,128)(2,1)}, bf16[512,896]{1,0:T(8,128)(2,1)}, u32[]{:S(2)}, u32[]{:S(2)}) collective-permute-start(bf16[512,896]{1,0:T(8,128)(2,1)} %in_order.3.x3), channel_id=1, source_target_pairs={{0,1},{1,0},{2,3},{3,2},{4,5},{5,4},{6,7},{7,6},{8,9},{9,8},{10,11... | collective-permute-start | bytes 2752520 | tf_op jit(solution)/shard_map/ppermute | solution.py:586
  55.2 38.7 %copy-start.3 = (s32[8]{0:T(128)S(1)}, s32[8]{0:T(128)}, u32[]{:S(2)}) copy-start(s32[8]{0:T(128)} %reduce.refs_1_.refs_0_) | copy-start | bytes 100
  55.2 39.3 %copy-start = (bf16[512,896]{1,0:T(8,128)(2,1)S(1)}, bf16[512,896]{1,0:T(8,128)(2,1)}, u32[]{:S(2)}) copy-start(bf16[512,896]{1,0:T(8,128)(2,1)} %slab_ref.1) | copy-start | bytes 2752516
  81.7 20.3 %copy-start.1 = (bf16[512,896]{1,0:T(8,128)(2,1)S(1)}, bf16[512,896]{1,0:T(8,128)(2,1)}, u32[]{:S(2)}) copy-start(bf16[512,896]{1,0:T(8,128)(2,1)} %memory_ref.1) | copy-start | bytes 2752516
  81.7 12.2 %all-to-all-start.2 = ((f32[8,16,128]{2,1,0:T(8,128)}), f32[8,16,128]{2,1,0:T(8,128)S(1)}, u32[]{:S(2)}, u32[]{:S(2)}) async-start(f32[8,16,128]{2,1,0:T(8,128)} %get-tuple-element.47), calls=%async_computation.2 | async-start | bytes 131072 | tf_op jit(solution)/shard_map/all_to_all | solution.py:787
  87.0 7.5 %collective-permute-start.8 = (f32[40,512]{1,0:T(8,128)}, f32[40,512]{1,0:T(8,128)S(1)}, u32[]{:S(2)}, u32[]{:S(2)}) collective-permute-start(f32[40,512]{1,0:T(8,128)} %get-tuple-element.46), channel_id=1, source_target_pairs={{0,3},{1,2},{2,1},{3,0},{4,7},{5,6},{6,5},{7,4},{8,11},{9,10},{10,... | collective-permute-start | bytes 245768 | tf_op jit(solution)/shard_map/ppermute | solution.py:586
  88.0 6.5 %collective-permute-start.7 = (f32[40,512]{1,0:T(8,128)}, f32[40,512]{1,0:T(8,128)S(1)}, u32[]{:S(2)}, u32[]{:S(2)}) collective-permute-start(f32[40,512]{1,0:T(8,128)} %get-tuple-element.46), channel_id=1, source_target_pairs={{0,2},{1,3},{2,0},{3,1},{4,6},{5,7},{6,4},{7,5},{8,10},{9,11},{10,... | collective-permute-start | bytes 245768 | tf_op jit(solution)/shard_map/ppermute | solution.py:586
  89.0 5.6 %collective-permute-start.6 = (f32[40,512]{1,0:T(8,128)}, f32[40,512]{1,0:T(8,128)S(1)}, u32[]{:S(2)}, u32[]{:S(2)}) collective-permute-start(f32[40,512]{1,0:T(8,128)} %get-tuple-element.46), channel_id=1, source_target_pairs={{0,1},{1,0},{2,3},{3,2},{4,5},{5,4},{6,7},{7,6},{8,9},{9,8},{10,11... | collective-permute-start | bytes 245768 | tf_op jit(solution)/shard_map/ppermute | solution.py:586
  94.6 0.9 copy-start.2
  96.2 5.8 %collective-permute-start.12 = (f32[16,1920]{1,0:T(8,128)S(1)}, f32[16,1920]{1,0:T(8,128)S(1)}, u32[]{:S(2)}, u32[]{:S(2)}) collective-permute-start(f32[16,1920]{1,0:T(8,128)S(1)} %get-tuple-element.50.q0), channel_id=1, source_target_pairs={{0,4},{4,0},{8,12},{12,8},{16,20},{20,16},{24,28},{28,24},{1,5},{5... | collective-permute-start | bytes 368648 | tf_op jit(solution)/shard_map/ppermute | solution.py:586
  97.4 3.5 %collective-permute-start.11 = (f32[16,512]{1,0:T(8,128)S(1)}, f32[16,512]{1,0:T(8,128)S(1)}, u32[]{:S(2)}, u32[]{:S(2)}) collective-permute-start(f32[16,512]{1,0:T(8,128)S(1)} %owned_cotangent.1.dep_ref.c0), channel_id=1, source_target_pairs={{0,3},{1,2},{2,1},{3,0},{4,7},{5,6},{6,5},{7,4},{8,11},{9,10},{10,... | collective-permute-start | bytes 98312 | tf_op jit(solution)/shard_map/ppermute | solution.py:586
  97.9 4.1 %collective-permute-start.10 = (f32[16,512]{1,0:T(8,128)S(1)}, f32[16,512]{1,0:T(8,128)S(1)}, u32[]{:S(2)}, u32[]{:S(2)}) collective-permute-start(f32[16,512]{1,0:T(8,128)S(1)} %owned_cotangent.1.dep_ref.c0), channel_id=1, source_target_pairs={{0,2},{1,3},{2,0},{3,1},{4,6},{5,7},{6,4},{7,5},{8,10},{9,11},{10,... | collective-permute-start | bytes 98312 | tf_op jit(solution)/shard_map/ppermute | solution.py:586
  98.7 3.3 %collective-permute-start.9 = (f32[16,512]{1,0:T(8,128)S(1)}, f32[16,512]{1,0:T(8,128)S(1)}, u32[]{:S(2)}, u32[]{:S(2)}) collective-permute-start(f32[16,512]{1,0:T(8,128)S(1)} %owned_cotangent.1.dep_ref.c0), channel_id=1, source_target_pairs={{0,1},{1,0},{2,3},{3,2},{4,5},{5,4},{6,7},{7,6},{8,9},{9,8},{10,11... | collective-permute-start | bytes 98312 | tf_op jit(solution)/shard_map/ppermute | solution.py:586
  102.3 5.7 %collective-permute-start.13 = (f32[16,1920]{1,0:T(8,128)S(1)}, f32[16,1920]{1,0:T(8,128)S(1)}, u32[]{:S(2)}, u32[]{:S(2)}) collective-permute-start(f32[16,1920]{1,0:T(8,128)S(1)} %get-tuple-element.51.q0), channel_id=1, source_target_pairs={{0,8},{4,12},{8,0},{12,4},{16,24},{20,28},{24,16},{28,20},{1,9},{5... | collective-permute-start | bytes 368648 | tf_op jit(solution)/shard_map/ppermute | solution.py:586
  103.8 4.2 %collective-permute-start.14 = (f32[16,896]{1,0:T(8,128)S(1)}, f32[16,896]{1,0:T(8,128)S(1)}, u32[]{:S(2)}, u32[]{:S(2)}) collective-permute-start(f32[16,896]{1,0:T(8,128)S(1)} %get-tuple-element.52.v0), channel_id=1, source_target_pairs={{0,4},{4,0},{8,12},{12,8},{16,20},{20,16},{24,28},{28,24},{1,5},{5... | collective-permute-start | bytes 172040 | tf_op jit(solution)/shard_map/ppermute | solution.py:586
  108.0 8.1 %collective-permute-start.15 = (bf16[16,2816]{1,0:T(8,128)(2,1)S(1)}, bf16[16,2816]{1,0:T(8,128)(2,1)S(1)}, u32[]{:S(2)}, u32[]{:S(2)}) collective-permute-start(bf16[16,2816]{1,0:T(8,128)(2,1)S(1)} %get-tuple-element.53.here_ref), channel_id=1, source_target_pairs={{0,16},{4,20},{8,24},{12,28},{16,0},{20,4},{24,8},{28,12},{1,17},{... | collective-permute-start | bytes 270344 | tf_op jit(solution)/shard_map/ppermute | solution.py:586
  110.4 5.7 %collective-permute-start.17 = (bf16[16,896]{1,0:T(8,128)(2,1)S(1)}, bf16[16,896]{1,0:T(8,128)(2,1)S(1)}, u32[]{:S(2)}, u32[]{:S(2)}) collective-permute-start(bf16[16,896]{1,0:T(8,128)(2,1)S(1)} %get-tuple-element.54), channel_id=1, source_target_pairs={{0,24},{4,28},{8,16},{12,20},{16,8},{20,12},{24,0},{28,4},{1,25},{... | collective-permute-start | bytes 86024 | tf_op jit(solution)/shard_map/ppermute | solution.py:586
  111.4 4.7 %collective-permute-start.16 = (bf16[16,896]{1,0:T(8,128)(2,1)S(1)}, bf16[16,896]{1,0:T(8,128)(2,1)S(1)}, u32[]{:S(2)}, u32[]{:S(2)}) collective-permute-start(bf16[16,896]{1,0:T(8,128)(2,1)S(1)} %get-tuple-element.54), channel_id=1, source_target_pairs={{0,8},{4,12},{8,0},{12,4},{16,24},{20,28},{24,16},{28,20},{1,9},{5... | collective-permute-start | bytes 86024 | tf_op jit(solution)/shard_map/ppermute | solution.py:586

commit v11 on v10

--- a/solution.py
+++ b/solution.py
@@ -408,15 +408,21 @@
     (q_s, k_own, v_own, low_s, low_m_s, grad_ref, grad_t_ref, k_all, v_all, kt_all, vt_all, kt_own, vt_own, bias_s, s_s, dp_s,
      p_s, ds_s, att_s, dq_s, dv_s, up_ref, more_sems) = refs[27:]
     seen = peers * BLK
-    groups = project_pieces(place_ref, (2,), (x2,), hbm, scratch, sems)
-    pairs = list(zip(early, sum_refs))
+    pairs = []
     for b in range(peers):
         at = slice(b * BLK, (b + 1) * BLK)
         pairs.append((got.at[b, pl.ds(0, BLK), :], k_all.at[at, :]))
         pairs.append((got.at[b, pl.ds(BLK, BLK), :], v_all.at[at, :]))
         pairs.append((got.at[b, pl.ds(2 * BLK, RANK), :], low_m_s.at[b]))
-    pairs += [(grad_hbm, grad_ref), (grad_t_hbm, grad_t_ref)]
-    copies = start_copies(pairs, more_sems)
+    fetched = start_copies(pairs, more_sems)
+    groups = project_pieces(place_ref, (2,), (x2,), hbm, scratch, sems)
+    pairs = list(zip(early, sum_refs)) + [(grad_hbm, grad_ref), (grad_t_hbm, grad_t_ref)]
+    copies = start_copies(pairs, more_sems, len(fetched))
+    wait_all(fetched)
+    for b in range(peers):
+        at = slice(b * BLK, (b + 1) * BLK)
+        kt_all[:, at] = jnp.transpose(k_all[at, :])
+        vt_all[:, at] = jnp.transpose(v_all[at, :])
     wait_all(groups[0])
     terms = project_terms(0, scratch)
     wait_all(copies[:3])
@@ -426,12 +432,7 @@
     k_own[...] = kv_acc[:, :HD].astype(jnp.bfloat16)
     v_own[...] = (kv_acc[:, HD:] + dot_nn(low[:, RANK:], vup_ref[...])).astype(jnp.bfloat16)
     low_s[...] = jnp.transpose(low_acc).astype(jnp.bfloat16)
-    wait_all(copies[3 : 3 + 3 * peers])
-    for b in range(peers):
-        at = slice(b * BLK, (b + 1) * BLK)
-        kt_all[:, at] = jnp.transpose(k_all[at, :])
-        vt_all[:, at] = jnp.transpose(v_all[at, :])
-    wait_all(copies[3 + 3 * peers : -1])
+    wait_all(copies[3:-1])
     dv_s[...] = jnp.zeros_like(dv_s)
     up_ref[...] = jnp.zeros_like(up_ref)
     scale = HD ** (-0.5)
@@ -534,15 +535,18 @@
         at += RANK
 
 
-def own_kernel(peers, asked_ref, back_ref, out_ref, sum_s):
+def own_kernel(peers, asked_ref, back_ref, mine_hbm, out_ref, mine_ref, sum_s, sem):
+    copy = pltpu.make_async_copy(mine_hbm, mine_ref, sem)
+    copy.start()
     sum_s[...] = jnp.zeros_like(sum_s)
     for r in range(peers):
         block = asked_ref[r]
         sum_s[block] = sum_s[block] + back_ref[r]
     out_ref[...] = jnp.concatenate([sum_s[m] for m in range(sum_s.shape[0])], 1)
-
-
-def first_down_kernel(mine_ref, c1, c2, c3, slab_ref, dep_ref, logit_ref, query_ref, value_ref):
+    copy.wait()
+
+
+def first_down_kernel(mine_ref, c1, c2, c3, slab_ref, logit_ref, query_ref, value_ref):
     own, wide = c1.shape
     cot = (mine_ref[:own, :] + c1[...]) + (c2[...] + c3[...])
     logit_ref[...] = cot[2 * RANK :]
@@ -785,24 +789,24 @@
     )(place, boundary, tok_cross, *weights, *early, got, grad, grad_t, query_up, value_up, tag_t)
 
     back = lax.all_to_all(mcot, "tm", split_axis=0, concat_axis=0, tiled=True)
-    cots = [mine] + [swap(cot, d) for d in range(1, 4)]
-    own = run(
+    own, mine = run(
         lambda *refs: own_kernel(peers, *refs),
         "owned_cotangent",
-        shaped(RANK, mem_rows),
-        [smem()] + [vmem()],
-        [pltpu.VMEM((blocks, RANK, BLK), f32)],
+        (shaped(RANK, mem_rows), shaped(*mine.shape)),
+        [smem(), vmem(), anywhere()],
+        [pltpu.VMEM((blocks, RANK, BLK), f32), pltpu.SemaphoreType.DMA],
         room=8,
-    )(asked, back)
+    )(asked, back, mine)
+    cots = [mine] + [swap(cot, d) for d in range(1, 4)]
     logits, query_sum, value_part = run(
         first_down_kernel,
         "first_down",
         (shaped(tags, tok_rows), shaped(RANK, width + query_width + HD), shaped(RANK, width)),
-        [vmem()] * 5 + [anywhere()],
+        [vmem()] * 5,
         flops=4 * RANK * tok_rows * width,
         moved=2 * tok_rows * width,
         room=8,
-    )(*cots, slab_tokens, own)
+    )(*cots, slab_tokens)
     owns = [own] + [swap(own, d) for d in range(1, 4)]
     value_sum, query_sum = run(
         second_down_kernel,

time: 117 us -> 116 us (level)
  transfers between devices with their start and end apart: 20 -> 20, of which waited for: 7 -> 8; matrix products, arithmetic and copies ran while one was open for 1% -> 1% of each run, Pallas kernels for 23% -> 23%
where the time goes in v11:
time: 116 us
  Pallas kernels  54.7 us (47%)
  starting transfers between devices  26.1 us (22%)
  waiting for transfers between devices  18.7 us (16%)
  blocking collectives  13.1 us (11%)
  local copies, waits for them, and re-layouts  1.66 us (1%)
    pallas_call x1, Pallas kernels, fast(): run(lambda *refs: attention_kernel(peers, heads, *refs), 'span_attention'...  26.3 us
    ppermute x18, starting transfers between devices, swap(): lax.ppermute(x, axis, [(i, i ^ bit) for i in range(lax.axis_size(axis))])  14.9 us
    all_to_all x1, blocking collectives, fast(): lax.all_to_all(wanted, 'tm', split_axis=0, concat_axis=0, tiled=True)  13.1 us
    ppermute x18, waiting for transfers between devices, swap(): lax.ppermute(x, axis, [(i, i ^ bit) for i in range(lax.axis_size(axis))])  12.9 us
    pallas_call x1, Pallas kernels, fast(): run(project_early_kernel, 'project_near_half', (shaped(tok_rows, query_wi...  8.91 us
    pallas_call x1, Pallas kernels, fast(): run(project_middle_kernel, 'project_far_quarter', (shaped(tok_rows, query...  5.82 us
    all_to_all x1, starting transfers between devices, fast(): got = lax.all_to_all(pairs, 'tm', split_axis=0, concat_axis=0, tiled=True)  5.82 us
    all_to_all x1, starting transfers between devices, fast(): back = lax.all_to_all(mcot, 'tm', split_axis=0, concat_axis=0, tiled=True)  5.41 us
  transfers between devices with their start and end apart: 20, of which 8 were waited for; matrix products, arithmetic and copies ran while one was open for 1% of the time, Pallas kernels for 23%

profile of v11, /device:TPU:0, one launch (start us, length us, event | category | flops | bytes accessed | tf_op | source)
XLA Modules:
  0.0 115.8 jit_solution(9323535125111571032)
XLA Ops:
  0.6 0.5 collective-permute-start
  1.1 2.6 %collective-permute-start.3 = (bf16[512,896]{1,0:T(8,128)(2,1)}, bf16[512,896]{1,0:T(8,128)(2,1)}, u32[]{:S(2)}, u32[]{:S(2)}) collective-permute-start(bf16[512,896]{1,0:T(8,128)(2,1)} %memory_ref.1), channel_id=1, source_target_pairs={{0,2},{1,3},{2,0},{3,1},{4,6},{5,7},{6,4},{7,5},{8,10},{9,11},{10,... | collective-permute-start | bytes 2752520 | tf_op jit(solution)/shard_map/ppermute | solution.py:590
  3.7 0.2 collective-permute-start.1
  3.9 0.0 collective-permute-done.refs_3_
  3.9 4.3 %memory_near_half.1 = (f32[512,256]{1,0:T(8,128)}, f32[512,16]{1,0:T(8,128)}, s32[8]{0:T(128)}) custom-call(s32[1]{0:T(128)} %bitcast.refs_0_.place_ref, s32[4,8]{1,0:T(4,128)} %refs_1_.5, bf16[512,896]{1,0:T(8,128)(2,1)} %memory_ref.1, bf16[512,896]{1,0:T(8,128)(2,1)} %collective-permute-done.refs_3_, bf16[3584,128]{1,0:T(8,128)(2,1)} %refs_4_.7, ...), custom_call_target="tpu_custom_call" | custom-call | tf_op jit(solution)/shard_map/memory_near_half/pallas_call | solution.py:697
  8.2 0.7 copy.21
  8.9 13.1 %all_to_all.21 = s32[8,1,1]{2,1,0:T(1,128)S(1)} all-to-all(s32[8,1,1]{2,1,0:T(1,128)S(1)} %copy.21), channel_id=1, replica_groups=mesh['tm'=8,'heads'=4] {'tm'}, dimensions={0} | all-to-all | bytes 64 | tf_op jit(solution)/shard_map/all_to_all | solution.py:705
  22.0 0.8 reduce.refs_1_.refs_0_
  22.8 2.2 %collective-permute-done.3.refs_0_ = bf16[512,896]{1,0:T(8,128)(2,1)} collective-permute-done((bf16[512,896]{1,0:T(8,128)(2,1)}, bf16[512,896]{1,0:T(8,128)(2,1)}, u32[]{:S(2)}, u32[]{:S(2)}) %collective-permute-start.3) | collective-permute-done | bytes 917536 | tf_op jit(solution)/shard_map/ppermute | solution.py:590
  25.0 0.0 collective-permute-start.4
  25.0 0.0 collective-permute-done.1.x1
  25.0 1.8 %collective-permute-start.2 = (bf16[512,896]{1,0:T(8,128)(2,1)}, bf16[512,896]{1,0:T(8,128)(2,1)}, u32[]{:S(2)}, u32[]{:S(2)}) collective-permute-start(bf16[512,896]{1,0:T(8,128)(2,1)} %collective-permute-done.1.x1), channel_id=1, source_target_pairs={{0,2},{1,3},{2,0},{3,1},{4,6},{5,7},{6,4},{7,5},{8,10},{9,11},{10,... | collective-permute-start | bytes 2752520 | tf_op jit(solution)/shard_map/ppermute | solution.py:590
  26.8 3.0 %memory_far_quarter.1 = (f32[512,256]{1,0:T(8,128)}, f32[512,16]{1,0:T(8,128)}) custom-call(s32[1]{0:T(128)} %bitcast.refs_0_.place_ref, bf16[512,896]{1,0:T(8,128)(2,1)} %in_order.2.x2, f32[512,256]{1,0:T(8,128)} %get-tuple-element.35.acc_hbm, f32[512,16]{1,0:T(8,128)} %get-tuple-element.36.low_hbm, bf16[3584,128]{1,0:T(8,128)(2,1)} %refs_4_.7, ...), custom_call_target="tpu_custom_call" | custom-call | tf_op jit(solution)/shard_map/memory_far_quarter/pallas_call | solution.py:710
  29.8 0.0 collective-permute-done.4.refs_2_
  29.9 3.8 %memory_pairs.1.refs_7_ = bf16[8,272,128]{2,1,0:T(8,128)(2,1)} custom-call(s32[1]{0:T(128)} %bitcast.refs_0_.place_ref, s32[8]{0:T(128)} %reduce.refs_1_.refs_0_, bf16[512,896]{1,0:T(8,128)(2,1)} %collective-permute-done.4.refs_2_, f32[512,256]{1,0:T(8,128)} %get-tuple-element.37.refs_3_, f32[512,16]{1,0:T(8,128)} %get-tuple-element.38.refs_4_, ...), custom_call_target="tpu_custom_call" | custom-call | tf_op jit(solution)/shard_map/memory_pairs/pallas_call | solution.py:717
  33.7 5.8 %all-to-all-start.1 = ((bf16[8,272,128]{2,1,0:T(8,128)(2,1)}), bf16[8,272,128]{2,1,0:T(8,128)(2,1)}, u32[]{:S(2)}, u32[]{:S(2)}) async-start(bf16[8,272,128]{2,1,0:T(8,128)(2,1)} %memory_pairs.1.refs_7_), calls=%async_computation.1 | async-start | bytes 1114112 | tf_op jit(solution)/shard_map/all_to_all | solution.py:724
  39.5 8.9 %project_near_half.1 = (f32[512,896]{1,0:T(8,128)}, f32[512,256]{1,0:T(8,128)}, f32[512,32]{1,0:T(8,128)}, bf16[512,896]{1,0:T(8,128)(2,1)}, bf16[896,512]{1,0:T(8,128)(2,1)}) custom-call(s32[1]{0:T(128)} %bitcast.refs_0_.place_ref, bf16[512,896]{1,0:T(8,128)(2,1)} %slab_ref.1, bf16[512,896]{1,0:T(8,128)(2,1)} %collective-permute-done.1.x1, ...), custom_call_target="tpu_custom_call" | custom-call | tf_op jit(solution)/shard_map/project_near_half/pallas_call | solution.py:725
  48.4 0.0 collective-permute-done.2.refs_0_
  48.5 0.1 collective-permute-start.5
  48.5 5.8 %project_far_quarter.1 = (f32[512,896]{1,0:T(8,128)}, f32[512,256]{1,0:T(8,128)}, f32[512,32]{1,0:T(8,128)}) custom-call(s32[1]{0:T(128)} %bitcast.refs_0_.place_ref, bf16[512,896]{1,0:T(8,128)(2,1)} %in_order.3.x3, bf16[3584,896]{1,0:T(8,128)(2,1)} %refs_3_.5, bf16[3584,128]{1,0:T(8,128)(2,1)} %refs_4_.7, bf16[3584,128]{1,0:T(8,128)(2,1)} %refs_5_.5, ...), custom_call_target="tpu_custom_call" | custom-call | tf_op jit(solution)/shard_map/project_far_quarter/pallas_call | solution.py:740
  54.4 0.0 collective-permute-done.5.refs_2_
  54.4 0.8 all-to-all-done.1.refs_11_
  55.2 0.0 copy-start.3
  55.2 0.0 copy-start
  55.2 26.3 %span_attention.1 = (f32[40,512]{1,0:T(8,128)}, f32[72,512]{1,0:T(8,128)}, f32[8,16,128]{2,1,0:T(8,128)}) custom-call(s32[1]{0:T(128)} %bitcast.refs_0_.place_ref, s32[4]{0:T(128)} %refs_1_.9, bf16[512,896]{1,0:T(8,128)(2,1)} %collective-permute-done.5.refs_2_, bf16[3584,896]{1,0:T(8,128)(2,1)} %refs_3_.5, bf16[3584,128]{1,0:T(8,128)(2,1)} %refs_4_.7, ...), custom_call_target="tpu_custom_call" | custom-call | flops 10569646080 | bytes 1835008 | tf_op jit(solution)/shard_map/span_attention/pallas_call | solution.py:750
  81.5 0.0 copy-start.1
  81.5 5.4 %all-to-all-start.2 = ((f32[8,16,128]{2,1,0:T(8,128)}), f32[8,16,128]{2,1,0:T(8,128)S(1)}, u32[]{:S(2)}, u32[]{:S(2)}) async-start(f32[8,16,128]{2,1,0:T(8,128)} %get-tuple-element.47), calls=%async_computation.2 | async-start | bytes 131072 | tf_op jit(solution)/shard_map/all_to_all | solution.py:791
  86.9 1.0 collective-permute-start.8
  87.9 0.9 collective-permute-start.7
  88.8 0.0 collective-permute-start.6
  88.8 5.0 %all-to-all-done.2.refs_1_ = f32[8,16,128]{2,1,0:T(8,128)S(1)} async-done(((f32[8,16,128]{2,1,0:T(8,128)}), f32[8,16,128]{2,1,0:T(8,128)S(1)}, u32[]{:S(2)}, u32[]{:S(2)}) %all-to-all-start.2) | async-done | bytes 65568 | tf_op jit(solution)/shard_map/all_to_all | solution.py:791
  93.8 0.0 copy-done.3
  93.8 0.0 copy-start.2
  93.8 0.9 copy-done.2
  94.7 0.8 owned_cotangent.1
  95.5 0.0 collective-permute-done.8.c3
  95.5 0.0 collective-permute-done.7.c2
  95.5 0.0 collective-permute-done.6.c1
  95.5 0.0 copy-done
  95.5 0.8 first_down.1
  96.3 0.4 collective-permute-start.12
  96.7 0.2 collective-permute-start.11
  96.9 1.0 collective-permute-start.10
  97.9 0.7 collective-permute-start.9
  98.6 1.6 %collective-permute-done.11.c3 = f32[16,512]{1,0:T(8,128)S(1)} collective-permute-done((f32[16,512]{1,0:T(8,128)S(1)}, f32[16,512]{1,0:T(8,128)S(1)}, u32[]{:S(2)}, u32[]{:S(2)}) %collective-permute-start.11) | collective-permute-done | bytes 32800 | tf_op jit(solution)/shard_map/ppermute | solution.py:590
  100.1 0.9 collective-permute-done.10.c2
  101.0 0.0 collective-permute-done.9.c1
  101.0 0.2 collective-permute-done.12.q1
  101.2 0.0 copy-done.1
  101.2 0.3 second_down.1
  101.4 1.3 %collective-permute-start.13 = (f32[16,1920]{1,0:T(8,128)S(1)}, f32[16,1920]{1,0:T(8,128)S(1)}, u32[]{:S(2)}, u32[]{:S(2)}) collective-permute-start(f32[16,1920]{1,0:T(8,128)S(1)} %get-tuple-element.55.q0), channel_id=1, source_target_pairs={{0,8},{4,12},{8,0},{12,4},{16,24},{20,28},{24,16},{28,20},{1,9},{5... | collective-permute-start | bytes 368648 | tf_op jit(solution)/shard_map/ppermute | solution.py:590
  102.8 0.7 collective-permute-start.14
  103.5 3.5 %collective-permute-done.14.v1 = f32[16,896]{1,0:T(8,128)S(1)} collective-permute-done((f32[16,896]{1,0:T(8,128)S(1)}, f32[16,896]{1,0:T(8,128)S(1)}, u32[]{:S(2)}, u32[]{:S(2)}) %collective-permute-start.14) | collective-permute-done | bytes 57376 | tf_op jit(solution)/shard_map/ppermute | solution.py:590
  106.9 0.0 collective-permute-done.13.q1
  107.0 2.4 %collective-permute-start.15 = (bf16[16,2816]{1,0:T(8,128)(2,1)S(1)}, bf16[16,2816]{1,0:T(8,128)(2,1)S(1)}, u32[]{:S(2)}, u32[]{:S(2)}) collective-permute-start(bf16[16,2816]{1,0:T(8,128)(2,1)S(1)} %get-tuple-element.57.here_ref), channel_id=1, source_target_pairs={{0,16},{4,20},{8,24},{12,28},{16,0},{20,4},{24,8},{28,12},{1,17},{... | collective-permute-start | bytes 270344 | tf_op jit(solution)/shard_map/ppermute | solution.py:590
  109.4 1.0 collective-permute-start.17
  110.4 0.1 collective-permute-start.16
  110.5 4.5 %collective-permute-done.17.v3 = bf16[16,896]{1,0:T(8,128)(2,1)S(1)} collective-permute-done((bf16[16,896]{1,0:T(8,128)(2,1)S(1)}, bf16[16,896]{1,0:T(8,128)(2,1)S(1)}, u32[]{:S(2)}, u32[]{:S(2)}) %collective-permute-start.17) | collective-permute-done | bytes 28704 | tf_op jit(solution)/shard_map/ppermute | solution.py:590
  115.1 0.0 collective-permute-done.16.v1
  115.1 0.0 collective-permute-done.15.there_ref
  115.1 0.7 finish_outputs.1
  (3 shorter events, 0.0 us)
Async XLA Ops:
  0.6 3.3 %collective-permute-start = (bf16[512,896]{1,0:T(8,128)(2,1)}, bf16[512,896]{1,0:T(8,128)(2,1)}, u32[]{:S(2)}, u32[]{:S(2)}) collective-permute-start(bf16[512,896]{1,0:T(8,128)(2,1)} %memory_ref.1), channel_id=1, source_target_pairs={{0,1},{1,0},{2,3},{3,2},{4,5},{5,4},{6,7},{7,6},{8,9},{9,8},{10,11... | collective-permute-start | bytes 2752520 | tf_op jit(solution)/shard_map/ppermute | solution.py:590
  1.1 23.9 %collective-permute-start.3 = (bf16[512,896]{1,0:T(8,128)(2,1)}, bf16[512,896]{1,0:T(8,128)(2,1)}, u32[]{:S(2)}, u32[]{:S(2)}) collective-permute-start(bf16[512,896]{1,0:T(8,128)(2,1)} %memory_ref.1), channel_id=1, source_target_pairs={{0,2},{1,3},{2,0},{3,1},{4,6},{5,7},{6,4},{7,5},{8,10},{9,11},{10,... | collective-permute-start | bytes 2752520 | tf_op jit(solution)/shard_map/ppermute | solution.py:590
  3.7 21.3 %collective-permute-start.1 = (bf16[512,896]{1,0:T(8,128)(2,1)}, bf16[512,896]{1,0:T(8,128)(2,1)}, u32[]{:S(2)}, u32[]{:S(2)}) collective-permute-start(bf16[512,896]{1,0:T(8,128)(2,1)} %slab_ref.1), channel_id=1, source_target_pairs={{0,1},{1,0},{2,3},{3,2},{4,5},{5,4},{6,7},{7,6},{8,9},{9,8},{10,11... | collective-permute-start | bytes 2752520 | tf_op jit(solution)/shard_map/ppermute | solution.py:590
  25.0 4.8 %collective-permute-start.4 = (bf16[512,896]{1,0:T(8,128)(2,1)}, bf16[512,896]{1,0:T(8,128)(2,1)}, u32[]{:S(2)}, u32[]{:S(2)}) collective-permute-start(bf16[512,896]{1,0:T(8,128)(2,1)} %in_order.2.x2), channel_id=1, source_target_pairs={{0,1},{1,0},{2,3},{3,2},{4,5},{5,4},{6,7},{7,6},{8,9},{9,8},{10,11... | collective-permute-start | bytes 2752520 | tf_op jit(solution)/shard_map/ppermute | solution.py:590
  25.0 23.4 %collective-permute-start.2 = (bf16[512,896]{1,0:T(8,128)(2,1)}, bf16[512,896]{1,0:T(8,128)(2,1)}, u32[]{:S(2)}, u32[]{:S(2)}) collective-permute-start(bf16[512,896]{1,0:T(8,128)(2,1)} %collective-permute-done.1.x1), channel_id=1, source_target_pairs={{0,2},{1,3},{2,0},{3,1},{4,6},{5,7},{6,4},{7,5},{8,10},{9,11},{10,... | collective-permute-start | bytes 2752520 | tf_op jit(solution)/shard_map/ppermute | solution.py:590
  33.7 21.5 %all-to-all-start.1 = ((bf16[8,272,128]{2,1,0:T(8,128)(2,1)}), bf16[8,272,128]{2,1,0:T(8,128)(2,1)}, u32[]{:S(2)}, u32[]{:S(2)}) async-start(bf16[8,272,128]{2,1,0:T(8,128)(2,1)} %memory_pairs.1.refs_7_), calls=%async_computation.1 | async-start | bytes 1114112 | tf_op jit(solution)/shard_map/all_to_all | solution.py:724
  48.5 5.9 %collective-permute-start.5 = (bf16[512,896]{1,0:T(8,128)(2,1)}, bf16[512,896]{1,0:T(8,128)(2,1)}, u32[]{:S(2)}, u32[]{:S(2)}) collective-permute-start(bf16[512,896]{1,0:T(8,128)(2,1)} %in_order.3.x3), channel_id=1, source_target_pairs={{0,1},{1,0},{2,3},{3,2},{4,5},{5,4},{6,7},{7,6},{8,9},{9,8},{10,11... | collective-permute-start | bytes 2752520 | tf_op jit(solution)/shard_map/ppermute | solution.py:590
  55.2 38.7 %copy-start.3 = (s32[8]{0:T(128)S(1)}, s32[8]{0:T(128)}, u32[]{:S(2)}) copy-start(s32[8]{0:T(128)} %reduce.refs_1_.refs_0_) | copy-start | bytes 100
  55.2 40.4 %copy-start = (bf16[512,896]{1,0:T(8,128)(2,1)S(1)}, bf16[512,896]{1,0:T(8,128)(2,1)}, u32[]{:S(2)}) copy-start(bf16[512,896]{1,0:T(8,128)(2,1)} %slab_ref.1) | copy-start | bytes 2752516
  81.5 19.7 %copy-start.1 = (bf16[512,896]{1,0:T(8,128)(2,1)S(1)}, bf16[512,896]{1,0:T(8,128)(2,1)}, u32[]{:S(2)}) copy-start(bf16[512,896]{1,0:T(8,128)(2,1)} %memory_ref.1) | copy-start | bytes 2752516
  81.5 12.3 %all-to-all-start.2 = ((f32[8,16,128]{2,1,0:T(8,128)}), f32[8,16,128]{2,1,0:T(8,128)S(1)}, u32[]{:S(2)}, u32[]{:S(2)}) async-start(f32[8,16,128]{2,1,0:T(8,128)} %get-tuple-element.47), calls=%async_computation.2 | async-start | bytes 131072 | tf_op jit(solution)/shard_map/all_to_all | solution.py:791
  86.9 8.6 %collective-permute-start.8 = (f32[40,512]{1,0:T(8,128)}, f32[40,512]{1,0:T(8,128)S(1)}, u32[]{:S(2)}, u32[]{:S(2)}) collective-permute-start(f32[40,512]{1,0:T(8,128)} %get-tuple-element.50), channel_id=1, source_target_pairs={{0,3},{1,2},{2,1},{3,0},{4,7},{5,6},{6,5},{7,4},{8,11},{9,10},{10,... | collective-permute-start | bytes 245768 | tf_op jit(solution)/shard_map/ppermute | solution.py:590
  87.9 7.6 %collective-permute-start.7 = (f32[40,512]{1,0:T(8,128)}, f32[40,512]{1,0:T(8,128)S(1)}, u32[]{:S(2)}, u32[]{:S(2)}) collective-permute-start(f32[40,512]{1,0:T(8,128)} %get-tuple-element.50), channel_id=1, source_target_pairs={{0,2},{1,3},{2,0},{3,1},{4,6},{5,7},{6,4},{7,5},{8,10},{9,11},{10,... | collective-permute-start | bytes 245768 | tf_op jit(solution)/shard_map/ppermute | solution.py:590
  88.8 6.7 %collective-permute-start.6 = (f32[40,512]{1,0:T(8,128)}, f32[40,512]{1,0:T(8,128)S(1)}, u32[]{:S(2)}, u32[]{:S(2)}) collective-permute-start(f32[40,512]{1,0:T(8,128)} %get-tuple-element.50), channel_id=1, source_target_pairs={{0,1},{1,0},{2,3},{3,2},{4,5},{5,4},{6,7},{7,6},{8,9},{9,8},{10,11... | collective-permute-start | bytes 245768 | tf_op jit(solution)/shard_map/ppermute | solution.py:590
  93.8 0.9 copy-start.2
  96.3 4.9 %collective-permute-start.12 = (f32[16,1920]{1,0:T(8,128)S(1)}, f32[16,1920]{1,0:T(8,128)S(1)}, u32[]{:S(2)}, u32[]{:S(2)}) collective-permute-start(f32[16,1920]{1,0:T(8,128)S(1)} %get-tuple-element.54.q0), channel_id=1, source_target_pairs={{0,4},{4,0},{8,12},{12,8},{16,20},{20,16},{24,28},{28,24},{1,5},{5... | collective-permute-start | bytes 368648 | tf_op jit(solution)/shard_map/ppermute | solution.py:590
  96.7 3.4 %collective-permute-start.11 = (f32[16,512]{1,0:T(8,128)S(1)}, f32[16,512]{1,0:T(8,128)S(1)}, u32[]{:S(2)}, u32[]{:S(2)}) collective-permute-start(f32[16,512]{1,0:T(8,128)S(1)} %get-tuple-element.52.c0), channel_id=1, source_target_pairs={{0,3},{1,2},{2,1},{3,0},{4,7},{5,6},{6,5},{7,4},{8,11},{9,10},{10,... | collective-permute-start | bytes 98312 | tf_op jit(solution)/shard_map/ppermute | solution.py:590
  96.9 4.1 %collective-permute-start.10 = (f32[16,512]{1,0:T(8,128)S(1)}, f32[16,512]{1,0:T(8,128)S(1)}, u32[]{:S(2)}, u32[]{:S(2)}) collective-permute-start(f32[16,512]{1,0:T(8,128)S(1)} %get-tuple-element.52.c0), channel_id=1, source_target_pairs={{0,2},{1,3},{2,0},{3,1},{4,6},{5,7},{6,4},{7,5},{8,10},{9,11},{10,... | collective-permute-start | bytes 98312 | tf_op jit(solution)/shard_map/ppermute | solution.py:590
  97.9 3.1 %collective-permute-start.9 = (f32[16,512]{1,0:T(8,128)S(1)}, f32[16,512]{1,0:T(8,128)S(1)}, u32[]{:S(2)}, u32[]{:S(2)}) collective-permute-start(f32[16,512]{1,0:T(8,128)S(1)} %get-tuple-element.52.c0), channel_id=1, source_target_pairs={{0,1},{1,0},{2,3},{3,2},{4,5},{5,4},{6,7},{7,6},{8,9},{9,8},{10,11... | collective-permute-start | bytes 98312 | tf_op jit(solution)/shard_map/ppermute | solution.py:590
  101.4 5.5 %collective-permute-start.13 = (f32[16,1920]{1,0:T(8,128)S(1)}, f32[16,1920]{1,0:T(8,128)S(1)}, u32[]{:S(2)}, u32[]{:S(2)}) collective-permute-start(f32[16,1920]{1,0:T(8,128)S(1)} %get-tuple-element.55.q0), channel_id=1, source_target_pairs={{0,8},{4,12},{8,0},{12,4},{16,24},{20,28},{24,16},{28,20},{1,9},{5... | collective-permute-start | bytes 368648 | tf_op jit(solution)/shard_map/ppermute | solution.py:590
  102.8 4.2 %collective-permute-start.14 = (f32[16,896]{1,0:T(8,128)S(1)}, f32[16,896]{1,0:T(8,128)S(1)}, u32[]{:S(2)}, u32[]{:S(2)}) collective-permute-start(f32[16,896]{1,0:T(8,128)S(1)} %get-tuple-element.56.v0), channel_id=1, source_target_pairs={{0,4},{4,0},{8,12},{12,8},{16,20},{20,16},{24,28},{28,24},{1,5},{5... | collective-permute-start | bytes 172040 | tf_op jit(solution)/shard_map/ppermute | solution.py:590
  107.0 8.1 %collective-permute-start.15 = (bf16[16,2816]{1,0:T(8,128)(2,1)S(1)}, bf16[16,2816]{1,0:T(8,128)(2,1)S(1)}, u32[]{:S(2)}, u32[]{:S(2)}) collective-permute-start(bf16[16,2816]{1,0:T(8,128)(2,1)S(1)} %get-tuple-element.57.here_ref), channel_id=1, source_target_pairs={{0,16},{4,20},{8,24},{12,28},{16,0},{20,4},{24,8},{28,12},{1,17},{... | collective-permute-start | bytes 270344 | tf_op jit(solution)/shard_map/ppermute | solution.py:590
  109.4 5.7 %collective-permute-start.17 = (bf16[16,896]{1,0:T(8,128)(2,1)S(1)}, bf16[16,896]{1,0:T(8,128)(2,1)S(1)}, u32[]{:S(2)}, u32[]{:S(2)}) collective-permute-start(bf16[16,896]{1,0:T(8,128)(2,1)S(1)} %get-tuple-element.58), channel_id=1, source_target_pairs={{0,24},{4,28},{8,16},{12,20},{16,8},{20,12},{24,0},{28,4},{1,25},{... | collective-permute-start | bytes 86024 | tf_op jit(solution)/shard_map/ppermute | solution.py:590
  110.4 4.7 %collective-permute-start.16 = (bf16[16,896]{1,0:T(8,128)(2,1)S(1)}, bf16[16,896]{1,0:T(8,128)(2,1)S(1)}, u32[]{:S(2)}, u32[]{:S(2)}) collective-permute-start(bf16[16,896]{1,0:T(8,128)(2,1)S(1)} %get-tuple-element.58), channel_id=1, source_target_pairs={{0,8},{4,12},{8,0},{12,4},{16,24},{20,28},{24,16},{28,20},{1,9},{5... | collective-permute-start | bytes 86024 | tf_op jit(solution)/shard_map/ppermute | solution.py:590
